TPU v7x, 128 devices: a whole 4x4x4 slice. The times are simulated.
128 devices in a mesh: rep: 8 (over x, y_hi), shard: 16 (over z, y_lo, core).
Axes of the slice: x: 4, y: 4 (y_hi: 2, y_lo: 2; y = y_hi * 2 + y_lo), z: 4, core: 2. Of those that a mesh axis runs over, the one named last changes fastest.
Arguments:
- layer_input: bfloat16 [24576, 1536], P(('rep', 'shard')), may hold values from -6 to 6
- grad_output: bfloat16 [24576, 1536], P(('rep', 'shard')), may hold values from -24 to 24
- routes: int32 [24576, 8], P(('rep', 'shard')), may hold values from 0 to 9, all different within a row
- route_logits: float32 [24576, 8], P(('rep', 'shard')), may hold values from -3 to 3
- norm_gains: bfloat16 [2, 1536], P(None, 'shard'), may hold values from 0.5 to 1.5
- inward: bfloat16 [1536, 2560], P('shard')
- outward: bfloat16 [1536, 1536], P('shard'), may hold values from -0.875 to 0.875
- lifting: bfloat16 [1536, 10, 1024], P('shard'), may hold values from -0.15625 to 0.15625
- lowering: bfloat16 [512, 10, 1536], P('shard'), may hold values from -1 to 1
- mean_gains: bfloat16 [2, 1536], P(None, 'shard')
- mean_inward: bfloat16 [1536, 2560], P('shard')
- mean_outward: bfloat16 [1536, 1536], P('shard')
- mean_lifting: bfloat16 [1536, 10, 1024], P('shard')
- mean_lowering: bfloat16 [512, 10, 1536], P('shard')
- square_gains: bfloat16 [2, 1536], P(None, 'shard'), as said below
- square_inward: bfloat16 [1536, 2560], P('shard'), as said below
- square_outward: bfloat16 [1536, 1536], P('shard'), as said below
- square_lifting: bfloat16 [1536, 10, 1024], P('shard'), as said below
- square_lowering: bfloat16 [512, 10, 1536], P('shard'), as said below
Outputs:
- layer_output: float32 [24576, 1536], P(('rep', 'shard'))
- input_grad: float32 [24576, 1536], P(('rep', 'shard'))
- moment_gains: float32 [2, 1536], P(None, 'shard')
- moment_inward: float32 [1536, 2560], P('shard')
- moment_outward: float32 [1536, 1536], P('shard')
- moment_lifting: float32 [1536, 10, 1024], P('shard')
- moment_lowering: float32 [512, 10, 1536], P('shard')
- variance_gains: float32 [2, 1536], P(None, 'shard')
- variance_inward: float32 [1536, 2560], P('shard')
- variance_outward: float32 [1536, 1536], P('shard')
- variance_lifting: float32 [1536, 10, 1024], P('shard')
- variance_lowering: float32 [512, 10, 1536], P('shard')
- updated_gains: float32 [2, 1536], P(None, 'shard')
- updated_inward: float32 [1536, 2560], P('shard')
- updated_outward: float32 [1536, 1536], P('shard')
- updated_lifting: float32 [1536, 10, 1024], P('shard')
- updated_lowering: float32 [512, 10, 1536], P('shard')
Inputs may be any that keep to these rules, and one draw needn't show every extreme that they name: `routes`: each row names 8 different experts; every expert is named by some row. `square_gains`: Positive. `square_inward`: Positive. `square_outward`: Positive. `square_lifting`: Positive. `square_lowering`: Positive.
All inputs are finite; a program needn't handle non-finite values.
Results may differ from a plain program's by a relative error of at most 0.017.
Values may be sent and summed in bfloat16 or wider, within the bound.
A program may use at most 384 MiB of HBM per device.

v0:
```python
import jax
import jax.numpy as jnp
from jax import lax
from jax.sharding import PartitionSpec as P

HEADS = 24
KV_HEADS = 8
HEAD = 64
FF_EXP = 512
EXPERTS = 10
STEP = 10


norm_epsilon = 1e-06
beta_one = 0.9
beta_two = 0.95
adam_epsilon = 1e-08
weight_decay = 0.1
rate_gains = 0.5
rate_inward = 0.05
rate_outward = 0.3
rate_lifting = 0.05
rate_lowering = 0.3


def angles(position):
    half_width = HEAD // 2
    frequency = 10000.0 ** (-(2.0 * jnp.arange(half_width).astype(jnp.float32)) / HEAD)
    phases = position.astype(jnp.float32)[:, None] * frequency[None, :]
    return (jnp.cos(phases)[:, None, :], jnp.sin(phases)[:, None, :])


def rotate(heads, cosine, sine_table):
    half_width = HEAD // 2
    first = heads[..., :half_width]
    second = heads[..., half_width:]
    return jnp.concatenate(
        [first * cosine - second * sine_table, second * cosine + first * sine_table], -1
    )


def unrotate(heads, cosine, sine_table):
    half_width = HEAD // 2
    first = heads[..., :half_width]
    second = heads[..., half_width:]
    return jnp.concatenate(
        [first * cosine + second * sine_table, second * cosine - first * sine_table], -1
    )


def normalize(stream, gain):
    inverse = lax.rsqrt(jnp.mean(stream * stream, -1, keepdims=True) + norm_epsilon)
    unit_rows = stream * inverse
    return (unit_rows * gain, unit_rows, inverse)


def norm_back(grad_normed, unit_rows, inverse, gain):
    scaled = grad_normed * gain
    stream_grad = inverse * (scaled - unit_rows * jnp.mean(scaled * unit_rows, -1, keepdims=True))
    return (stream_grad, jnp.sum(grad_normed * unit_rows, 0))


def adam(weight, old_mean, square, gradient, step_rate, decay_rate):
    values = weight.astype(jnp.float32)
    moment = beta_one * old_mean.astype(jnp.float32) + (1.0 - beta_one) * gradient
    variance = beta_two * square.astype(jnp.float32) + (1.0 - beta_two) * gradient * gradient
    normed_step = (
        moment
        / (1.0 - beta_one**STEP)
        / (jnp.sqrt(variance / (1.0 - beta_two**STEP)) + adam_epsilon)
    )
    return (moment, variance, values - step_rate * (normed_step + decay_rate * values))


def per_device(
    layer_input,
    grad_output,
    routes,
    route_logits,
    norm_gains,
    inward,
    outward,
    lifting,
    lowering,
    mean_gains,
    mean_inward,
    mean_outward,
    mean_lifting,
    mean_lowering,
    square_gains,
    square_inward,
    square_outward,
    square_lifting,
    square_lowering,
):
    tokens = layer_input.shape[0]
    length = tokens * lax.axis_size("shard")
    attend_width = HEADS * HEAD
    key_width = KV_HEADS * HEAD
    groups = HEADS // KV_HEADS
    factor = HEAD ** (-0.5)
    position = lax.axis_index("shard") * tokens + jnp.arange(tokens, dtype=jnp.int32)
    allowed = jnp.arange(length, dtype=jnp.int32)[None, :] <= position[:, None]
    cosine, sine_table = angles(position)
    gains_all, inward_all, outward_all = (
        lax.all_gather(norm_gains, "shard", axis=1, tiled=True),
        lax.all_gather(inward, "shard", axis=0, tiled=True),
        lax.all_gather(outward, "shard", axis=0, tiled=True),
    )
    lifting_all, lowering_all = (
        lax.all_gather(lifting, "shard", axis=0, tiled=True),
        lax.all_gather(lowering, "shard", axis=0, tiled=True),
    )
    gain_values = gains_all.astype(jnp.float32)
    stream = layer_input.astype(jnp.float32)
    normed_one, unit_one, inverse_one = normalize(stream, gain_values[0])
    low_one = normed_one.astype(jnp.bfloat16)
    joined = jnp.dot(low_one, inward_all, preferred_element_type=jnp.float32)
    query_rows = rotate(
        joined[:, :attend_width].reshape(tokens, HEADS, HEAD), cosine, sine_table
    ).astype(jnp.bfloat16)
    key_rows = rotate(
        joined[:, attend_width : attend_width + key_width].reshape(tokens, KV_HEADS, HEAD),
        cosine,
        sine_table,
    )
    local_pairs = jnp.concatenate(
        [key_rows.reshape(tokens, key_width), joined[:, attend_width + key_width :]], 1
    ).astype(jnp.bfloat16)
    gathered = lax.all_gather(local_pairs, "shard", axis=0, tiled=True)
    key_heads = gathered[:, :key_width].reshape(length, KV_HEADS, HEAD).transpose(1, 0, 2)
    value_heads = gathered[:, key_width:].reshape(length, KV_HEADS, HEAD).transpose(1, 0, 2)
    query_heads = query_rows.reshape(tokens, KV_HEADS, groups, HEAD).transpose(1, 0, 2, 3)

    def probabilities(query_head, key_head):
        scores = (
            jnp.einsum("trd,sd->rts", query_head, key_head, preferred_element_type=jnp.float32)
            * factor
        )
        return jax.nn.softmax(jnp.where(allowed[None], scores, -1e30), axis=-1)

    def head_forward(operands):
        query_head, key_head, value_head = operands
        weights = probabilities(query_head, key_head).astype(jnp.bfloat16)
        return jnp.einsum("rts,sd->trd", weights, value_head, preferred_element_type=jnp.float32)

    attended = lax.map(head_forward, (query_heads, key_heads, value_heads))
    attended = attended.transpose(1, 0, 2, 3).reshape(tokens, attend_width).astype(jnp.bfloat16)
    mixed = stream + jnp.dot(attended, outward_all, preferred_element_type=jnp.float32)
    normed_two, unit_two, inverse_two = normalize(mixed, gain_values[1])
    low_two = normed_two.astype(jnp.bfloat16)
    gate_weights = jax.nn.softmax(route_logits, axis=-1)
    picked = routes[:, :, None] == jnp.arange(EXPERTS, dtype=jnp.int32)[None, None, :]
    combine = jnp.sum(jnp.where(picked, gate_weights[:, :, None], 0.0), axis=1)
    lifted = jnp.einsum("td,def->tef", low_two, lifting_all, preferred_element_type=jnp.float32)
    gate_part = lifted[..., :FF_EXP]
    up_part = lifted[..., FF_EXP:]
    squashed = jax.nn.sigmoid(gate_part)
    activation = (gate_part * squashed * up_part).astype(jnp.bfloat16)
    expert_out = jnp.einsum(
        "tef,fed->ted", activation, lowering_all, preferred_element_type=jnp.float32
    )
    layer_output = mixed + jnp.sum(combine[:, :, None] * expert_out, axis=1)
    grad_stream = grad_output.astype(jnp.float32)
    grad_expert = (combine[:, :, None] * grad_stream[:, None, :]).astype(jnp.bfloat16)
    ordered = lax.optimization_barrier(
        (grad_expert, norm_gains, inward, outward, lifting, lowering)
    )
    gains_back, inward_back, outward_back = (
        lax.all_gather(ordered[1], "shard", axis=1, tiled=True),
        lax.all_gather(ordered[2], "shard", axis=0, tiled=True),
        lax.all_gather(ordered[3], "shard", axis=0, tiled=True),
    )
    lifting_back, lowering_back = (
        lax.all_gather(ordered[4], "shard", axis=0, tiled=True),
        lax.all_gather(ordered[5], "shard", axis=0, tiled=True),
    )
    back_gains = gains_back.astype(jnp.float32)
    grad_act = jnp.einsum(
        "ted,fed->tef", grad_expert, lowering_back, preferred_element_type=jnp.float32
    )
    grad_gate = grad_act * up_part * squashed * (1.0 + gate_part * (1.0 - squashed))
    grad_up = grad_act * gate_part * squashed
    grad_lift = jnp.concatenate([grad_gate, grad_up], -1).astype(jnp.bfloat16)
    grad_normed_two = jnp.einsum(
        "tef,def->td", grad_lift, lifting_back, preferred_element_type=jnp.float32
    )
    rows_used = low_two
    owned_lifting = lax.psum_scatter(
        jnp.einsum("td,tef->def", rows_used, grad_lift, preferred_element_type=jnp.float32),
        "shard",
        scatter_dimension=0,
        tiled=True,
    )
    rows_used = activation
    owned_lowering = lax.psum_scatter(
        jnp.einsum("tef,ted->fed", rows_used, grad_expert, preferred_element_type=jnp.float32),
        "shard",
        scatter_dimension=0,
        tiled=True,
    )
    grad_mixed_norm, gain_two_grad = norm_back(
        grad_normed_two, unit_two, inverse_two, back_gains[1]
    )
    grad_mixed = grad_stream + grad_mixed_norm
    low_mixed = grad_mixed.astype(jnp.bfloat16)
    full_outward = jnp.einsum("ta,td->ad", attended, low_mixed, preferred_element_type=jnp.float32)
    grad_attended = jnp.einsum(
        "td,ad->ta", low_mixed, outward_back, preferred_element_type=jnp.float32
    ).astype(jnp.bfloat16)
    grad_heads = grad_attended.reshape(tokens, KV_HEADS, groups, HEAD).transpose(1, 0, 2, 3)

    def head_backward(operands):
        query_head, key_head, value_head, grad_head = operands
        prob = probabilities(query_head, key_head)
        low_prob = prob.astype(jnp.bfloat16)
        grad_prob = jnp.einsum(
            "trd,sd->rts", grad_head, value_head, preferred_element_type=jnp.float32
        )
        grad_score = (prob * (grad_prob - jnp.sum(prob * grad_prob, -1, keepdims=True))).astype(
            jnp.bfloat16
        )
        grad_query = (
            jnp.einsum("rts,sd->trd", grad_score, key_head, preferred_element_type=jnp.float32)
            * factor
        )
        grad_key = (
            jnp.einsum("rts,trd->sd", grad_score, query_head, preferred_element_type=jnp.float32)
            * factor
        )
        grad_value = jnp.einsum(
            "rts,trd->sd", low_prob, grad_head, preferred_element_type=jnp.float32
        )
        return (grad_query, grad_key, grad_value)

    query_grads, key_grads, value_grads = lax.map(
        head_backward, (query_heads, key_heads, value_heads, grad_heads)
    )
    query_grads = query_grads.transpose(1, 0, 2, 3).reshape(tokens, HEADS, HEAD)
    spread_pairs = jnp.concatenate(
        [
            key_grads.transpose(1, 0, 2).reshape(length, key_width),
            value_grads.transpose(1, 0, 2).reshape(length, key_width),
        ],
        1,
    )
    own_pairs = lax.psum_scatter(spread_pairs, "shard", scatter_dimension=0, tiled=True)
    grad_joined = jnp.concatenate(
        [
            unrotate(query_grads, cosine, sine_table).reshape(tokens, attend_width),
            unrotate(
                own_pairs[:, :key_width].reshape(tokens, KV_HEADS, HEAD), cosine, sine_table
            ).reshape(tokens, key_width),
            own_pairs[:, key_width:],
        ],
        1,
    ).astype(jnp.bfloat16)
    grad_normed_one = jnp.einsum(
        "tc,dc->td", grad_joined, inward_back, preferred_element_type=jnp.float32
    )
    full_inward = jnp.einsum("td,tc->dc", low_one, grad_joined, preferred_element_type=jnp.float32)
    grad_stream_norm, gain_one_grad = norm_back(
        grad_normed_one, unit_one, inverse_one, back_gains[0]
    )
    input_grad = grad_mixed + grad_stream_norm
    full_gains = jnp.stack([gain_one_grad, gain_two_grad])
    owned_gains, owned_inward, owned_outward = (
        lax.psum_scatter(full_gains, "shard", scatter_dimension=1, tiled=True),
        lax.psum_scatter(full_inward, "shard", scatter_dimension=0, tiled=True),
        lax.psum_scatter(full_outward, "shard", scatter_dimension=0, tiled=True),
    )
    owned_gains, owned_inward, owned_outward, owned_lifting, owned_lowering = lax.psum(
        (owned_gains, owned_inward, owned_outward, owned_lifting, owned_lowering), "rep"
    )
    new_gains = adam(norm_gains, mean_gains, square_gains, owned_gains, rate_gains, 0.0)
    new_inward = adam(inward, mean_inward, square_inward, owned_inward, rate_inward, weight_decay)
    new_outward = adam(
        outward, mean_outward, square_outward, owned_outward, rate_outward, weight_decay
    )
    new_lifting = adam(
        lifting, mean_lifting, square_lifting, owned_lifting, rate_lifting, weight_decay
    )
    new_lowering = adam(
        lowering, mean_lowering, square_lowering, owned_lowering, rate_lowering, weight_decay
    )
    return (
        layer_output,
        input_grad,
        new_gains[0],
        new_inward[0],
        new_outward[0],
        new_lifting[0],
        new_lowering[0],
        new_gains[1],
        new_inward[1],
        new_outward[1],
        new_lifting[1],
        new_lowering[1],
        new_gains[2],
        new_inward[2],
        new_outward[2],
        new_lifting[2],
        new_lowering[2],
    )


def solution(mesh):
    return jax.shard_map(
        per_device,
        mesh=mesh,
        in_specs=(
            P(("rep", "shard"), None),
            P(("rep", "shard"), None),
            P(("rep", "shard"), None),
            P(("rep", "shard"), None),
            P(None, "shard"),
            P("shard", None),
            P("shard", None),
            P("shard", None, None),
            P("shard", None, None),
            P(None, "shard"),
            P("shard", None),
            P("shard", None),
            P("shard", None, None),
            P("shard", None, None),
            P(None, "shard"),
            P("shard", None),
            P("shard", None),
            P("shard", None, None),
            P("shard", None, None),
        ),
        out_specs=(
            P(("rep", "shard"), None),
            P(("rep", "shard"), None),
            P(None, "shard"),
            P("shard", None),
            P("shard", None),
            P("shard", None, None),
            P("shard", None, None),
            P(None, "shard"),
            P("shard", None),
            P("shard", None),
            P("shard", None, None),
            P("shard", None, None),
            P(None, "shard"),
            P("shard", None),
            P("shard", None),
            P("shard", None, None),
            P("shard", None, None),
        ),
        check_vma=False,
    )
```

profile of v0, /device:TPU:1, one launch (start us, length us, event | category | flops | bytes accessed | tf_op | source)
XLA Modules:
  0.0 2965.2 jit_solution(18203793224632785100)
XLA Ops:
  8.0 22.3 all-gather
  32.0 31.1 %all-gather.12.cloned.1.call-done = bf16[1536,2560]{1,0:T(8,128)(2,1)} async-done(((bf16[96,2560]{1,0:T(8,128)(2,1)}), bf16[1536,2560]{1,0:T(8,128)(2,1)}) %all-gather.12.cloned.1.call-update) | async-done | bytes 7864336 | tf_op jit(solution)/shard_map/all_gather | solution.py:107
  75.9 19.0 all-gather.1
  100.0 14.5 all-gather.14.cloned.1.call-done
  127.3 75.2 %while.28 = (s32[]{:T(128)}, bf16[8,192,3,64]{1,3,2,0:T(8,128)(2,1)}, bf16[8,3072,64]{1,2,0:T(8,128)(2,1)}, bf16[8,3072,64]{1,2,0:T(8,128)(2,1)}, bf16[8,192,3,64]{1,3,2,0:T(8,128)(2,1)}, /*index=5*/s32[192]{0:T(256)S(1)}) while((s32[]{:T(128)}, bf16[8,192,3,64]{1,3,2,0:T(8,128)(2,1)}, bf16[8,3072,64]{1,2,0:T(8,128)(2,1)}, ...), condition=%wide.region_4.5_spmd.clone.clone, body=%wide.region_1.4_spmd.clone.sunk.clone | while | flops 695999040 | bytes 3350861 | solution.py:147
  131.4 5.3 fusion.253
  140.8 5.3 fusion.253
  150.2 5.3 fusion.253
  159.6 5.3 fusion.253
  169.0 5.3 fusion.253
  178.4 5.3 fusion.253
  187.8 5.3 fusion.253
  197.2 5.3 fusion.253
  206.4 111.6 %all-gather.18.cloned.1.call-done = bf16[1536,10,1024]{2,0,1:T(8,128)(2,1)} async-done(((bf16[96,10,1024]{2,0,1:T(8,128)(2,1)}), bf16[1536,10,1024]{2,0,1:T(8,128)(2,1)}) %all-gather.18.cloned.1.call-update) | async-done | bytes 31457296 | tf_op jit(solution)/shard_map/all_gather | solution.py:111
  317.9 15.8 fusion.159
  333.8 73.4 %all-gather.22.cloned.1.call-done = bf16[512,10,1536]{2,0,1:T(8,128)(2,1)} async-done(((bf16[32,10,1536]{2,0,1:T(8,128)(2,1)}), bf16[512,10,1536]{2,0,1:T(8,128)(2,1)}) %all-gather.22.cloned.1.call-update) | async-done | bytes 15728656 | tf_op jit(solution)/shard_map/all_gather | solution.py:176
  407.2 13.0 fusion.124
  420.2 150.3 %all-gather.24.cloned.1.call-done = bf16[1536,10,1024]{2,0,1:T(8,128)(2,1)} async-done(((bf16[96,10,1024]{2,0,1:T(8,128)(2,1)}), bf16[1536,10,1024]{2,0,1:T(8,128)(2,1)}) %all-gather.24.cloned.1.call-update) | async-done | bytes 31457296 | tf_op jit(solution)/shard_map/all_gather | solution.py:175
  570.5 17.8 multiply_reduce_fusion
  588.8 71.0 %all-gather.20.cloned.1.call-done = bf16[512,10,1536]{2,0,1:T(8,128)(2,1)} async-done(((bf16[32,10,1536]{2,0,1:T(8,128)(2,1)}), bf16[512,10,1536]{2,0,1:T(8,128)(2,1)}) %all-gather.20.cloned.1.call-update) | async-done | bytes 15728656 | tf_op jit(solution)/shard_map/all_gather | solution.py:112
  659.9 9.5 fusion.118
  670.9 30.3 %all-gather.26.cloned.1.call-done = bf16[1536,1536]{1,0:T(8,128)(2,1)} async-done(((bf16[96,1536]{1,0:T(8,128)(2,1)}), bf16[1536,1536]{1,0:T(8,128)(2,1)}) %all-gather.26.cloned.1.call-update) | async-done | bytes 4718608 | tf_op jit(solution)/shard_map/all_gather | solution.py:172
  706.5 192.7 %while.29 = (s32[]{:T(128)}, f32[8,192,3,64]{1,3,2,0:T(8,128)S(1)}, f32[8,3072,64]{1,2,0:T(8,128)}, f32[8,3072,64]{1,2,0:T(8,128)}, bf16[8,3072,64]{1,2,0:T(8,12...) while((s32[]{:T(128)}, f32[8,192,3,64]{1,3,2,0:T(8,128)S(1)}, ...), condition=%wide.region_15.16_spmd.clone.clone, body=%wide.region_11.15_spmd.clone.sunk.clone | while | flops 1388095488 | bytes 72864144 | solution.py:236
  707.1 6.4 fusion.264
  731.1 6.4 fusion.264
  755.2 6.4 fusion.264
  779.2 6.4 fusion.264
  803.3 6.4 fusion.264
  827.4 6.5 fusion.264
  851.4 6.5 fusion.264
  875.5 6.4 fusion.264
  899.2 11.3 pad_maximum_fusion
  910.5 12.6 copy.111
  925.1 13.3 convolution_bitcast_fusion.1
  938.4 39.1 %copy.109 = f32[512,10,1536]{2,1,0:T(8,128)} copy(f32[512,10,1536]{0,2,1:T(8,128)} %convolution_bitcast_fusion.1) | data formatting | bytes 62914560 | tf_op jit(solution)/shard_map/tef,ted->fed/transpose | solution.py:197
  985.8 75.7 %reduce-scatter.19.cloned.1.call-done = f32[192,1024]{1,0:T(8,128)} async-done(((f32[3072,1024]{1,0:T(8,128)}), f32[192,1024]{1,0:T(8,128)}) %reduce-scatter.19.cloned.1.call-update) | async-done | bytes 786448
  1064.7 8.9 fusion.149
  1074.9 26.0 fusion.127
  1101.7 12.0 all-gather.28.cloned.1.call-done
  1113.7 7.1 fusion.140
  1122.0 512.7 %reduce-scatter.17.cloned.1.call-done = f32[32,10,1536]{2,1,0:T(8,128)} async-done(((f32[512,10,1536]{2,1,0:T(8,128)}), f32[32,10,1536]{2,1,0:T(8,128)}) %reduce-scatter.17.cloned.1.call-update) | async-done | bytes 1966096 | tf_op jit(solution)/shard_map/reduce_scatter | solution.py:196
  1639.0 105.1 %reduce-scatter.13.cloned.1.call-done = f32[96,1536]{1,0:T(8,128)} async-done(((f32[1536,1536]{1,0:T(8,128)}), f32[96,1536]{1,0:T(8,128)}) %reduce-scatter.13.cloned.1.call-update) | async-done | bytes 589840 | tf_op jit(solution)/shard_map/reduce_scatter | solution.py:270
  1744.2 173.0 %reduce-scatter.11.cloned.1.call-done = f32[96,2560]{1,0:T(8,128)} async-done(((f32[1536,2560]{1,0:T(8,128)}), f32[96,2560]{1,0:T(8,128)}) %reduce-scatter.11.cloned.1.call-update) | async-done | bytes 983056 | tf_op jit(solution)/shard_map/reduce_scatter | solution.py:269
  1917.2 647.4 %reduce-scatter.15.cloned.1.call-done = f32[96,10,1024]{2,0,1:T(8,128)} async-done(((f32[1536,10,1024]{2,0,1:T(8,128)}), f32[96,10,1024]{2,0,1:T(8,128)}) %reduce-scatter.15.cloned.1.call-update) | async-done | bytes 3932176 | tf_op jit(solution)/shard_map/reduce_scatter | solution.py:189
  2567.2 58.0 %reduce-scatter.21.cloned.1.call-done = f32[96,2]{1,0:T(8,128)} async-done(((f32[1536,2]{1,0:T(8,128)}), f32[96,2]{1,0:T(8,128)}) %reduce-scatter.21.cloned.1.call-update) | async-done | bytes 784
  2626.1 21.0 psum.35
  2647.7 293.2 %all-reduce.3.cloned.1.call-done = (f32[96,2560]{1,0:T(8,128)}, f32[96,1536]{1,0:T(8,128)}, f32[96,10,1024]{2,0,1:T(8,128)}, f32[32,10,1536]{2,0,1:T(8,128)}) async-done(((f32[96,2560]{1,0:T(8,128)}, f32[96,1536]{1,0:T(8,128)}, f32[96,10,1024]{2,0,1:T(8,128)}, f32[32,10,1536]{2,0,1:T(8,128)}), (f32[96,2560]{1,0:T(8,128)}, f32[96,1536]{1,0:T(8,128)}, f32[96,10,1024]{2,0,1:T(8,128)}, ...) | async-done | bytes 7471120 | tf_op jit(solution)/shard_map/psum | solution.py:272
  2947.5 7.0 convert_subtract_fusion
  (313 shorter events, 252.5 us)
Async XLA Ops:
  7.2 55.9 %all-gather.12.cloned.1.call-start = ((), (), s32[]{:S(2)}) async-start(), calls=%async_computation.6 | async-start | bytes 8355840 | tf_op jit(solution)/shard_map/all_gather | solution.py:107
  7.9 106.6 %all-gather.14.cloned.1.call-start = ((), (), s32[]{:S(2)}) async-start(), calls=%async_computation.7 | async-start | bytes 6684672 | tf_op jit(solution)/shard_map/all_gather | solution.py:130
  30.5 37.8 %copy-start.36 = (f32[1536]{0:T(1024)}, f32[1536]{0:T(1024)S(1)}, u32[]{:S(2)}) copy-start(f32[1536]{0:T(1024)S(1)} %get-tuple-element.223) | copy-start | bytes 18436
  30.5 287.4 %copy-start.41 = (f32[1536]{0:T(1024)}, f32[1536]{0:T(1024)S(1)}, u32[]{:S(2)}) copy-start(f32[1536]{0:T(1024)S(1)} %get-tuple-element.222) | copy-start | bytes 18436
  31.8 36.5 %copy-start.45 = (f32[192]{0:T(256)}, f32[192]{0:T(256)S(1)}, u32[]{:S(2)}) copy-start(f32[192]{0:T(256)S(1)} %add_rsqrt_fusion.1) | copy-start | bytes 2308
  32.0 66.7 %copy-start.29 = (f32[192,32]{0,1:T(8,128)}, f32[192,32]{0,1:T(8,128)S(1)}, u32[]{:S(2)}) copy-start(f32[192,32]{0,1:T(8,128)S(1)} %get-tuple-element.292) | copy-start | bytes 73732
  32.0 66.7 %copy-start.31 = (f32[192,32]{0,1:T(8,128)}, f32[192,32]{0,1:T(8,128)S(1)}, u32[]{:S(2)}) copy-start(f32[192,32]{0,1:T(8,128)S(1)} %get-tuple-element.293) | copy-start | bytes 73732
  70.9 131.6 %all-gather.16.cloned.1.call-start = ((), (), s32[]{:S(2)}) async-start(), calls=%async_computation.8 | async-start | bytes 5013504 | tf_op jit(solution)/shard_map/all_gather | solution.py:108
  71.6 24.0 copy-start.17
  71.7 246.3 %all-gather.18.cloned.1.call-start = ((), (), s32[]{:S(2)}) async-start(), calls=%async_computation.9 | async-start | bytes 33423360 | tf_op jit(solution)/shard_map/all_gather | solution.py:111
  72.2 334.9 %all-gather.22.cloned.1.call-start = ((), (), s32[]{:S(2)}) async-start(), calls=%async_computation.11 | async-start | bytes 16711680 | tf_op jit(solution)/shard_map/all_gather | solution.py:176
  72.8 23.9 copy-start.40
  72.8 24.0 copy-start.51
  72.8 497.6 %all-gather.24.cloned.1.call-start = ((), (), s32[]{:S(2)}) async-start(), calls=%async_computation.12 | async-start | bytes 33423360 | tf_op jit(solution)/shard_map/all_gather | solution.py:175
  73.4 586.4 %all-gather.20.cloned.1.call-start = ((), (), s32[]{:S(2)}) async-start(), calls=%async_computation.10 | async-start | bytes 16711680 | tf_op jit(solution)/shard_map/all_gather | solution.py:112
  74.2 627.0 %all-gather.26.cloned.1.call-start = ((), (), s32[]{:S(2)}) async-start(), calls=%async_computation.13 | async-start | bytes 5013504 | tf_op jit(solution)/shard_map/all_gather | solution.py:172
  74.9 986.6 %reduce-scatter.19.cloned.1.call-start = ((), (), s32[]{:S(2)}) async-start(), calls=%async_computation.19 | async-start | bytes 13369344
  96.9 563.0 %copy-start.34 = (f32[192,10]{0,1:T(8,128)}, f32[192,10]{0,1:T(8,128)S(1)}, u32[]{:S(2)}) copy-start(f32[192,10]{0,1:T(8,128)S(1)} %select_reduce_fusion) | copy-start | bytes 23044
  127.3 75.2 %copy-start.6 = (bf16[192,1536]{1,0:T(8,128)(2,1)S(1)}, bf16[192,1536]{1,0:T(8,128)(2,1)}, u32[]{:S(2)}) copy-start(bf16[192,1536]{1,0:T(8,128)(2,1)} %param.23) | copy-start | bytes 1769476
  206.3 463.0 %copy-start.8 = (f32[192,1536]{1,0:T(8,128)}, f32[192,1536]{1,0:T(8,128)S(1)}, u32[]{:S(2)}) copy-start(f32[192,1536]{1,0:T(8,128)S(1)} %get-tuple-element.295) | copy-start | bytes 3538948
  206.4 127.4 %copy-start.47 = (f32[192]{0:T(256)}, f32[192]{0:T(256)S(1)}, u32[]{:S(2)}) copy-start(f32[192]{0:T(256)S(1)} %add_rsqrt_fusion) | copy-start | bytes 2308
  317.9 89.2 %copy-start.3 = (f32[192,1536]{1,0:T(8,128)S(1)}, f32[192,1536]{1,0:T(8,128)}, u32[]{:S(2)}) copy-start(f32[192,1536]{1,0:T(8,128)} %convert_element_type.122) | copy-start | bytes 3538948
  659.8 9.5 copy-start.18
  659.9 9.5 copy-start.44
  659.9 9.5 copy-start.48
  659.9 9.5 copy-start.54
  670.9 34.5 %copy-start = (f32[192,1536]{1,0:T(8,128)}, f32[192,1536]{1,0:T(8,128)S(1)}, u32[]{:S(2)}) copy-start(f32[192,1536]{1,0:T(8,128)S(1)} %get-tuple-element.286) | copy-start | bytes 3538948
  899.2 11.3 copy-start.23
  923.2 190.5 %all-gather.28.cloned.1.call-start = ((), (), s32[]{:S(2)}) async-start(), calls=%async_computation.14 | async-start | bytes 8355840 | tf_op jit(solution)/shard_map/all_gather | solution.py:171
  923.8 710.9 %reduce-scatter.17.cloned.1.call-start = ((), (), s32[]{:S(2)}) async-start(), calls=%async_computation.18 | async-start | bytes 53477376 | tf_op jit(solution)/shard_map/reduce_scatter | solution.py:196
  977.5 766.6 %reduce-scatter.13.cloned.1.call-start = ((), (), s32[]{:S(2)}) async-start(), calls=%async_computation.16 | async-start | bytes 10027008 | tf_op jit(solution)/shard_map/reduce_scatter | solution.py:270
  984.0 933.2 %reduce-scatter.11.cloned.1.call-start = ((), (), s32[]{:S(2)}) async-start(), calls=%async_computation.15 | async-start | bytes 16711680 | tf_op jit(solution)/shard_map/reduce_scatter | solution.py:269
  985.6 79.1 %copy-start.7 = (bf16[192,1536]{1,0:T(8,128)(2,1)S(1)}, bf16[192,1536]{1,0:T(8,128)(2,1)}, u32[]{:S(2)}) copy-start(bf16[192,1536]{1,0:T(8,128)(2,1)} %param.23) | copy-start | bytes 1769476
  985.6 79.1 %copy-start.37 = (f32[1536]{0:T(1024)S(1)}, f32[1536]{0:T(1024)}, u32[]{:S(2)}) copy-start(f32[1536]{0:T(1024)} %copy-done.36) | copy-start | bytes 18436
  985.6 79.1 %copy-start.46 = (f32[192]{0:T(256)S(1)}, f32[192]{0:T(256)}, u32[]{:S(2)}) copy-start(f32[192]{0:T(256)} %copy-done.45) | copy-start | bytes 2308
  985.8 87.9 %copy-start.14 = (bf16[192,24,64]{0,2,1:T(8,128)(2,1)}, bf16[192,24,64]{0,2,1:T(8,128)(2,1)S(1)}, u32[]{:S(2)}) copy-start(bf16[192,24,64]{0,2,1:T(8,128)(2,1)S(1)} %pad_maximum_fusion.5) | copy-start | bytes 1769476
  1073.7 1490.9 %reduce-scatter.15.cloned.1.call-start = ((), (), s32[]{:S(2)}) async-start(), calls=%async_computation.17 | async-start | bytes 66846720 | tf_op jit(solution)/shard_map/reduce_scatter | solution.py:189
  1100.9 12.7 copy-start.15
  1101.0 12.7 copy-start.26
  1101.0 12.7 copy-start.43
  1101.0 1524.3 %reduce-scatter.21.cloned.1.call-start = ((), (), s32[]{:S(2)}) async-start(), calls=%async_computation.20 | async-start | bytes 835584
  1122.0 1818.9 %all-reduce.3.cloned.1.call-start = ((), (), s32[]{:S(2)}) async-start(), calls=%async_computation.21 | async-start | bytes 14942208 | tf_op jit(solution)/shard_map/psum | solution.py:272
  2564.6 82.5 %copy-start.53 = (bf16[2,96]{1,0:T(2,128)(2,1)S(1)}, bf16[2,96]{1,0:T(2,128)(2,1)}, u32[]{:S(2)}) copy-start(bf16[2,96]{1,0:T(2,128)(2,1)} %param.27) | copy-start | bytes 1156
  2564.6 82.5 %copy-start.55 = (bf16[2,96]{1,0:T(2,128)(2,1)S(1)}, bf16[2,96]{1,0:T(2,128)(2,1)}, u32[]{:S(2)}) copy-start(bf16[2,96]{1,0:T(2,128)(2,1)} %param.37) | copy-start | bytes 1156
  2564.7 82.5 %copy-start.56 = (bf16[2,96]{1,0:T(2,128)(2,1)S(1)}, bf16[2,96]{1,0:T(2,128)(2,1)}, u32[]{:S(2)}) copy-start(bf16[2,96]{1,0:T(2,128)(2,1)} %param.32) | copy-start | bytes 1156
  2564.7 376.2 %copy-start.10 = (bf16[96,2560]{1,0:T(8,128)(2,1)S(1)}, bf16[96,2560]{1,0:T(8,128)(2,1)}, u32[]{:S(2)}) copy-start(bf16[96,2560]{1,0:T(8,128)(2,1)} %param.28) | copy-start | bytes 1474564
  2567.2 377.4 %copy-start.16 = (bf16[96,1536]{1,0:T(8,128)(2,1)S(1)}, bf16[96,1536]{1,0:T(8,128)(2,1)}, u32[]{:S(2)}) copy-start(bf16[96,1536]{1,0:T(8,128)(2,1)} %param.29) | copy-start | bytes 884740
  2567.2 377.4 %copy-start.33 = (bf16[96,1536]{1,0:T(8,128)(2,1)S(1)}, bf16[96,1536]{1,0:T(8,128)(2,1)}, u32[]{:S(2)}) copy-start(bf16[96,1536]{1,0:T(8,128)(2,1)} %param.39) | copy-start | bytes 884740
  (41 other events, 164.5 us)
Sparse Core Ops, SparseCore 0:
  9.7 53.3 all-gather.11
  71.0 43.4 all-gather.13
  116.2 39.4 all-gather.15
  157.2 160.6 all-gather.17
  319.4 87.6 all-gather.21
  408.7 161.7 all-gather.23
  572.1 87.6 all-gather.19
  661.5 39.6 all-gather.25
  923.3 138.1 reduce-scatter.18
  1063.0 50.5 all-gather.27
  1116.1 518.5 reduce-scatter.16
  1637.0 107.1 reduce-scatter.12
  1746.6 170.5 reduce-scatter.10
  1919.5 645.0 reduce-scatter.14
  2567.4 57.8 reduce-scatter.20
  2628.7 312.1 all-reduce.2
where the time goes:
time: 2980 us; the launch traced here: 2970 us
  waiting for transfers between devices  2360 us (79%)
  matrix products  368 us (12%)
  local copies, waits for them, and re-layouts  92 us (3%)
  blocking collectives  62.3 us (2%)
  other arithmetic  61.9 us (2%)
    reduce_scatter x1, waiting for transfers between devices, per_device(): lax.psum_scatter(jnp.einsum('td,tef->def', rows_used, grad_lift, preferre...  647 us
    reduce_scatter x1, waiting for transfers between devices, per_device(): lax.psum_scatter(jnp.einsum('tef,ted->fed', rows_used, grad_expert, prefe...  513 us
    psum x1, waiting for transfers between devices, per_device(): lax.psum((owned_gains, owned_inward, owned_outward, owned_lifting, owned_...  293 us
    reduce_scatter x1, waiting for transfers between devices, per_device(): lax.psum_scatter(full_inward, 'shard', scatter_dimension=0, tiled=True)  173 us
    all_gather x1, waiting for transfers between devices, per_device(): lax.all_gather(ordered[4], 'shard', axis=0, tiled=True)  150 us
    unnamed x18, waiting for transfers between devices  139 us
    all_gather x1, waiting for transfers between devices, per_device(): lax.all_gather(lifting, 'shard', axis=0, tiled=True)  112 us
    reduce_scatter x1, waiting for transfers between devices, per_device(): lax.psum_scatter(full_outward, 'shard', scatter_dimension=0, tiled=True)  105 us
  transfers between devices with their start and end apart: 16, of which 15 were waited for; matrix products, arithmetic and copies ran while one was open for 9% of the time, Pallas kernels for 0%

commit v1 on v0

v1 whole, which is shorter than its diff:
```python
import functools

import jax
import jax.numpy as jnp
import numpy as np
from jax import lax
from jax.experimental import pallas as pl
from jax.experimental.pallas import tpu as pltpu
from jax.sharding import PartitionSpec as P

HEADS = 24
KV_HEADS = 8
HEAD = 64
GROUP = HEADS // KV_HEADS
FF_EXP = 512
EXPERTS = 10
STEP = 10

norm_epsilon = 1e-06
beta_one = 0.9
beta_two = 0.95
adam_epsilon = 1e-08
weight_decay = 0.1
rate_gains = 0.5
rate_inward = 0.05
rate_outward = 0.3
rate_lifting = 0.05
rate_lowering = 0.3

SHARDS = 16
CHIPS = 8
REPS = 8
OWN = 192
SEQ = OWN * SHARDS
D = 1536
HID = 320
PAD = 384
BLOCKS = 8
ROWS = GROUP * OWN
KEYS = 2 * OWN

MESH = pl.DeviceIdType.MESH
bf16 = jnp.bfloat16
f32 = jnp.float32


def place():
    rep = lax.axis_index("rep")
    shard = lax.axis_index("shard")
    return rep, shard


def greet(devices):
    barrier = pltpu.get_barrier_semaphore()
    for device in devices:
        pl.semaphore_signal(barrier, inc=1, device_id=device, device_id_type=MESH)
    pl.semaphore_wait(barrier, len(devices))


def send(src, dst, send_sem, recv_sem, device):
    copy = pltpu.make_async_remote_copy(
        src_ref=src,
        dst_ref=dst,
        send_sem=send_sem,
        recv_sem=recv_sem,
        device_id=device,
        device_id_type=MESH,
    )
    copy.start()
    return copy


def params(collective, vmem=None):
    return pltpu.CompilerParams(
        collective_id=collective, has_side_effects=True, vmem_limit_bytes=vmem
    )


ANY = pl.BlockSpec(memory_space=pl.ANY)
VMEM = pl.BlockSpec(memory_space=pltpu.VMEM)


def gather_kernel(x_ref, o_ref, local_sem, send_sem, recv_sem):
    rep, shard = place()
    half = x_ref.shape[0] // 2
    core = lax.rem(shard, 2)
    y = lax.rem(shard // 2, 2)
    sib = shard + 1 - 2 * core
    pair = shard + 2 - 4 * y
    up = lax.rem(shard + 4, 16)
    down = lax.rem(shard + 12, 16)
    far = lax.rem(shard + 8, 16)

    def other(block):
        return block + 2 - 4 * y

    greet([(rep, sib), (rep, pair), (rep, up), (rep, down)])
    own = pltpu.make_async_copy(x_ref, o_ref.at[shard], local_sem)
    own.start()
    sent = []

    def put(src, dst, slot, device):
        sent.append(send(src, dst, send_sem.at[len(sent)], recv_sem.at[slot], (rep, device)))

    def forward(block, slot, device, rows=None):
        ref = o_ref.at[block] if rows is None else o_ref.at[block, rows]
        put(ref, ref, slot, device)

    def arrived(block, slot, rows=None):
        ref = o_ref.at[block] if rows is None else o_ref.at[block, rows]
        pltpu.make_async_remote_copy(
            src_ref=ref,
            dst_ref=ref,
            send_sem=send_sem.at[0],
            recv_sem=recv_sem.at[slot],
            device_id=(rep, sib),
            device_id_type=MESH,
        ).wait_recv()

    top, bottom = pl.ds(0, half), pl.ds(half, half)
    put(x_ref, o_ref.at[shard], 0, pair)
    put(x_ref, o_ref.at[shard], 1, up)
    put(x_ref, o_ref.at[shard], 5, down)
    put(x_ref, o_ref.at[shard], 9, sib)
    arrived(pair, 0)
    forward(pair, 2, up)
    forward(pair, 6, down)
    forward(pair, 10, sib)
    arrived(down, 1)
    forward(down, 3, up, top)
    forward(down, 11, sib)
    arrived(up, 5)
    forward(up, 7, down, bottom)
    forward(up, 12, sib)
    arrived(other(down), 2)
    forward(other(down), 4, up, top)
    forward(other(down), 13, sib)
    arrived(other(up), 6)
    forward(other(up), 8, down, bottom)
    forward(other(up), 14, sib)
    arrived(far, 3, top)
    forward(far, 15, sib, top)
    arrived(far, 7, bottom)
    forward(far, 16, sib, bottom)
    arrived(other(far), 4, top)
    forward(other(far), 17, sib, top)
    arrived(other(far), 8, bottom)
    forward(other(far), 18, sib, bottom)

    def twin(block):
        return block + 1 - 2 * core

    arrived(twin(shard), 9)
    arrived(twin(pair), 10)
    arrived(twin(down), 11)
    arrived(twin(up), 12)
    arrived(twin(other(down)), 13)
    arrived(twin(other(up)), 14)
    arrived(twin(far), 15, top)
    arrived(twin(far), 16, bottom)
    arrived(twin(other(far)), 17, top)
    arrived(twin(other(far)), 18, bottom)
    for copy in sent:
        copy.wait_send()
    own.wait()


def gather(x, collective):
    rows, columns = x.shape
    out = pl.pallas_call(
        gather_kernel,
        out_shape=jax.ShapeDtypeStruct((SHARDS, rows, columns), x.dtype),
        in_specs=[ANY],
        out_specs=ANY,
        scratch_shapes=[
            pltpu.SemaphoreType.DMA,
            pltpu.SemaphoreType.DMA((21,)),
            pltpu.SemaphoreType.DMA((19,)),
        ],
        compiler_params=params(collective),
        name="gather_rows",
    )(x)
    return out.reshape(SHARDS * rows, columns)


def exchange_kernel(kinds, *refs):
    count = len(kinds)
    ins, outs = refs[:count], refs[count : 2 * count]
    local_sem, send_sem, recv_sem = refs[2 * count :]
    rep, shard = place()
    core = lax.rem(shard, 2)
    chip = shard // 2
    greet([(rep, lax.rem(shard + i, 16)) for i in range(1, 16)])
    sent, due = [], []

    def mine(device):
        return lax.rem(lax.rem(device, 2) + lax.rem(device // 2, 2), 2)

    for n, kind in enumerate(kinds):
        x, o = ins[n], outs[n]
        if kind == "all":
            local = pltpu.make_async_copy(x.at[shard], o.at[shard], local_sem.at[n])
            local.start()
            due.append(local)
            for i in range(1, 16):
                to = lax.rem(shard + i, 16)
                sent.append(
                    send(x.at[to], o.at[shard], send_sem.at[n, i], recv_sem.at[n, i], (rep, to))
                )
        elif kind == "heads":
            local = pltpu.make_async_copy(x.at[chip], o.at[shard], local_sem.at[n])
            local.start()
            due.append(local)
            for i in range(1, 16):
                to = lax.rem(shard + i, 16)
                sent.append(
                    send(
                        x.at[to // 2], o.at[shard], send_sem.at[n, i], recv_sem.at[n, i], (rep, to)
                    )
                )
        elif kind == "home":
            for i in range(8):
                c = lax.rem(chip + i, 8)
                to = 2 * c + lax.rem(c + core, 2)
                if i == 0:
                    same = to == shard

                    @pl.when(same)
                    def _(x=x, o=o, c=c, n=n):
                        local = pltpu.make_async_copy(x.at[c], o.at[chip], local_sem.at[n])
                        local.start()
                        local.wait()

                    @pl.when(jnp.logical_not(same))
                    def _(x=x, o=o, c=c, n=n, to=to):
                        copy = send(
                            x.at[c], o.at[chip], send_sem.at[n, 0], recv_sem.at[n, 0], (rep, to)
                        )
                        copy.wait_send()

                else:
                    sent.append(
                        send(
                            x.at[c], o.at[chip], send_sem.at[n, i], recv_sem.at[n, i], (rep, to)
                        )
                    )
        elif kind == "away":
            for i in range(8):
                c = lax.rem(chip + i, 8)
                to = 2 * c + mine(shard)
                if i == 0:
                    same = to == shard

                    @pl.when(same)
                    def _(x=x, o=o, c=c, n=n):
                        local = pltpu.make_async_copy(x.at[c], o.at[chip], local_sem.at[n])
                        local.start()
                        local.wait()

                    @pl.when(jnp.logical_not(same))
                    def _(x=x, o=o, c=c, n=n, to=to):
                        copy = send(
                            x.at[c], o.at[chip], send_sem.at[n, 0], recv_sem.at[n, 0], (rep, to)
                        )
                        copy.wait_send()

                else:
                    sent.append(
                        send(
                            x.at[c], o.at[chip], send_sem.at[n, i], recv_sem.at[n, i], (rep, to)
                        )
                    )

    def arrived(ref, n, i):
        pltpu.make_async_remote_copy(
            src_ref=ref,
            dst_ref=ref,
            send_sem=send_sem.at[n, 0],
            recv_sem=recv_sem.at[n, i],
            device_id=(rep, lax.rem(shard + 1, 16)),
            device_id_type=MESH,
        ).wait_recv()

    for n, kind in enumerate(kinds):
        o = outs[n]
        if kind in ("all", "heads"):
            for i in range(1, 16):
                arrived(o.at[lax.rem(shard + 16 - i, 16)], n, i)
        else:
            away = kind == "away"
            first = (
                2 * chip + lax.rem(chip + core, 2) if away else 2 * chip + mine(shard)
            )

            @pl.when(first != shard)
            def _(o=o, n=n):
                arrived(o.at[chip], n, 0)

            for i in range(1, 8):
                arrived(o.at[lax.rem(chip + 8 - i, 8)], n, i)
    for copy in sent:
        copy.wait_send()
    for copy in due:
        copy.wait()


def exchange(arrays, kinds, collective, name):
    shapes = []
    for x, kind in zip(arrays, kinds):
        lead = 16 if kind in ("all", "heads") else 8
        shapes.append(jax.ShapeDtypeStruct((lead,) + x.shape[1:], x.dtype))
    n = len(arrays)
    return pl.pallas_call(
        functools.partial(exchange_kernel, kinds),
        out_shape=tuple(shapes),
        in_specs=[ANY] * n,
        out_specs=(ANY,) * n,
        scratch_shapes=[
            pltpu.SemaphoreType.DMA((n,)),
            pltpu.SemaphoreType.DMA((n, 16)),
            pltpu.SemaphoreType.DMA((n, 16)),
        ],
        compiler_params=params(collective),
        name=name,
    )(*arrays)


def reduce_kernel(count, *refs):
    ins, outs = refs[:count], refs[count : 2 * count]
    held, near, landed, load_sem, s_near, r_near, s_far, r_far = refs[2 * count :]
    rep, shard = place()
    core = lax.rem(shard, 2)
    chip = shard // 2
    sib = shard + 1 - 2 * core
    peers = [2 * lax.rem(chip + i, 8) + core for i in range(1, 8)]
    greet([(rep, sib)] + [(rep, p) for p in peers])
    nears, loads, fars = [], [], []
    order = [1, 7, 2, 6, 3, 5, 4, 0]
    for n in range(count):
        for i in order:
            c = lax.rem(chip + i, 8)
            nears.append(
                send(
                    ins[n].at[2 * c + 1 - core],
                    near.at[n, i],
                    s_near.at[n, i],
                    r_near.at[n, i],
                    (rep, sib),
                )
            )
            load = pltpu.make_async_copy(
                ins[n].at[2 * c + core], held.at[n, i], load_sem.at[n, i]
            )
            load.start()
            loads.append(load)
    for n in range(count):
        for j, i in enumerate(order):
            nears[8 * n + j].wait_recv()
            loads[8 * n + j].wait()
            held[n, i] = (held[n, i].astype(f32) + near[n, i].astype(f32)).astype(bf16)
            if i:
                c = lax.rem(chip + i, 8)
                fars.append(
                    send(
                        held.at[n, i],
                        landed.at[n, i - 1],
                        s_far.at[n, i],
                        r_far.at[n, i],
                        (rep, 2 * c + core),
                    )
                )
    for n in range(count):
        for j in range(7):
            fars[7 * n + j].wait_recv()
        rows = outs[n].shape[0]
        step = 32

        def add(t, _, n=n):
            at = pl.ds(pl.multiple_of(t * step, step), step)
            total = held[n, 0, at].astype(f32)
            for i in range(7):
                total = total + landed[n, i, at].astype(f32)
            outs[n][at] = total
            return 0

        lax.fori_loop(0, rows // step, add, 0)
    for copy in nears + fars:
        copy.wait_send()


def reduce_blocks(arrays, collective):
    n = len(arrays)
    rows, columns = arrays[0].shape[1:]
    slot = (n, 8, rows, columns)
    return pl.pallas_call(
        functools.partial(reduce_kernel, n),
        out_shape=tuple(jax.ShapeDtypeStruct((rows, columns), f32) for _ in arrays),
        in_specs=[ANY] * n,
        out_specs=(VMEM,) * n,
        scratch_shapes=[
            pltpu.VMEM(slot, bf16),
            pltpu.VMEM(slot, bf16),
            pltpu.VMEM((n, 7, rows, columns), bf16),
            pltpu.SemaphoreType.DMA((n, 8)),
            pltpu.SemaphoreType.DMA((n, 8)),
            pltpu.SemaphoreType.DMA((n, 8)),
            pltpu.SemaphoreType.DMA((n, 8)),
            pltpu.SemaphoreType.DMA((n, 8)),
        ],
        compiler_params=params(collective, 60 * 2**20),
        name="reduce_rows",
    )(*arrays)


def total_kernel(count, *refs):
    ins, outs = refs[:count], refs[count : 2 * count]
    landed = refs[2 * count : 3 * count]
    local_sem, s_one, r_one, s_two, r_two = refs[3 * count :]
    rep, shard = place()
    greet([(lax.rem(rep + i, 8), shard) for i in range(1, 8)])
    ones, twos, locals_ = [], [], []
    for n in range(count):
        local = pltpu.make_async_copy(ins[n].at[rep], landed[n].at[0], local_sem.at[n])
        local.start()
        locals_.append(local)
        for i in range(1, 8):
            to = lax.rem(rep + i, 8)
            ones.append(
                send(ins[n].at[to], landed[n].at[i], s_one.at[n, i], r_one.at[n, i], (to, shard))
            )
    for n in range(count):
        locals_[n].wait()
        for i in range(7):
            ones[7 * n + i].wait_recv()
        rows = landed[n].shape[1]
        step = 16

        def add(t, _, n=n):
            at = pl.ds(pl.multiple_of(t * step, step), step)
            total = landed[n][0, at].astype(f32)
            for i in range(1, 8):
                total = total + landed[n][i, at].astype(f32)
            landed[n][0, at] = total.astype(bf16)
            return 0

        lax.fori_loop(0, rows // step, add, 0)
        local = pltpu.make_async_copy(landed[n].at[0], outs[n].at[rep], local_sem.at[n])
        local.start()
        locals_.append(local)
        for i in range(1, 8):
            to = lax.rem(rep + i, 8)
            twos.append(
                send(
                    landed[n].at[0], outs[n].at[rep], s_two.at[n, i], r_two.at[n, i], (to, shard)
                )
            )
    for n in range(count):
        locals_[count + n].wait()
        for i in range(1, 8):
            ref = outs[n].at[lax.rem(rep + 8 - i, 8)]
            pltpu.make_async_remote_copy(
                src_ref=ref,
                dst_ref=ref,
                send_sem=s_two.at[n, 0],
                recv_sem=r_two.at[n, i],
                device_id=(lax.rem(rep + 1, 8), shard),
                device_id_type=MESH,
            ).wait_recv()
    for copy in ones + twos:
        copy.wait_send()


def total_over_reps(arrays, collective):
    n = len(arrays)
    return pl.pallas_call(
        functools.partial(total_kernel, n),
        out_shape=tuple(jax.ShapeDtypeStruct(x.shape, x.dtype) for x in arrays),
        in_specs=[ANY] * n,
        out_specs=(ANY,) * n,
        scratch_shapes=[pltpu.VMEM(x.shape, bf16) for x in arrays]
        + [pltpu.SemaphoreType.DMA((n,))]
        + [pltpu.SemaphoreType.DMA((n, 8)) for _ in range(4)],
        compiler_params=params(collective, 60 * 2**20),
        name="total_over_reps",
    )(*arrays)


def swap_halves(values):
    lanes = values.shape[1]
    lane = lax.broadcasted_iota(jnp.int32, values.shape, 1)
    ahead = pltpu.roll(values, lanes - HEAD // 2, 1)
    behind = pltpu.roll(values, HEAD // 2, 1)
    return jnp.where(lax.rem(lane, HEAD) < HEAD // 2, ahead, behind)


def project_kernel(x_ref, w_ref, g_ref, cos_ref, sin_ref, q_ref, k_ref, v_ref, u_ref):
    i = pl.program_id(0)
    stream = x_ref[...].astype(f32)
    u_ref[...] = (stream * inverse_root(stream) * g_ref[...]).astype(bf16)
    core = lax.rem(lax.axis_index("shard"), 2)
    first = pl.multiple_of(lax.rem(i + core, 2) * OWN, OWN)
    own = pl.ds(first, OWN)
    queries = jnp.dot(u_ref[own, :], w_ref[:, :256], preferred_element_type=f32)
    cos, sin = cos_ref[own, :], sin_ref[own, :]
    cos, sin = jnp.concatenate([cos, cos], 1), jnp.concatenate([sin, sin], 1)
    turned = (queries * cos + swap_halves(queries) * sin).astype(bf16)
    turned = turned * jnp.bfloat16(HEAD**-0.5)
    for r in range(GROUP):
        q_ref[0, r * OWN : (r + 1) * OWN, :] = turned[:, r * HEAD : (r + 1) * HEAD]
    pairs = jnp.dot(u_ref[...], w_ref[:, 256:], preferred_element_type=f32)
    keys = pairs * cos_ref[...] + swap_halves(pairs) * sin_ref[...]
    k_ref[...] = keys[:, :HEAD].astype(bf16)
    lane = lax.broadcasted_iota(jnp.int32, pairs.shape, 1)
    v_ref[...] = jnp.where(lane < HEAD, pltpu.roll(pairs, HEAD, 1), 1.0).astype(bf16)


def project(x_all, weight, gain, cos, sin):
    return pl.pallas_call(
        project_kernel,
        grid=(BLOCKS,),
        in_specs=[
            pl.BlockSpec((KEYS, D), lambda i: (i, 0)),
            pl.BlockSpec((D, 384), lambda i: (0, 0)),
            pl.BlockSpec((1, D), lambda i: (0, 0)),
            pl.BlockSpec((KEYS, 128), lambda i: (i, 0)),
            pl.BlockSpec((KEYS, 128), lambda i: (i, 0)),
        ],
        out_specs=(
            pl.BlockSpec((1, ROWS, HEAD), lambda i: (i, 0, 0)),
            pl.BlockSpec((KEYS, HEAD), lambda i: (i, 0)),
            pl.BlockSpec((KEYS, 128), lambda i: (i, 0)),
            pl.BlockSpec((KEYS, D), lambda i: (i, 0)),
        ),
        out_shape=(
            jax.ShapeDtypeStruct((BLOCKS, ROWS, HEAD), bf16),
            jax.ShapeDtypeStruct((SEQ, HEAD), bf16),
            jax.ShapeDtypeStruct((SEQ, 128), bf16),
            jax.ShapeDtypeStruct((SEQ, D), bf16),
        ),
        compiler_params=pltpu.CompilerParams(vmem_limit_bytes=48 * 2**20),
        name="project_heads",
    )(x_all, weight, gain, cos, sin)


def contract(a, b, dims):
    return lax.dot_general(a, b, ((dims[0], dims[1]), ((), ())), preferred_element_type=f32)


def attend_kernel(q_ref, k_ref, v_ref, o_ref, l_ref):
    i = pl.program_id(0)
    core = lax.rem(lax.axis_index("shard"), 2)
    shift = lax.rem(i + core, 2) * OWN
    q = q_ref[0]

    def step(c, carry, last=False):
        top, total = carry
        at = pl.ds(pl.multiple_of(c * KEYS, KEYS), KEYS)
        scores = contract(q, k_ref[at, :], ((1,), (1,)))
        if last:
            row = lax.broadcasted_iota(jnp.int32, (OWN, KEYS), 0)
            column = lax.broadcasted_iota(jnp.int32, (OWN, KEYS), 1)
            bias = jnp.where(column <= row + shift, 0.0, -1e30)
            scores = scores + jnp.concatenate([bias] * GROUP, 0)
        high = jnp.maximum(top, jnp.max(scores, 1, keepdims=True))
        prob = jnp.exp(scores - high).astype(bf16)
        total = total * jnp.exp(top - high) + jnp.dot(
            prob, v_ref[at, :], preferred_element_type=f32
        )
        return high, total

    carry = (jnp.full((ROWS, 1), -1e30, f32), jnp.zeros((ROWS, 128), f32))
    carry = lax.fori_loop(0, i, step, carry)
    top, total = step(i, carry, True)
    weight = total[:, HEAD : HEAD + 1]
    result = (total[:, :HEAD] / weight).astype(bf16)
    o_ref[0] = jnp.concatenate([result[r * OWN : (r + 1) * OWN] for r in range(GROUP)], 1)
    l_ref[0] = jnp.broadcast_to(top + jnp.log(weight), (ROWS, 8))


def attend(q, k, v):
    return pl.pallas_call(
        attend_kernel,
        grid=(BLOCKS,),
        in_specs=[
            pl.BlockSpec((1, ROWS, HEAD), lambda i: (i, 0, 0)),
            pl.BlockSpec((SEQ, HEAD), lambda i: (0, 0)),
            pl.BlockSpec((SEQ, 128), lambda i: (0, 0)),
        ],
        out_specs=(
            pl.BlockSpec((1, OWN, GROUP * HEAD), lambda i: (i, 0, 0)),
            pl.BlockSpec((1, ROWS, 8), lambda i: (i, 0, 0)),
        ),
        out_shape=(
            jax.ShapeDtypeStruct((BLOCKS, OWN, GROUP * HEAD), bf16),
            jax.ShapeDtypeStruct((BLOCKS, ROWS, 8), f32),
        ),
        compiler_params=pltpu.CompilerParams(vmem_limit_bytes=48 * 2**20),
        name="attend",
    )(q, k, v)


def attend_back_kernel(
    q_ref, k_ref, v_ref, g_ref, l_ref, d_ref, cos_ref, sin_ref, qcos_ref, qsin_ref, dq_ref, dkv_ref,
    dk, dv, dq,
):
    i = pl.program_id(0)
    core = lax.rem(lax.axis_index("shard"), 2)
    shift = lax.rem(i + core, 2) * OWN

    @pl.when(i == 0)
    def _():
        dk[...] = jnp.zeros_like(dk)
        dv[...] = jnp.zeros_like(dv)

    q = q_ref[0]
    grad = jnp.concatenate([g_ref[0][:, r * HEAD : (r + 1) * HEAD] for r in range(GROUP)], 0)
    dq[...] = jnp.zeros_like(dq)

    def step(c, _, last=False):
        at = pl.ds(pl.multiple_of(c * KEYS, KEYS), KEYS)
        keys = k_ref[at, :]
        scores = contract(keys, q, ((1,), (1,)))
        if last:
            key = lax.broadcasted_iota(jnp.int32, (KEYS, OWN), 0)
            token = lax.broadcasted_iota(jnp.int32, (KEYS, OWN), 1)
            bias = jnp.where(key <= token + shift, 0.0, -1e30)
            scores = scores + jnp.concatenate([bias] * GROUP, 1)
        prob = jnp.exp(scores - l_ref[0])
        back = contract(v_ref[at, :HEAD], grad, ((1,), (1,)))
        slope = (prob * (back - d_ref[0])).astype(bf16)
        dv[at, :] += jnp.dot(prob.astype(bf16), grad, preferred_element_type=f32)
        dk[at, :] += jnp.dot(slope, q, preferred_element_type=f32)
        dq[...] += contract(slope, keys, ((0,), (0,)))
        return 0

    lax.fori_loop(0, i, step, 0)
    step(i, 0, True)
    wide = jnp.concatenate(
        [dq[r * OWN : (r + 1) * OWN, :] for r in range(GROUP)] + [jnp.zeros((OWN, HEAD), f32)], 1
    )
    wide = wide * (HEAD**-0.5)
    cos, sin = qcos_ref[...], qsin_ref[...]
    cos, sin = jnp.concatenate([cos, cos], 1), jnp.concatenate([sin, sin], 1)
    wide = wide * cos - swap_halves(wide) * sin
    dq_ref[0] = wide[:, : GROUP * HEAD].astype(bf16)

    @pl.when(i == BLOCKS - 1)
    def _():
        def turn(c, _):
            at = pl.ds(pl.multiple_of(c * OWN, OWN), OWN)
            both = jnp.concatenate([dk[at, :], dv[at, :]], 1)
            lane = lax.broadcasted_iota(jnp.int32, both.shape, 1)
            turned = both * cos_ref[at, :] - swap_halves(both) * sin_ref[at, :]
            dkv_ref[at, :] = jnp.where(lane < HEAD, turned, both).astype(bf16)
            return 0

        lax.fori_loop(0, SHARDS, turn, 0)


def attend_back(q, k, v, grad, lse, delta, cos, sin, core):
    def own(i):
        return (2 * i + lax.rem(i + lax.rem(lax.axis_index("shard"), 2), 2), 0)

    whole = lambda i: (0, 0)
    block = lambda i: (i, 0, 0)
    return pl.pallas_call(
        attend_back_kernel,
        grid=(BLOCKS,),
        in_specs=[
            pl.BlockSpec((1, ROWS, HEAD), block),
            pl.BlockSpec((SEQ, HEAD), whole),
            pl.BlockSpec((SEQ, 128), whole),
            pl.BlockSpec((1, OWN, GROUP * HEAD), block),
            pl.BlockSpec((1, 1, ROWS), block),
            pl.BlockSpec((1, 1, ROWS), block),
            pl.BlockSpec((SEQ, 128), whole),
            pl.BlockSpec((SEQ, 128), whole),
            pl.BlockSpec((OWN, 128), own),
            pl.BlockSpec((OWN, 128), own),
        ],
        out_specs=(
            pl.BlockSpec((1, OWN, GROUP * HEAD), block),
            pl.BlockSpec((SEQ, 128), whole),
        ),
        out_shape=(
            jax.ShapeDtypeStruct((BLOCKS, OWN, GROUP * HEAD), bf16),
            jax.ShapeDtypeStruct((SEQ, 128), bf16),
        ),
        scratch_shapes=[
            pltpu.VMEM((SEQ, HEAD), f32),
            pltpu.VMEM((SEQ, HEAD), f32),
            pltpu.VMEM((ROWS, HEAD), f32),
        ],
        compiler_params=pltpu.CompilerParams(vmem_limit_bytes=48 * 2**20),
        name="attend_back",
    )(q, k, v, grad, lse, delta, cos, sin, cos, sin)


def experts_kernel(u_ref, y_ref, c_ref, wl_ref, wd_ref, e_ref, out_ref, du_ref, act_ref, gl_ref):
    u = u_ref[...]
    lift = jnp.dot(u, wl_ref[...], preferred_element_type=f32)
    back = contract(y_ref[...], wd_ref[...], ((1,), (1,)))
    share = jnp.dot(c_ref[...], e_ref[...], preferred_element_type=f32)
    gate, raised = lift[:, :PAD], lift[:, PAD:]
    s = jax.nn.sigmoid(gate)
    swish = gate * s
    act = (share * swish * raised).astype(bf16)
    act_ref[...] = act
    back = back * share
    grad_gate = back * raised * s * (1.0 + gate * (1.0 - s))
    gl_ref[:, :PAD] = grad_gate.astype(bf16)
    gl_ref[:, PAD:] = (back * swish).astype(bf16)
    out_ref[...] = jnp.dot(act, wd_ref[...], preferred_element_type=f32).astype(bf16)
    du_ref[...] = contract(gl_ref[...], wl_ref[...], ((1,), (1,))).astype(bf16)


def experts(u_all, y_all, shares, wl, wd, spread):
    step = 384
    rows = lambda i: (i, 0)
    whole = lambda i: (0, 0)
    return pl.pallas_call(
        experts_kernel,
        grid=(SEQ // step,),
        in_specs=[
            pl.BlockSpec((step, D), rows),
            pl.BlockSpec((step, D), rows),
            pl.BlockSpec((step, 128), lambda i: (i, D // 128)),
            pl.BlockSpec((D, 2 * PAD), whole),
            pl.BlockSpec((PAD, D), whole),
            pl.BlockSpec((128, PAD), whole),
        ],
        out_specs=(
            pl.BlockSpec((step, D), rows),
            pl.BlockSpec((step, D), rows),
            pl.BlockSpec((step, PAD), rows),
            pl.BlockSpec((step, 2 * PAD), rows),
        ),
        out_shape=(
            jax.ShapeDtypeStruct((SEQ, D), bf16),
            jax.ShapeDtypeStruct((SEQ, D), bf16),
            jax.ShapeDtypeStruct((SEQ, PAD), bf16),
            jax.ShapeDtypeStruct((SEQ, 2 * PAD), bf16),
        ),
        compiler_params=pltpu.CompilerParams(vmem_limit_bytes=56 * 2**20),
        name="experts",
    )(u_all, y_all, shares, wl, wd, spread)


def tables():
    half = HEAD // 2
    frequency = np.float32(10000.0) ** (-(2.0 * np.arange(half, dtype=np.float32)) / HEAD)
    phases = np.arange(SEQ, dtype=np.float32)[:, None] * frequency[None, :].astype(np.float32)
    cos, sin = np.cos(phases).astype(np.float32), np.sin(phases).astype(np.float32)
    return (
        np.concatenate([cos, cos, cos, cos], 1),
        np.concatenate([-sin, sin, -sin, sin], 1),
    )


def spread_table():
    table = np.zeros((128, PAD), np.float32)
    for e in range(EXPERTS):
        table[e, 32 * e : 32 * e + 32] = 1.0
        table[16 + e, 32 * e : 32 * e + 32] = 1.0
    return table


def inverse_root(stream):
    return lax.rsqrt(jnp.mean(stream * stream, -1, keepdims=True) + norm_epsilon)


def norm_back(scaled, unit, inverse):
    return inverse * (scaled - unit * jnp.mean(scaled * unit, -1, keepdims=True))


def adam(weight, old_mean, square, gradient, step_rate, decay_rate):
    values = weight.astype(f32)
    moment = beta_one * old_mean.astype(f32) + (1.0 - beta_one) * gradient
    variance = beta_two * square.astype(f32) + (1.0 - beta_two) * gradient * gradient
    normed_step = (
        moment
        / (1.0 - beta_one**STEP)
        / (jnp.sqrt(variance / (1.0 - beta_two**STEP)) + adam_epsilon)
    )
    return (moment, variance, values - step_rate * (normed_step + decay_rate * values))


def per_device(
    layer_input,
    grad_output,
    routes,
    route_logits,
    norm_gains,
    inward,
    outward,
    lifting,
    lowering,
    mean_gains,
    mean_inward,
    mean_outward,
    mean_lifting,
    mean_lowering,
    square_gains,
    square_inward,
    square_outward,
    square_lifting,
    square_lowering,
):
    gains = norm_gains.astype(f32)
    cos, sin = (jnp.asarray(t) for t in tables())
    core = lax.rem(lax.axis_index("shard"), 2)

    by_head = jnp.concatenate(
        [
            inward[:, :1536].reshape(96, KV_HEADS, 192),
            jnp.broadcast_to(
                jnp.pad(norm_gains.T, ((0, 0), (0, HEAD - 2)))[:, None, :], (96, KV_HEADS, HEAD)
            ),
            inward[:, 1536:2048].reshape(96, KV_HEADS, HEAD),
            inward[:, 2048:].reshape(96, KV_HEADS, HEAD),
        ],
        2,
    ).transpose(1, 0, 2)
    by_unit = (
        lifting.reshape(96, EXPERTS, 2, SHARDS, 32)
        .transpose(3, 0, 2, 1, 4)
        .reshape(SHARDS, 96, 2, HID)
    )
    by_unit = jnp.pad(by_unit, ((0, 0), (0, 0), (0, 0), (0, PAD - HID)))
    by_unit = by_unit.reshape(SHARDS, 96, 2 * PAD)

    x_all = gather(layer_input, 2)

    head_weight, unit_weight = exchange((by_head, by_unit), ("heads", "all"), 1, "spread_weights")
    head_weight = head_weight.reshape(D, 384)
    unit_weight = unit_weight.reshape(D, 2 * PAD)
    down_weight = lowering.transpose(1, 0, 2).reshape(HID, D)
    down_weight = jnp.pad(down_weight, ((0, PAD - HID), (0, 0)))

    gain_rows = head_weight[:, 192:194].T.astype(f32)
    gain_one, gain_two = gain_rows[0:1], gain_rows[1:2]

    stream = layer_input.astype(f32)
    inverse_one = inverse_root(stream)
    unit_one = stream * inverse_one

    gates = jax.nn.softmax(route_logits, axis=-1)
    picked = routes[:, :, None] == jnp.arange(EXPERTS, dtype=jnp.int32)[None, None, :]
    combine = jnp.sum(jnp.where(picked, gates[:, :, None], 0.0), axis=1)
    high = lax.reduce_precision(combine, 8, 7)
    rest = combine - high
    shares = jnp.concatenate(
        [jnp.pad(high, ((0, 0), (0, 6))), jnp.pad(rest, ((0, 0), (0, 102)))], 1
    ).astype(bf16)
    y_all = lax.all_gather(
        jnp.concatenate([grad_output, shares], 1), "shard", axis=0, tiled=True
    )
    outward_all = lax.all_gather(outward, "shard", axis=0, tiled=True)

    q, k, v, u_one = project(x_all, head_weight, gain_one, cos, sin)
    attended, lse = attend(q, k, v)
    (own_attended,) = exchange((attended,), ("home",), 3, "attended_home")
    low_attended = own_attended.transpose(1, 0, 2).reshape(OWN, HEADS * HEAD)

    mixed = stream + jnp.dot(low_attended, outward_all, preferred_element_type=f32)
    inverse_two = inverse_root(mixed)
    unit_two = mixed * inverse_two
    low_two = (unit_two * gain_two).astype(bf16)
    u_two = gather(low_two, 4)

    out_part, du_part, act, grad_lift = experts(
        u_two, y_all, y_all, unit_weight, down_weight, jnp.asarray(spread_table(), bf16)
    )
    du, expert_out = reduce_blocks(
        (du_part.reshape(SHARDS, OWN, D), out_part.reshape(SHARDS, OWN, D)), 5
    )
    layer_output = mixed + expert_out
    lift_part = contract(u_two, grad_lift, ((0,), (0,))).astype(bf16)
    down_part = contract(act, y_all[:, :D], ((0,), (0,))).astype(bf16)

    grad_mixed = grad_output.astype(f32) + norm_back(du * gain_two, unit_two, inverse_two)
    low_mixed = grad_mixed.astype(bf16)
    grad_attended = contract(low_mixed, outward_all, ((1,), (1,))).astype(bf16)
    (head_grads,) = exchange(
        (grad_attended.reshape(OWN, KV_HEADS, 192).transpose(1, 0, 2),), ("away",), 6, "grads_away"
    )
    outward_part = contract(low_attended, low_mixed, ((0,), (0,))).astype(bf16)
    outward_own = lax.psum_scatter(outward_part, "shard", scatter_dimension=0, tiled=True)

    lse = lse[:, :, 0].reshape(BLOCKS, 1, ROWS)
    delta = jnp.sum(
        (attended.astype(f32) * head_grads.astype(f32)).reshape(BLOCKS, OWN, GROUP, HEAD), -1
    )
    delta = delta.transpose(0, 2, 1).reshape(BLOCKS, 1, ROWS)
    dq, dkv = attend_back(q, k, v, head_grads, lse, delta, cos, sin, core)
    inward_all = lax.all_gather(inward, "shard", axis=0, tiled=True)

    own_dq, own_dkv = exchange(
        (dq, dkv.reshape(SHARDS, OWN, 128)), ("home", "all"), 7, "pairs_home"
    )
    pairs = jnp.sum(own_dkv.reshape(CHIPS, 2, OWN, 128).astype(f32), 1)
    grad_joined = jnp.concatenate(
        [
            own_dq.transpose(1, 0, 2).reshape(OWN, 1536),
            pairs[:, :, :HEAD].transpose(1, 0, 2).reshape(OWN, 512).astype(bf16),
            pairs[:, :, HEAD:].transpose(1, 0, 2).reshape(OWN, 512).astype(bf16),
        ],
        1,
    )
    dh = contract(grad_joined, inward_all, ((1,), (1,)))
    input_grad = grad_mixed + norm_back(dh * gain_one, unit_one, inverse_one)

    u_pairs = u_one.reshape(BLOCKS, 2, OWN, D)
    even = u_pairs[:, 0]
    odd = u_pairs[:, 1]
    pick = (lax.rem(jnp.arange(BLOCKS), 2) == core)[:, None, None]
    u_own = jnp.where(pick, even, odd).reshape(BLOCKS * OWN, D)
    query_part = contract(u_own, dq.reshape(BLOCKS * OWN, 192), ((0,), (0,)))
    pair_part = contract(u_one, dkv, ((0,), (0,)))
    inward_part = jnp.concatenate([query_part, pair_part], 1).astype(bf16)
    inward_pad = jnp.pad(inward_part, ((0, 0), (0, 64)))
    lift_got, inward_got = exchange(
        (lift_part.reshape(SHARDS, 96, 2 * PAD), inward_pad.reshape(SHARDS, 96, 384)),
        ("all", "all"),
        8,
        "grads_to_owners",
    )
    inward_sum = jnp.sum(inward_got.reshape(CHIPS, 2, 96, 384).astype(f32), 1).astype(bf16)
    lift_sum, down_sum, inward_sum, outward_sum = total_over_reps(
        (
            lift_got.reshape(REPS, 192, 2 * PAD),
            down_part.reshape(REPS, 48, D),
            inward_sum,
            outward_own.reshape(REPS, 16, 1152),
        ),
        9,
    )
    lift_grad = (
        lift_sum.reshape(SHARDS, 96, 2, PAD)[..., :HID]
        .reshape(SHARDS, 96, 2, EXPERTS, 32)
        .transpose(1, 3, 2, 0, 4)
        .reshape(96, EXPERTS, 1024)
        .astype(f32)
    )
    down_grad = down_sum.reshape(PAD, D)[:HID].reshape(EXPERTS, 32, D).transpose(1, 0, 2).astype(f32)
    inward_sum = inward_sum.transpose(1, 0, 2)
    inward_grad = jnp.concatenate(
        [
            inward_sum[:, :, :192].reshape(96, 1536),
            inward_sum[:, :, 192:256].reshape(96, 512),
            inward_sum[:, :, 256:320].reshape(96, 512),
        ],
        1,
    ).astype(f32)
    outward_grad = outward_sum.reshape(96, D).astype(f32)
    gain_grad = jnp.stack(
        [
            jnp.sum(inward.astype(f32) * inward_grad, 1),
            jnp.sum(lifting.astype(f32) * lift_grad, (1, 2)),
        ]
    )
    gain_grad = gain_grad / gains

    new_gains = adam(norm_gains, mean_gains, square_gains, gain_grad, rate_gains, 0.0)
    new_inward = adam(inward, mean_inward, square_inward, inward_grad, rate_inward, weight_decay)
    new_outward = adam(
        outward, mean_outward, square_outward, outward_grad, rate_outward, weight_decay
    )
    new_lifting = adam(lifting, mean_lifting, square_lifting, lift_grad, rate_lifting, weight_decay)
    new_lowering = adam(
        lowering, mean_lowering, square_lowering, down_grad, rate_lowering, weight_decay
    )
    return (
        layer_output,
        input_grad,
        new_gains[0],
        new_inward[0],
        new_outward[0],
        new_lifting[0],
        new_lowering[0],
        new_gains[1],
        new_inward[1],
        new_outward[1],
        new_lifting[1],
        new_lowering[1],
        new_gains[2],
        new_inward[2],
        new_outward[2],
        new_lifting[2],
        new_lowering[2],
    )


def solution(mesh):
    tokens = P(("rep", "shard"), None)
    gains, flat, deep = P(None, "shard"), P("shard", None), P("shard", None, None)
    weights = (gains, flat, flat, deep, deep)
    return jax.shard_map(
        per_device,
        mesh=mesh,
        in_specs=(tokens,) * 4 + weights * 3,
        out_specs=(tokens,) * 2 + weights * 3,
        check_vma=False,
    )
```

time: 2980 us -> 850 us (0.29)
  waiting for transfers between devices: 2360 us -> 1.42 us
  Pallas kernels: 0 us -> 648 us
  matrix products: 368 us -> 43.5 us
  blocking collectives: 62.3 us -> 0 us
    reduce_scatter x4 -> x1, waiting for transfers between devices: 1440 us -> 0.01 us  [per_device(): lax.psum_scatter(outward_part, 'shard', scatter_dimension=0, tiled=True)]
    pallas_call x0 -> x13, Pallas kernels: none -> 648 us  [the longest x5 189 us: exchange(): pl.pallas_call(functools.partial(exchange_kernel, kinds), out_shape=tuple...]
    all_gather x9 -> x3, waiting for transfers between devices: 494 us -> 0.02 us  [the longest x1 0.02 us: per_device(): lax.all_gather(jnp.concatenate([grad_output, shares], 1), 'shard', axis=0...]
    psum x1 -> x0, waiting for transfers between devices: 293 us -> none  [per_device(): lax.psum((owned_gains, owned_inward, owned_outward, owned_lifting, owned_...]
    dot_general x52 -> x8, matrix products: 287 us -> 43.5 us  [the longest x7 39.6 us: contract(): lax.dot_general(a, b, ((dims[0], dims[1]), ((), ())), preferred_element_t...]
    unnamed x18 -> x4, waiting for transfers between devices: 139 us -> 1.39 us
    sub x16 -> x0, matrix products: 81.2 us -> none  [probabilities(): return jax.nn.softmax(jnp.where(allowed[None], scores, -1e+30), axis=-1)]
    all_gather x2 -> x0, blocking collectives: 41.3 us -> none  [the longest x1 22.3 us: per_device(): lax.all_gather(norm_gains, 'shard', axis=1, tiled=True)]
  transfers between devices with their start and end apart: 16 -> 4, of which waited for: 15 -> 0; matrix products, arithmetic and copies ran while one was open for 9% -> 13% of each run, Pallas kernels for 0% -> 63%
where the time goes in v1:
time: 850 us; the launch traced here: 835 us
  Pallas kernels  648 us (76%)
  local copies, waits for them, and re-layouts  84.6 us (10%)
  matrix products  43.5 us (5%)
  other arithmetic  41.9 us (5%)
  between operations  15.1 us (2%)
    pallas_call x5, Pallas kernels, exchange(): pl.pallas_call(functools.partial(exchange_kernel, kinds), out_shape=tuple...  189 us
    pallas_call x1, Pallas kernels, total_over_reps(): pl.pallas_call(functools.partial(total_kernel, n), out_shape=tuple((jax.S...  122 us
    pallas_call x2, Pallas kernels, gather(): pl.pallas_call(gather_kernel, out_shape=jax.ShapeDtypeStruct((SHARDS, row...  121 us
    pallas_call x1, Pallas kernels, reduce_blocks(): pl.pallas_call(functools.partial(reduce_kernel, n), out_shape=tuple((jax....  111 us
    unnamed x106, local copies, waits for them, and re-layouts  45.6 us
    dot_general x7, matrix products, contract(): lax.dot_general(a, b, ((dims[0], dims[1]), ((), ())), preferred_element_t...  39.6 us
    pallas_call x1, Pallas kernels, attend_back(): pl.pallas_call(attend_back_kernel, grid=(BLOCKS,), in_specs=[pl.BlockSpec...  37.4 us
    pallas_call x1, Pallas kernels, experts(): pl.pallas_call(experts_kernel, grid=(SEQ // step,), in_specs=[pl.BlockSpe...  32.1 us
  transfers between devices with their start and end apart: 4, of which 0 were waited for; matrix products, arithmetic and copies ran while one was open for 13% of the time, Pallas kernels for 63%

profile of v1, /device:TPU:1, one launch (start us, length us, event | category | flops | bytes accessed | tf_op | source)
XLA Modules:
  0.0 834.9 jit_solution(14685494573789771014)
XLA Ops:
  11.2 1.9 concatenate.20
  17.0 3.1 copy.172
  22.4 2.6 copy.207.refs_1_
  25.7 2.1 maximum_bitcast_fusion.refs_0_
  27.9 62.5 %spread_weights.1 = (bf16[16,96,384]{2,1,0:T(8,128)(2,1)}, bf16[16,96,768]{2,1,0:T(8,128)(2,1)}) custom-call(bf16[8,96,384]{2,1,0:T(8,128)(2,1)} %maximum_bitcast_fusion.refs_0_, bf16[16,96,768]{2,1,0:T(8,128)(2,1)} %copy.207.refs_1_), custom_call_target="tpu_custom_call" | custom-call | tf_op jit(solution)/shard_map/spread_weights/pallas_call | solution.py:313
  91.8 71.9 %gather_rows.2 = bf16[16,192,1536]{2,1,0:T(8,128)(2,1)} custom-call(bf16[192,1536]{1,0:T(8,128)(2,1)} %x_ref.1), custom_call_target="tpu_custom_call" | custom-call | tf_op jit(solution)/shard_map/gather_rows/pallas_call | solution.py:170
  165.1 13.5 %project_heads.1 = (bf16[8,576,64]{2,1,0:T(8,128)(2,1)S(1)}, bf16[3072,64]{1,0:T(8,128)(2,1)S(1)}, bf16[3072,128]{1,0:T(8,128)(2,1)S(1)}, bf16[3072,1536]{1,0:T(8,128)(2,1)}) custom-call(bf16[3072,1536]{1,0:T(8,128)(2,1)} %bitcast.120, bf16[1536,384]{1,0:T(8,128)(2,1)S(1)} %bitcast.114, f32[1,1536]{1,0:T(1,128)S(1)} %get-tuple-element.162.g_ref, ...), custom_call_target="tpu_custom_call" | custom-call | tf_op jit(solution)/shard_map/project_heads/pallas_call | solution.py:518
  178.6 22.8 %attend.1 = (bf16[8,192,192]{2,1,0:T(8,128)(2,1)S(1)}, f32[8,576,8]{2,1,0:T(8,128)S(1)}) custom-call(bf16[8,576,64]{2,1,0:T(8,128)(2,1)S(1)} %get-tuple-element.42.q_ref, bf16[3072,64]{1,0:T(8,128)(2,1)S(1)} %get-tuple-element.43.k_ref, bf16[3072,128]{1,0:T(8,128)(2,1)S(1)} %get-tuple-element.44.v_ref), custom_call_target="tpu_custom_call" | custom-call | tf_op jit(solution)/shard_map/attend/pallas_call | solution.py:581
  204.6 27.1 %attended_home.1 = bf16[8,192,192]{2,1,0:T(8,128)(2,1)} custom-call(bf16[8,192,192]{2,1,0:T(8,128)(2,1)} %copy-done.4), custom_call_target="tpu_custom_call" | custom-call | tf_op jit(solution)/shard_map/attended_home/pallas_call | solution.py:313
  231.7 2.4 copy.176
  234.1 2.5 reshape.190
  237.7 3.9 multiply_reduce_fusion.1
  242.7 48.6 %gather_rows.3 = bf16[16,192,1536]{2,1,0:T(8,128)(2,1)} custom-call(bf16[192,1536]{1,0:T(8,128)(2,1)} %multiply_convert_fusion.x_ref), custom_call_target="tpu_custom_call" | custom-call | tf_op jit(solution)/shard_map/gather_rows/pallas_call | solution.py:170
  291.4 32.1 %experts.1 = (bf16[3072,1536]{1,0:T(8,128)(2,1)}, bf16[3072,1536]{1,0:T(8,128)(2,1)}, bf16[3072,384]{1,0:T(8,128)(2,1)}, bf16[3072,768]{1,0:T(8,128)(2,1)}) custom-call(bf16[3072,1536]{1,0:T(8,128)(2,1)} %bitcast.118, bf16[3072,1664]{1,0:T(8,128)(2,1)} %all-gather.6.cloned.1.call-done.y_ref.c_ref, ...), custom_call_target="tpu_custom_call" | custom-call | tf_op jit(solution)/shard_map/experts/pallas_call | solution.py:721
  323.4 111.4 %reduce_rows.1 = (f32[192,1536]{1,0:T(8,128)}, f32[192,1536]{1,0:T(8,128)}) custom-call(bf16[16,192,1536]{2,1,0:T(8,128)(2,1)} %bitcast.126, bf16[16,192,1536]{2,1,0:T(8,128)(2,1)} %bitcast.125), custom_call_target="tpu_custom_call" | custom-call | tf_op jit(solution)/shard_map/reduce_rows/pallas_call | solution.py:395
  434.9 1.7 multiply_reduce_fusion
  436.6 3.1 multiply_add_fusion
  439.8 3.5 convolution_convert_fusion
  443.3 2.4 copy.181
  445.7 4.3 copy.201
  450.0 4.3 copy.202
  456.6 4.9 convolution_convert_fusion.2
  461.5 1.8 reshape.196
  464.3 25.8 %grads_away.1.g_ref = bf16[8,192,192]{2,1,0:T(8,128)(2,1)} custom-call(bf16[8,192,192]{2,1,0:T(8,128)(2,1)} %bitcast.132), custom_call_target="tpu_custom_call" | custom-call | tf_op jit(solution)/shard_map/grads_away/pallas_call | solution.py:313
  490.1 2.4 convert_multiply_fusion.9
  492.6 3.3 copy.182
  495.9 2.2 reduce_sum.107
  498.1 1.5 reshape.218.d_ref
  501.0 37.4 %attend_back.1 = (bf16[8,192,192]{2,1,0:T(8,128)(2,1)S(1)}, bf16[3072,128]{1,0:T(8,128)(2,1)S(1)}) custom-call(bf16[8,576,64]{2,1,0:T(8,128)(2,1)S(1)} %get-tuple-element.42.q_ref, bf16[3072,64]{1,0:T(8,128)(2,1)S(1)} %get-tuple-element.43.k_ref, bf16[3072,128]{1,0:T(8,128)(2,1)S(1)} %copy-done.3, bf16[8,192,192]{2,1,0:T(8,128)(2,1)S(1)} %copy-done.1, ...), custom_call_target="tpu_custom_call" | custom-call | tf_op jit(solution)/shard_map/attend_back/pallas_call | solution.py:666
  538.4 5.8 fusion.17
  544.3 1.5 convolution_convert_fusion.3
  547.7 28.1 %pairs_home.1 = (bf16[8,192,192]{2,1,0:T(8,128)(2,1)}, bf16[16,192,128]{2,1,0:T(8,128)(2,1)}) custom-call(bf16[8,192,192]{2,1,0:T(8,128)(2,1)} %copy-done.8, bf16[16,192,128]{2,1,0:T(8,128)(2,1)} %bitcast.115), custom_call_target="tpu_custom_call" | custom-call | tf_op jit(solution)/shard_map/pairs_home/pallas_call | solution.py:313
  579.3 12.8 %convolution_convert_fusion.1 = bf16[1536,768]{1,0:T(8,128)(2,1)} fusion(bf16[3072,1536]{1,0:T(8,128)(2,1)} %bitcast.119, bf16[3072,768]{1,0:T(8,128)(2,1)} %get-tuple-element.56), kind=kOutput, calls=%fused_computation.19 | convolution fusion | flops 7248936960 | bytes 16515072 | tf_op jit(solution)/shard_map/dot_general | solution.py:546
  592.2 45.3 %grads_to_owners.1 = (bf16[16,96,768]{2,1,0:T(8,128)(2,1)}, bf16[16,96,384]{2,1,0:T(8,128)(2,1)}) custom-call(bf16[16,96,768]{2,1,0:T(8,128)(2,1)} %bitcast.136, bf16[16,96,384]{2,1,0:T(8,128)(2,1)} %bitcast.129), custom_call_target="tpu_custom_call" | custom-call | tf_op jit(solution)/shard_map/grads_to_owners/pallas_call | solution.py:313
  637.5 2.4 bitcast_reduce_fusion.refs_2_
  639.9 6.2 fusion.27
  648.2 4.9 fusion.11
  653.1 1.9 reshape.207.refs_3_
  655.1 121.8 %total_over_reps.1 = (bf16[8,192,768]{2,1,0:T(8,128)(2,1)}, bf16[8,48,1536]{2,1,0:T(8,128)(2,1)}, bf16[8,96,384]{2,1,0:T(8,128)(2,1)}, bf16[8,16,1152]{2,1,0:T(8,128)(2,1)}) custom-call(bf16[8,192,768]{2,1,0:T(8,128)(2,1)} %bitcast.135, bf16[8,48,1536]{2,1,0:T(8,128)(2,1)} %bitcast.137, bf16[8,96,384]{2,1,0:T(8,128)(2,1)} %bitcast_reduce_fusion.refs_2_, ...), custom_call_target="tpu_custom_call" | custom-call | tf_op jit(solution)/shard_map/total_over_reps/pallas_call | solution.py:475
  780.3 2.2 reshape.211
  782.5 5.1 copy.213
  791.6 7.7 convert_subtract_fusion
  799.3 5.8 copy.203
  805.1 5.5 copy.204
  810.7 5.5 copy.205
  817.9 5.3 convert_subtract_fusion.1
  823.2 1.5 convert_subtract_fusion.3
  824.9 2.3 convert_subtract_fusion.2
  (169 shorter events, 41.2 us)
Async XLA Ops:
  7.2 6.7 copy-start.22
  7.2 230.5 %all-gather.4.cloned.1.call-start = ((), (), s32[]{:S(2)}) async-start(), calls=%async_computation.1 | async-start | bytes 5013504 | tf_op jit(solution)/shard_map/all_gather | solution.py:858
  7.9 283.4 %all-gather.6.cloned.1.call-start = ((), (), s32[]{:S(2)}) async-start(), calls=%async_computation.2 | async-start | bytes 10862592 | tf_op jit(solution)/shard_map/all_gather | solution.py:855
  13.1 3.1 copy-start.35
  13.1 626.8 %all-gather.8.cloned.1.call-start = ((), (), s32[]{:S(2)}) async-start(), calls=%async_computation.3 | async-start | bytes 8355840 | tf_op jit(solution)/shard_map/all_gather | solution.py:896
  13.8 639.3 %reduce-scatter.2.cloned.1.call-start = ((), (), s32[]{:S(2)}) async-start(), calls=%async_computation.4 | async-start | bytes 5013504 | tf_op jit(solution)/shard_map/reduce_scatter | solution.py:888
  20.1 1.5 copy-start.12
  91.8 72.0 %copy-start = (f32[3072,128]{1,0:T(8,128)S(1)}, f32[3072,128]{1,0:T(8,128)}, u32[]{:S(2)}) copy-start(f32[3072,128]{1,0:T(8,128)} %constant.44.clone.cos_ref.qcos_ref) | copy-start | bytes 4718596
  163.8 1.3 copy-start.7
  201.4 0.9 copy-start.2
  203.2 1.4 copy-start.6
  204.6 32.0 %copy-start.24 = (bf16[32,10,1536]{2,0,1:T(8,128)(2,1)S(1)}, bf16[32,10,1536]{2,0,1:T(8,128)(2,1)}, u32[]{:S(2)}) copy-start(bf16[32,10,1536]{2,0,1:T(8,128)(2,1)} %param.30) | copy-start | bytes 2949124
  241.6 193.3 %copy-start.16 = (f32[192,1536]{1,0:T(8,128)}, f32[192,1536]{1,0:T(8,128)S(1)}, u32[]{:S(2)}) copy-start(f32[192,1536]{1,0:T(8,128)S(1)} %get-tuple-element.164) | copy-start | bytes 3538948
  434.8 1.7 copy-start.21
  434.9 1.8 copy-start.26
  436.6 3.1 copy-start.20
  439.8 16.9 %copy-start.14 = (f32[192,1536]{1,0:T(8,128)}, f32[192,1536]{1,0:T(8,128)S(1)}, u32[]{:S(2)}) copy-start(f32[192,1536]{1,0:T(8,128)S(1)} %get-tuple-element.151) | copy-start | bytes 3538948
  461.5 28.7 %copy-start.5 = (bf16[8,192,192]{2,1,0:T(8,128)(2,1)S(1)}, bf16[8,192,192]{2,1,0:T(8,128)(2,1)}, u32[]{:S(2)}) copy-start(bf16[8,192,192]{2,1,0:T(8,128)(2,1)} %copy-done.4) | copy-start | bytes 1769476
  492.6 6.9 copy-start.1
  492.6 6.9 copy-start.3
  501.0 37.4 %copy-start.40 = (pred[8]{0:T(512)(128)(4,1)S(1)}, pred[8]{0:T(512)(128)(4,1)}, u32[]{:S(2)}) copy-start(pred[8]{0:T(512)(128)(4,1)} %and_compare_fusion) | copy-start | bytes 28
  501.0 43.3 %slice-start.3 = ((s8[9437184]{0:T(1024)(128)(4,1)}), s8[4194304]{0:T(1024)(128)(4,1)S(1)}, s32[]{:S(2)}) async-start(s8[9437184]{0:T(1024)(128)(4,1)} %bitcast.154), calls=%async_computation.8 | async-start | bytes 8388608
  538.4 5.9 copy-start.8
  538.4 5.9 copy-start.9
  538.4 5.9 slice-start.4
  538.4 5.9 slice-start.5
  577.1 1.1 copy-start.29
  592.2 47.7 %copy-start.19 = (bf16[192,1536]{1,0:T(8,128)(2,1)S(1)}, bf16[192,1536]{1,0:T(8,128)(2,1)}, u32[]{:S(2)}) copy-start(bf16[192,1536]{1,0:T(8,128)(2,1)} %x_ref.1) | copy-start | bytes 1769476
  592.2 55.3 %slice-start = ((s8[10223616]{0:T(1024)(128)(4,1)}), s8[1835008]{0:T(1024)(128)(4,1)S(1)}, s32[]{:S(2)}) async-start(s8[10223616]{0:T(1024)(128)(4,1)} %bitcast.116), calls=%async_computation.5 | async-start | bytes 3670016
  639.9 6.2 copy-start.15
  639.9 7.6 slice-start.1
  639.9 7.6 slice-start.2
  646.1 2.1 copy-start.39
  776.9 3.4 copy-start.27
  788.3 1.7 copy-start.13
  788.3 2.5 copy-start.17
  788.3 3.3 copy-start.18
  816.2 1.4 copy-start.34
  816.2 1.6 copy-start.25
  817.8 5.3 copy-start.28
  817.8 5.3 copy-start.32
  817.9 5.3 copy-start.33
  823.2 1.6 copy-start.23
  823.2 1.6 copy-start.30
  823.2 1.7 copy-start.31
  824.9 2.3 copy-start.36
  824.9 2.3 copy-start.37
  824.9 2.4 copy-start.38
  (3 other events, 2.3 us)
Sparse Core Ops, SparseCore 0:
  9.7 79.3 all-gather.3
  91.4 89.8 all-gather.5
  183.0 59.9 all-gather.7
  443.4 78.1 reduce-scatter.1

commit v2 on v1

--- a/solution.py
+++ b/solution.py
@@ -34,7 +34,6 @@
 SEQ = OWN * SHARDS
 D = 1536
 HID = 320
-PAD = 384
 BLOCKS = 8
 ROWS = GROUP * OWN
 KEYS = 2 * OWN
@@ -80,22 +79,31 @@
 VMEM = pl.BlockSpec(memory_space=pltpu.VMEM)
 
 
-def gather_kernel(x_ref, o_ref, local_sem, send_sem, recv_sem):
+def gather_kernel(with_parts, *refs):
+    if with_parts:
+        x_ref, w_ref, o_ref, p_ref, local_sem, send_sem, recv_sem, s_part, r_part = refs
+    else:
+        x_ref, o_ref, local_sem, send_sem, recv_sem = refs
     rep, shard = place()
     half = x_ref.shape[0] // 2
     core = lax.rem(shard, 2)
-    y = lax.rem(shard // 2, 2)
+    chip = shard // 2
+    y = lax.rem(chip, 2)
     sib = shard + 1 - 2 * core
     pair = shard + 2 - 4 * y
     up = lax.rem(shard + 4, 16)
     down = lax.rem(shard + 12, 16)
     far = lax.rem(shard + 8, 16)
+    peers = [2 * lax.rem(chip + i, 8) + core for i in range(1, 8)]
 
     def other(block):
         return block + 2 - 4 * y
 
-    greet([(rep, sib), (rep, pair), (rep, up), (rep, down)])
-    own = pltpu.make_async_copy(x_ref, o_ref.at[shard], local_sem)
+    if with_parts:
+        greet([(rep, sib)] + [(rep, p) for p in peers])
+    else:
+        greet([(rep, sib), (rep, pair), (rep, up), (rep, down)])
+    own = pltpu.make_async_copy(x_ref, o_ref.at[shard], local_sem.at[0])
     own.start()
     sent = []
 
@@ -106,22 +114,38 @@
         ref = o_ref.at[block] if rows is None else o_ref.at[block, rows]
         put(ref, ref, slot, device)
 
-    def arrived(block, slot, rows=None):
-        ref = o_ref.at[block] if rows is None else o_ref.at[block, rows]
+    def landed(ref, sem):
         pltpu.make_async_remote_copy(
             src_ref=ref,
             dst_ref=ref,
             send_sem=send_sem.at[0],
-            recv_sem=recv_sem.at[slot],
+            recv_sem=sem,
             device_id=(rep, sib),
             device_id_type=MESH,
         ).wait_recv()
+
+    def arrived(block, slot, rows=None):
+        landed(o_ref.at[block] if rows is None else o_ref.at[block, rows], recv_sem.at[slot])
 
     top, bottom = pl.ds(0, half), pl.ds(half, half)
     put(x_ref, o_ref.at[shard], 0, pair)
     put(x_ref, o_ref.at[shard], 1, up)
     put(x_ref, o_ref.at[shard], 5, down)
     put(x_ref, o_ref.at[shard], 9, sib)
+    parts = []
+    if with_parts:
+        mine = pltpu.make_async_copy(w_ref.at[chip], p_ref.at[shard], local_sem.at[1])
+        mine.start()
+        parts.append(
+            send(w_ref.at[chip], p_ref.at[shard], s_part.at[0], r_part.at[0], (rep, sib))
+        )
+        for i in range(1, 8):
+            c = lax.rem(chip + i, 8)
+            parts.append(
+                send(
+                    w_ref.at[c], p_ref.at[shard], s_part.at[i], r_part.at[i], (rep, 2 * c + core)
+                )
+            )
     arrived(pair, 0)
     forward(pair, 2, up)
     forward(pair, 6, down)
@@ -138,6 +162,15 @@
     arrived(other(up), 6)
     forward(other(up), 8, down, bottom)
     forward(other(up), 14, sib)
+    if with_parts:
+        for i in range(1, 8):
+            block = 2 * lax.rem(chip + 8 - i, 8) + core
+            landed(p_ref.at[block], r_part.at[i])
+            parts.append(
+                send(
+                    p_ref.at[block], p_ref.at[block], s_part.at[7 + i], r_part.at[7 + i], (rep, sib)
+                )
+            )
     arrived(far, 3, top)
     forward(far, 15, sib, top)
     arrived(far, 7, bottom)
@@ -150,6 +183,11 @@
     def twin(block):
         return block + 1 - 2 * core
 
+    if with_parts:
+        landed(p_ref.at[sib], r_part.at[0])
+        for i in range(1, 8):
+            landed(p_ref.at[twin(2 * lax.rem(chip + 8 - i, 8) + core)], r_part.at[7 + i])
+        mine.wait()
     arrived(twin(shard), 9)
     arrived(twin(pair), 10)
     arrived(twin(down), 11)
@@ -160,27 +198,32 @@
     arrived(twin(far), 16, bottom)
     arrived(twin(other(far)), 17, top)
     arrived(twin(other(far)), 18, bottom)
-    for copy in sent:
+    for copy in sent + parts:
         copy.wait_send()
     own.wait()
 
 
-def gather(x, collective):
+def gather(x, collective, parts=None):
     rows, columns = x.shape
+    extra = () if parts is None else (parts,)
+    shapes = (jax.ShapeDtypeStruct((SHARDS, rows, columns), x.dtype),)
+    if extra:
+        shapes += (jax.ShapeDtypeStruct((SHARDS,) + parts.shape[1:], parts.dtype),)
     out = pl.pallas_call(
-        gather_kernel,
-        out_shape=jax.ShapeDtypeStruct((SHARDS, rows, columns), x.dtype),
-        in_specs=[ANY],
-        out_specs=ANY,
+        functools.partial(gather_kernel, bool(extra)),
+        out_shape=shapes,
+        in_specs=[ANY] * len(shapes),
+        out_specs=(ANY,) * len(shapes),
         scratch_shapes=[
-            pltpu.SemaphoreType.DMA,
+            pltpu.SemaphoreType.DMA((2,)),
             pltpu.SemaphoreType.DMA((21,)),
             pltpu.SemaphoreType.DMA((19,)),
-        ],
+        ]
+        + [pltpu.SemaphoreType.DMA((15,))] * (2 * len(extra)),
         compiler_params=params(collective),
         name="gather_rows",
-    )(x)
-    return out.reshape(SHARDS * rows, columns)
+    )(x, *extra)
+    return (out[0].reshape(SHARDS * rows, columns),) + tuple(out[1:])
 
 
 def exchange_kernel(kinds, *refs):
@@ -325,91 +368,287 @@
     )(*arrays)
 
 
-def reduce_kernel(count, *refs):
-    ins, outs = refs[:count], refs[count : 2 * count]
-    held, near, landed, load_sem, s_near, r_near, s_far, r_far = refs[2 * count :]
+SPLIT = 768
+
+
+def reduce_kernel(*refs):
+    du_ref, out_ref, lift_ref, down_ref = refs[:4]
+    ins = (du_ref, out_ref)
+    outs, lift_o, down_o = refs[4:6], refs[6], refs[7]
+    (
+        held, near, land_a, land_b, land_c, land_d,
+        lift_own, lift_land, lift_half, down_own, down_land, down_half,
+        load_sem, s_near, r_near, s_one, r_one, s_two, r_two,
+        a_load, a_s1, a_r1, a_s2, a_r2, a_s3, a_r3, a_s4, a_r4, a_out,
+    ) = refs[8:]
     rep, shard = place()
     core = lax.rem(shard, 2)
     chip = shard // 2
+    y = lax.rem(chip, 2)
+    z = chip // 2
     sib = shard + 1 - 2 * core
-    peers = [2 * lax.rem(chip + i, 8) + core for i in range(1, 8)]
-    greet([(rep, sib)] + [(rep, p) for p in peers])
-    nears, loads, fars = [], [], []
-    order = [1, 7, 2, 6, 3, 5, 4, 0]
-    for n in range(count):
-        for i in order:
-            c = lax.rem(chip + i, 8)
-            nears.append(
+    pair = shard + 2 - 4 * y
+    x, far_y = rep // 2, lax.rem(rep, 2)
+    mate = rep + 1 - 2 * far_y
+    first, last = pl.ds(0, SPLIT), pl.ds(SPLIT, D - SPLIT)
+
+    def ahead(dz):
+        return lax.rem(z + dz, 4)
+
+    def device(zz, yy):
+        return 4 * zz + 2 * yy + core
+
+    def along(dx):
+        return 2 * lax.rem(x + dx, 4) + far_y
+
+    greet(
+        [(rep, sib), (rep, pair)]
+        + [(rep, device(ahead(dz), y)) for dz in (1, 2, 3)]
+        + [(along(dx), shard) for dx in (1, 2, 3)]
+        + [(mate, shard)]
+    )
+
+    def block(j):
+        dz, dy = j // 2, j % 2
+        return 2 * ahead(dz) + (y if dy == 0 else 1 - y)
+
+    order = [1, 3, 5, 7, 2, 4, 6, 0]
+    nears, loads = {}, {}
+    for n in range(2):
+        for j in order:
+            c = block(j)
+            nears[n, j] = send(
+                ins[n].at[2 * c + 1 - core], near.at[n, j], s_near.at[n, j], r_near.at[n, j], (rep, sib)
+            )
+            loads[n, j] = pltpu.make_async_copy(
+                ins[n].at[2 * c + core], held.at[n, j], load_sem.at[n, j]
+            )
+            loads[n, j].start()
+    sums = ((lift_ref, lift_own, lift_land, lift_half, lift_o), (down_ref, down_own, down_land, down_half, down_o))
+    steps_one, steps_load = [], []
+    for m, (src, own, land, half, dst) in enumerate(sums):
+        load = pltpu.make_async_copy(src.at[x], own, a_load.at[m])
+        load.start()
+        steps_load.append(load)
+        for dx in (1, 2, 3):
+            steps_one.append(
                 send(
-                    ins[n].at[2 * c + 1 - core],
-                    near.at[n, i],
-                    s_near.at[n, i],
-                    r_near.at[n, i],
-                    (rep, sib),
+                    src.at[lax.rem(x + dx, 4)], land.at[dx - 1], a_s1.at[m, dx], a_r1.at[m, dx],
+                    (along(dx), shard),
                 )
             )
-            load = pltpu.make_async_copy(
-                ins[n].at[2 * c + core], held.at[n, i], load_sem.at[n, i]
+    ones = {}
+    for n in range(2):
+        for j in order:
+            nears[n, j].wait_recv()
+            loads[n, j].wait()
+
+            def add(t, _, n=n, j=j):
+                at = pl.ds(pl.multiple_of(t * 32, 32), 32)
+                held[n, j, at] = (
+                    held[n, j, at].astype(f32) + near[n, j, at].astype(f32)
+                ).astype(bf16)
+                return 0
+
+            lax.fori_loop(0, OWN // 32, add, 0)
+            dz, dy = j // 2, j % 2
+            if dy:
+                ones[n, 0, j] = send(
+                    held.at[n, j, :, first], land_a.at[n, dz], s_one.at[n, 0, j], r_one.at[n, 0, j],
+                    (rep, pair),
+                )
+            if dz:
+                ones[n, 1, j] = send(
+                    held.at[n, j, :, last], land_b.at[n, j - 2], s_one.at[n, 1, j], r_one.at[n, 1, j],
+                    (rep, device(ahead(dz), y)),
+                )
+
+    step = 32
+
+    def rows_of(t):
+        return pl.ds(pl.multiple_of(t * step, step), step)
+
+    twos = {}
+
+    def first_sums(n):
+        for dz in (1, 2, 3, 0):
+            ones[n, 0, 2 * dz + 1].wait_recv()
+
+            def add(t, _, dz=dz):
+                at = rows_of(t)
+                held[n, 2 * dz, at, first] = (
+                    held[n, 2 * dz, at, first].astype(f32) + land_a[n, dz, at].astype(f32)
+                ).astype(bf16)
+                return 0
+
+            lax.fori_loop(0, OWN // step, add, 0)
+            if dz:
+                twos[n, 0, dz] = send(
+                    held.at[n, 2 * dz, :, first], land_c.at[n, dz - 1], s_two.at[n, dz], r_two.at[n, dz],
+                    (rep, device(ahead(dz), y)),
+                )
+        for dy in (1, 0):
+            for dz in (1, 2, 3):
+                ones[n, 1, 2 * dz + dy].wait_recv()
+
+            def add(t, _, dy=dy):
+                at = rows_of(t)
+                total = held[n, dy, at, last].astype(f32)
+                for dz in (1, 2, 3):
+                    total = total + land_b[n, 2 * dz + dy - 2, at].astype(f32)
+                held[n, dy, at, last] = total.astype(bf16)
+                return 0
+
+            lax.fori_loop(0, OWN // step, add, 0)
+            if dy:
+                twos[n, 1, 0] = send(
+                    held.at[n, 1, :, last], land_d.at[n], s_two.at[n, 0], r_two.at[n, 0], (rep, pair)
+                )
+
+    def last_sums(n):
+        for dz in (1, 2, 3):
+            twos[n, 0, dz].wait_recv()
+        twos[n, 1, 0].wait_recv()
+
+        def add(t, _):
+            at = rows_of(t)
+            total = held[n, 0, at, first].astype(f32)
+            for dz in (1, 2, 3):
+                total = total + land_c[n, dz - 1, at].astype(f32)
+            outs[n][at, first] = total
+            outs[n][at, last] = held[n, 0, at, last].astype(f32) + land_d[n, at].astype(f32)
+            return 0
+
+        lax.fori_loop(0, OWN // step, add, 0)
+
+    first_sums(0)
+    for load in steps_load:
+        load.wait()
+    steps_two = []
+    for m, (src, own, land, half, dst) in enumerate(sums):
+        for dx in (1, 2, 3):
+            steps_one[3 * m + dx - 1].wait_recv()
+        size = own.shape[1]
+        for h in (0, 1):
+
+            def add(t, _, own=own, land=land, h=h):
+                at = pl.ds(pl.multiple_of(t * 16, 16), 16)
+                total = own[h, at].astype(f32)
+                for dx in range(3):
+                    total = total + land[dx, h, at].astype(f32)
+                own[h, at] = total.astype(bf16)
+                return 0
+
+            lax.fori_loop(0, size // 16, add, 0)
+        steps_two.append(
+            send(own.at[1 - far_y], half, a_s2.at[m], a_r2.at[m], (mate, shard))
+        )
+    first_sums(1)
+    steps_three, steps_four = [], []
+    for m, (src, own, land, half, dst) in enumerate(sums):
+        steps_two[m].wait_recv()
+
+        def add(t, _, own=own, half=half):
+            at = pl.ds(pl.multiple_of(t * 16, 16), 16)
+            half[at] = (own[far_y, at].astype(f32) + half[at].astype(f32)).astype(bf16)
+            return 0
+
+        lax.fori_loop(0, own.shape[1] // 16, add, 0)
+        steps_three.append(
+            send(half, dst.at[x, far_y], a_s3.at[m], a_r3.at[m], (mate, shard))
+        )
+        keep = pltpu.make_async_copy(half, dst.at[x, far_y], a_out.at[m])
+        keep.start()
+        steps_load.append(keep)
+        for dx in (1, 2, 3):
+            steps_four.append(
+                send(
+                    half, dst.at[x, far_y], a_s4.at[m, 0, dx], a_r4.at[m, 0, dx], (along(dx), shard)
+                )
             )
-            load.start()
-            loads.append(load)
-    for n in range(count):
-        for j, i in enumerate(order):
-            nears[8 * n + j].wait_recv()
-            loads[8 * n + j].wait()
-            held[n, i] = (held[n, i].astype(f32) + near[n, i].astype(f32)).astype(bf16)
-            if i:
-                c = lax.rem(chip + i, 8)
-                fars.append(
-                    send(
-                        held.at[n, i],
-                        landed.at[n, i - 1],
-                        s_far.at[n, i],
-                        r_far.at[n, i],
-                        (rep, 2 * c + core),
-                    )
-                )
-    for n in range(count):
-        for j in range(7):
-            fars[7 * n + j].wait_recv()
-        rows = outs[n].shape[0]
-        step = 32
-
-        def add(t, _, n=n):
-            at = pl.ds(pl.multiple_of(t * step, step), step)
-            total = held[n, 0, at].astype(f32)
-            for i in range(7):
-                total = total + landed[n, i, at].astype(f32)
-            outs[n][at] = total
-            return 0
-
-        lax.fori_loop(0, rows // step, add, 0)
-    for copy in nears + fars:
-        copy.wait_send()
-
-
-def reduce_blocks(arrays, collective):
-    n = len(arrays)
-    rows, columns = arrays[0].shape[1:]
-    slot = (n, 8, rows, columns)
-    return pl.pallas_call(
-        functools.partial(reduce_kernel, n),
-        out_shape=tuple(jax.ShapeDtypeStruct((rows, columns), f32) for _ in arrays),
-        in_specs=[ANY] * n,
-        out_specs=(VMEM,) * n,
+    last_sums(0)
+
+    def landed(ref, sem):
+        pltpu.make_async_remote_copy(
+            src_ref=ref,
+            dst_ref=ref,
+            send_sem=a_s3.at[0],
+            recv_sem=sem,
+            device_id=(mate, shard),
+            device_id_type=MESH,
+        ).wait_recv()
+
+    for m, (src, own, land, half, dst) in enumerate(sums):
+        landed(dst.at[x, 1 - far_y], a_r3.at[m])
+        for dx in (1, 2, 3):
+            ref = dst.at[x, 1 - far_y]
+            steps_four.append(
+                send(ref, ref, a_s4.at[m, 1, dx], a_r4.at[m, 1, dx], (along(dx), shard))
+            )
+    last_sums(1)
+    for m, (src, own, land, half, dst) in enumerate(sums):
+        for dx in (1, 2, 3):
+            back = lax.rem(x + 4 - dx, 4)
+            landed(dst.at[back, far_y], a_r4.at[m, 0, dx])
+            landed(dst.at[back, 1 - far_y], a_r4.at[m, 1, dx])
+    for keep in steps_load[2:]:
+        keep.wait()
+    for copies in (nears.values(), ones.values(), twos.values(), steps_one, steps_two, steps_three, steps_four):
+        for copy in copies:
+            copy.wait_send()
+
+
+def reduce_blocks(du, out, lift, down, collective):
+    lift = lift.reshape(4, 2, 192, 2 * HID)
+    down = down.reshape(4, 80, 2, D // 2).transpose(0, 2, 1, 3)
+    dma = pltpu.SemaphoreType.DMA
+    result = pl.pallas_call(
+        reduce_kernel,
+        out_shape=(
+            jax.ShapeDtypeStruct((OWN, D), f32),
+            jax.ShapeDtypeStruct((OWN, D), f32),
+            jax.ShapeDtypeStruct(lift.shape, bf16),
+            jax.ShapeDtypeStruct(down.shape, bf16),
+        ),
+        in_specs=[ANY] * 4,
+        out_specs=(VMEM, VMEM, ANY, ANY),
         scratch_shapes=[
-            pltpu.VMEM(slot, bf16),
-            pltpu.VMEM(slot, bf16),
-            pltpu.VMEM((n, 7, rows, columns), bf16),
-            pltpu.SemaphoreType.DMA((n, 8)),
-            pltpu.SemaphoreType.DMA((n, 8)),
-            pltpu.SemaphoreType.DMA((n, 8)),
-            pltpu.SemaphoreType.DMA((n, 8)),
-            pltpu.SemaphoreType.DMA((n, 8)),
+            pltpu.VMEM((2, 8, OWN, D), bf16),
+            pltpu.VMEM((2, 8, OWN, D), bf16),
+            pltpu.VMEM((2, 4, OWN, SPLIT), bf16),
+            pltpu.VMEM((2, 6, OWN, D - SPLIT), bf16),
+            pltpu.VMEM((2, 3, OWN, SPLIT), bf16),
+            pltpu.VMEM((2, OWN, D - SPLIT), bf16),
+            pltpu.VMEM(lift.shape[1:], bf16),
+            pltpu.VMEM((3,) + lift.shape[1:], bf16),
+            pltpu.VMEM(lift.shape[2:], bf16),
+            pltpu.VMEM(down.shape[1:], bf16),
+            pltpu.VMEM((3,) + down.shape[1:], bf16),
+            pltpu.VMEM(down.shape[2:], bf16),
+            dma((2, 8)),
+            dma((2, 8)),
+            dma((2, 8)),
+            dma((2, 2, 8)),
+            dma((2, 2, 8)),
+            dma((2, 4)),
+            dma((2, 4)),
+            dma((2,)),
+            dma((2, 4)),
+            dma((2, 4)),
+            dma((2,)),
+            dma((2,)),
+            dma((2,)),
+            dma((2,)),
+            dma((2, 2, 4)),
+            dma((2, 2, 4)),
+            dma((2,)),
         ],
         compiler_params=params(collective, 60 * 2**20),
         name="reduce_rows",
-    )(*arrays)
+    )(du, out, lift, down)
+    du, out, lift, down = result
+    down = down.transpose(0, 2, 1, 3).reshape(HID, D)
+    return du, out, lift.reshape(D, 2 * HID), down
 
 
 def total_kernel(count, *refs):
@@ -542,12 +781,52 @@
     )(x_all, weight, gain, cos, sin)
 
 
-def contract(a, b, dims):
-    return lax.dot_general(a, b, ((dims[0], dims[1]), ((), ())), preferred_element_type=f32)
-
-
-def attend_kernel(q_ref, k_ref, v_ref, o_ref, l_ref):
+def contract(a, b, dims, precision=None):
+    return lax.dot_general(
+        a, b, ((dims[0], dims[1]), ((), ())), preferred_element_type=f32, precision=precision
+    )
+
+
+def behind(x, o, local_sem, s_sem, r_sem):
+    rep, shard = place()
+    local = pltpu.make_async_copy(x.at[shard], o.at[shard], local_sem)
+
+    def copy(i, slot):
+        to = lax.rem(shard + i, 16)
+        return pltpu.make_async_remote_copy(
+            src_ref=x.at[to],
+            dst_ref=o.at[slot],
+            send_sem=s_sem.at[i],
+            recv_sem=r_sem.at[i],
+            device_id=(rep, to),
+            device_id_type=MESH,
+        )
+
+    def start():
+        local.start()
+        for i in range(1, 16):
+            copy(i, shard).start()
+
+    def wait():
+        local.wait()
+        for i in range(1, 16):
+            copy(i, lax.rem(shard + 16 - i, 16)).wait_recv()
+        for i in range(1, 16):
+            copy(i, shard).wait_send()
+
+    return start, wait
+
+
+def attend_kernel(q_ref, k_ref, v_ref, b_ref, o_ref, l_ref, bo_ref, local_sem, s_sem, r_sem):
     i = pl.program_id(0)
+    start, wait = behind(b_ref, bo_ref, local_sem.at[0], s_sem, r_sem)
+
+    @pl.when(i == 0)
+    def _():
+        rep, shard = place()
+        greet([(rep, lax.rem(shard + n, 16)) for n in range(1, 16)])
+        start()
+
     core = lax.rem(lax.axis_index("shard"), 2)
     shift = lax.rem(i + core, 2) * OWN
     q = q_ref[0]
@@ -574,10 +853,20 @@
     weight = total[:, HEAD : HEAD + 1]
     result = (total[:, :HEAD] / weight).astype(bf16)
     o_ref[0] = jnp.concatenate([result[r * OWN : (r + 1) * OWN] for r in range(GROUP)], 1)
-    l_ref[0] = jnp.broadcast_to(top + jnp.log(weight), (ROWS, 8))
-
-
-def attend(q, k, v):
+    column = lax.broadcasted_iota(jnp.int32, (8, 8), 1)
+    l_ref[0] = contract(
+        jnp.where(column == 0, 1.0, 0.0).astype(f32),
+        jnp.broadcast_to(top + jnp.log(weight), (ROWS, 8)),
+        ((1,), (1,)),
+        lax.Precision.HIGHEST,
+    )
+
+    @pl.when(i == BLOCKS - 1)
+    def _():
+        wait()
+
+
+def attend(q, k, v, units, collective):
     return pl.pallas_call(
         attend_kernel,
         grid=(BLOCKS,),
@@ -585,36 +874,104 @@
             pl.BlockSpec((1, ROWS, HEAD), lambda i: (i, 0, 0)),
             pl.BlockSpec((SEQ, HEAD), lambda i: (0, 0)),
             pl.BlockSpec((SEQ, 128), lambda i: (0, 0)),
+            ANY,
         ],
         out_specs=(
             pl.BlockSpec((1, OWN, GROUP * HEAD), lambda i: (i, 0, 0)),
-            pl.BlockSpec((1, ROWS, 8), lambda i: (i, 0, 0)),
+            pl.BlockSpec((1, 8, ROWS), lambda i: (i, 0, 0)),
+            ANY,
         ),
         out_shape=(
             jax.ShapeDtypeStruct((BLOCKS, OWN, GROUP * HEAD), bf16),
-            jax.ShapeDtypeStruct((BLOCKS, ROWS, 8), f32),
+            jax.ShapeDtypeStruct((BLOCKS, 8, ROWS), f32),
+            jax.ShapeDtypeStruct(units.shape, bf16),
         ),
-        compiler_params=pltpu.CompilerParams(vmem_limit_bytes=48 * 2**20),
+        scratch_shapes=[
+            pltpu.SemaphoreType.DMA((1,)),
+            pltpu.SemaphoreType.DMA((16,)),
+            pltpu.SemaphoreType.DMA((16,)),
+        ],
+        compiler_params=params(collective, 48 * 2**20),
         name="attend",
-    )(q, k, v)
+    )(q, k, v, units)
 
 
 def attend_back_kernel(
-    q_ref, k_ref, v_ref, g_ref, l_ref, d_ref, cos_ref, sin_ref, qcos_ref, qsin_ref, dq_ref, dkv_ref,
-    dk, dv, dq,
+    q_ref, k_ref, v_ref, g_ref, a_ref, l_ref, cos_ref, sin_ref, qcos_ref, qsin_ref, lift_ref, part_ref,
+    dq_ref, dkv_ref, lift_out, part_out,
+    dk, dv, dq, held, near, landed, local_sem, s_sem, r_sem, h_sem, s_near, r_near, s_far, r_far,
 ):
     i = pl.program_id(0)
-    core = lax.rem(lax.axis_index("shard"), 2)
+    rep, shard = place()
+    core = lax.rem(shard, 2)
+    chip = shard // 2
+    sib = shard + 1 - 2 * core
     shift = lax.rem(i + core, 2) * OWN
+    start, wait = behind(lift_ref, lift_out, local_sem.at[0], s_sem, r_sem)
+
+    def copy_near(j):
+        return pltpu.make_async_remote_copy(
+            src_ref=part_ref.at[2 * lax.rem(chip + j, 8) + 1 - core],
+            dst_ref=near.at[j],
+            send_sem=s_near.at[j],
+            recv_sem=r_near.at[j],
+            device_id=(rep, sib),
+            device_id_type=MESH,
+        )
+
+    def copy_own(j):
+        return pltpu.make_async_copy(
+            part_ref.at[2 * lax.rem(chip + j, 8) + core], held.at[j], h_sem.at[j]
+        )
+
+    def copy_far(j):
+        return pltpu.make_async_remote_copy(
+            src_ref=held.at[j],
+            dst_ref=landed.at[j - 1],
+            send_sem=s_far.at[j],
+            recv_sem=r_far.at[j],
+            device_id=(rep, 2 * lax.rem(chip + j, 8) + core),
+            device_id_type=MESH,
+        )
 
     @pl.when(i == 0)
     def _():
+        greet([(rep, lax.rem(shard + n, 16)) for n in range(1, 16)])
+        for j in range(8):
+            copy_near(j).start()
+            copy_own(j).start()
+        start()
         dk[...] = jnp.zeros_like(dk)
         dv[...] = jnp.zeros_like(dv)
+
+    @pl.when(i == 3)
+    def _():
+        for j in range(8):
+            copy_near(j).wait_recv()
+            copy_own(j).wait()
+
+            def add(t, _, j=j):
+                at = pl.ds(pl.multiple_of(t * 32, 32), 32)
+                held[j, at] = (held[j, at].astype(f32) + near[j, at].astype(f32)).astype(bf16)
+                return 0
+
+            lax.fori_loop(0, 3, add, 0)
+            if j:
+                copy_far(j).start()
 
     q = q_ref[0]
     grad = jnp.concatenate([g_ref[0][:, r * HEAD : (r + 1) * HEAD] for r in range(GROUP)], 0)
     dq[...] = jnp.zeros_like(dq)
+    lse = l_ref[0][:1]
+    lane = lax.broadcasted_iota(jnp.int32, (8, GROUP * HEAD), 1)
+    row = lax.broadcasted_iota(jnp.int32, (8, GROUP * HEAD), 0)
+    sums = contract(
+        jnp.where(lane // HEAD == row, 1.0, 0.0).astype(f32),
+        g_ref[0].astype(f32) * a_ref[0].astype(f32),
+        ((1,), (1,)),
+        lax.Precision.HIGHEST,
+    )
+    delta = jnp.concatenate([sums[r : r + 1] for r in range(GROUP)], 1)
 
     def step(c, _, last=False):
         at = pl.ds(pl.multiple_of(c * KEYS, KEYS), KEYS)
@@ -625,9 +982,9 @@
             token = lax.broadcasted_iota(jnp.int32, (KEYS, OWN), 1)
             bias = jnp.where(key <= token + shift, 0.0, -1e30)
             scores = scores + jnp.concatenate([bias] * GROUP, 1)
-        prob = jnp.exp(scores - l_ref[0])
+        prob = jnp.exp(scores - lse)
         back = contract(v_ref[at, :HEAD], grad, ((1,), (1,)))
-        slope = (prob * (back - d_ref[0])).astype(bf16)
+        slope = (prob * (back - delta)).astype(bf16)
         dv[at, :] += jnp.dot(prob.astype(bf16), grad, preferred_element_type=f32)
         dk[at, :] += jnp.dot(slope, q, preferred_element_type=f32)
         dq[...] += contract(slope, keys, ((0,), (0,)))
@@ -655,9 +1012,26 @@
             return 0
 
         lax.fori_loop(0, SHARDS, turn, 0)
-
-
-def attend_back(q, k, v, grad, lse, delta, cos, sin, core):
+        for j in range(1, 8):
+            copy_far(j).wait_recv()
+
+        def add(t, _):
+            at = pl.ds(pl.multiple_of(t * 32, 32), 32)
+            total = held[0, at].astype(f32)
+            for j in range(7):
+                total = total + landed[j, at].astype(f32)
+            part_out[at] = total.astype(bf16)
+            return 0
+
+        lax.fori_loop(0, 3, add, 0)
+        wait()
+        for j in range(8):
+            copy_near(j).wait_send()
+            if j:
+                copy_far(j).wait_send()
+
+
+def attend_back(q, k, v, grad, attended, lse, cos, sin, lift, part, collective):
     def own(i):
         return (2 * i + lax.rem(i + lax.rem(lax.axis_index("shard"), 2), 2), 0)
 
@@ -671,50 +1045,77 @@
             pl.BlockSpec((SEQ, HEAD), whole),
             pl.BlockSpec((SEQ, 128), whole),
             pl.BlockSpec((1, OWN, GROUP * HEAD), block),
-            pl.BlockSpec((1, 1, ROWS), block),
-            pl.BlockSpec((1, 1, ROWS), block),
+            pl.BlockSpec((1, OWN, GROUP * HEAD), block),
+            pl.BlockSpec((1, 8, ROWS), block),
             pl.BlockSpec((SEQ, 128), whole),
             pl.BlockSpec((SEQ, 128), whole),
             pl.BlockSpec((OWN, 128), own),
             pl.BlockSpec((OWN, 128), own),
+            ANY,
+            ANY,
         ],
         out_specs=(
             pl.BlockSpec((1, OWN, GROUP * HEAD), block),
             pl.BlockSpec((SEQ, 128), whole),
+            ANY,
+            pl.BlockSpec(part.shape[1:], whole),
         ),
         out_shape=(
             jax.ShapeDtypeStruct((BLOCKS, OWN, GROUP * HEAD), bf16),
             jax.ShapeDtypeStruct((SEQ, 128), bf16),
+            jax.ShapeDtypeStruct(lift.shape, bf16),
+            jax.ShapeDtypeStruct(part.shape[1:], bf16),
         ),
         scratch_shapes=[
             pltpu.VMEM((SEQ, HEAD), f32),
             pltpu.VMEM((SEQ, HEAD), f32),
             pltpu.VMEM((ROWS, HEAD), f32),
-        ],
-        compiler_params=pltpu.CompilerParams(vmem_limit_bytes=48 * 2**20),
+            pltpu.VMEM((8,) + part.shape[1:], bf16),
+            pltpu.VMEM((8,) + part.shape[1:], bf16),
+            pltpu.VMEM((7,) + part.shape[1:], bf16),
+            pltpu.SemaphoreType.DMA((1,)),
+            pltpu.SemaphoreType.DMA((16,)),
+            pltpu.SemaphoreType.DMA((16,)),
+        ]
+        + [pltpu.SemaphoreType.DMA((8,))] * 5,
+        compiler_params=params(collective, 48 * 2**20),
         name="attend_back",
-    )(q, k, v, grad, lse, delta, cos, sin, cos, sin)
-
-
-def experts_kernel(u_ref, y_ref, c_ref, wl_ref, wd_ref, e_ref, out_ref, du_ref, act_ref, gl_ref):
-    u = u_ref[...]
-    lift = jnp.dot(u, wl_ref[...], preferred_element_type=f32)
-    back = contract(y_ref[...], wd_ref[...], ((1,), (1,)))
+    )(q, k, v, grad, attended, lse, cos, sin, cos, sin, lift, part)
+
+
+def experts_kernel(
+    u_ref, y_ref, c_ref, wl_ref, wd_ref, e_ref, out_ref, du_ref, lift_ref, down_ref, lift, down
+):
+    i = pl.program_id(0)
+    u, y = u_ref[...], y_ref[...]
+    lifted = jnp.dot(u, wl_ref[...], preferred_element_type=f32)
+    back = contract(y, wd_ref[...], ((1,), (1,)))
     share = jnp.dot(c_ref[...], e_ref[...], preferred_element_type=f32)
-    gate, raised = lift[:, :PAD], lift[:, PAD:]
+    gate, raised = lifted[:, :HID], lifted[:, HID:]
     s = jax.nn.sigmoid(gate)
     swish = gate * s
     act = (share * swish * raised).astype(bf16)
-    act_ref[...] = act
     back = back * share
     grad_gate = back * raised * s * (1.0 + gate * (1.0 - s))
-    gl_ref[:, :PAD] = grad_gate.astype(bf16)
-    gl_ref[:, PAD:] = (back * swish).astype(bf16)
+    grad_lift = jnp.concatenate([grad_gate, back * swish], 1).astype(bf16)
     out_ref[...] = jnp.dot(act, wd_ref[...], preferred_element_type=f32).astype(bf16)
-    du_ref[...] = contract(gl_ref[...], wl_ref[...], ((1,), (1,))).astype(bf16)
-
-
-def experts(u_all, y_all, shares, wl, wd, spread):
+    du_ref[...] = contract(grad_lift, wl_ref[...], ((1,), (1,))).astype(bf16)
+
+    @pl.when(i == 0)
+    def _():
+        lift[...] = jnp.zeros_like(lift)
+        down[...] = jnp.zeros_like(down)
+
+    lift[...] += contract(u, grad_lift, ((0,), (0,)))
+    down[...] += contract(act, y, ((0,), (0,)))
+
+    @pl.when(i == pl.num_programs(0) - 1)
+    def _():
+        lift_ref[...] = lift[...].astype(bf16)
+        down_ref[...] = down[...].astype(bf16)
+
+
+def experts(u_all, y_all, wl, wd, spread):
     step = 384
     rows = lambda i: (i, 0)
     whole = lambda i: (0, 0)
@@ -725,25 +1126,188 @@
             pl.BlockSpec((step, D), rows),
             pl.BlockSpec((step, D), rows),
             pl.BlockSpec((step, 128), lambda i: (i, D // 128)),
-            pl.BlockSpec((D, 2 * PAD), whole),
-            pl.BlockSpec((PAD, D), whole),
-            pl.BlockSpec((128, PAD), whole),
+            pl.BlockSpec((D, 2 * HID), whole),
+            pl.BlockSpec((HID, D), whole),
+            pl.BlockSpec((128, HID), whole),
         ],
         out_specs=(
             pl.BlockSpec((step, D), rows),
             pl.BlockSpec((step, D), rows),
-            pl.BlockSpec((step, PAD), rows),
-            pl.BlockSpec((step, 2 * PAD), rows),
+            pl.BlockSpec((D, 2 * HID), whole),
+            pl.BlockSpec((HID, D), whole),
         ),
         out_shape=(
             jax.ShapeDtypeStruct((SEQ, D), bf16),
             jax.ShapeDtypeStruct((SEQ, D), bf16),
-            jax.ShapeDtypeStruct((SEQ, PAD), bf16),
-            jax.ShapeDtypeStruct((SEQ, 2 * PAD), bf16),
+            jax.ShapeDtypeStruct((D, 2 * HID), bf16),
+            jax.ShapeDtypeStruct((HID, D), bf16),
         ),
+        scratch_shapes=[pltpu.VMEM((D, 2 * HID), f32), pltpu.VMEM((HID, D), f32)],
+        compiler_params=pltpu.CompilerParams(vmem_limit_bytes=58 * 2**20),
+        name="experts",
+    )(u_all, y_all, y_all, wl, wd, spread)
+
+
+def one_step(kernel, arrays, shapes, name):
+    return pl.pallas_call(
+        kernel,
+        in_specs=[VMEM] * len(arrays),
+        out_specs=(VMEM,) * len(shapes),
+        out_shape=tuple(jax.ShapeDtypeStruct(shape, dtype) for shape, dtype in shapes),
         compiler_params=pltpu.CompilerParams(vmem_limit_bytes=56 * 2**20),
-        name="experts",
-    )(u_all, y_all, shares, wl, wd, spread)
+        name=name,
+    )(*arrays)
+
+
+def side_by_side(ref):
+    return jnp.concatenate([ref[c] for c in range(CHIPS)], 1)
+
+
+def mix_kernel(a_ref, w_ref, x_ref, g_ref, mixed_ref, low_ref):
+    mixed = x_ref[...].astype(f32) + jnp.dot(
+        side_by_side(a_ref), w_ref[...], preferred_element_type=f32
+    )
+    mixed_ref[...] = mixed
+    low_ref[...] = (mixed * inverse_root(mixed) * g_ref[...]).astype(bf16)
+
+
+def unmix_kernel(du_ref, e_ref, mixed_ref, y_ref, g_ref, w_ref, a_ref, out_ref, dz_ref, ga_ref, part_ref):
+    mixed = mixed_ref[...]
+    out_ref[...] = mixed + e_ref[...]
+    inverse = inverse_root(mixed)
+    dz = y_ref[...].astype(f32) + norm_back(du_ref[...] * g_ref[...], mixed * inverse, inverse)
+    dz_ref[...] = dz
+    low = dz.astype(bf16)
+    back = contract(low, w_ref[...], ((1,), (1,))).astype(bf16)
+    for c in range(CHIPS):
+        ga_ref[c] = back[:, c * 192 : (c + 1) * 192]
+    part = contract(side_by_side(a_ref), low, ((0,), (0,))).astype(bf16)
+    for s in range(SHARDS):
+        part_ref[s] = part[s * 96 : (s + 1) * 96]
+
+
+def finish_kernel(dq_ref, dkv_ref, w_ref, dz_ref, x_ref, g_ref, out_ref):
+    pairs = [dkv_ref[2 * c].astype(f32) + dkv_ref[2 * c + 1].astype(f32) for c in range(CHIPS)]
+    joined = jnp.concatenate(
+        [side_by_side(dq_ref)]
+        + [p[:, :HEAD].astype(bf16) for p in pairs]
+        + [p[:, HEAD:].astype(bf16) for p in pairs],
+        1,
+    )
+    dh = contract(joined, w_ref[...], ((1,), (1,)))
+    stream = x_ref[...].astype(f32)
+    inverse = inverse_root(stream)
+    out_ref[...] = dz_ref[...] + norm_back(dh * g_ref[...], stream * inverse, inverse)
+
+
+def inward_part_kernel(u_ref, dq_ref, dkv_ref, out_ref, total):
+    i = pl.program_id(0)
+    core = lax.rem(lax.axis_index("shard"), 2)
+    first = pl.multiple_of(lax.rem(i + core, 2) * OWN, OWN)
+
+    @pl.when(i == 0)
+    def _():
+        total[...] = jnp.zeros_like(total)
+
+    total[:, :192] += contract(u_ref[pl.ds(first, OWN), :], dq_ref[0], ((0,), (0,)))
+    total[:, 256:] += contract(u_ref[...], dkv_ref[...], ((0,), (0,)))
+
+    @pl.when(i == BLOCKS - 1)
+    def _():
+        both = jnp.concatenate([total[:, :192], total[:, 256:]], 1).astype(bf16)
+        for s in range(SHARDS):
+            out_ref[s] = both[s * 96 : (s + 1) * 96]
+
+
+def inward_parts(u_all, dq, dkv):
+    return pl.pallas_call(
+        inward_part_kernel,
+        grid=(BLOCKS,),
+        in_specs=[
+            pl.BlockSpec((KEYS, D), lambda i: (i, 0)),
+            pl.BlockSpec((1, OWN, GROUP * HEAD), lambda i: (i, 0, 0)),
+            pl.BlockSpec((KEYS, 128), lambda i: (i, 0)),
+        ],
+        out_specs=pl.BlockSpec((SHARDS, 96, 320), lambda i: (0, 0, 0)),
+        out_shape=jax.ShapeDtypeStruct((SHARDS, 96, 320), bf16),
+        scratch_shapes=[pltpu.VMEM((D, 384), f32)],
+        compiler_params=pltpu.CompilerParams(vmem_limit_bytes=48 * 2**20),
+        name="inward_parts",
+    )(u_all, dq, dkv)
+
+
+def adam(weight, old_mean, square, gradient, step_rate, decay_rate):
+    values = weight.astype(f32)
+    moment = beta_one * old_mean.astype(f32) + (1.0 - beta_one) * gradient
+    variance = beta_two * square.astype(f32) + (1.0 - beta_two) * gradient * gradient
+    normed_step = (
+        moment
+        / (1.0 - beta_one**STEP)
+        / (jnp.sqrt(variance / (1.0 - beta_two**STEP)) + adam_epsilon)
+    )
+    return (moment, variance, values - step_rate * (normed_step + decay_rate * values))
+
+
+def adam_lifting_kernel(w_ref, m_ref, s_ref, g_ref, mo_ref, so_ref, wo_ref, dot_ref, grad):
+    e = pl.program_id(0)
+    for k in range(EXPERTS):
+
+        @pl.when(e == k)
+        def _(k=k):
+            for part in range(2):
+                low = HID * part + 32 * k
+                grad[:, FF_EXP * part : FF_EXP * (part + 1)] = jnp.concatenate(
+                    [g_ref[s][:, low : low + 32].astype(f32) for s in range(SHARDS)], 1
+                )
+
+    @pl.when(e == 0)
+    def _():
+        dot_ref[...] = jnp.zeros_like(dot_ref)
+
+    dot = jnp.sum(w_ref[0].astype(f32) * grad[...], 1, keepdims=True)
+    dot_ref[...] += jnp.broadcast_to(dot, dot_ref.shape)
+    mo_ref[0], so_ref[0], wo_ref[0] = adam(
+        w_ref[0], m_ref[0], s_ref[0], grad[...], rate_lifting, weight_decay
+    )
+
+
+def adam_lifting(weight, mean, square, grad):
+    block = pl.BlockSpec((1, 96, 2 * FF_EXP), lambda e: (e, 0, 0))
+    shape = jax.ShapeDtypeStruct(weight.shape, f32)
+    return pl.pallas_call(
+        adam_lifting_kernel,
+        grid=(EXPERTS,),
+        in_specs=[block, block, block, pl.BlockSpec(grad.shape, lambda e: (0, 0, 0))],
+        out_specs=(block, block, block, pl.BlockSpec((96, 128), lambda e: (0, 0))),
+        out_shape=(shape, shape, shape, jax.ShapeDtypeStruct((96, 128), f32)),
+        scratch_shapes=[pltpu.VMEM((96, 2 * FF_EXP), f32)],
+        compiler_params=pltpu.CompilerParams(vmem_limit_bytes=48 * 2**20),
+        name="adam_lifting",
+    )(weight, mean, square, grad)
+
+
+def adam_inward_kernel(w_ref, m_ref, s_ref, g_ref, mo_ref, so_ref, wo_ref, dot_ref):
+    parts = [g_ref[c].astype(f32) for c in range(CHIPS)]
+    grad = jnp.concatenate(
+        [p[:, :192] for p in parts] + [p[:, 192:256] for p in parts] + [p[:, 256:] for p in parts], 1
+    )
+    dot = jnp.sum(w_ref[...].astype(f32) * grad, 1, keepdims=True)
+    dot_ref[...] = jnp.broadcast_to(dot, dot_ref.shape)
+    mo_ref[...], so_ref[...], wo_ref[...] = adam(
+        w_ref[...], m_ref[...], s_ref[...], grad, rate_inward, weight_decay
+    )
+
+
+def adam_inward(weight, mean, square, grad):
+    shape = jax.ShapeDtypeStruct(weight.shape, f32)
+    return pl.pallas_call(
+        adam_inward_kernel,
+        in_specs=[VMEM] * 4,
+        out_specs=(VMEM,) * 4,
+        out_shape=(shape, shape, shape, jax.ShapeDtypeStruct((96, 128), f32)),
+        compiler_params=pltpu.CompilerParams(vmem_limit_bytes=48 * 2**20),
+        name="adam_inward",
+    )(weight, mean, square, grad)
 
 
 def tables():
@@ -758,7 +1322,7 @@
 
 
 def spread_table():
-    table = np.zeros((128, PAD), np.float32)
+    table = np.zeros((128, HID), np.float32)
     for e in range(EXPERTS):
         table[e, 32 * e : 32 * e + 32] = 1.0
         table[16 + e, 32 * e : 32 * e + 32] = 1.0
@@ -771,18 +1335,6 @@
 
 def norm_back(scaled, unit, inverse):
     return inverse * (scaled - unit * jnp.mean(scaled * unit, -1, keepdims=True))
-
-
-def adam(weight, old_mean, square, gradient, step_rate, decay_rate):
-    values = weight.astype(f32)
-    moment = beta_one * old_mean.astype(f32) + (1.0 - beta_one) * gradient
-    variance = beta_two * square.astype(f32) + (1.0 - beta_two) * gradient * gradient
-    normed_step = (
-        moment
-        / (1.0 - beta_one**STEP)
-        / (jnp.sqrt(variance / (1.0 - beta_two**STEP)) + adam_epsilon)
-    )
-    return (moment, variance, values - step_rate * (normed_step + decay_rate * values))
 
 
 def per_device(
@@ -808,7 +1360,6 @@
 ):
     gains = norm_gains.astype(f32)
     cos, sin = (jnp.asarray(t) for t in tables())
-    core = lax.rem(lax.axis_index("shard"), 2)
 
     by_head = jnp.concatenate(
         [
@@ -821,28 +1372,18 @@
         ],
         2,
     ).transpose(1, 0, 2)
+    lifting_rows = lifting.transpose(1, 0, 2)
     by_unit = (
         lifting.reshape(96, EXPERTS, 2, SHARDS, 32)
         .transpose(3, 0, 2, 1, 4)
-        .reshape(SHARDS, 96, 2, HID)
-    )
-    by_unit = jnp.pad(by_unit, ((0, 0), (0, 0), (0, 0), (0, PAD - HID)))
-    by_unit = by_unit.reshape(SHARDS, 96, 2 * PAD)
-
-    x_all = gather(layer_input, 2)
-
-    head_weight, unit_weight = exchange((by_head, by_unit), ("heads", "all"), 1, "spread_weights")
+        .reshape(SHARDS, 96, 2 * HID)
+    )
+    down_weight = lowering.transpose(1, 0, 2).reshape(HID, D)
+
+    x_all, head_weight = gather(layer_input, 2, by_head)
     head_weight = head_weight.reshape(D, 384)
-    unit_weight = unit_weight.reshape(D, 2 * PAD)
-    down_weight = lowering.transpose(1, 0, 2).reshape(HID, D)
-    down_weight = jnp.pad(down_weight, ((0, PAD - HID), (0, 0)))
-
     gain_rows = head_weight[:, 192:194].T.astype(f32)
     gain_one, gain_two = gain_rows[0:1], gain_rows[1:2]
-
-    stream = layer_input.astype(f32)
-    inverse_one = inverse_root(stream)
-    unit_one = stream * inverse_one
 
     gates = jax.nn.softmax(route_logits, axis=-1)
     picked = routes[:, :, None] == jnp.arange(EXPERTS, dtype=jnp.int32)[None, None, :]
@@ -852,121 +1393,74 @@
     shares = jnp.concatenate(
         [jnp.pad(high, ((0, 0), (0, 6))), jnp.pad(rest, ((0, 0), (0, 102)))], 1
     ).astype(bf16)
-    y_all = lax.all_gather(
-        jnp.concatenate([grad_output, shares], 1), "shard", axis=0, tiled=True
-    )
-    outward_all = lax.all_gather(outward, "shard", axis=0, tiled=True)
+    late_outward, late_y, x_all = lax.optimization_barrier(
+        (outward, jnp.concatenate([grad_output, shares], 1), x_all)
+    )
+    outward_all = lax.all_gather(late_outward, "shard", axis=0, tiled=True)
+    y_all = lax.all_gather(late_y, "shard", axis=0, tiled=True)
 
     q, k, v, u_one = project(x_all, head_weight, gain_one, cos, sin)
-    attended, lse = attend(q, k, v)
+    attended, lse, unit_weight = attend(q, k, v, by_unit, 1)
+    unit_weight = unit_weight.reshape(D, 2 * HID)
     (own_attended,) = exchange((attended,), ("home",), 3, "attended_home")
-    low_attended = own_attended.transpose(1, 0, 2).reshape(OWN, HEADS * HEAD)
-
-    mixed = stream + jnp.dot(low_attended, outward_all, preferred_element_type=f32)
-    inverse_two = inverse_root(mixed)
-    unit_two = mixed * inverse_two
-    low_two = (unit_two * gain_two).astype(bf16)
-    u_two = gather(low_two, 4)
-
-    out_part, du_part, act, grad_lift = experts(
-        u_two, y_all, y_all, unit_weight, down_weight, jnp.asarray(spread_table(), bf16)
-    )
-    du, expert_out = reduce_blocks(
-        (du_part.reshape(SHARDS, OWN, D), out_part.reshape(SHARDS, OWN, D)), 5
-    )
-    layer_output = mixed + expert_out
-    lift_part = contract(u_two, grad_lift, ((0,), (0,))).astype(bf16)
-    down_part = contract(act, y_all[:, :D], ((0,), (0,))).astype(bf16)
-
-    grad_mixed = grad_output.astype(f32) + norm_back(du * gain_two, unit_two, inverse_two)
-    low_mixed = grad_mixed.astype(bf16)
-    grad_attended = contract(low_mixed, outward_all, ((1,), (1,))).astype(bf16)
-    (head_grads,) = exchange(
-        (grad_attended.reshape(OWN, KV_HEADS, 192).transpose(1, 0, 2),), ("away",), 6, "grads_away"
-    )
-    outward_part = contract(low_attended, low_mixed, ((0,), (0,))).astype(bf16)
-    outward_own = lax.psum_scatter(outward_part, "shard", scatter_dimension=0, tiled=True)
-
-    lse = lse[:, :, 0].reshape(BLOCKS, 1, ROWS)
-    delta = jnp.sum(
-        (attended.astype(f32) * head_grads.astype(f32)).reshape(BLOCKS, OWN, GROUP, HEAD), -1
-    )
-    delta = delta.transpose(0, 2, 1).reshape(BLOCKS, 1, ROWS)
-    dq, dkv = attend_back(q, k, v, head_grads, lse, delta, cos, sin, core)
-    inward_all = lax.all_gather(inward, "shard", axis=0, tiled=True)
-
-    own_dq, own_dkv = exchange(
-        (dq, dkv.reshape(SHARDS, OWN, 128)), ("home", "all"), 7, "pairs_home"
-    )
-    pairs = jnp.sum(own_dkv.reshape(CHIPS, 2, OWN, 128).astype(f32), 1)
-    grad_joined = jnp.concatenate(
-        [
-            own_dq.transpose(1, 0, 2).reshape(OWN, 1536),
-            pairs[:, :, :HEAD].transpose(1, 0, 2).reshape(OWN, 512).astype(bf16),
-            pairs[:, :, HEAD:].transpose(1, 0, 2).reshape(OWN, 512).astype(bf16),
-        ],
-        1,
-    )
-    dh = contract(grad_joined, inward_all, ((1,), (1,)))
-    input_grad = grad_mixed + norm_back(dh * gain_one, unit_one, inverse_one)
-
-    u_pairs = u_one.reshape(BLOCKS, 2, OWN, D)
-    even = u_pairs[:, 0]
-    odd = u_pairs[:, 1]
-    pick = (lax.rem(jnp.arange(BLOCKS), 2) == core)[:, None, None]
-    u_own = jnp.where(pick, even, odd).reshape(BLOCKS * OWN, D)
-    query_part = contract(u_own, dq.reshape(BLOCKS * OWN, 192), ((0,), (0,)))
-    pair_part = contract(u_one, dkv, ((0,), (0,)))
-    inward_part = jnp.concatenate([query_part, pair_part], 1).astype(bf16)
-    inward_pad = jnp.pad(inward_part, ((0, 0), (0, 64)))
-    lift_got, inward_got = exchange(
-        (lift_part.reshape(SHARDS, 96, 2 * PAD), inward_pad.reshape(SHARDS, 96, 384)),
-        ("all", "all"),
-        8,
-        "grads_to_owners",
-    )
-    inward_sum = jnp.sum(inward_got.reshape(CHIPS, 2, 96, 384).astype(f32), 1).astype(bf16)
-    lift_sum, down_sum, inward_sum, outward_sum = total_over_reps(
-        (
-            lift_got.reshape(REPS, 192, 2 * PAD),
-            down_part.reshape(REPS, 48, D),
-            inward_sum,
-            outward_own.reshape(REPS, 16, 1152),
-        ),
-        9,
-    )
-    lift_grad = (
-        lift_sum.reshape(SHARDS, 96, 2, PAD)[..., :HID]
-        .reshape(SHARDS, 96, 2, EXPERTS, 32)
-        .transpose(1, 3, 2, 0, 4)
-        .reshape(96, EXPERTS, 1024)
-        .astype(f32)
-    )
-    down_grad = down_sum.reshape(PAD, D)[:HID].reshape(EXPERTS, 32, D).transpose(1, 0, 2).astype(f32)
-    inward_sum = inward_sum.transpose(1, 0, 2)
-    inward_grad = jnp.concatenate(
-        [
-            inward_sum[:, :, :192].reshape(96, 1536),
-            inward_sum[:, :, 192:256].reshape(96, 512),
-            inward_sum[:, :, 256:320].reshape(96, 512),
-        ],
-        1,
-    ).astype(f32)
+    mixed, low_two = one_step(
+        mix_kernel,
+        (own_attended, outward_all, layer_input, gain_two),
+        (((OWN, D), f32), ((OWN, D), bf16)),
+        "mix",
+    )
+    (u_two,) = gather(low_two, 4)
+    late_inward, u_two = lax.optimization_barrier((inward, u_two))
+    inward_all = lax.all_gather(late_inward, "shard", axis=0, tiled=True)
+
+    out_part, du_part, lift_part, down_part = experts(
+        u_two, y_all, unit_weight, down_weight, jnp.asarray(spread_table(), bf16)
+    )
+    du, expert_out, lift_sum, down_sum = reduce_blocks(
+        du_part.reshape(SHARDS, OWN, D), out_part.reshape(SHARDS, OWN, D), lift_part, down_part, 5
+    )
+    layer_output, grad_mixed, away, outward_part = one_step(
+        unmix_kernel,
+        (du, expert_out, mixed, grad_output, gain_two, outward_all, own_attended),
+        (((OWN, D), f32), ((OWN, D), f32), ((CHIPS, OWN, 192), bf16), ((SHARDS, 96, D), bf16)),
+        "unmix",
+    )
+    (head_grads,) = exchange((away,), ("away",), 6, "grads_away")
+    dq, dkv, lift_got, outward_own = attend_back(
+        q, k, v, head_grads, attended, lse, cos, sin,
+        lift_sum.reshape(SHARDS, 96, 2 * HID), outward_part, 8,
+    )
+    inward_part = inward_parts(u_one, dq, dkv)
+    own_dq, own_dkv, inward_got = exchange(
+        (dq, dkv.reshape(SHARDS, OWN, 128), inward_part),
+        ("home", "all", "all"),
+        7,
+        "pairs_home",
+    )
+    (input_grad,) = one_step(
+        finish_kernel,
+        (own_dq, own_dkv, inward_all, grad_mixed, layer_input, gain_one),
+        (((OWN, D), f32),),
+        "finish",
+    )
+    inward_sum = jnp.sum(inward_got.reshape(CHIPS, 2, 96, 320).astype(f32), 1).astype(bf16)
+    inward_sum, outward_sum = total_over_reps(
+        (inward_sum, outward_own.reshape(REPS, 16, 1152)), 9
+    )
     outward_grad = outward_sum.reshape(96, D).astype(f32)
-    gain_grad = jnp.stack(
-        [
-            jnp.sum(inward.astype(f32) * inward_grad, 1),
-            jnp.sum(lifting.astype(f32) * lift_grad, (1, 2)),
-        ]
-    )
-    gain_grad = gain_grad / gains
-
+    down_grad = down_sum.reshape(EXPERTS, 32, D).transpose(1, 0, 2).astype(f32)
+
+    new_lifting = adam_lifting(
+        lifting_rows, mean_lifting.transpose(1, 0, 2), square_lifting.transpose(1, 0, 2), lift_got
+    )
+    lifting_dot = new_lifting[3]
+    new_lifting = tuple(t.transpose(1, 0, 2) for t in new_lifting[:3])
+    new_inward = adam_inward(inward, mean_inward, square_inward, inward_sum)
+    gain_grad = jnp.stack([new_inward[3][:, 0], lifting_dot[:, 0]]) / gains
     new_gains = adam(norm_gains, mean_gains, square_gains, gain_grad, rate_gains, 0.0)
-    new_inward = adam(inward, mean_inward, square_inward, inward_grad, rate_inward, weight_decay)
     new_outward = adam(
         outward, mean_outward, square_outward, outward_grad, rate_outward, weight_decay
     )
-    new_lifting = adam(lifting, mean_lifting, square_lifting, lift_grad, rate_lifting, weight_decay)
     new_lowering = adam(
         lowering, mean_lowering, square_lowering, down_grad, rate_lowering, weight_decay
     )

time: 850 us -> 622 us (0.73); the launches traced: 835 us -> 616 us
  Pallas kernels: 648 us -> 539 us
  matrix products: 43.5 us -> 0 us
  local copies, waits for them, and re-layouts: 84.6 us -> 46.5 us
  other arithmetic: 41.9 us -> 13.7 us
    pallas_call x5 -> x3, Pallas kernels: 189 us -> 82.7 us  [exchange(): pl.pallas_call(functools.partial(exchange_kernel, kinds), out_shape=tuple...]
    pallas_call x1, Pallas kernels: 122 us -> 23.9 us  [total_over_reps(): pl.pallas_call(functools.partial(total_kernel, n), out_shape=tuple((jax.S...]
    pallas_call x3 -> x9, Pallas kernels: 232 us -> 285 us  [the longest x2 129 us: gather(): pl.pallas_call(functools.partial(gather_kernel, bool(extra)), out_shape=s...]
    dot_general x8 -> x0, matrix products: 43.5 us -> none  [the longest x7 39.6 us: contract(): lax.dot_general(a, b, ((dims[0], dims[1]), ((), ())), preferred_element_t...]
    unnamed x106 -> x85, local copies, waits for them, and re-layouts: 45.6 us -> 19 us
    pallas_call x1, Pallas kernels: 37.4 us -> 56.2 us  [attend_back(): pl.pallas_call(attend_back_kernel, grid=(BLOCKS,), in_specs=[pl.BlockSpec...]
    pallas_call x1, Pallas kernels: 32.1 us -> 50.1 us  [experts(): pl.pallas_call(experts_kernel, grid=(SEQ // step,), in_specs=[pl.BlockSpe...]
    sub x5 -> x3, other arithmetic: 17.5 us -> 5.79 us  [adam(): values - step_rate * (normed_step + decay_rate * values)]
  transfers between devices with their start and end apart: 4 -> 3, of which waited for: 0 -> 0; matrix products, arithmetic and copies ran while one was open for 13% -> 6% of each run, Pallas kernels for 63% -> 77%
where the time goes in v2:
time: 622 us; the launch traced here: 616 us
  Pallas kernels  539 us (87%)
  local copies, waits for them, and re-layouts  46.5 us (7%)
  between operations  14.5 us (2%)
  other arithmetic  13.7 us (2%)
    pallas_call x2, Pallas kernels, gather(): pl.pallas_call(functools.partial(gather_kernel, bool(extra)), out_shape=s...  129 us
    pallas_call x1, Pallas kernels, reduce_blocks(): pl.pallas_call(reduce_kernel, out_shape=(jax.ShapeDtypeStruct((OWN, D), f...  108 us
    pallas_call x3, Pallas kernels, exchange(): pl.pallas_call(functools.partial(exchange_kernel, kinds), out_shape=tuple...  82.7 us
    pallas_call x1, Pallas kernels, attend_back(): pl.pallas_call(attend_back_kernel, grid=(BLOCKS,), in_specs=[pl.BlockSpec...  56.2 us
    pallas_call x1, Pallas kernels, experts(): pl.pallas_call(experts_kernel, grid=(SEQ // step,), in_specs=[pl.BlockSpe...  50.1 us
    pallas_call x1, Pallas kernels, attend(): pl.pallas_call(attend_kernel, grid=(BLOCKS,), in_specs=[pl.BlockSpec((1,...  28.6 us
    pallas_call x1, Pallas kernels, total_over_reps(): pl.pallas_call(functools.partial(total_kernel, n), out_shape=tuple((jax.S...  23.9 us
    pallas_call x3, Pallas kernels, one_step(): pl.pallas_call(kernel, in_specs=[VMEM] * len(arrays), out_specs=(VMEM,) *...  22.5 us
  transfers between devices with their start and end apart: 3, of which 0 were waited for; matrix products, arithmetic and copies ran while one was open for 6% of the time, Pallas kernels for 77%

profile of v2, /device:TPU:1, one launch (start us, length us, event | category | flops | bytes accessed | tf_op | source)
XLA Modules:
  0.0 615.5 jit_solution(7914149439724075960)
XLA Ops:
  9.4 0.7 select_reduce_fusion
  10.2 1.0 fusion.16
  11.2 1.0 slice.24
  13.5 1.1 maximum_bitcast_fusion.refs_1_
  14.6 54.6 %gather_rows.2 = (bf16[16,192,1536]{2,1,0:T(8,128)(2,1)}, bf16[16,96,384]{2,1,0:T(8,128)(2,1)}) custom-call(bf16[192,1536]{1,0:T(8,128)(2,1)} %x_ref.3, bf16[8,96,384]{2,1,0:T(8,128)(2,1)} %maximum_bitcast_fusion.refs_1_), custom_call_target="tpu_custom_call" | custom-call | tf_op jit(solution)/shard_map/gather_rows/pallas_call | solution.py:212
  69.3 1.0 concatenate.9
  71.7 1.2 slice_convert_fusion
  73.1 2.5 copy.83
  75.6 4.0 copy.84
  79.7 4.4 copy.85.b_ref
  84.6 1.3 copy-done.16
  85.9 13.5 %project_heads.1 = (bf16[8,576,64]{2,1,0:T(8,128)(2,1)S(1)}, bf16[3072,64]{1,0:T(8,128)(2,1)S(1)}, bf16[3072,128]{1,0:T(8,128)(2,1)S(1)}, bf16[3072,1536]{1,0:T(8,128)(2,1)}) custom-call(bf16[3072,1536]{1,0:T(8,128)(2,1)} %bitcast.54, bf16[1536,384]{1,0:T(8,128)(2,1)S(1)} %bitcast.47, f32[1,1536]{1,0:T(1,128)S(1)} %get-tuple-element.121.g_ref, ...), custom_call_target="tpu_custom_call" | custom-call | tf_op jit(solution)/shard_map/project_heads/pallas_call | solution.py:757
  99.4 28.6 %attend.1 = (bf16[8,192,192]{2,1,0:T(8,128)(2,1)S(1)}, f32[8,8,576]{2,1,0:T(8,128)S(1)}, bf16[16,96,640]{2,1,0:T(8,128)(2,1)S(1)}) custom-call(bf16[8,576,64]{2,1,0:T(8,128)(2,1)S(1)} %get-tuple-element.65.q_ref, bf16[3072,64]{1,0:T(8,128)(2,1)S(1)} %get-tuple-element.66.k_ref, bf16[3072,128]{1,0:T(8,128)(2,1)S(1)} %get-tuple-element.67.v_ref, ...), custom_call_target="tpu_custom_call" | custom-call | tf_op jit(solution)/shard_map/attend/pallas_call | solution.py:870
  128.1 0.9 copy-done.9
  128.9 1.3 copy-done.17
  130.9 25.1 %attended_home.1.a_ref = bf16[8,192,192]{2,1,0:T(8,128)(2,1)} custom-call(bf16[8,192,192]{2,1,0:T(8,128)(2,1)} %copy-done.9), custom_call_target="tpu_custom_call" | custom-call | tf_op jit(solution)/shard_map/attended_home/pallas_call | solution.py:356
  156.0 5.2 mix.1
  161.2 74.0 %gather_rows.3 = bf16[16,192,1536]{2,1,0:T(8,128)(2,1)} custom-call(bf16[192,1536]{1,0:T(8,128)(2,1)} %get-tuple-element.70.refs_0_), custom_call_target="tpu_custom_call" | custom-call | tf_op jit(solution)/shard_map/gather_rows/pallas_call | solution.py:212
  235.2 50.1 %experts.1 = (bf16[3072,1536]{1,0:T(8,128)(2,1)}, bf16[3072,1536]{1,0:T(8,128)(2,1)}, bf16[1536,640]{1,0:T(8,128)(2,1)}, bf16[320,1536]{1,0:T(8,128)(2,1)}) custom-call(bf16[3072,1536]{1,0:T(8,128)(2,1)} %bitcast.51, bf16[3072,1664]{1,0:T(8,128)(2,1)} %all-gather.6.cloned.1.call-done.y_ref.c_ref, ...), custom_call_target="tpu_custom_call" | custom-call | tf_op jit(solution)/shard_map/experts/pallas_call | solution.py:1122
  285.3 2.7 reshape.108
  288.0 1.0 copy.94
  289.1 107.9 %reduce_rows.1 = (f32[192,1536]{1,0:T(8,128)}, f32[192,1536]{1,0:T(8,128)}, bf16[4,2,192,640]{3,2,1,0:T(8,128)(2,1)}, bf16[4,2,80,768]{3,2,1,0:T(8,128)(2,1)}) custom-call(bf16[16,192,1536]{2,1,0:T(8,128)(2,1)} %bitcast.56, bf16[16,192,1536]{2,1,0:T(8,128)(2,1)} %bitcast.55, bf16[4,2,192,640]{3,2,1,0:T(8,128)(2,1)} %bitcast.60, bf16[4,2,80,768]{3,2,1,0:T(8,128)(2,1)} %bitcast.58), custom_call_target="tpu_custom_call" | custom-call | tf_op jit(solution)/shard_map/reduce_rows/pallas_call | solution.py:605
  396.9 9.2 %unmix.1 = (f32[192,1536]{1,0:T(8,128)}, f32[192,1536]{1,0:T(8,128)}, bf16[8,192,192]{2,1,0:T(8,128)(2,1)}, bf16[16,96,1536]{2,1,0:T(8,128)(2,1)}) custom-call(f32[192,1536]{1,0:T(8,128)} %get-tuple-element.78.du_ref, f32[192,1536]{1,0:T(8,128)} %get-tuple-element.79.e_ref, f32[192,1536]{1,0:T(8,128)} %get-tuple-element.80.mixed_ref, ...), custom_call_target="tpu_custom_call" | custom-call | tf_op jit(solution)/shard_map/unmix/pallas_call | solution.py:1152
  406.1 17.6 %grads_away.1.g_ref = bf16[8,192,192]{2,1,0:T(8,128)(2,1)} custom-call(bf16[8,192,192]{2,1,0:T(8,128)(2,1)} %get-tuple-element.82.refs_0_), custom_call_target="tpu_custom_call" | custom-call | tf_op jit(solution)/shard_map/grads_away/pallas_call | solution.py:356
  423.7 1.1 copy-done.10
  424.9 1.1 copy-done.11
  426.0 0.9 copy-done.25
  426.9 56.2 %attend_back.1 = (bf16[8,192,192]{2,1,0:T(8,128)(2,1)S(1)}, bf16[3072,128]{1,0:T(8,128)(2,1)S(1)}, bf16[16,96,640]{2,1,0:T(8,128)(2,1)}, bf16[96,1536]{1,0:T(8,128)(2,1)S(1)}) custom-call(bf16[8,576,64]{2,1,0:T(8,128)(2,1)} %copy-done.2, bf16[3072,64]{1,0:T(8,128)(2,1)S(1)} %copy-done.6, bf16[3072,128]{1,0:T(8,128)(2,1)S(1)} %copy-done.8, ...), custom_call_target="tpu_custom_call" | custom-call | tf_op jit(solution)/shard_map/attend_back/pallas_call | solution.py:1040
  483.1 0.9 copy-done.12
  484.0 0.9 copy-done.14
  485.6 1.9 reshape.111.refs_1_
  487.5 1.1 copy-done.13
  488.6 1.1 copy-done.15
  489.7 9.6 %inward_parts.1.refs_2_ = bf16[16,96,320]{2,1,0:T(8,128)(2,1)S(1)} custom-call(bf16[3072,1536]{1,0:T(8,128)(2,1)} %get-tuple-element.88.u_ref, bf16[8,192,192]{2,1,0:T(8,128)(2,1)S(1)} %copy-done.13, bf16[3072,128]{1,0:T(8,128)(2,1)S(1)} %copy-done.15), custom_call_target="tpu_custom_call" | custom-call | tf_op jit(solution)/shard_map/inward_parts/pallas_call | solution.py:1223
  499.4 1.0 copy-done.3
  500.4 40.1 %pairs_home.1 = (bf16[8,192,192]{2,1,0:T(8,128)(2,1)}, bf16[16,192,128]{2,1,0:T(8,128)(2,1)}, bf16[16,96,320]{2,1,0:T(8,128)(2,1)}) custom-call(bf16[8,192,192]{2,1,0:T(8,128)(2,1)} %copy-done.12, bf16[16,192,128]{2,1,0:T(8,128)(2,1)} %bitcast.45, bf16[16,96,320]{2,1,0:T(8,128)(2,1)} %copy-done.3), custom_call_target="tpu_custom_call" | custom-call | tf_op jit(solution)/shard_map/pairs_home/pallas_call | solution.py:356
  540.5 2.5 bitcast_reduce_fusion.refs_0_
  543.0 23.9 %total_over_reps.1 = (bf16[8,96,320]{2,1,0:T(8,128)(2,1)}, bf16[8,16,1152]{2,1,0:T(8,128)(2,1)}) custom-call(bf16[8,96,320]{2,1,0:T(8,128)(2,1)} %bitcast_reduce_fusion.refs_0_, bf16[8,16,1152]{2,1,0:T(8,128)(2,1)} %reshape.111.refs_1_), custom_call_target="tpu_custom_call" | custom-call | tf_op jit(solution)/shard_map/total_over_reps/pallas_call | solution.py:714
  566.9 2.0 reshape.112
  569.1 2.8 copy.87
  571.9 3.9 reshape.113
  575.8 1.2 copy-done.22
  577.0 2.6 adam_inward.1
  579.6 1.5 copy-done.19
  581.2 13.3 %adam_lifting.1 = (f32[10,96,1024]{2,1,0:T(8,128)}, f32[10,96,1024]{2,1,0:T(8,128)}, f32[10,96,1024]{2,1,0:T(8,128)}, f32[96,128]{1,0:T(8,128)S(1)}) custom-call(bf16[10,96,1024]{2,1,0:T(8,128)(2,1)S(1)} %bitcast.44, bf16[10,96,1024]{2,1,0:T(8,128)(2,1)S(1)} %bitcast.49, bf16[10,96,1024]{2,1,0:T(8,128)(2,1)S(1)} %bitcast.50, ...), custom_call_target="tpu_custom_call" | custom-call | tf_op jit(solution)/shard_map/adam_lifting/pallas_call | solution.py:1277
  595.4 1.5 convert_subtract_fusion.1
  596.9 3.7 convert_subtract_fusion
  600.6 8.1 %finish.1 = f32[192,1536]{1,0:T(8,128)} custom-call(bf16[8,192,192]{2,1,0:T(8,128)(2,1)} %get-tuple-element.89.dq_ref, bf16[16,192,128]{2,1,0:T(8,128)(2,1)} %get-tuple-element.90.dkv_ref, bf16[1536,2560]{1,0:T(8,128)(2,1)} %all-gather.8.cloned.1.call-done.w_ref, f32[192,1536]{1,0:T(8,128)} %get-tuple-element.92.dz_ref, bf16[192,1536]{1,0:T(8,128)(2,1)} %x_ref.3, ...), custom_call_target="tpu_custom_call" | custom-call | tf_op jit(solution)/shard_map/finish/pallas_call | solution.py:1152
  (100 shorter events, 8.3 us)
Async XLA Ops:
  7.2 148.8 %all-gather.4.cloned.1.call-start = ((), (), s32[]{:S(2)}) async-start(), calls=%async_computation | async-start | bytes 5013504 | tf_op jit(solution)/shard_map/all_gather | solution.py:1399
  11.2 2.2 copy-start.37
  13.3 56.0 %copy-start.29 = (bf16[192,1536]{1,0:T(8,128)(2,1)S(1)}, bf16[192,1536]{1,0:T(8,128)(2,1)}, u32[]{:S(2)}) copy-start(bf16[192,1536]{1,0:T(8,128)(2,1)} %y_ref.1) | copy-start | bytes 1769476
  69.3 3.8 copy-start.1
  70.3 164.9 %all-gather.6.cloned.1.call-start = ((), (), s32[]{:S(2)}) async-start(), calls=%async_computation.1 | async-start | bytes 10862592 | tf_op jit(solution)/shard_map/all_gather | solution.py:1400
  71.1 529.5 %all-gather.8.cloned.1.call-start = ((), (), s32[]{:S(2)}) async-start(), calls=%async_computation.2 | async-start | bytes 8355840 | tf_op jit(solution)/shard_map/all_gather | solution.py:1414
  79.7 5.0 copy-start
  84.6 14.8 %copy-start.26 = (f32[1,1536]{1,0:T(1,128)}, f32[1,1536]{1,0:T(1,128)S(1)}, u32[]{:S(2)}) copy-start(f32[1,1536]{1,0:T(1,128)S(1)} %get-tuple-element.121.g_ref) | copy-start | bytes 18436
  84.6 1.3 copy-start.16
  99.4 28.6 %copy-start.2 = (bf16[8,576,64]{2,1,0:T(8,128)(2,1)}, bf16[8,576,64]{2,1,0:T(8,128)(2,1)S(1)}, u32[]{:S(2)}) copy-start(bf16[8,576,64]{2,1,0:T(8,128)(2,1)S(1)} %get-tuple-element.65.q_ref) | copy-start | bytes 1769476
  99.4 28.6 %copy-start.5 = (bf16[3072,64]{1,0:T(8,128)(2,1)}, bf16[3072,64]{1,0:T(8,128)(2,1)S(1)}, u32[]{:S(2)}) copy-start(bf16[3072,64]{1,0:T(8,128)(2,1)S(1)} %get-tuple-element.66.k_ref) | copy-start | bytes 1179652
  99.4 28.6 %copy-start.7 = (bf16[3072,128]{1,0:T(8,128)(2,1)}, bf16[3072,128]{1,0:T(8,128)(2,1)S(1)}, u32[]{:S(2)}) copy-start(bf16[3072,128]{1,0:T(8,128)(2,1)S(1)} %get-tuple-element.67.v_ref) | copy-start | bytes 2359300
  128.1 0.9 copy-start.9
  128.9 1.3 copy-start.17
  130.2 0.7 copy-start.24
  406.1 17.6 %copy-start.6 = (bf16[3072,64]{1,0:T(8,128)(2,1)S(1)}, bf16[3072,64]{1,0:T(8,128)(2,1)}, u32[]{:S(2)}) copy-start(bf16[3072,64]{1,0:T(8,128)(2,1)} %copy-done.5) | copy-start | bytes 1179652
  406.1 17.6 %copy-start.8 = (bf16[3072,128]{1,0:T(8,128)(2,1)S(1)}, bf16[3072,128]{1,0:T(8,128)(2,1)}, u32[]{:S(2)}) copy-start(bf16[3072,128]{1,0:T(8,128)(2,1)} %copy-done.7) | copy-start | bytes 2359300
  423.7 1.1 copy-start.10
  424.9 1.1 copy-start.11
  426.0 0.9 copy-start.25
  483.1 0.9 copy-start.12
  484.0 0.9 copy-start.14
  484.8 0.7 copy-start.23
  487.5 1.1 copy-start.13
  488.6 1.1 copy-start.15
  499.4 1.0 copy-start.3
  540.5 28.4 %copy-start.32 = (bf16[4,2,80,768]{3,2,1,0:T(8,128)(2,1)S(1)}, bf16[4,2,80,768]{3,2,1,0:T(8,128)(2,1)}, u32[]{:S(2)}) copy-start(bf16[4,2,80,768]{3,2,1,0:T(8,128)(2,1)} %get-tuple-element.102) | copy-start | bytes 2949124
  571.9 3.9 copy-start.4
  571.9 3.9 copy-start.20
  571.9 3.9 copy-start.21
  575.8 3.8 copy-start.18
  575.8 1.2 copy-start.22
  579.6 1.5 copy-start.19
  581.1 13.6 %copy-start.38 = (bf16[2,96]{1,0:T(2,128)(2,1)S(1)}, bf16[2,96]{1,0:T(2,128)(2,1)}, u32[]{:S(2)}) copy-start(bf16[2,96]{1,0:T(2,128)(2,1)} %param.36) | copy-start | bytes 1156
  581.1 13.6 %copy-start.39 = (bf16[2,96]{1,0:T(2,128)(2,1)S(1)}, bf16[2,96]{1,0:T(2,128)(2,1)}, u32[]{:S(2)}) copy-start(bf16[2,96]{1,0:T(2,128)(2,1)} %param.31) | copy-start | bytes 1156
  581.1 14.2 %copy-start.30 = (f32[96,1536]{1,0:T(8,128)S(1)}, f32[96,1536]{1,0:T(8,128)}, u32[]{:S(2)}) copy-start(f32[96,1536]{1,0:T(8,128)} %reshape.112) | copy-start | bytes 1769476
  581.1 14.2 %copy-start.31 = (bf16[96,1536]{1,0:T(8,128)(2,1)S(1)}, bf16[96,1536]{1,0:T(8,128)(2,1)}, u32[]{:S(2)}) copy-start(bf16[96,1536]{1,0:T(8,128)(2,1)} %param.28) | copy-start | bytes 884740
  581.2 14.2 %copy-start.35 = (bf16[96,1536]{1,0:T(8,128)(2,1)S(1)}, bf16[96,1536]{1,0:T(8,128)(2,1)}, u32[]{:S(2)}) copy-start(bf16[96,1536]{1,0:T(8,128)(2,1)} %param.38) | copy-start | bytes 884740
  581.2 14.2 %copy-start.36 = (bf16[96,1536]{1,0:T(8,128)(2,1)S(1)}, bf16[96,1536]{1,0:T(8,128)(2,1)}, u32[]{:S(2)}) copy-start(bf16[96,1536]{1,0:T(8,128)(2,1)} %param.33) | copy-start | bytes 884740
  581.2 15.8 %copy-start.33 = (bf16[32,10,1536]{2,0,1:T(8,128)(2,1)S(1)}, bf16[32,10,1536]{2,0,1:T(8,128)(2,1)}, u32[]{:S(2)}) copy-start(bf16[32,10,1536]{2,0,1:T(8,128)(2,1)} %param.40) | copy-start | bytes 2949124
  581.2 15.7 %copy-start.34 = (bf16[32,10,1536]{2,0,1:T(8,128)(2,1)S(1)}, bf16[32,10,1536]{2,0,1:T(8,128)(2,1)}, u32[]{:S(2)}) copy-start(bf16[32,10,1536]{2,0,1:T(8,128)(2,1)} %param.35) | copy-start | bytes 2949124
  594.5 2.4 copy-start.27
  594.5 2.4 copy-start.28
Sparse Core Ops, SparseCore 0:
  70.5 40.9 all-gather.3
  113.7 113.3 all-gather.5
  235.3 49.9 all-gather.7

commit v3 on v2

--- a/solution.py
+++ b/solution.py
@@ -33,7 +33,11 @@
 OWN = 192
 SEQ = OWN * SHARDS
 D = 1536
-HID = 320
+PEERS = 8
+FLAT = 40
+FLAT_PAD = 48
+HID = SHARDS * FLAT
+EXP = 2 * HID
 BLOCKS = 8
 ROWS = GROUP * OWN
 KEYS = 2 * OWN
@@ -79,11 +83,124 @@
 VMEM = pl.BlockSpec(memory_space=pltpu.VMEM)
 
 
-def gather_kernel(with_parts, *refs):
-    if with_parts:
-        x_ref, w_ref, o_ref, p_ref, local_sem, send_sem, recv_sem, s_part, r_part = refs
-    else:
-        x_ref, o_ref, local_sem, send_sem, recv_sem = refs
+def along_x(rep, dx):
+    return 2 * lax.rem(rep // 2 + dx, 4) + lax.rem(rep, 2)
+
+
+def landed_on(ref, recv_sem, any_send_sem, device):
+    pltpu.make_async_remote_copy(
+        src_ref=ref,
+        dst_ref=ref,
+        send_sem=any_send_sem,
+        recv_sem=recv_sem,
+        device_id=device,
+        device_id_type=MESH,
+    ).wait_recv()
+
+
+def x_gather(x_ref, o_ref, local_sem, send_sem, recv_sem):
+    rep, shard = place()
+    core = lax.rem(shard, 2)
+    sib = shard + 1 - 2 * core
+    half = x_ref.shape[0] // 2
+    top, bottom = pl.ds(0, half), pl.ds(half, half)
+    up, down, far = (along_x(rep, d) for d in (1, 3, 2))
+
+    def block(r, other=False):
+        return 2 * (r // 2) + (1 - core if other else core)
+
+    mine = block(rep)
+    own = pltpu.make_async_copy(x_ref, o_ref.at[mine], local_sem)
+    sent = []
+
+    def put(ref, dst, slot, device):
+        sent.append(send(ref, dst, send_sem.at[len(sent)], recv_sem.at[slot], device))
+
+    def arrived(ref, slot):
+        landed_on(ref, recv_sem.at[slot], send_sem.at[0], (rep, sib))
+
+    def start():
+        own.start()
+        put(x_ref, o_ref.at[mine], 0, (up, shard))
+        put(x_ref, o_ref.at[mine], 1, (down, shard))
+        put(x_ref, o_ref.at[mine], 4, (rep, sib))
+
+    def relay():
+        ref = o_ref.at[block(down)]
+        arrived(ref, 0)
+        put(o_ref.at[block(down), top], o_ref.at[block(down), top], 2, (up, shard))
+        put(ref, ref, 5, (rep, sib))
+        ref = o_ref.at[block(up)]
+        arrived(ref, 1)
+        put(o_ref.at[block(up), bottom], o_ref.at[block(up), bottom], 3, (down, shard))
+        put(ref, ref, 6, (rep, sib))
+
+    def relay_far():
+        for slot, part in ((2, top), (3, bottom)):
+            ref = o_ref.at[block(far), part]
+            arrived(ref, slot)
+            put(ref, ref, slot + 5, (rep, sib))
+
+    def finish():
+        arrived(o_ref.at[block(rep, True)], 4)
+        arrived(o_ref.at[block(down, True)], 5)
+        arrived(o_ref.at[block(up, True)], 6)
+        arrived(o_ref.at[block(far, True), top], 7)
+        arrived(o_ref.at[block(far, True), bottom], 8)
+        for copy in sent:
+            copy.wait_send()
+        own.wait()
+
+    return start, relay, relay_far, finish
+
+
+def spread(x_ref, o_ref, local_sem, send_sem, recv_sem):
+    rep, shard = place()
+    core = lax.rem(shard, 2)
+    chip = shard // 2
+    sib = shard + 1 - 2 * core
+    own = pltpu.make_async_copy(x_ref.at[core], o_ref.at[shard], local_sem)
+
+    def copy(src, slot, kind, i):
+        return pltpu.make_async_remote_copy(
+            src_ref=src,
+            dst_ref=o_ref.at[slot],
+            send_sem=send_sem.at[kind, i],
+            recv_sem=recv_sem.at[kind, i],
+            device_id=(rep, 2 * lax.rem(chip + i, 8) + core if i else sib),
+            device_id_type=MESH,
+        )
+
+    def start():
+        own.start()
+        copy(x_ref.at[1 - core], shard, 1, 0).start()
+        for i in range(1, 8):
+            copy(x_ref.at[core], shard, 0, i).start()
+
+    def relay():
+        copy(x_ref.at[core], sib, 1, 0).wait_recv()
+        for i in range(1, 8):
+            copy(o_ref.at[sib], sib, 1, i).start()
+
+    def finish():
+        own.wait()
+        copy(x_ref.at[1 - core], shard, 1, 0).wait_send()
+        for i in range(1, 8):
+            back = 2 * lax.rem(chip + 8 - i, 8)
+            copy(x_ref.at[core], back + core, 0, i).wait_recv()
+            copy(x_ref.at[core], back + 1 - core, 1, i).wait_recv()
+        for i in range(1, 8):
+            copy(x_ref.at[core], shard, 0, i).wait_send()
+            copy(o_ref.at[sib], sib, 1, i).wait_send()
+
+    return start, relay, finish
+
+
+def start_kernel(
+    x_ref, w_ref, t_ref, o_ref, p_ref, g_ref,
+    local_sem, send_sem, recv_sem, s_part, r_part, s_x, r_x,
+):
+    with_parts = True
     rep, shard = place()
     half = x_ref.shape[0] // 2
     core = lax.rem(shard, 2)
@@ -99,10 +216,12 @@
     def other(block):
         return block + 2 - 4 * y
 
-    if with_parts:
-        greet([(rep, sib)] + [(rep, p) for p in peers])
-    else:
-        greet([(rep, sib), (rep, pair), (rep, up), (rep, down)])
+    greet(
+        [(rep, sib)]
+        + [(rep, p) for p in peers]
+        + [(along_x(rep, 1), shard), (along_x(rep, 3), shard)]
+    )
+    x_steps = x_gather(t_ref, g_ref, local_sem.at[2], s_x, r_x)
     own = pltpu.make_async_copy(x_ref, o_ref.at[shard], local_sem.at[0])
     own.start()
     sent = []
@@ -132,6 +251,7 @@
     put(x_ref, o_ref.at[shard], 1, up)
     put(x_ref, o_ref.at[shard], 5, down)
     put(x_ref, o_ref.at[shard], 9, sib)
+    x_steps[0]()
     parts = []
     if with_parts:
         mine = pltpu.make_async_copy(w_ref.at[chip], p_ref.at[shard], local_sem.at[1])
@@ -156,12 +276,14 @@
     arrived(up, 5)
     forward(up, 7, down, bottom)
     forward(up, 12, sib)
+    x_steps[1]()
     arrived(other(down), 2)
     forward(other(down), 4, up, top)
     forward(other(down), 13, sib)
     arrived(other(up), 6)
     forward(other(up), 8, down, bottom)
     forward(other(up), 14, sib)
+    x_steps[2]()
     if with_parts:
         for i in range(1, 8):
             block = 2 * lax.rem(chip + 8 - i, 8) + core
@@ -198,32 +320,65 @@
     arrived(twin(far), 16, bottom)
     arrived(twin(other(far)), 17, top)
     arrived(twin(other(far)), 18, bottom)
+    x_steps[3]()
     for copy in sent + parts:
         copy.wait_send()
     own.wait()
 
 
-def gather(x, collective, parts=None):
+def start(x, parts, tokens, collective):
     rows, columns = x.shape
-    extra = () if parts is None else (parts,)
-    shapes = (jax.ShapeDtypeStruct((SHARDS, rows, columns), x.dtype),)
-    if extra:
-        shapes += (jax.ShapeDtypeStruct((SHARDS,) + parts.shape[1:], parts.dtype),)
-    out = pl.pallas_call(
-        functools.partial(gather_kernel, bool(extra)),
-        out_shape=shapes,
-        in_specs=[ANY] * len(shapes),
-        out_specs=(ANY,) * len(shapes),
-        scratch_shapes=[
-            pltpu.SemaphoreType.DMA((2,)),
-            pltpu.SemaphoreType.DMA((21,)),
-            pltpu.SemaphoreType.DMA((19,)),
-        ]
-        + [pltpu.SemaphoreType.DMA((15,))] * (2 * len(extra)),
+    dma = pltpu.SemaphoreType.DMA
+    gathered, parts, tokens = pl.pallas_call(
+        start_kernel,
+        out_shape=(
+            jax.ShapeDtypeStruct((SHARDS, rows, columns), x.dtype),
+            jax.ShapeDtypeStruct((SHARDS,) + parts.shape[1:], parts.dtype),
+            jax.ShapeDtypeStruct((PEERS,) + tokens.shape, tokens.dtype),
+        ),
+        in_specs=[ANY] * 3,
+        out_specs=(ANY,) * 3,
+        scratch_shapes=[dma((3,)), dma((21,)), dma((19,)), dma((15,)), dma((15,)), dma((9,)), dma((9,))],
         compiler_params=params(collective),
-        name="gather_rows",
-    )(x, *extra)
-    return (out[0].reshape(SHARDS * rows, columns),) + tuple(out[1:])
+        name="start",
+    )(x, parts, tokens)
+    return gathered.reshape(SHARDS * rows, columns), parts, tokens.reshape(PEERS * rows, -1)
+
+
+def second_kernel(x_ref, w_ref, o_ref, wo_ref, local_sem, s_x, r_x, s_w, r_w):
+    rep, shard = place()
+    core = lax.rem(shard, 2)
+    chip = shard // 2
+    greet(
+        [(rep, shard + 1 - 2 * core)]
+        + [(rep, 2 * lax.rem(chip + i, 8) + core) for i in range(1, 8)]
+        + [(along_x(rep, 1), shard), (along_x(rep, 3), shard)]
+    )
+    steps = x_gather(x_ref, o_ref, local_sem.at[0], s_x, r_x)
+    begin, relay, finish = spread(w_ref, wo_ref, local_sem.at[1], s_w, r_w)
+    steps[0]()
+    begin()
+    relay()
+    for step in steps[1:]:
+        step()
+    finish()
+
+
+def second(x, weights, collective):
+    dma = pltpu.SemaphoreType.DMA
+    gathered, weights = pl.pallas_call(
+        second_kernel,
+        out_shape=(
+            jax.ShapeDtypeStruct((PEERS,) + x.shape, x.dtype),
+            jax.ShapeDtypeStruct((SHARDS,) + weights.shape[1:], weights.dtype),
+        ),
+        in_specs=[ANY] * 2,
+        out_specs=(ANY,) * 2,
+        scratch_shapes=[dma((2,)), dma((9,)), dma((9,)), dma((2, 8)), dma((2, 8))],
+        compiler_params=params(collective),
+        name="second_gather",
+    )(x, weights)
+    return gathered.reshape(PEERS * OWN, D), weights
 
 
 def exchange_kernel(kinds, *refs):
@@ -368,360 +523,491 @@
     )(*arrays)
 
 
-SPLIT = 768
-
-
 def reduce_kernel(*refs):
-    du_ref, out_ref, lift_ref, down_ref = refs[:4]
-    ins = (du_ref, out_ref)
-    outs, lift_o, down_o = refs[4:6], refs[6], refs[7]
-    (
-        held, near, land_a, land_b, land_c, land_d,
-        lift_own, lift_land, lift_half, down_own, down_land, down_half,
-        load_sem, s_near, r_near, s_one, r_one, s_two, r_two,
-        a_load, a_s1, a_r1, a_s2, a_r2, a_s3, a_r3, a_s4, a_r4, a_out,
-    ) = refs[8:]
+    ins, grads = refs[:2], refs[2:4]
+    outs, grad_outs = refs[4:6], refs[6:8]
+    token_held, token_near, token_land = refs[8:11]
+    scratch = (refs[11:16], refs[16:21])
+    t_load, t_sn, t_rn, t_s, t_r, g_load, s_one, r_one, s_two, r_two = refs[21:]
     rep, shard = place()
     core = lax.rem(shard, 2)
     chip = shard // 2
     y = lax.rem(chip, 2)
     z = chip // 2
+    x = rep // 2
     sib = shard + 1 - 2 * core
     pair = shard + 2 - 4 * y
-    x, far_y = rep // 2, lax.rem(rep, 2)
-    mate = rep + 1 - 2 * far_y
-    first, last = pl.ds(0, SPLIT), pl.ds(SPLIT, D - SPLIT)
 
     def ahead(dz):
         return lax.rem(z + dz, 4)
 
-    def device(zz, yy):
-        return 4 * zz + 2 * yy + core
-
-    def along(dx):
-        return 2 * lax.rem(x + dx, 4) + far_y
+    def device(dz):
+        return (rep, 4 * ahead(dz) + 2 * y + core)
 
     greet(
         [(rep, sib), (rep, pair)]
-        + [(rep, device(ahead(dz), y)) for dz in (1, 2, 3)]
-        + [(along(dx), shard) for dx in (1, 2, 3)]
-        + [(mate, shard)]
-    )
-
-    def block(j):
-        dz, dy = j // 2, j % 2
-        return 2 * ahead(dz) + (y if dy == 0 else 1 - y)
-
-    order = [1, 3, 5, 7, 2, 4, 6, 0]
-    nears, loads = {}, {}
+        + [device(dz) for dz in (1, 2, 3)]
+        + [(along_x(rep, dx), shard) for dx in (1, 2, 3)]
+    )
+    near_copies, loads, token_sends = {}, {}, {}
     for n in range(2):
-        for j in order:
-            c = block(j)
-            nears[n, j] = send(
-                ins[n].at[2 * c + 1 - core], near.at[n, j], s_near.at[n, j], r_near.at[n, j], (rep, sib)
+        for dx in (2, 1, 3, 0):
+            to = lax.rem(x + dx, 4)
+            near_copies[n, dx] = send(
+                ins[n].at[2 * to + 1 - core], token_near.at[n, dx], t_sn.at[n, dx], t_rn.at[n, dx],
+                (rep, sib),
             )
-            loads[n, j] = pltpu.make_async_copy(
-                ins[n].at[2 * c + core], held.at[n, j], load_sem.at[n, j]
+            loads[n, dx] = pltpu.make_async_copy(
+                ins[n].at[2 * to + core], token_held.at[n, dx], t_load.at[n, dx]
             )
-            loads[n, j].start()
-    sums = ((lift_ref, lift_own, lift_land, lift_half, lift_o), (down_ref, down_own, down_land, down_half, down_o))
-    steps_one, steps_load = [], []
-    for m, (src, own, land, half, dst) in enumerate(sums):
-        load = pltpu.make_async_copy(src.at[x], own, a_load.at[m])
-        load.start()
-        steps_load.append(load)
-        for dx in (1, 2, 3):
-            steps_one.append(
-                send(
-                    src.at[lax.rem(x + dx, 4)], land.at[dx - 1], a_s1.at[m, dx], a_r1.at[m, dx],
-                    (along(dx), shard),
+            loads[n, dx].start()
+
+    ones, twos, grad_loads = {}, {}, {}
+    for m in range(2):
+        held, land_a, land_b, land_c, land_d = scratch[m]
+        columns = grads[m].shape[2]
+        first, last = pl.ds(0, columns // 2), pl.ds(columns // 2, columns // 2)
+        for j in (3, 5, 7, 1, 4, 2, 6, 0):
+            dz, dy = j // 2, j % 2
+            block = grads[m].at[2 * ahead(dz) + (1 - y if dy else y)]
+            if dy:
+                ones[m, 0, j] = send(
+                    block.at[:, first], land_a.at[dz], s_one.at[m, 0, j], r_one.at[m, 0, j], (rep, pair)
                 )
-            )
-    ones = {}
-    for n in range(2):
-        for j in order:
-            nears[n, j].wait_recv()
-            loads[n, j].wait()
-
-            def add(t, _, n=n, j=j):
-                at = pl.ds(pl.multiple_of(t * 32, 32), 32)
-                held[n, j, at] = (
-                    held[n, j, at].astype(f32) + near[n, j, at].astype(f32)
+            if dz:
+                ones[m, 1, j] = send(
+                    block.at[:, last], land_b.at[j - 2], s_one.at[m, 1, j], r_one.at[m, 1, j], device(dz)
+                )
+            if dy == 0 or dz == 0:
+                slot = dz if dy == 0 else 4
+                grad_loads[m, slot] = pltpu.make_async_copy(block, held.at[slot], g_load.at[m, slot])
+                grad_loads[m, slot].start()
+
+    def rows_of(t, step):
+        return pl.ds(pl.multiple_of(t * step, step), step)
+
+    def token_sums(n):
+        for dx in (2, 1, 3, 0):
+            near_copies[n, dx].wait_recv()
+            loads[n, dx].wait()
+
+            def add(t, _, dx=dx):
+                at = rows_of(t, 32)
+                token_held[n, dx, at] = (
+                    token_held[n, dx, at].astype(f32) + token_near[n, dx, at].astype(f32)
                 ).astype(bf16)
                 return 0
 
             lax.fori_loop(0, OWN // 32, add, 0)
-            dz, dy = j // 2, j % 2
-            if dy:
-                ones[n, 0, j] = send(
-                    held.at[n, j, :, first], land_a.at[n, dz], s_one.at[n, 0, j], r_one.at[n, 0, j],
-                    (rep, pair),
+            if dx:
+                token_sends[n, dx] = send(
+                    token_held.at[n, dx], token_land.at[n, dx - 1], t_s.at[n, dx], t_r.at[n, dx],
+                    (along_x(rep, dx), shard),
                 )
-            if dz:
-                ones[n, 1, j] = send(
-                    held.at[n, j, :, last], land_b.at[n, j - 2], s_one.at[n, 1, j], r_one.at[n, 1, j],
-                    (rep, device(ahead(dz), y)),
-                )
-
-    step = 32
-
-    def rows_of(t):
-        return pl.ds(pl.multiple_of(t * step, step), step)
-
-    twos = {}
-
-    def first_sums(n):
-        for dz in (1, 2, 3, 0):
-            ones[n, 0, 2 * dz + 1].wait_recv()
+
+    def token_result(n):
+        for dx in (1, 2, 3):
+            token_sends[n, dx].wait_recv()
+
+        def add(t, _):
+            at = rows_of(t, 32)
+            total = token_held[n, 0, at].astype(f32)
+            for dx in (1, 2, 3):
+                total = total + token_land[n, dx - 1, at].astype(f32)
+            outs[n][at] = total
+            return 0
+
+        lax.fori_loop(0, OWN // 32, add, 0)
+
+    def first_sums(m):
+        held, land_a, land_b, land_c, land_d = scratch[m]
+        rows, columns = held.shape[1:]
+        first, last = pl.ds(0, columns // 2), pl.ds(columns // 2, columns // 2)
+        for slot in range(5):
+            grad_loads[m, slot].wait()
+        for dz in (2, 1, 3, 0):
+            ones[m, 0, 2 * dz + 1].wait_recv()
 
             def add(t, _, dz=dz):
-                at = rows_of(t)
-                held[n, 2 * dz, at, first] = (
-                    held[n, 2 * dz, at, first].astype(f32) + land_a[n, dz, at].astype(f32)
+                at = rows_of(t, 16)
+                held[dz, at, first] = (
+                    held[dz, at, first].astype(f32) + land_a[dz, at].astype(f32)
                 ).astype(bf16)
                 return 0
 
-            lax.fori_loop(0, OWN // step, add, 0)
+            lax.fori_loop(0, rows // 16, add, 0)
             if dz:
-                twos[n, 0, dz] = send(
-                    held.at[n, 2 * dz, :, first], land_c.at[n, dz - 1], s_two.at[n, dz], r_two.at[n, dz],
-                    (rep, device(ahead(dz), y)),
+                twos[m, dz] = send(
+                    held.at[dz, :, first], land_c.at[dz - 1], s_two.at[m, dz], r_two.at[m, dz], device(dz)
                 )
         for dy in (1, 0):
             for dz in (1, 2, 3):
-                ones[n, 1, 2 * dz + dy].wait_recv()
-
-            def add(t, _, dy=dy):
-                at = rows_of(t)
-                total = held[n, dy, at, last].astype(f32)
+                ones[m, 1, 2 * dz + dy].wait_recv()
+            slot = 4 if dy else 0
+
+            def add(t, _, dy=dy, slot=slot):
+                at = rows_of(t, 16)
+                total = held[slot, at, last].astype(f32)
                 for dz in (1, 2, 3):
-                    total = total + land_b[n, 2 * dz + dy - 2, at].astype(f32)
-                held[n, dy, at, last] = total.astype(bf16)
+                    total = total + land_b[2 * dz + dy - 2, at].astype(f32)
+                held[slot, at, last] = total.astype(bf16)
                 return 0
 
-            lax.fori_loop(0, OWN // step, add, 0)
+            lax.fori_loop(0, rows // 16, add, 0)
             if dy:
-                twos[n, 1, 0] = send(
-                    held.at[n, 1, :, last], land_d.at[n], s_two.at[n, 0], r_two.at[n, 0], (rep, pair)
+                twos[m, 0] = send(
+                    held.at[4, :, last], land_d, s_two.at[m, 0], r_two.at[m, 0], (rep, pair)
                 )
 
-    def last_sums(n):
-        for dz in (1, 2, 3):
-            twos[n, 0, dz].wait_recv()
-        twos[n, 1, 0].wait_recv()
+    def last_sums(m):
+        held, land_a, land_b, land_c, land_d = scratch[m]
+        rows, columns = held.shape[1:]
+        first, last = pl.ds(0, columns // 2), pl.ds(columns // 2, columns // 2)
+        for dz in range(4):
+            twos[m, dz].wait_recv()
 
         def add(t, _):
-            at = rows_of(t)
-            total = held[n, 0, at, first].astype(f32)
+            at = rows_of(t, 16)
+            total = held[0, at, first].astype(f32)
             for dz in (1, 2, 3):
-                total = total + land_c[n, dz - 1, at].astype(f32)
-            outs[n][at, first] = total
-            outs[n][at, last] = held[n, 0, at, last].astype(f32) + land_d[n, at].astype(f32)
+                total = total + land_c[dz - 1, at].astype(f32)
+            grad_outs[m][at, first] = total.astype(bf16)
+            grad_outs[m][at, last] = (
+                held[0, at, last].astype(f32) + land_d[at].astype(f32)
+            ).astype(bf16)
             return 0
 
-        lax.fori_loop(0, OWN // step, add, 0)
-
+        lax.fori_loop(0, rows // 16, add, 0)
+
+    token_sums(0)
+    token_sums(1)
     first_sums(0)
-    for load in steps_load:
-        load.wait()
-    steps_two = []
-    for m, (src, own, land, half, dst) in enumerate(sums):
-        for dx in (1, 2, 3):
-            steps_one[3 * m + dx - 1].wait_recv()
-        size = own.shape[1]
-        for h in (0, 1):
-
-            def add(t, _, own=own, land=land, h=h):
-                at = pl.ds(pl.multiple_of(t * 16, 16), 16)
-                total = own[h, at].astype(f32)
-                for dx in range(3):
-                    total = total + land[dx, h, at].astype(f32)
-                own[h, at] = total.astype(bf16)
-                return 0
-
-            lax.fori_loop(0, size // 16, add, 0)
-        steps_two.append(
-            send(own.at[1 - far_y], half, a_s2.at[m], a_r2.at[m], (mate, shard))
-        )
+    token_result(0)
     first_sums(1)
-    steps_three, steps_four = [], []
-    for m, (src, own, land, half, dst) in enumerate(sums):
-        steps_two[m].wait_recv()
-
-        def add(t, _, own=own, half=half):
-            at = pl.ds(pl.multiple_of(t * 16, 16), 16)
-            half[at] = (own[far_y, at].astype(f32) + half[at].astype(f32)).astype(bf16)
-            return 0
-
-        lax.fori_loop(0, own.shape[1] // 16, add, 0)
-        steps_three.append(
-            send(half, dst.at[x, far_y], a_s3.at[m], a_r3.at[m], (mate, shard))
-        )
-        keep = pltpu.make_async_copy(half, dst.at[x, far_y], a_out.at[m])
-        keep.start()
-        steps_load.append(keep)
-        for dx in (1, 2, 3):
-            steps_four.append(
-                send(
-                    half, dst.at[x, far_y], a_s4.at[m, 0, dx], a_r4.at[m, 0, dx], (along(dx), shard)
-                )
-            )
+    token_result(1)
     last_sums(0)
-
-    def landed(ref, sem):
-        pltpu.make_async_remote_copy(
-            src_ref=ref,
-            dst_ref=ref,
-            send_sem=a_s3.at[0],
-            recv_sem=sem,
-            device_id=(mate, shard),
-            device_id_type=MESH,
-        ).wait_recv()
-
-    for m, (src, own, land, half, dst) in enumerate(sums):
-        landed(dst.at[x, 1 - far_y], a_r3.at[m])
-        for dx in (1, 2, 3):
-            ref = dst.at[x, 1 - far_y]
-            steps_four.append(
-                send(ref, ref, a_s4.at[m, 1, dx], a_r4.at[m, 1, dx], (along(dx), shard))
-            )
     last_sums(1)
-    for m, (src, own, land, half, dst) in enumerate(sums):
-        for dx in (1, 2, 3):
-            back = lax.rem(x + 4 - dx, 4)
-            landed(dst.at[back, far_y], a_r4.at[m, 0, dx])
-            landed(dst.at[back, 1 - far_y], a_r4.at[m, 1, dx])
-    for keep in steps_load[2:]:
-        keep.wait()
-    for copies in (nears.values(), ones.values(), twos.values(), steps_one, steps_two, steps_three, steps_four):
-        for copy in copies:
+    for copies in (near_copies, token_sends, ones, twos):
+        for copy in copies.values():
             copy.wait_send()
 
 
 def reduce_blocks(du, out, lift, down, collective):
-    lift = lift.reshape(4, 2, 192, 2 * HID)
-    down = down.reshape(4, 80, 2, D // 2).transpose(0, 2, 1, 3)
     dma = pltpu.SemaphoreType.DMA
-    result = pl.pallas_call(
+
+    def slots(rows, columns):
+        half = columns // 2
+        return [
+            pltpu.VMEM((5, rows, columns), bf16),
+            pltpu.VMEM((4, rows, half), bf16),
+            pltpu.VMEM((6, rows, half), bf16),
+            pltpu.VMEM((3, rows, half), bf16),
+            pltpu.VMEM((rows, half), bf16),
+        ]
+
+    return pl.pallas_call(
         reduce_kernel,
         out_shape=(
             jax.ShapeDtypeStruct((OWN, D), f32),
             jax.ShapeDtypeStruct((OWN, D), f32),
-            jax.ShapeDtypeStruct(lift.shape, bf16),
-            jax.ShapeDtypeStruct(down.shape, bf16),
+            jax.ShapeDtypeStruct(lift.shape[1:], bf16),
+            jax.ShapeDtypeStruct(down.shape[1:], bf16),
         ),
         in_specs=[ANY] * 4,
-        out_specs=(VMEM, VMEM, ANY, ANY),
+        out_specs=(VMEM,) * 4,
         scratch_shapes=[
-            pltpu.VMEM((2, 8, OWN, D), bf16),
-            pltpu.VMEM((2, 8, OWN, D), bf16),
-            pltpu.VMEM((2, 4, OWN, SPLIT), bf16),
-            pltpu.VMEM((2, 6, OWN, D - SPLIT), bf16),
-            pltpu.VMEM((2, 3, OWN, SPLIT), bf16),
-            pltpu.VMEM((2, OWN, D - SPLIT), bf16),
-            pltpu.VMEM(lift.shape[1:], bf16),
-            pltpu.VMEM((3,) + lift.shape[1:], bf16),
-            pltpu.VMEM(lift.shape[2:], bf16),
-            pltpu.VMEM(down.shape[1:], bf16),
-            pltpu.VMEM((3,) + down.shape[1:], bf16),
-            pltpu.VMEM(down.shape[2:], bf16),
-            dma((2, 8)),
-            dma((2, 8)),
-            dma((2, 8)),
-            dma((2, 2, 8)),
-            dma((2, 2, 8)),
-            dma((2, 4)),
-            dma((2, 4)),
-            dma((2,)),
-            dma((2, 4)),
-            dma((2, 4)),
-            dma((2,)),
-            dma((2,)),
-            dma((2,)),
-            dma((2,)),
-            dma((2, 2, 4)),
-            dma((2, 2, 4)),
-            dma((2,)),
-        ],
+            pltpu.VMEM((2, 4, OWN, D), bf16),
+            pltpu.VMEM((2, 4, OWN, D), bf16),
+            pltpu.VMEM((2, 3, OWN, D), bf16),
+        ]
+        + slots(*lift.shape[1:])
+        + slots(*down.shape[1:])
+        + [dma((2, 4))] * 5
+        + [dma((2, 5)), dma((2, 2, 8)), dma((2, 2, 8)), dma((2, 4)), dma((2, 4))],
         compiler_params=params(collective, 60 * 2**20),
         name="reduce_rows",
     )(du, out, lift, down)
-    du, out, lift, down = result
-    down = down.transpose(0, 2, 1, 3).reshape(HID, D)
-    return du, out, lift.reshape(D, 2 * HID), down
-
-
-def total_kernel(count, *refs):
-    ins, outs = refs[:count], refs[count : 2 * count]
-    landed = refs[2 * count : 3 * count]
-    local_sem, s_one, r_one, s_two, r_two = refs[3 * count :]
+
+
+def away_kernel(
+    x_ref, lift_ref, down_ref, o_ref, lift_o, down_o,
+    lift_own, lift_land, down_own, down_land,
+    local_sem, s_x, r_x, s_mate, r_mate, s_sib, r_sib,
+):
     rep, shard = place()
-    greet([(lax.rem(rep + i, 8), shard) for i in range(1, 8)])
-    ones, twos, locals_ = [], [], []
-    for n in range(count):
-        local = pltpu.make_async_copy(ins[n].at[rep], landed[n].at[0], local_sem.at[n])
-        local.start()
-        locals_.append(local)
+    core = lax.rem(shard, 2)
+    chip = shard // 2
+    sib = shard + 1 - 2 * core
+    mate = rep + 1 - 2 * lax.rem(rep, 2)
+    greet([(rep, lax.rem(shard + i, 16)) for i in range(1, 16)] + [(mate, shard)])
+    sent = []
+    for i in range(1, 8):
+        c = lax.rem(chip + i, 8)
+        sent.append(
+            send(
+                x_ref.at[c], o_ref.at[chip], s_x.at[i], r_x.at[i],
+                (rep, 2 * c + lax.rem(core + chip, 2)),
+            )
+        )
+    mates, loads = [], []
+    for n, (src, own, land) in enumerate(
+        ((lift_ref, lift_own, lift_land), (down_ref, down_own, down_land))
+    ):
+        mates.append(send(src, land, s_mate.at[n], r_mate.at[n], (mate, shard)))
+        load = pltpu.make_async_copy(src, own, local_sem.at[n])
+        load.start()
+        loads.append(load)
+    same = lax.rem(chip, 2) == 0
+
+    @pl.when(same)
+    def _():
+        copy = pltpu.make_async_copy(x_ref.at[chip], o_ref.at[chip], local_sem.at[2])
+        copy.start()
+        copy.wait()
+
+    @pl.when(jnp.logical_not(same))
+    def _():
+        send(x_ref.at[chip], o_ref.at[chip], s_x.at[0], r_x.at[0], (rep, sib)).wait_send()
+        landed_on(o_ref.at[chip], r_x.at[0], s_x.at[0], (rep, sib))
+
+    keeps, halves = [], []
+    for n, (own, land, out) in enumerate(
+        ((lift_own, lift_land, lift_o), (down_own, down_land, down_o))
+    ):
+        loads[n].wait()
+        mates[n].wait_recv()
+        for k in range(2):
+
+            def add(t, _, own=own, land=land, k=k):
+                at = pl.ds(pl.multiple_of(t * 16, 16), 16)
+                own[k, at] = (own[k, at].astype(f32) + land[k, at].astype(f32)).astype(bf16)
+                return 0
+
+            lax.fori_loop(0, own.shape[1] // 16, add, 0)
+        halves.append(
+            send(own.at[1 - core], out.at[core], s_sib.at[n], r_sib.at[n], (rep, sib))
+        )
+        keep = pltpu.make_async_copy(own.at[core], out.at[core], local_sem.at[3 + n])
+        keep.start()
+        keeps.append(keep)
+    for i in range(1, 8):
+        landed_on(o_ref.at[lax.rem(chip + 8 - i, 8)], r_x.at[i], s_x.at[0], (rep, sib))
+    for n, out in enumerate((lift_o, down_o)):
+        landed_on(out.at[1 - core], r_sib.at[n], s_x.at[0], (rep, sib))
+        keeps[n].wait()
+    for copy in sent + mates + halves:
+        copy.wait_send()
+
+
+def grads_away(x, lift, down, collective):
+    dma = pltpu.SemaphoreType.DMA
+    return pl.pallas_call(
+        away_kernel,
+        out_shape=tuple(jax.ShapeDtypeStruct(a.shape, a.dtype) for a in (x, lift, down)),
+        in_specs=[ANY] * 3,
+        out_specs=(ANY,) * 3,
+        scratch_shapes=[
+            pltpu.VMEM(lift.shape, bf16),
+            pltpu.VMEM(lift.shape, bf16),
+            pltpu.VMEM(down.shape, bf16),
+            pltpu.VMEM(down.shape, bf16),
+            dma((5,)),
+            dma((8,)),
+            dma((8,)),
+        ]
+        + [dma((2,))] * 4,
+        compiler_params=params(collective, 32 * 2**20),
+        name="grads_away",
+    )(x, lift, down)
+
+
+PART = (48, 384)
+
+
+def part_of(r):
+    rows = pl.ds(pl.multiple_of((r // 4) * PART[0], PART[0]), PART[0])
+    return rows, pl.ds(pl.multiple_of(lax.rem(r, 4) * PART[1], PART[1]), PART[1])
+
+
+def tail_kernel(
+    dq_ref, dkv_ref, in_ref, out_ref, w_ref,
+    dh_ref, in_sum, out_sum,
+    held_k, near_k, held_i, near_i, got_q, got_k, got_i, land_i, land_o, own_o, sum_i, sum_o,
+    l_sem, s_q, r_q, s_nk, r_nk, s_ni, r_ni, s_k, r_k, s_i, r_i, s_ri, r_ri, s_ro, r_ro, s_gi, r_gi, s_go, r_go,
+):
+    rep, shard = place()
+    core = lax.rem(shard, 2)
+    chip = shard // 2
+    sib = shard + 1 - 2 * core
+    greet(
+        [(rep, lax.rem(shard + i, 16)) for i in range(1, 16)]
+        + [(lax.rem(rep + i, 8), shard) for i in range(1, 8)]
+    )
+    sent = []
+
+    def put(src, dst, s_sem, r_sem, device):
+        copy = send(src, dst, s_sem, r_sem, device)
+        sent.append(copy)
+        return copy
+
+    def landed(ref, sem):
+        pltpu.make_async_remote_copy(
+            src_ref=ref, dst_ref=ref, send_sem=s_q.at[0], recv_sem=sem,
+            device_id=(rep, sib), device_id_type=MESH,
+        ).wait_recv()
+
+    order = [1, 7, 2, 6, 3, 5, 4, 0]
+    nears, loads = {}, {}
+    for name, src, held, near, s_n, r_n, base in (
+        ("i", in_ref, held_i, near_i, s_ni, r_ni, 0),
+        ("k", dkv_ref, held_k, near_k, s_nk, r_nk, 8),
+    ):
+        for j in order:
+            c = lax.rem(chip + j, 8)
+            nears[name, j] = put(
+                src.at[2 * c + 1 - core], near.at[j], s_n.at[j], r_n.at[j], (rep, sib)
+            )
+            loads[name, j] = pltpu.make_async_copy(
+                src.at[2 * c + core], held.at[j], l_sem.at[base + j]
+            )
+            loads[name, j].start()
+    own = pltpu.make_async_copy(out_ref.at[part_of(rep)], own_o, l_sem.at[16])
+    own.start()
+    for i in range(1, 8):
+        c = lax.rem(chip + i, 8)
+        put(
+            dq_ref.at[c], got_q.at[chip], s_q.at[i], r_q.at[i],
+            (rep, 2 * c + lax.rem(c + core, 2)),
+        )
+    mine = lax.rem(chip, 2) == 0
+
+    @pl.when(mine)
+    def _():
+        copy = pltpu.make_async_copy(dq_ref.at[chip], got_q.at[chip], l_sem.at[17])
+        copy.start()
+        copy.wait()
+
+    @pl.when(jnp.logical_not(mine))
+    def _():
+        send(dq_ref.at[chip], got_q.at[chip], s_q.at[0], r_q.at[0], (rep, sib)).wait_send()
+
+    def add_near(name, held, near, j, rows, step):
+        nears[name, j].wait_recv()
+        loads[name, j].wait()
+
+        def add(t, _):
+            at = pl.ds(pl.multiple_of(t * step, step), step)
+            held[j, at] = (held[j, at].astype(f32) + near[j, at].astype(f32)).astype(bf16)
+            return 0
+
+        lax.fori_loop(0, rows // step, add, 0)
+
+    for name, held, near, got, s_x, r_x, rows in (
+        ("i", held_i, near_i, got_i, s_i, r_i, 96),
+        ("k", held_k, near_k, got_k, s_k, r_k, OWN),
+    ):
+        for j in order:
+            add_near(name, held, near, j, rows, 32)
+            if j:
+                c = lax.rem(chip + j, 8)
+                put(held.at[j], got.at[chip], s_x.at[j], r_x.at[j], (rep, 2 * c + core))
+            else:
+
+                def keep(t, _, held=held, got=got):
+                    at = pl.ds(pl.multiple_of(t * 32, 32), 32)
+                    got[chip, at] = held[0, at]
+                    return 0
+
+                lax.fori_loop(0, rows // 32, keep, 0)
+    for i in range(1, 8):
+        to = lax.rem(rep + i, 8)
+        put(out_ref.at[part_of(to)], land_o.at[i - 1], s_ro.at[i], r_ro.at[i], (to, shard))
+    for i in range(1, 8):
+        landed(got_i.at[lax.rem(chip + 8 - i, 8)], r_i.at[i])
+    for i in range(1, 8):
+        to = lax.rem(rep + i, 8)
+        put(got_i.at[to], land_i.at[i - 1], s_ri.at[i], r_ri.at[i], (to, shard))
+
+    @pl.when(jnp.logical_not(mine))
+    def _():
+        landed(got_q.at[chip], r_q.at[0])
+
+    for i in range(1, 8):
+        landed(got_q.at[lax.rem(chip + 8 - i, 8)], r_q.at[i])
+        landed(got_k.at[lax.rem(chip + 8 - i, 8)], r_k.at[i])
+    joined = jnp.concatenate(
+        [got_q[c] for c in range(CHIPS)]
+        + [got_k[c][:, :HEAD] for c in range(CHIPS)]
+        + [got_k[c][:, HEAD:] for c in range(CHIPS)],
+        1,
+    )
+    dh_ref[...] = contract(joined, w_ref[...], ((1,), (1,)))
+
+    own.wait()
+    for land, total, part, r_x in ((land_o, sum_o, None, r_ro), (land_i, sum_i, got_i, r_ri)):
         for i in range(1, 8):
-            to = lax.rem(rep + i, 8)
-            ones.append(
-                send(ins[n].at[to], landed[n].at[i], s_one.at[n, i], r_one.at[n, i], (to, shard))
-            )
-    for n in range(count):
-        locals_[n].wait()
-        for i in range(7):
-            ones[7 * n + i].wait_recv()
-        rows = landed[n].shape[1]
-        step = 16
-
-        def add(t, _, n=n):
-            at = pl.ds(pl.multiple_of(t * step, step), step)
-            total = landed[n][0, at].astype(f32)
-            for i in range(1, 8):
-                total = total + landed[n][i, at].astype(f32)
-            landed[n][0, at] = total.astype(bf16)
+            landed(land.at[i - 1], r_x.at[i])
+
+        def add(t, _, land=land, total=total, part=part):
+            at = pl.ds(pl.multiple_of(t * 16, 16), 16)
+            value = own_o[at] if part is None else part[rep, at]
+            value = value.astype(f32)
+            for i in range(7):
+                value = value + land[i, at].astype(f32)
+            total[at] = value.astype(bf16)
             return 0
 
-        lax.fori_loop(0, rows // step, add, 0)
-        local = pltpu.make_async_copy(landed[n].at[0], outs[n].at[rep], local_sem.at[n])
-        local.start()
-        locals_.append(local)
-        for i in range(1, 8):
-            to = lax.rem(rep + i, 8)
-            twos.append(
-                send(
-                    landed[n].at[0], outs[n].at[rep], s_two.at[n, i], r_two.at[n, i], (to, shard)
-                )
-            )
-    for n in range(count):
-        locals_[count + n].wait()
-        for i in range(1, 8):
-            ref = outs[n].at[lax.rem(rep + 8 - i, 8)]
-            pltpu.make_async_remote_copy(
-                src_ref=ref,
-                dst_ref=ref,
-                send_sem=s_two.at[n, 0],
-                recv_sem=r_two.at[n, i],
-                device_id=(lax.rem(rep + 1, 8), shard),
-                device_id_type=MESH,
-            ).wait_recv()
-    for copy in ones + twos:
+        lax.fori_loop(0, total.shape[0] // 16, add, 0)
+    keeps = [
+        pltpu.make_async_copy(sum_o, out_sum.at[part_of(rep)], l_sem.at[18]),
+        pltpu.make_async_copy(sum_i, in_sum.at[rep], l_sem.at[19]),
+    ]
+    for keep in keeps:
+        keep.start()
+    for i in range(1, 8):
+        to = lax.rem(rep + i, 8)
+        put(sum_o, out_sum.at[part_of(rep)], s_go.at[i], r_go.at[i], (to, shard))
+        put(sum_i, in_sum.at[rep], s_gi.at[i], r_gi.at[i], (to, shard))
+    for i in range(1, 8):
+        back = lax.rem(rep + 8 - i, 8)
+        landed(out_sum.at[part_of(back)], r_go.at[i])
+        landed(in_sum.at[back], r_gi.at[i])
+    for keep in keeps:
+        keep.wait()
+    for copy in sent:
         copy.wait_send()
 
 
-def total_over_reps(arrays, collective):
-    n = len(arrays)
+def tail(dq, dkv, inward_part, outward_own, inward_all, collective):
+    dma = pltpu.SemaphoreType.DMA
     return pl.pallas_call(
-        functools.partial(total_kernel, n),
-        out_shape=tuple(jax.ShapeDtypeStruct(x.shape, x.dtype) for x in arrays),
-        in_specs=[ANY] * n,
-        out_specs=(ANY,) * n,
-        scratch_shapes=[pltpu.VMEM(x.shape, bf16) for x in arrays]
-        + [pltpu.SemaphoreType.DMA((n,))]
-        + [pltpu.SemaphoreType.DMA((n, 8)) for _ in range(4)],
-        compiler_params=params(collective, 60 * 2**20),
-        name="total_over_reps",
-    )(*arrays)
+        tail_kernel,
+        out_shape=(
+            jax.ShapeDtypeStruct((OWN, D), f32),
+            jax.ShapeDtypeStruct((CHIPS, 96, 320), bf16),
+            jax.ShapeDtypeStruct((96, D), bf16),
+        ),
+        in_specs=[ANY, ANY, ANY, ANY, VMEM],
+        out_specs=(VMEM, ANY, ANY),
+        scratch_shapes=[
+            pltpu.VMEM((8, OWN, 128), bf16),
+            pltpu.VMEM((8, OWN, 128), bf16),
+            pltpu.VMEM((8, 96, 320), bf16),
+            pltpu.VMEM((8, 96, 320), bf16),
+            pltpu.VMEM((8, OWN, 192), bf16),
+            pltpu.VMEM((8, OWN, 128), bf16),
+            pltpu.VMEM((8, 96, 320), bf16),
+            pltpu.VMEM((7, 96, 320), bf16),
+            pltpu.VMEM((7,) + PART, bf16),
+            pltpu.VMEM(PART, bf16),
+            pltpu.VMEM((96, 320), bf16),
+            pltpu.VMEM(PART, bf16),
+            dma((20,)),
+        ]
+        + [dma((8,))] * 18,
+        compiler_params=params(collective, 56 * 2**20),
+        name="tail",
+    )(dq, dkv, inward_part, outward_own, inward_all)
 
 
 def swap_halves(values):
@@ -787,47 +1073,25 @@
     )
 
 
-def behind(x, o, local_sem, s_sem, r_sem):
-    rep, shard = place()
-    local = pltpu.make_async_copy(x.at[shard], o.at[shard], local_sem)
-
-    def copy(i, slot):
-        to = lax.rem(shard + i, 16)
-        return pltpu.make_async_remote_copy(
-            src_ref=x.at[to],
-            dst_ref=o.at[slot],
-            send_sem=s_sem.at[i],
-            recv_sem=r_sem.at[i],
-            device_id=(rep, to),
-            device_id_type=MESH,
-        )
-
-    def start():
-        local.start()
-        for i in range(1, 16):
-            copy(i, shard).start()
-
-    def wait():
-        local.wait()
-        for i in range(1, 16):
-            copy(i, lax.rem(shard + 16 - i, 16)).wait_recv()
-        for i in range(1, 16):
-            copy(i, shard).wait_send()
-
-    return start, wait
-
-
 def attend_kernel(q_ref, k_ref, v_ref, b_ref, o_ref, l_ref, bo_ref, local_sem, s_sem, r_sem):
     i = pl.program_id(0)
-    start, wait = behind(b_ref, bo_ref, local_sem.at[0], s_sem, r_sem)
+    core = lax.rem(lax.axis_index("shard"), 2)
+    begin, relay, finish = spread(b_ref, bo_ref, local_sem.at[0], s_sem, r_sem)
 
     @pl.when(i == 0)
     def _():
         rep, shard = place()
-        greet([(rep, lax.rem(shard + n, 16)) for n in range(1, 16)])
-        start()
-
-    core = lax.rem(lax.axis_index("shard"), 2)
+        chip = shard // 2
+        greet(
+            [(rep, shard + 1 - 2 * core)]
+            + [(rep, 2 * lax.rem(chip + n, 8) + core) for n in range(1, 8)]
+        )
+        begin()
+
+    @pl.when(i == 1)
+    def _():
+        relay()
+
     shift = lax.rem(i + core, 2) * OWN
     q = q_ref[0]
 
@@ -863,7 +1127,7 @@
 
     @pl.when(i == BLOCKS - 1)
     def _():
-        wait()
+        finish()
 
 
 def attend(q, k, v, units, collective):
@@ -884,12 +1148,12 @@
         out_shape=(
             jax.ShapeDtypeStruct((BLOCKS, OWN, GROUP * HEAD), bf16),
             jax.ShapeDtypeStruct((BLOCKS, 8, ROWS), f32),
-            jax.ShapeDtypeStruct(units.shape, bf16),
+            jax.ShapeDtypeStruct((SHARDS,) + units.shape[1:], bf16),
         ),
         scratch_shapes=[
             pltpu.SemaphoreType.DMA((1,)),
-            pltpu.SemaphoreType.DMA((16,)),
-            pltpu.SemaphoreType.DMA((16,)),
+            pltpu.SemaphoreType.DMA((2, 8)),
+            pltpu.SemaphoreType.DMA((2, 8)),
         ],
         compiler_params=params(collective, 48 * 2**20),
         name="attend",
@@ -897,8 +1161,8 @@
 
 
 def attend_back_kernel(
-    q_ref, k_ref, v_ref, g_ref, a_ref, l_ref, cos_ref, sin_ref, qcos_ref, qsin_ref, lift_ref, part_ref,
-    dq_ref, dkv_ref, lift_out, part_out,
+    q_ref, k_ref, v_ref, g_ref, a_ref, l_ref, cos_ref, sin_ref, qcos_ref, qsin_ref, part_ref,
+    lift_ref, down_ref, dq_ref, dkv_ref, part_out, lift_out, down_out,
     dk, dv, dq, held, near, landed, local_sem, s_sem, r_sem, h_sem, s_near, r_near, s_far, r_far,
 ):
     i = pl.program_id(0)
@@ -907,7 +1171,24 @@
     chip = shard // 2
     sib = shard + 1 - 2 * core
     shift = lax.rem(i + core, 2) * OWN
-    start, wait = behind(lift_ref, lift_out, local_sem.at[0], s_sem, r_sem)
+    x = rep // 2
+    kept = [
+        (n, src, dst)
+        for n, (src, dst) in enumerate(((lift_ref, lift_out), (down_ref, down_out)))
+    ]
+
+    def copy_same(n, src, dst):
+        return pltpu.make_async_copy(src, dst.at[pl.ds(2 * x, 2)], local_sem.at[n])
+
+    def copy_x(n, src, dst, dx, at):
+        return pltpu.make_async_remote_copy(
+            src_ref=src,
+            dst_ref=dst.at[pl.ds(2 * at, 2)],
+            send_sem=s_sem.at[n, dx],
+            recv_sem=r_sem.at[n, dx],
+            device_id=(along_x(rep, dx), shard),
+            device_id_type=MESH,
+        )
 
     def copy_near(j):
         return pltpu.make_async_remote_copy(
@@ -936,11 +1217,18 @@
 
     @pl.when(i == 0)
     def _():
-        greet([(rep, lax.rem(shard + n, 16)) for n in range(1, 16)])
+        greet(
+            [(rep, sib)]
+            + [(rep, 2 * lax.rem(chip + n, 8) + core) for n in range(1, 8)]
+            + [(along_x(rep, dx), shard) for dx in (1, 2, 3)]
+        )
         for j in range(8):
             copy_near(j).start()
             copy_own(j).start()
-        start()
+        for n, src, dst in kept:
+            copy_same(n, src, dst).start()
+            for dx in (1, 2, 3):
+                copy_x(n, src, dst, dx, x).start()
         dk[...] = jnp.zeros_like(dk)
         dv[...] = jnp.zeros_like(dv)
 
@@ -1024,14 +1312,19 @@
             return 0
 
         lax.fori_loop(0, 3, add, 0)
-        wait()
+        for n, src, dst in kept:
+            copy_same(n, src, dst).wait()
+            for dx in (1, 2, 3):
+                copy_x(n, src, dst, dx, lax.rem(x + 4 - dx, 4)).wait_recv()
+            for dx in (1, 2, 3):
+                copy_x(n, src, dst, dx, x).wait_send()
         for j in range(8):
             copy_near(j).wait_send()
             if j:
                 copy_far(j).wait_send()
 
 
-def attend_back(q, k, v, grad, attended, lse, cos, sin, lift, part, collective):
+def attend_back(q, k, v, grad, attended, lse, cos, sin, part, lift, down, collective):
     def own(i):
         return (2 * i + lax.rem(i + lax.rem(lax.axis_index("shard"), 2), 2), 0)
 
@@ -1053,18 +1346,21 @@
             pl.BlockSpec((OWN, 128), own),
             ANY,
             ANY,
+            ANY,
         ],
         out_specs=(
             pl.BlockSpec((1, OWN, GROUP * HEAD), block),
             pl.BlockSpec((SEQ, 128), whole),
+            pl.BlockSpec(part.shape[1:], whole),
             ANY,
-            pl.BlockSpec(part.shape[1:], whole),
+            ANY,
         ),
         out_shape=(
             jax.ShapeDtypeStruct((BLOCKS, OWN, GROUP * HEAD), bf16),
             jax.ShapeDtypeStruct((SEQ, 128), bf16),
-            jax.ShapeDtypeStruct(lift.shape, bf16),
             jax.ShapeDtypeStruct(part.shape[1:], bf16),
+            jax.ShapeDtypeStruct((PEERS,) + lift.shape[1:], bf16),
+            jax.ShapeDtypeStruct((PEERS,) + down.shape[1:], bf16),
         ),
         scratch_shapes=[
             pltpu.VMEM((SEQ, HEAD), f32),
@@ -1073,14 +1369,14 @@
             pltpu.VMEM((8,) + part.shape[1:], bf16),
             pltpu.VMEM((8,) + part.shape[1:], bf16),
             pltpu.VMEM((7,) + part.shape[1:], bf16),
-            pltpu.SemaphoreType.DMA((1,)),
-            pltpu.SemaphoreType.DMA((16,)),
-            pltpu.SemaphoreType.DMA((16,)),
+            pltpu.SemaphoreType.DMA((2,)),
+            pltpu.SemaphoreType.DMA((2, 4)),
+            pltpu.SemaphoreType.DMA((2, 4)),
         ]
         + [pltpu.SemaphoreType.DMA((8,))] * 5,
         compiler_params=params(collective, 48 * 2**20),
         name="attend_back",
-    )(q, k, v, grad, attended, lse, cos, sin, cos, sin, lift, part)
+    )(q, k, v, grad, attended, lse, cos, sin, cos, sin, part, lift, down)
 
 
 def experts_kernel(
@@ -1119,33 +1415,53 @@
     step = 384
     rows = lambda i: (i, 0)
     whole = lambda i: (0, 0)
+    once = pl.Buffered(1)
     return pl.pallas_call(
         experts_kernel,
-        grid=(SEQ // step,),
+        grid=(PEERS * OWN // step,),
         in_specs=[
             pl.BlockSpec((step, D), rows),
             pl.BlockSpec((step, D), rows),
             pl.BlockSpec((step, 128), lambda i: (i, D // 128)),
-            pl.BlockSpec((D, 2 * HID), whole),
-            pl.BlockSpec((HID, D), whole),
-            pl.BlockSpec((128, HID), whole),
+            pl.BlockSpec((D, EXP), whole, pipeline_mode=once),
+            pl.BlockSpec((HID, D), whole, pipeline_mode=once),
+            pl.BlockSpec((128, HID), whole, pipeline_mode=once),
         ],
         out_specs=(
             pl.BlockSpec((step, D), rows),
             pl.BlockSpec((step, D), rows),
-            pl.BlockSpec((D, 2 * HID), whole),
+            pl.BlockSpec((D, EXP), whole),
             pl.BlockSpec((HID, D), whole),
         ),
         out_shape=(
-            jax.ShapeDtypeStruct((SEQ, D), bf16),
-            jax.ShapeDtypeStruct((SEQ, D), bf16),
-            jax.ShapeDtypeStruct((D, 2 * HID), bf16),
+            jax.ShapeDtypeStruct((PEERS * OWN, D), bf16),
+            jax.ShapeDtypeStruct((PEERS * OWN, D), bf16),
+            jax.ShapeDtypeStruct((D, EXP), bf16),
             jax.ShapeDtypeStruct((HID, D), bf16),
         ),
-        scratch_shapes=[pltpu.VMEM((D, 2 * HID), f32), pltpu.VMEM((HID, D), f32)],
-        compiler_params=pltpu.CompilerParams(vmem_limit_bytes=58 * 2**20),
+        scratch_shapes=[pltpu.VMEM((D, EXP), f32), pltpu.VMEM((HID, D), f32)],
+        compiler_params=pltpu.CompilerParams(vmem_limit_bytes=60 * 2**20),
         name="experts",
     )(u_all, y_all, y_all, wl, wd, spread)
+
+
+def units_kernel(w_ref, code_ref, out_ref):
+    x = lax.axis_index("rep") // 2
+    row = lax.broadcasted_iota(jnp.int32, (FF_EXP, HID), 0)
+    there = (row // 32) * 1024 + lax.rem(row, 32)
+    here = jnp.broadcast_to(code_ref[...], (FF_EXP, HID))
+    base = (5 * x) // 2
+    for k in range(2):
+        for part in range(2):
+            total = jnp.zeros((96, HID), f32)
+            for i in range(3):
+                chosen = there + 32 * (base + i) == here + FLAT * (2 * x + k)
+                total = total + jnp.dot(
+                    w_ref[base + i][:, FF_EXP * part : FF_EXP * (part + 1)],
+                    jnp.where(chosen, 1.0, 0.0).astype(bf16),
+                    preferred_element_type=f32,
+                )
+            out_ref[k, :, HID * part : HID * (part + 1)] = total.astype(bf16)
 
 
 def one_step(kernel, arrays, shapes, name):
@@ -1186,18 +1502,10 @@
         part_ref[s] = part[s * 96 : (s + 1) * 96]
 
 
-def finish_kernel(dq_ref, dkv_ref, w_ref, dz_ref, x_ref, g_ref, out_ref):
-    pairs = [dkv_ref[2 * c].astype(f32) + dkv_ref[2 * c + 1].astype(f32) for c in range(CHIPS)]
-    joined = jnp.concatenate(
-        [side_by_side(dq_ref)]
-        + [p[:, :HEAD].astype(bf16) for p in pairs]
-        + [p[:, HEAD:].astype(bf16) for p in pairs],
-        1,
-    )
-    dh = contract(joined, w_ref[...], ((1,), (1,)))
+def finish_kernel(dh_ref, dz_ref, x_ref, g_ref, out_ref):
     stream = x_ref[...].astype(f32)
     inverse = inverse_root(stream)
-    out_ref[...] = dz_ref[...] + norm_back(dh * g_ref[...], stream * inverse, inverse)
+    out_ref[...] = dz_ref[...] + norm_back(dh_ref[...] * g_ref[...], stream * inverse, inverse)
 
 
 def inward_part_kernel(u_ref, dq_ref, dkv_ref, out_ref, total):
@@ -1248,17 +1556,20 @@
     return (moment, variance, values - step_rate * (normed_step + decay_rate * values))
 
 
-def adam_lifting_kernel(w_ref, m_ref, s_ref, g_ref, mo_ref, so_ref, wo_ref, dot_ref, grad):
+def adam_lifting_kernel(w_ref, m_ref, s_ref, g_ref, code_ref, mo_ref, so_ref, wo_ref, dot_ref, grad):
     e = pl.program_id(0)
-    for k in range(EXPERTS):
-
-        @pl.when(e == k)
-        def _(k=k):
-            for part in range(2):
-                low = HID * part + 32 * k
-                grad[:, FF_EXP * part : FF_EXP * (part + 1)] = jnp.concatenate(
-                    [g_ref[s][:, low : low + 32].astype(f32) for s in range(SHARDS)], 1
-                )
+    first, last = (4 * e) // 5, (4 * e + 3) // 5
+    column = lax.broadcasted_iota(jnp.int32, (HID, FF_EXP), 1)
+    there = (column // 32) * 1024 + lax.rem(column, 32) + 32 * e
+    here = jnp.broadcast_to(code_ref[...], (HID, FF_EXP))
+    chosen_first = jnp.where(there == here + FLAT * first, 1.0, 0.0).astype(bf16)
+    skip = jnp.where(first == last, 1 << 20, 0)
+    chosen_last = jnp.where(there == here + (FLAT * last + skip), 1.0, 0.0).astype(bf16)
+    for part in range(2):
+        columns = slice(HID * part, HID * (part + 1))
+        grad[:, FF_EXP * part : FF_EXP * (part + 1)] = jnp.dot(
+            g_ref[first][:, columns], chosen_first, preferred_element_type=f32
+        ) + jnp.dot(g_ref[last][:, columns], chosen_last, preferred_element_type=f32)
 
     @pl.when(e == 0)
     def _():
@@ -1271,19 +1582,25 @@
     )
 
 
-def adam_lifting(weight, mean, square, grad):
+def adam_lifting(weight, mean, square, grad, code):
     block = pl.BlockSpec((1, 96, 2 * FF_EXP), lambda e: (e, 0, 0))
     shape = jax.ShapeDtypeStruct(weight.shape, f32)
     return pl.pallas_call(
         adam_lifting_kernel,
         grid=(EXPERTS,),
-        in_specs=[block, block, block, pl.BlockSpec(grad.shape, lambda e: (0, 0, 0))],
+        in_specs=[
+            block,
+            block,
+            block,
+            pl.BlockSpec(grad.shape, lambda e: (0, 0, 0)),
+            pl.BlockSpec(code.shape, lambda e: (0, 0)),
+        ],
         out_specs=(block, block, block, pl.BlockSpec((96, 128), lambda e: (0, 0))),
         out_shape=(shape, shape, shape, jax.ShapeDtypeStruct((96, 128), f32)),
         scratch_shapes=[pltpu.VMEM((96, 2 * FF_EXP), f32)],
         compiler_params=pltpu.CompilerParams(vmem_limit_bytes=48 * 2**20),
         name="adam_lifting",
-    )(weight, mean, square, grad)
+    )(weight, mean, square, grad, code)
 
 
 def adam_inward_kernel(w_ref, m_ref, s_ref, g_ref, mo_ref, so_ref, wo_ref, dot_ref):
@@ -1321,12 +1638,9 @@
     )
 
 
-def spread_table():
-    table = np.zeros((128, HID), np.float32)
-    for e in range(EXPERTS):
-        table[e, 32 * e : 32 * e + 32] = 1.0
-        table[16 + e, 32 * e : 32 * e + 32] = 1.0
-    return table
+def unit_codes():
+    unit = np.arange(HID, dtype=np.int32)
+    return (unit // FLAT) * 1024 + unit % FLAT
 
 
 def inverse_root(stream):
@@ -1373,17 +1687,18 @@
         2,
     ).transpose(1, 0, 2)
     lifting_rows = lifting.transpose(1, 0, 2)
-    by_unit = (
-        lifting.reshape(96, EXPERTS, 2, SHARDS, 32)
-        .transpose(3, 0, 2, 1, 4)
-        .reshape(SHARDS, 96, 2 * HID)
-    )
-    down_weight = lowering.transpose(1, 0, 2).reshape(HID, D)
-
-    x_all, head_weight = gather(layer_input, 2, by_head)
-    head_weight = head_weight.reshape(D, 384)
-    gain_rows = head_weight[:, 192:194].T.astype(f32)
-    gain_one, gain_two = gain_rows[0:1], gain_rows[1:2]
+    codes = jnp.asarray(unit_codes())
+    x = lax.axis_index("rep") // 2
+    position = 2 * x + lax.rem(lax.axis_index("shard"), 2)
+    (by_unit,) = one_step(
+        units_kernel, (lifting_rows, codes[None, :]), (((2, 96, EXP), bf16),), "choose_units"
+    )
+    low_rows = lowering.transpose(1, 0, 2).reshape(EXPERTS * 32, D)
+    low_rows = lax.dynamic_slice(low_rows, (2 * FLAT * x, 0), (2 * FLAT, D)).reshape(2, FLAT, D)
+    low_rows = jnp.pad(low_rows, ((0, 0), (0, FLAT_PAD - FLAT), (0, 0)))
+    expert = (FLAT * position + lax.rem(jnp.arange(HID), FLAT)) // 32
+    row = jnp.arange(128)[:, None]
+    share_table = ((row == expert) | (row == expert + 16)).astype(bf16)
 
     gates = jax.nn.softmax(route_logits, axis=-1)
     picked = routes[:, :, None] == jnp.arange(EXPERTS, dtype=jnp.int32)[None, None, :]
@@ -1393,15 +1708,18 @@
     shares = jnp.concatenate(
         [jnp.pad(high, ((0, 0), (0, 6))), jnp.pad(rest, ((0, 0), (0, 102)))], 1
     ).astype(bf16)
-    late_outward, late_y, x_all = lax.optimization_barrier(
-        (outward, jnp.concatenate([grad_output, shares], 1), x_all)
-    )
+    x_all, head_weight, y_all = start(
+        layer_input, by_head, jnp.concatenate([grad_output, shares], 1), 2
+    )
+    head_weight = head_weight.reshape(D, 384)
+    gain_rows = head_weight[:, 192:194].T.astype(f32)
+    gain_one, gain_two = gain_rows[0:1], gain_rows[1:2]
+    late_outward, x_all = lax.optimization_barrier((outward, x_all))
     outward_all = lax.all_gather(late_outward, "shard", axis=0, tiled=True)
-    y_all = lax.all_gather(late_y, "shard", axis=0, tiled=True)
 
     q, k, v, u_one = project(x_all, head_weight, gain_one, cos, sin)
     attended, lse, unit_weight = attend(q, k, v, by_unit, 1)
-    unit_weight = unit_weight.reshape(D, 2 * HID)
+    unit_weight = unit_weight.reshape(D, EXP)
     (own_attended,) = exchange((attended,), ("home",), 3, "attended_home")
     mixed, low_two = one_step(
         mix_kernel,
@@ -1409,15 +1727,20 @@
         (((OWN, D), f32), ((OWN, D), bf16)),
         "mix",
     )
-    (u_two,) = gather(low_two, 4)
+    u_two, down_weight = second(low_two, low_rows, 4)
+    down_weight = down_weight[:, :FLAT].reshape(HID, D)
     late_inward, u_two = lax.optimization_barrier((inward, u_two))
     inward_all = lax.all_gather(late_inward, "shard", axis=0, tiled=True)
 
     out_part, du_part, lift_part, down_part = experts(
-        u_two, y_all, unit_weight, down_weight, jnp.asarray(spread_table(), bf16)
+        u_two, y_all, unit_weight, down_weight, share_table
     )
     du, expert_out, lift_sum, down_sum = reduce_blocks(
-        du_part.reshape(SHARDS, OWN, D), out_part.reshape(SHARDS, OWN, D), lift_part, down_part, 5
+        du_part.reshape(PEERS, OWN, D),
+        out_part.reshape(PEERS, OWN, D),
+        lift_part.reshape(CHIPS, 192, EXP),
+        down_part.reshape(CHIPS, 2 * FLAT, D),
+        5,
     )
     layer_output, grad_mixed, away, outward_part = one_step(
         unmix_kernel,
@@ -1425,33 +1748,31 @@
         (((OWN, D), f32), ((OWN, D), f32), ((CHIPS, OWN, 192), bf16), ((SHARDS, 96, D), bf16)),
         "unmix",
     )
-    (head_grads,) = exchange((away,), ("away",), 6, "grads_away")
-    dq, dkv, lift_got, outward_own = attend_back(
-        q, k, v, head_grads, attended, lse, cos, sin,
-        lift_sum.reshape(SHARDS, 96, 2 * HID), outward_part, 8,
+    down_sum = jnp.pad(down_sum.reshape(2, FLAT, D), ((0, 0), (0, FLAT_PAD - FLAT), (0, 0)))
+    head_grads, lift_pair, down_pair = grads_away(
+        away, lift_sum.reshape(2, 96, EXP), down_sum, 6
+    )
+    dq, dkv, outward_own, lift_got, down_got = attend_back(
+        q, k, v, head_grads, attended, lse, cos, sin, outward_part, lift_pair, down_pair, 8
     )
     inward_part = inward_parts(u_one, dq, dkv)
-    own_dq, own_dkv, inward_got = exchange(
-        (dq, dkv.reshape(SHARDS, OWN, 128), inward_part),
-        ("home", "all", "all"),
-        7,
-        "pairs_home",
+    dh, inward_sum, outward_sum = tail(
+        dq, dkv.reshape(SHARDS, OWN, 128), inward_part, outward_own, inward_all, 7
     )
     (input_grad,) = one_step(
-        finish_kernel,
-        (own_dq, own_dkv, inward_all, grad_mixed, layer_input, gain_one),
-        (((OWN, D), f32),),
-        "finish",
-    )
-    inward_sum = jnp.sum(inward_got.reshape(CHIPS, 2, 96, 320).astype(f32), 1).astype(bf16)
-    inward_sum, outward_sum = total_over_reps(
-        (inward_sum, outward_own.reshape(REPS, 16, 1152)), 9
-    )
-    outward_grad = outward_sum.reshape(96, D).astype(f32)
-    down_grad = down_sum.reshape(EXPERTS, 32, D).transpose(1, 0, 2).astype(f32)
+        finish_kernel, (dh, grad_mixed, layer_input, gain_one), (((OWN, D), f32),), "finish"
+    )
+    outward_grad = outward_sum.astype(f32)
+    down_grad = (
+        down_got[:, :FLAT].reshape(EXPERTS, 32, D).transpose(1, 0, 2).astype(f32)
+    )
 
     new_lifting = adam_lifting(
-        lifting_rows, mean_lifting.transpose(1, 0, 2), square_lifting.transpose(1, 0, 2), lift_got
+        lifting_rows,
+        mean_lifting.transpose(1, 0, 2),
+        square_lifting.transpose(1, 0, 2),
+        lift_got,
+        codes[:, None],
     )
     lifting_dot = new_lifting[3]
     new_lifting = tuple(t.transpose(1, 0, 2) for t in new_lifting[:3])

time: 622 us -> 516 us (0.83)
  Pallas kernels: 539 us -> 465 us
  local copies, waits for them, and re-layouts: 46.5 us -> 19.2 us
    pallas_call x3 -> x1, Pallas kernels: 82.7 us -> 19.8 us  [exchange(): pl.pallas_call(functools.partial(exchange_kernel, kinds), out_shape=tuple...]
    pallas_call x1, Pallas kernels: 108 us -> 62.7 us  [reduce_blocks(): pl.pallas_call(reduce_kernel, out_shape=(jax.ShapeDtypeStruct((OWN, D), f...]
    pallas_call x1, Pallas kernels: 28.6 us -> 60.3 us  [attend(): pl.pallas_call(attend_kernel, grid=(BLOCKS,), in_specs=[pl.BlockSpec((1,...]
    pallas_call x1, Pallas kernels: 56.2 us -> 43.7 us  [attend_back(): pl.pallas_call(attend_back_kernel, grid=(BLOCKS,), in_specs=[pl.BlockSpec...]
    pallas_call x4 -> x5, Pallas kernels: 203 us -> 215 us  [the longest x1 56 us: start(): pl.pallas_call(start_kernel, out_shape=(jax.ShapeDtypeStruct((SHARDS, row...]
    unnamed x85 -> x74, local copies, waits for them, and re-layouts: 19 us -> 6.89 us
    reshape x4 -> x0, local copies, waits for them, and re-layouts: 10 us -> none  [the longest x1 4.36 us: per_device(): by_unit = lifting.reshape(96, EXPERTS, 2, SHARDS, 32).transpose(3, 0, 2,...]
    convert_element_type x3 -> x0, local copies, waits for them, and re-layouts: 8.68 us -> none  [the longest x2 6.68 us: per_device(): down_grad = down_sum.reshape(EXPERTS, 32, D).transpose(1, 0, 2).astype(f32)]
  transfers between devices with their start and end apart: 3 -> 2, of which waited for: 0 -> 0; matrix products, arithmetic and copies ran while one was open for 6% -> 3% of each run, Pallas kernels for 77% -> 62%
where the time goes in v3:
time: 516 us; the launch traced here: 511 us
  Pallas kernels  465 us (90%)
  local copies, waits for them, and re-layouts  19.2 us (4%)
  between operations  14.6 us (3%)
  other arithmetic  11.9 us (2%)
    pallas_call x1, Pallas kernels, reduce_blocks(): pl.pallas_call(reduce_kernel, out_shape=(jax.ShapeDtypeStruct((OWN, D), f...  62.7 us
    pallas_call x1, Pallas kernels, attend(): pl.pallas_call(attend_kernel, grid=(BLOCKS,), in_specs=[pl.BlockSpec((1,...  60.3 us
    pallas_call x1, Pallas kernels, start(): pl.pallas_call(start_kernel, out_shape=(jax.ShapeDtypeStruct((SHARDS, row...  56 us
    pallas_call x1, Pallas kernels, tail(): pl.pallas_call(tail_kernel, out_shape=(jax.ShapeDtypeStruct((OWN, D), f32...  49.6 us
    pallas_call x1, Pallas kernels, attend_back(): pl.pallas_call(attend_back_kernel, grid=(BLOCKS,), in_specs=[pl.BlockSpec...  43.7 us
    pallas_call x1, Pallas kernels, experts(): pl.pallas_call(experts_kernel, grid=(PEERS * OWN // step,), in_specs=[pl....  43.3 us
    pallas_call x1, Pallas kernels, grads_away(): pl.pallas_call(away_kernel, out_shape=tuple((jax.ShapeDtypeStruct(a.shape...  34.1 us
    pallas_call x1, Pallas kernels, second(): pl.pallas_call(second_kernel, out_shape=(jax.ShapeDtypeStruct((PEERS,) +...  31.9 us
  transfers between devices with their start and end apart: 2, of which 0 were waited for; matrix products, arithmetic and copies ran while one was open for 3% of the time, Pallas kernels for 62%

profile of v3, /device:TPU:1, one launch (start us, length us, event | category | flops | bytes accessed | tf_op | source)
XLA Modules:
  0.0 511.2 jit_solution(15718746246570930679)
XLA Ops:
  7.2 0.7 reduce_max.9
  8.0 0.7 fusion.12
  8.7 0.7 fusion.11
  9.4 0.7 select_reduce_fusion
  10.2 1.0 fusion.24
  11.2 1.0 slice.30
  12.6 0.2 copy.66
  12.7 0.1 copy.73
  12.9 0.2 copy.67
  13.0 0.3 reshape.119
  13.4 0.1 copy.75
  13.6 1.0 concatenate.10.t_ref
  14.6 1.1 maximum_bitcast_fusion.w_ref
  15.7 56.0 %start.1 = (bf16[16,192,1536]{2,1,0:T(8,128)(2,1)}, bf16[16,96,384]{2,1,0:T(8,128)(2,1)}, bf16[8,192,1664]{2,1,0:T(8,128)(2,1)}) custom-call(bf16[192,1536]{1,0:T(8,128)(2,1)} %x_ref.5, bf16[8,96,384]{2,1,0:T(8,128)(2,1)} %maximum_bitcast_fusion.w_ref, bf16[192,1664]{1,0:T(8,128)(2,1)} %concatenate.10.t_ref), custom_call_target="tpu_custom_call" | custom-call | tf_op jit(solution)/shard_map/start/pallas_call | solution.py:332
  71.8 1.3 slice_convert_fusion
  73.1 0.3 copy.76
  73.4 4.0 choose_units.1.b_ref
  77.3 0.6 fusion.25
  77.9 1.3 copy-done.11
  79.2 13.6 %project_heads.1 = (bf16[8,576,64]{2,1,0:T(8,128)(2,1)S(1)}, bf16[3072,64]{1,0:T(8,128)(2,1)S(1)}, bf16[3072,128]{1,0:T(8,128)(2,1)S(1)}, bf16[3072,1536]{1,0:T(8,128)(2,1)}) custom-call(bf16[3072,1536]{1,0:T(8,128)(2,1)} %bitcast.52, bf16[1536,384]{1,0:T(8,128)(2,1)S(1)} %bitcast.47, f32[1,1536]{1,0:T(1,128)S(1)} %get-tuple-element.129.g_ref, ...), custom_call_target="tpu_custom_call" | custom-call | tf_op jit(solution)/shard_map/project_heads/pallas_call | solution.py:1043
  92.8 60.3 %attend.1 = (bf16[8,192,192]{2,1,0:T(8,128)(2,1)S(1)}, f32[8,8,576]{2,1,0:T(8,128)S(1)}, bf16[16,96,1280]{2,1,0:T(8,128)(2,1)}) custom-call(bf16[8,576,64]{2,1,0:T(8,128)(2,1)S(1)} %get-tuple-element.69.q_ref, bf16[3072,64]{1,0:T(8,128)(2,1)S(1)} %get-tuple-element.70.k_ref, bf16[3072,128]{1,0:T(8,128)(2,1)S(1)} %get-tuple-element.71.v_ref, ...), custom_call_target="tpu_custom_call" | custom-call | tf_op jit(solution)/shard_map/attend/pallas_call | solution.py:1134
  153.2 0.9 copy-done.5
  154.1 0.7 copy-done.21
  154.7 19.8 %attended_home.1.a_ref = bf16[8,192,192]{2,1,0:T(8,128)(2,1)} custom-call(bf16[8,192,192]{2,1,0:T(8,128)(2,1)} %copy-done.5), custom_call_target="tpu_custom_call" | custom-call | tf_op jit(solution)/shard_map/attended_home/pallas_call | solution.py:511
  174.5 1.0 constant_dynamic-slice_fusion
  175.5 0.7 pad.24.w_ref
  176.2 5.1 mix.1
  181.3 31.9 %second_gather.1 = (bf16[8,192,1536]{2,1,0:T(8,128)(2,1)}, bf16[16,48,1536]{2,1,0:T(8,128)(2,1)}) custom-call(bf16[192,1536]{1,0:T(8,128)(2,1)} %get-tuple-element.74.x_ref, bf16[2,48,1536]{2,1,0:T(8,128)(2,1)} %pad.24.w_ref), custom_call_target="tpu_custom_call" | custom-call | tf_op jit(solution)/shard_map/second_gather/pallas_call | solution.py:369
  213.2 0.7 fusion.10.e_ref
  213.9 2.9 slice.36
  216.9 43.3 %experts.1 = (bf16[1536,1536]{1,0:T(8,128)(2,1)}, bf16[1536,1536]{1,0:T(8,128)(2,1)}, bf16[1536,1280]{1,0:T(8,128)(2,1)}, bf16[640,1536]{1,0:T(8,128)(2,1)}) custom-call(bf16[1536,1536]{1,0:T(8,128)(2,1)} %bitcast.54, bf16[1536,1664]{1,0:T(8,128)(2,1)} %bitcast.50, bf16[1536,1664]{1,0:T(8,128)(2,1)} %bitcast.51, bf16[1536,1280]{1,0:T(8,128)(2,1)} %bitcast.57, ...), custom_call_target="tpu_custom_call" | custom-call | tf_op jit(solution)/shard_map/experts/pallas_call | solution.py:1419
  260.2 62.7 %reduce_rows.1 = (f32[192,1536]{1,0:T(8,128)}, f32[192,1536]{1,0:T(8,128)}, bf16[192,1280]{1,0:T(8,128)(2,1)}, bf16[80,1536]{1,0:T(8,128)(2,1)}) custom-call(bf16[8,192,1536]{2,1,0:T(8,128)(2,1)} %bitcast.56, bf16[8,192,1536]{2,1,0:T(8,128)(2,1)} %bitcast.55, bf16[8,192,1280]{2,1,0:T(8,128)(2,1)} %bitcast.59, bf16[8,80,1536]{2,1,0:T(8,128)(2,1)} %bitcast.61), custom_call_target="tpu_custom_call" | custom-call | tf_op jit(solution)/shard_map/reduce_rows/pallas_call | solution.py:708
  322.9 1.0 pad.25.down_ref
  323.9 9.3 %unmix.1 = (f32[192,1536]{1,0:T(8,128)}, f32[192,1536]{1,0:T(8,128)}, bf16[8,192,192]{2,1,0:T(8,128)(2,1)}, bf16[16,96,1536]{2,1,0:T(8,128)(2,1)}) custom-call(f32[192,1536]{1,0:T(8,128)} %get-tuple-element.84.du_ref, f32[192,1536]{1,0:T(8,128)} %get-tuple-element.85.e_ref, f32[192,1536]{1,0:T(8,128)} %get-tuple-element.86.mixed_ref, ...), custom_call_target="tpu_custom_call" | custom-call | tf_op jit(solution)/shard_map/unmix/pallas_call | solution.py:1468
  333.3 1.2 copy-done.14
  334.5 34.1 %grads_away.1 = (bf16[8,192,192]{2,1,0:T(8,128)(2,1)S(1)}, bf16[2,96,1280]{2,1,0:T(8,128)(2,1)S(1)}, bf16[2,48,1536]{2,1,0:T(8,128)(2,1)S(1)}) custom-call(bf16[8,192,192]{2,1,0:T(8,128)(2,1)S(1)} %copy-done.14, bf16[2,96,1280]{2,1,0:T(8,128)(2,1)S(1)} %bitcast.49, bf16[2,48,1536]{2,1,0:T(8,128)(2,1)S(1)} %pad.25.down_ref), custom_call_target="tpu_custom_call" | custom-call | tf_op jit(solution)/shard_map/grads_away/pallas_call | solution.py:804
  368.6 43.7 %attend_back.1 = (bf16[8,192,192]{2,1,0:T(8,128)(2,1)S(1)}, bf16[3072,128]{1,0:T(8,128)(2,1)S(1)}, bf16[96,1536]{1,0:T(8,128)(2,1)S(1)}, bf16[8,96,1280]{2,1,0:T(8,128)(2,1)}, bf16[8,48,1536]{2,1,0:T(8,128)(2,1)}) custom-call(bf16[8,576,64]{2,1,0:T(8,128)(2,1)} %copy-done.3, bf16[3072,64]{1,0:T(8,128)(2,1)S(1)} %get-tuple-element.70.k_ref, ...), custom_call_target="tpu_custom_call" | custom-call | tf_op jit(solution)/shard_map/attend_back/pallas_call | solution.py:1333
  412.3 1.9 slice.39
  414.3 9.6 %inward_parts.1.in_ref = bf16[16,96,320]{2,1,0:T(8,128)(2,1)S(1)} custom-call(bf16[3072,1536]{1,0:T(8,128)(2,1)} %get-tuple-element.98.u_ref, bf16[8,192,192]{2,1,0:T(8,128)(2,1)S(1)} %get-tuple-element.96.dq_ref, bf16[3072,128]{1,0:T(8,128)(2,1)S(1)} %get-tuple-element.97.dkv_ref), custom_call_target="tpu_custom_call" | custom-call | tf_op jit(solution)/shard_map/inward_parts/pallas_call | solution.py:1531
  423.9 1.0 copy-done.2
  425.0 16.4 %adam_lifting.1 = (f32[10,96,1024]{2,1,0:T(8,128)}, f32[10,96,1024]{2,1,0:T(8,128)}, f32[10,96,1024]{2,1,0:T(8,128)}, f32[96,128]{1,0:T(8,128)S(1)}) custom-call(bf16[10,96,1024]{2,1,0:T(8,128)(2,1)S(1)} %bitcast.44, bf16[10,96,1024]{2,1,0:T(8,128)(2,1)S(1)} %bitcast.48, bf16[10,96,1024]{2,1,0:T(8,128)(2,1)} %bitcast.60, ...), custom_call_target="tpu_custom_call" | custom-call | tf_op jit(solution)/shard_map/adam_lifting/pallas_call | solution.py:1588
  441.6 3.7 convert_subtract_fusion
  445.3 49.6 %tail.1 = (f32[192,1536]{1,0:T(8,128)}, bf16[8,96,320]{2,1,0:T(8,128)(2,1)}, bf16[96,1536]{1,0:T(8,128)(2,1)}) custom-call(bf16[8,192,192]{2,1,0:T(8,128)(2,1)} %copy-done.9, bf16[16,192,128]{2,1,0:T(8,128)(2,1)} %bitcast.45, bf16[16,96,320]{2,1,0:T(8,128)(2,1)} %copy-done.2, bf16[96,1536]{1,0:T(8,128)(2,1)} %copy-done.20, ...), custom_call_target="tpu_custom_call" | custom-call | tf_op jit(solution)/shard_map/tail/pallas_call | solution.py:983
  495.0 1.1 copy-done.15
  496.0 2.6 adam_inward.1
  498.8 3.4 finish.1
  502.2 1.5 convert_subtract_fusion.1
  503.8 0.6 convert_subtract_fusion.2
  (83 shorter events, 1.0 us)
Async XLA Ops:
  7.2 169.0 %all-gather.3.cloned.1.call-start = ((), (), s32[]{:S(2)}) async-start(), calls=%async_computation | async-start | bytes 5013504 | tf_op jit(solution)/shard_map/all_gather | solution.py:1718
  11.2 2.2 copy-start.32
  11.2 2.4 copy-start.24
  71.8 373.5 %all-gather.5.cloned.1.call-start = ((), (), s32[]{:S(2)}) async-start(), calls=%async_computation.1 | async-start | bytes 8355840 | tf_op jit(solution)/shard_map/all_gather | solution.py:1733
  71.8 6.1 %copy-start = (f32[3072,128]{1,0:T(8,128)S(1)}, f32[3072,128]{1,0:T(8,128)}, u32[]{:S(2)}) copy-start(f32[3072,128]{1,0:T(8,128)} %constant.104.clone.cos_ref.qcos_ref) | copy-start | bytes 4718596
  77.9 14.9 %copy-start.23 = (f32[1,1536]{1,0:T(1,128)}, f32[1,1536]{1,0:T(1,128)S(1)}, u32[]{:S(2)}) copy-start(f32[1,1536]{1,0:T(1,128)S(1)} %get-tuple-element.129.g_ref) | copy-start | bytes 18436
  77.9 1.3 copy-start.11
  79.2 13.6 %copy-start.12 = (bf16[2,96,1280]{2,1,0:T(8,128)(2,1)S(1)}, bf16[2,96,1280]{2,1,0:T(8,128)(2,1)}, u32[]{:S(2)}) copy-start(bf16[2,96,1280]{2,1,0:T(8,128)(2,1)} %choose_units.1.b_ref) | copy-start | bytes 1474564
  92.8 60.4 %copy-start.7 = (bf16[3072,128]{1,0:T(8,128)(2,1)}, bf16[3072,128]{1,0:T(8,128)(2,1)S(1)}, u32[]{:S(2)}) copy-start(bf16[3072,128]{1,0:T(8,128)(2,1)S(1)} %get-tuple-element.71.v_ref) | copy-start | bytes 2359300
  92.8 81.7 %copy-start.3 = (bf16[8,576,64]{2,1,0:T(8,128)(2,1)}, bf16[8,576,64]{2,1,0:T(8,128)(2,1)S(1)}, u32[]{:S(2)}) copy-start(bf16[8,576,64]{2,1,0:T(8,128)(2,1)S(1)} %get-tuple-element.69.q_ref) | copy-start | bytes 1769476
  153.2 0.9 copy-start.5
  154.1 0.7 copy-start.21
  323.9 9.3 %copy-start.16 = (bf16[192,1280]{1,0:T(8,128)(2,1)S(1)}, bf16[192,1280]{1,0:T(8,128)(2,1)}, u32[]{:S(2)}) copy-start(bf16[192,1280]{1,0:T(8,128)(2,1)} %get-tuple-element.89) | copy-start | bytes 1474564
  323.9 44.6 %copy-start.22 = (f32[8,8,576]{2,1,0:T(8,128)S(1)}, f32[8,8,576]{2,1,0:T(8,128)}, u32[]{:S(2)}) copy-start(f32[8,8,576]{2,1,0:T(8,128)} %copy-done.21) | copy-start | bytes 442372
  333.2 35.3 %copy-start.6 = (bf16[8,192,192]{2,1,0:T(8,128)(2,1)S(1)}, bf16[8,192,192]{2,1,0:T(8,128)(2,1)}, u32[]{:S(2)}) copy-start(bf16[8,192,192]{2,1,0:T(8,128)(2,1)} %copy-done.5) | copy-start | bytes 1769476
  333.3 35.3 %copy-start.8 = (bf16[3072,128]{1,0:T(8,128)(2,1)S(1)}, bf16[3072,128]{1,0:T(8,128)(2,1)}, u32[]{:S(2)}) copy-start(bf16[3072,128]{1,0:T(8,128)(2,1)} %copy-done.7) | copy-start | bytes 2359300
  333.3 1.3 copy-start.14
  412.3 11.6 %copy-start.9 = (bf16[8,192,192]{2,1,0:T(8,128)(2,1)}, bf16[8,192,192]{2,1,0:T(8,128)(2,1)S(1)}, u32[]{:S(2)}) copy-start(bf16[8,192,192]{2,1,0:T(8,128)(2,1)S(1)} %get-tuple-element.96.dq_ref) | copy-start | bytes 1769476
  412.3 11.6 %copy-start.10 = (bf16[3072,128]{1,0:T(8,128)(2,1)}, bf16[3072,128]{1,0:T(8,128)(2,1)S(1)}, u32[]{:S(2)}) copy-start(bf16[3072,128]{1,0:T(8,128)(2,1)S(1)} %get-tuple-element.97.dkv_ref) | copy-start | bytes 2359300
  412.3 11.6 %copy-start.20 = (bf16[96,1536]{1,0:T(8,128)(2,1)}, bf16[96,1536]{1,0:T(8,128)(2,1)S(1)}, u32[]{:S(2)}) copy-start(bf16[96,1536]{1,0:T(8,128)(2,1)S(1)} %get-tuple-element.99.out_ref) | copy-start | bytes 884740
  414.3 10.7 %copy-start.1 = (bf16[96,10,1024]{2,0,1:T(8,128)(2,1)S(1)}, bf16[96,10,1024]{2,0,1:T(8,128)(2,1)}, u32[]{:S(2)}) copy-start(bf16[96,10,1024]{2,0,1:T(8,128)(2,1)} %param.29) | copy-start | bytes 5898244
  414.3 10.7 %copy-start.13 = (bf16[96,10,1024]{2,0,1:T(8,128)(2,1)S(1)}, bf16[96,10,1024]{2,0,1:T(8,128)(2,1)}, u32[]{:S(2)}) copy-start(bf16[96,10,1024]{2,0,1:T(8,128)(2,1)} %param.34) | copy-start | bytes 5898244
  414.3 10.7 %copy-start.19 = (s32[640,1]{1,0:T(8,128)S(1)}, s32[640,1]{1,0:T(8,128)}, u32[]{:S(2)}) copy-start(s32[640,1]{1,0:T(8,128)} %constant.122.code_ref) | copy-start | bytes 7684
  423.9 1.0 copy-start.2
  425.0 16.6 %copy-start.25 = (bf16[32,10,1536]{2,0,1:T(8,128)(2,1)S(1)}, bf16[32,10,1536]{2,0,1:T(8,128)(2,1)}, u32[]{:S(2)}) copy-start(bf16[32,10,1536]{2,0,1:T(8,128)(2,1)} %param.30) | copy-start | bytes 2949124
  425.0 16.6 %copy-start.27 = (bf16[32,10,1536]{2,0,1:T(8,128)(2,1)S(1)}, bf16[32,10,1536]{2,0,1:T(8,128)(2,1)}, u32[]{:S(2)}) copy-start(bf16[32,10,1536]{2,0,1:T(8,128)(2,1)} %param.40) | copy-start | bytes 2949124
  425.0 16.6 %copy-start.28 = (bf16[32,10,1536]{2,0,1:T(8,128)(2,1)S(1)}, bf16[32,10,1536]{2,0,1:T(8,128)(2,1)}, u32[]{:S(2)}) copy-start(bf16[32,10,1536]{2,0,1:T(8,128)(2,1)} %param.35) | copy-start | bytes 2949124
  445.3 49.7 %copy-start.4 = (bf16[96,2560]{1,0:T(8,128)(2,1)S(1)}, bf16[96,2560]{1,0:T(8,128)(2,1)}, u32[]{:S(2)}) copy-start(bf16[96,2560]{1,0:T(8,128)(2,1)} %w_ref.1) | copy-start | bytes 1474564
  445.3 49.7 %copy-start.17 = (bf16[96,2560]{1,0:T(8,128)(2,1)S(1)}, bf16[96,2560]{1,0:T(8,128)(2,1)}, u32[]{:S(2)}) copy-start(bf16[96,2560]{1,0:T(8,128)(2,1)} %m_ref.1) | copy-start | bytes 1474564
  445.3 49.7 %copy-start.18 = (bf16[96,2560]{1,0:T(8,128)(2,1)S(1)}, bf16[96,2560]{1,0:T(8,128)(2,1)}, u32[]{:S(2)}) copy-start(bf16[96,2560]{1,0:T(8,128)(2,1)} %s_ref.1) | copy-start | bytes 1474564
  495.0 1.1 copy-start.15
  498.8 3.4 copy-start.26
  498.8 3.4 copy-start.29
  498.8 3.4 copy-start.30
  498.8 3.4 copy-start.31
  502.2 1.6 copy-start.33
  502.2 1.6 copy-start.34
Sparse Core Ops, SparseCore 0:
  71.9 69.9 all-gather.2
  213.3 51.1 all-gather.4

commit v4 on v3

--- a/solution.py
+++ b/solution.py
@@ -81,6 +81,7 @@
 
 ANY = pl.BlockSpec(memory_space=pl.ANY)
 VMEM = pl.BlockSpec(memory_space=pltpu.VMEM)
+HBM = pl.BlockSpec(memory_space=pltpu.HBM)
 
 
 def along_x(rep, dx):
@@ -154,51 +155,111 @@
     return start, relay, relay_far, finish
 
 
-def spread(x_ref, o_ref, local_sem, send_sem, recv_sem):
+def ring_spread(x_ref, o_ref, split, local_sem, send_sem, recv_sem):
     rep, shard = place()
     core = lax.rem(shard, 2)
     chip = shard // 2
+    y = lax.rem(chip, 2)
     sib = shard + 1 - 2 * core
+    pair = chip + 1 - 2 * y
+    up, down, far = (lax.rem(chip + d, 8) for d in (2, 6, 4))
     own = pltpu.make_async_copy(x_ref.at[core], o_ref.at[shard], local_sem)
-
-    def copy(src, slot, kind, i):
+    first, last = pl.ds(0, split), pl.ds(split, x_ref.shape[2] - split)
+
+    def copy(src, dst, slot, chip_to=None):
         return pltpu.make_async_remote_copy(
             src_ref=src,
-            dst_ref=o_ref.at[slot],
-            send_sem=send_sem.at[kind, i],
-            recv_sem=recv_sem.at[kind, i],
-            device_id=(rep, 2 * lax.rem(chip + i, 8) + core if i else sib),
+            dst_ref=dst,
+            send_sem=send_sem.at[slot],
+            recv_sem=recv_sem.at[slot],
+            device_id=(rep, sib if chip_to is None else 2 * chip_to + core),
             device_id_type=MESH,
         )
 
+    def other(c):
+        return c + 1 - 2 * y
+
+    def block(c, columns, part=None):
+        if part is None:
+            return o_ref.at[pl.ds(2 * c, 2), :, columns]
+        return o_ref.at[2 * c + part, :, columns]
+
+    def push(ref, slot, to):
+        copy(ref, ref, slot, to).start()
+
+    def arrived(ref, slot):
+        copy(ref, ref, slot, pair).wait_recv()
+
     def start():
         own.start()
-        copy(x_ref.at[1 - core], shard, 1, 0).start()
-        for i in range(1, 8):
-            copy(x_ref.at[core], shard, 0, i).start()
-
-    def relay():
-        copy(x_ref.at[core], sib, 1, 0).wait_recv()
-        for i in range(1, 8):
-            copy(o_ref.at[sib], sib, 1, i).start()
+        copy(x_ref.at[1 - core], o_ref.at[shard], 0).start()
+
+    def one():
+        copy(o_ref.at[sib], o_ref.at[sib], 0).wait_recv()
+        own.wait()
+        push(block(chip, first), 1, pair)
+        push(block(chip, last), 10, up)
+        push(block(chip, last), 12, down)
+        push(block(chip, first), 2, up)
+        push(block(chip, first), 6, down)
+        push(block(chip, last), 14, pair)
+
+    def two():
+        arrived(block(pair, first), 1)
+        push(block(pair, first), 3, up)
+        push(block(pair, first), 7, down)
+        arrived(block(down, last), 10)
+        push(block(down, last), 15, pair)
+        push(block(down, last, 0), 11, up)
+        arrived(block(up, last), 12)
+        push(block(up, last), 16, pair)
+        push(block(up, last, 1), 13, down)
+
+    def three():
+        arrived(block(down, first), 2)
+        push(block(down, first, 0), 4, up)
+        arrived(block(up, first), 6)
+        push(block(up, first, 1), 8, down)
+        arrived(block(far, last, 0), 11)
+        push(block(far, last, 0), 17, pair)
+        arrived(block(far, last, 1), 13)
+        push(block(far, last, 1), 18, pair)
+        arrived(block(other(down), first), 3)
+        push(block(other(down), first, 0), 5, up)
+        arrived(block(other(up), first), 7)
+        push(block(other(up), first, 1), 9, down)
 
     def finish():
-        own.wait()
-        copy(x_ref.at[1 - core], shard, 1, 0).wait_send()
-        for i in range(1, 8):
-            back = 2 * lax.rem(chip + 8 - i, 8)
-            copy(x_ref.at[core], back + core, 0, i).wait_recv()
-            copy(x_ref.at[core], back + 1 - core, 1, i).wait_recv()
-        for i in range(1, 8):
-            copy(x_ref.at[core], shard, 0, i).wait_send()
-            copy(o_ref.at[sib], sib, 1, i).wait_send()
-
-    return start, relay, finish
+        arrived(block(far, first, 0), 4)
+        arrived(block(far, first, 1), 8)
+        arrived(block(other(far), first, 0), 5)
+        arrived(block(other(far), first, 1), 9)
+        arrived(block(pair, last), 14)
+        arrived(block(other(down), last), 15)
+        arrived(block(other(up), last), 16)
+        arrived(block(other(far), last, 0), 17)
+        arrived(block(other(far), last, 1), 18)
+        copy(x_ref.at[1 - core], o_ref.at[shard], 0).wait_send()
+        for slot in (1, 2, 3, 6, 7):
+            copy(block(chip, first), block(chip, first), slot, pair).wait_send()
+        for slot in (4, 5, 8, 9):
+            copy(block(chip, first, 0), block(chip, first, 0), slot, pair).wait_send()
+        for slot in (10, 12, 14, 15, 16):
+            copy(block(chip, last), block(chip, last), slot, pair).wait_send()
+        for slot in (11, 13, 17, 18):
+            copy(block(chip, last, 0), block(chip, last, 0), slot, pair).wait_send()
+
+    return start, one, two, three, finish
+
+
+START_SPLIT = 896
 
 
 def start_kernel(
-    x_ref, w_ref, t_ref, o_ref, p_ref, g_ref,
-    local_sem, send_sem, recv_sem, s_part, r_part, s_x, r_x,
+    x_ref, t_ref, in_hbm, gain_hbm, routes_hbm, logits_hbm, lift_hbm, code_hbm,
+    o_ref, p_ref, g_ref, share_o, unit_ref,
+    in_ref, gain_ref, routes_ref, logits_ref, lift_ref, code_ref, fetch_sem,
+    w_ref, share_ref, local_sem, send_sem, recv_sem, s_part, r_part, s_x, r_x, s_y, r_y,
 ):
     with_parts = True
     rep, shard = place()
@@ -211,6 +272,8 @@
     up = lax.rem(shard + 4, 16)
     down = lax.rem(shard + 12, 16)
     far = lax.rem(shard + 8, 16)
+    first, last = pl.ds(0, START_SPLIT), pl.ds(START_SPLIT, D - START_SPLIT)
+    rows, top, bottom = pl.ds(0, 2 * half), pl.ds(0, half), pl.ds(half, half)
     peers = [2 * lax.rem(chip + i, 8) + core for i in range(1, 8)]
 
     def other(block):
@@ -221,7 +284,23 @@
         + [(rep, p) for p in peers]
         + [(along_x(rep, 1), shard), (along_x(rep, 3), shard)]
     )
+    fetches = [
+        pltpu.make_async_copy(src, dst, fetch_sem.at[n])
+        for n, (src, dst) in enumerate(
+            (
+                (in_hbm, in_ref),
+                (gain_hbm, gain_ref),
+                (routes_hbm, routes_ref),
+                (logits_hbm, logits_ref),
+                (lift_hbm.at[pl.ds((5 * (rep // 2)) // 2, 3)], lift_ref),
+                (code_hbm, code_ref),
+            )
+        )
+    ]
+    for fetch in fetches:
+        fetch.start()
     x_steps = x_gather(t_ref, g_ref, local_sem.at[2], s_x, r_x)
+    y_steps = x_gather(share_ref, share_o, local_sem.at[3], s_y, r_y)
     own = pltpu.make_async_copy(x_ref, o_ref.at[shard], local_sem.at[0])
     own.start()
     sent = []
@@ -229,29 +308,61 @@
     def put(src, dst, slot, device):
         sent.append(send(src, dst, send_sem.at[len(sent)], recv_sem.at[slot], (rep, device)))
 
-    def forward(block, slot, device, rows=None):
-        ref = o_ref.at[block] if rows is None else o_ref.at[block, rows]
-        put(ref, ref, slot, device)
-
     def landed(ref, sem):
-        pltpu.make_async_remote_copy(
-            src_ref=ref,
-            dst_ref=ref,
-            send_sem=send_sem.at[0],
-            recv_sem=sem,
-            device_id=(rep, sib),
-            device_id_type=MESH,
-        ).wait_recv()
-
-    def arrived(block, slot, rows=None):
-        landed(o_ref.at[block] if rows is None else o_ref.at[block, rows], recv_sem.at[slot])
-
-    top, bottom = pl.ds(0, half), pl.ds(half, half)
-    put(x_ref, o_ref.at[shard], 0, pair)
-    put(x_ref, o_ref.at[shard], 1, up)
-    put(x_ref, o_ref.at[shard], 5, down)
-    put(x_ref, o_ref.at[shard], 9, sib)
+        landed_on(ref, sem, send_sem.at[0], (rep, sib))
+
+    arrivals = {
+        0: (pair, first, rows, ((2, up, rows), (6, down, rows))),
+        9: (down, last, rows, ((14, pair, rows), (10, up, top))),
+        1: (down, first, rows, ((3, up, top),)),
+        11: (up, last, rows, ((15, pair, rows), (12, down, bottom))),
+        5: (up, first, rows, ((7, down, bottom),)),
+        13: (pair, last, rows, ()),
+        2: (other(down), first, rows, ((4, up, top),)),
+        6: (other(up), first, rows, ((8, down, bottom),)),
+        10: (far, last, top, ((16, pair, top),)),
+        12: (far, last, bottom, ((17, pair, bottom),)),
+        3: (far, first, top, ()),
+        7: (far, first, bottom, ()),
+        14: (other(down), last, rows, ()),
+        15: (other(up), last, rows, ()),
+        4: (other(far), first, top, ()),
+        8: (other(far), first, bottom, ()),
+        16: (other(far), last, top, ()),
+        17: (other(far), last, bottom, ()),
+    }
+
+    def arrive(slots):
+        for slot in slots:
+            block, columns, part, onward = arrivals[slot]
+            ref = o_ref.at[block, part, columns]
+            landed(ref, recv_sem.at[slot])
+            for to_slot, device, rows_on in onward:
+                ref_on = o_ref.at[block, rows_on, columns]
+                put(ref_on, ref_on, to_slot, device)
+            put(ref, ref, 19 + slot, sib)
+
+    for columns, slots in ((first, (0, 1, 5)), (last, (13, 9, 11))):
+        for slot, device in zip(slots, (pair, up, down)):
+            put(x_ref.at[:, columns], o_ref.at[shard, :, columns], slot, device)
+    put(x_ref, o_ref.at[shard], 18, sib)
     x_steps[0]()
+
+    for fetch in fetches:
+        fetch.wait()
+    row, column = (lax.broadcasted_iota(jnp.int32, (96, 96), d) for d in (0, 1))
+    gains = contract(jnp.where(row == column, 1.0, 0.0).astype(bf16), gain_ref[...], ((1,), (1,)))
+    gains = jnp.concatenate([gains.astype(bf16), jnp.zeros((96, HEAD - 2), bf16)], 1)
+    for c in range(CHIPS):
+        w_ref[c] = jnp.concatenate(
+            [
+                in_ref[:, 192 * c : 192 * (c + 1)],
+                gains,
+                in_ref[:, 1536 + HEAD * c : 1536 + HEAD * (c + 1)],
+                in_ref[:, 2048 + HEAD * c : 2048 + HEAD * (c + 1)],
+            ],
+            1,
+        )
     parts = []
     if with_parts:
         mine = pltpu.make_async_copy(w_ref.at[chip], p_ref.at[shard], local_sem.at[1])
@@ -266,24 +377,25 @@
                     w_ref.at[c], p_ref.at[shard], s_part.at[i], r_part.at[i], (rep, 2 * c + core)
                 )
             )
-    arrived(pair, 0)
-    forward(pair, 2, up)
-    forward(pair, 6, down)
-    forward(pair, 10, sib)
-    arrived(down, 1)
-    forward(down, 3, up, top)
-    forward(down, 11, sib)
-    arrived(up, 5)
-    forward(up, 7, down, bottom)
-    forward(up, 12, sib)
+    logits = logits_ref[...]
+    gates = jnp.exp(logits - jnp.max(logits, 1, keepdims=True))
+    gates = gates / jnp.sum(gates, 1, keepdims=True)
+    lane = lax.broadcasted_iota(jnp.int32, (OWN, 128), 1)
+    shares = jnp.zeros((OWN, 128), f32)
+    for e in range(EXPERTS):
+        one = jnp.sum(jnp.where(routes_ref[...] == e, gates, 0.0), 1, keepdims=True)
+        shares = jnp.where(lane == e, one, shares)
+    high = shares.astype(bf16)
+    rest = pltpu.roll(shares - high.astype(f32), 16, 1)
+    share_ref[...] = jnp.where(lane < 16, high, rest.astype(bf16))
+    y_steps[0]()
+    choose_units(lift_ref, code_ref, unit_ref)
+    arrive((0, 9, 1, 11, 5, 13))
     x_steps[1]()
-    arrived(other(down), 2)
-    forward(other(down), 4, up, top)
-    forward(other(down), 13, sib)
-    arrived(other(up), 6)
-    forward(other(up), 8, down, bottom)
-    forward(other(up), 14, sib)
+    y_steps[1]()
+    arrive((2, 6, 10, 12))
     x_steps[2]()
+    y_steps[2]()
     if with_parts:
         for i in range(1, 8):
             block = 2 * lax.rem(chip + 8 - i, 8) + core
@@ -293,14 +405,7 @@
                     p_ref.at[block], p_ref.at[block], s_part.at[7 + i], r_part.at[7 + i], (rep, sib)
                 )
             )
-    arrived(far, 3, top)
-    forward(far, 15, sib, top)
-    arrived(far, 7, bottom)
-    forward(far, 16, sib, bottom)
-    arrived(other(far), 4, top)
-    forward(other(far), 17, sib, top)
-    arrived(other(far), 8, bottom)
-    forward(other(far), 18, sib, bottom)
+    arrive((3, 7, 14, 15, 4, 8, 16, 17))
 
     def twin(block):
         return block + 1 - 2 * core
@@ -310,75 +415,81 @@
         for i in range(1, 8):
             landed(p_ref.at[twin(2 * lax.rem(chip + 8 - i, 8) + core)], r_part.at[7 + i])
         mine.wait()
-    arrived(twin(shard), 9)
-    arrived(twin(pair), 10)
-    arrived(twin(down), 11)
-    arrived(twin(up), 12)
-    arrived(twin(other(down)), 13)
-    arrived(twin(other(up)), 14)
-    arrived(twin(far), 15, top)
-    arrived(twin(far), 16, bottom)
-    arrived(twin(other(far)), 17, top)
-    arrived(twin(other(far)), 18, bottom)
+    landed(o_ref.at[sib], recv_sem.at[18])
+    for slot, (block, columns, part, _) in arrivals.items():
+        landed(o_ref.at[twin(block), part, columns], recv_sem.at[19 + slot])
     x_steps[3]()
+    y_steps[3]()
     for copy in sent + parts:
         copy.wait_send()
     own.wait()
 
 
-def start(x, parts, tokens, collective):
+def start(x, tokens, inward, gains, routes, logits, lifting, codes, collective):
     rows, columns = x.shape
     dma = pltpu.SemaphoreType.DMA
-    gathered, parts, tokens = pl.pallas_call(
+    gathered, parts, tokens, shares, units = pl.pallas_call(
         start_kernel,
         out_shape=(
-            jax.ShapeDtypeStruct((SHARDS, rows, columns), x.dtype),
-            jax.ShapeDtypeStruct((SHARDS,) + parts.shape[1:], parts.dtype),
-            jax.ShapeDtypeStruct((PEERS,) + tokens.shape, tokens.dtype),
+            jax.ShapeDtypeStruct((SHARDS, rows, columns), bf16),
+            jax.ShapeDtypeStruct((SHARDS, 96, 384), bf16),
+            jax.ShapeDtypeStruct((PEERS, rows, columns), bf16),
+            jax.ShapeDtypeStruct((PEERS, rows, 128), bf16),
+            jax.ShapeDtypeStruct((2, 96, EXP), bf16),
         ),
-        in_specs=[ANY] * 3,
-        out_specs=(ANY,) * 3,
-        scratch_shapes=[dma((3,)), dma((21,)), dma((19,)), dma((15,)), dma((15,)), dma((9,)), dma((9,))],
-        compiler_params=params(collective),
+        in_specs=[HBM] * 8,
+        out_specs=(ANY,) * 4 + (VMEM,),
+        scratch_shapes=[
+            pltpu.VMEM(inward.shape, bf16),
+            pltpu.VMEM(gains.shape, bf16),
+            pltpu.VMEM(routes.shape, jnp.int32),
+            pltpu.VMEM(logits.shape, f32),
+            pltpu.VMEM((3,) + lifting.shape[1:], bf16),
+            pltpu.VMEM(codes.shape, jnp.int32),
+            dma((6,)),
+            pltpu.VMEM((CHIPS, 96, 384), bf16),
+            pltpu.VMEM((rows, 128), bf16),
+            dma((4,)),
+            dma((37,)),
+            dma((37,)),
+            dma((15,)),
+            dma((15,)),
+        ]
+        + [dma((9,))] * 4,
+        compiler_params=params(collective, 62 * 2**20),
         name="start",
-    )(x, parts, tokens)
-    return gathered.reshape(SHARDS * rows, columns), parts, tokens.reshape(PEERS * rows, -1)
-
-
-def second_kernel(x_ref, w_ref, o_ref, wo_ref, local_sem, s_x, r_x, s_w, r_w):
+    )(x, tokens, inward, gains, routes, logits, lifting, codes)
+    return (
+        gathered.reshape(SHARDS * rows, columns),
+        parts,
+        tokens.reshape(PEERS * rows, columns),
+        shares.reshape(PEERS * rows, 128),
+        units,
+    )
+
+
+def second_kernel(x_ref, o_ref, local_sem, s_x, r_x):
     rep, shard = place()
     core = lax.rem(shard, 2)
-    chip = shard // 2
     greet(
-        [(rep, shard + 1 - 2 * core)]
-        + [(rep, 2 * lax.rem(chip + i, 8) + core) for i in range(1, 8)]
-        + [(along_x(rep, 1), shard), (along_x(rep, 3), shard)]
-    )
-    steps = x_gather(x_ref, o_ref, local_sem.at[0], s_x, r_x)
-    begin, relay, finish = spread(w_ref, wo_ref, local_sem.at[1], s_w, r_w)
-    steps[0]()
-    begin()
-    relay()
-    for step in steps[1:]:
+        [(rep, shard + 1 - 2 * core), (along_x(rep, 1), shard), (along_x(rep, 3), shard)]
+    )
+    for step in x_gather(x_ref, o_ref, local_sem.at[0], s_x, r_x):
         step()
-    finish()
-
-
-def second(x, weights, collective):
+
+
+def second(x, collective):
     dma = pltpu.SemaphoreType.DMA
-    gathered, weights = pl.pallas_call(
+    gathered = pl.pallas_call(
         second_kernel,
-        out_shape=(
-            jax.ShapeDtypeStruct((PEERS,) + x.shape, x.dtype),
-            jax.ShapeDtypeStruct((SHARDS,) + weights.shape[1:], weights.dtype),
-        ),
-        in_specs=[ANY] * 2,
-        out_specs=(ANY,) * 2,
-        scratch_shapes=[dma((2,)), dma((9,)), dma((9,)), dma((2, 8)), dma((2, 8))],
-        compiler_params=params(collective),
+        out_shape=jax.ShapeDtypeStruct((PEERS,) + x.shape, x.dtype),
+        in_specs=[ANY],
+        out_specs=ANY,
+        scratch_shapes=[dma((1,)), dma((9,)), dma((9,))],
+        compiler_params=params(collective, 62 * 2**20),
         name="second_gather",
-    )(x, weights)
-    return gathered.reshape(PEERS * OWN, D), weights
+    )(x)
+    return gathered.reshape(PEERS * OWN, D)
 
 
 def exchange_kernel(kinds, *refs):
@@ -518,7 +629,7 @@
             pltpu.SemaphoreType.DMA((n, 16)),
             pltpu.SemaphoreType.DMA((n, 16)),
         ],
-        compiler_params=params(collective),
+        compiler_params=params(collective, 62 * 2**20),
         name=name,
     )(*arrays)
 
@@ -724,14 +835,15 @@
         + slots(*down.shape[1:])
         + [dma((2, 4))] * 5
         + [dma((2, 5)), dma((2, 2, 8)), dma((2, 2, 8)), dma((2, 4)), dma((2, 4))],
-        compiler_params=params(collective, 60 * 2**20),
+        compiler_params=params(collective, 62 * 2**20),
         name="reduce_rows",
     )(du, out, lift, down)
 
 
 def away_kernel(
-    x_ref, lift_ref, down_ref, o_ref, lift_o, down_o,
-    lift_own, lift_land, down_own, down_land,
+    du_ref, mixed_ref, y_ref, gain_ref, w_ref, a_ref, lift_ref, down_ref,
+    dz_ref, part_ref, o_ref, lift_o, down_o,
+    x_ref, lift_own, lift_land, down_own, down_land,
     local_sem, s_x, r_x, s_mate, r_mate, s_sib, r_sib,
 ):
     rep, shard = place()
@@ -741,6 +853,23 @@
     mate = rep + 1 - 2 * lax.rem(rep, 2)
     greet([(rep, lax.rem(shard + i, 16)) for i in range(1, 16)] + [(mate, shard)])
     sent = []
+    mates, loads = [], []
+    for n, (src, own, land) in enumerate(
+        ((lift_ref, lift_own, lift_land), (down_ref, down_own, down_land))
+    ):
+        mates.append(send(src, land, s_mate.at[n], r_mate.at[n], (mate, shard)))
+        load = pltpu.make_async_copy(src, own, local_sem.at[n])
+        load.start()
+        loads.append(load)
+
+    mixed = mixed_ref[...]
+    inverse = inverse_root(mixed)
+    dz = y_ref[...].astype(f32) + norm_back(du_ref[...] * gain_ref[...], mixed * inverse, inverse)
+    dz_ref[...] = dz
+    low = dz.astype(bf16)
+    back = contract(low, w_ref[...], ((1,), (1,))).astype(bf16)
+    for c in range(CHIPS):
+        x_ref[c] = back[:, c * 192 : (c + 1) * 192]
     for i in range(1, 8):
         c = lax.rem(chip + i, 8)
         sent.append(
@@ -749,14 +878,9 @@
                 (rep, 2 * c + lax.rem(core + chip, 2)),
             )
         )
-    mates, loads = [], []
-    for n, (src, own, land) in enumerate(
-        ((lift_ref, lift_own, lift_land), (down_ref, down_own, down_land))
-    ):
-        mates.append(send(src, land, s_mate.at[n], r_mate.at[n], (mate, shard)))
-        load = pltpu.make_async_copy(src, own, local_sem.at[n])
-        load.start()
-        loads.append(load)
+    part = contract(side_by_side(a_ref), low, ((0,), (0,))).astype(bf16)
+    for s in range(SHARDS):
+        part_ref[s] = part[s * 96 : (s + 1) * 96]
     same = lax.rem(chip, 2) == 0
 
     @pl.when(same)
@@ -799,14 +923,22 @@
         copy.wait_send()
 
 
-def grads_away(x, lift, down, collective):
+def grads_away(du, mixed, y, gain, outward_all, attended, lift, down, collective):
     dma = pltpu.SemaphoreType.DMA
+    heads = (CHIPS, OWN, 192)
     return pl.pallas_call(
         away_kernel,
-        out_shape=tuple(jax.ShapeDtypeStruct(a.shape, a.dtype) for a in (x, lift, down)),
-        in_specs=[ANY] * 3,
-        out_specs=(ANY,) * 3,
+        out_shape=(
+            jax.ShapeDtypeStruct((OWN, D), f32),
+            jax.ShapeDtypeStruct((SHARDS, 96, D), bf16),
+            jax.ShapeDtypeStruct(heads, bf16),
+            jax.ShapeDtypeStruct(lift.shape, bf16),
+            jax.ShapeDtypeStruct(down.shape, bf16),
+        ),
+        in_specs=[VMEM] * 6 + [ANY] * 2,
+        out_specs=(VMEM, VMEM, ANY, ANY, ANY),
         scratch_shapes=[
+            pltpu.VMEM(heads, bf16),
             pltpu.VMEM(lift.shape, bf16),
             pltpu.VMEM(lift.shape, bf16),
             pltpu.VMEM(down.shape, bf16),
@@ -816,9 +948,9 @@
             dma((8,)),
         ]
         + [dma((2,))] * 4,
-        compiler_params=params(collective, 32 * 2**20),
+        compiler_params=params(collective, 62 * 2**20),
         name="grads_away",
-    )(x, lift, down)
+    )(du, mixed, y, gain, outward_all, attended, lift, down)
 
 
 PART = (48, 384)
@@ -830,19 +962,44 @@
 
 
 def tail_kernel(
-    dq_ref, dkv_ref, in_ref, out_ref, w_ref,
+    dq_ref, dkv_ref, in_ref, out_ref, w_hbm,
     dh_ref, in_sum, out_sum,
-    held_k, near_k, held_i, near_i, got_q, got_k, got_i, land_i, land_o, own_o, sum_i, sum_o,
-    l_sem, s_q, r_q, s_nk, r_nk, s_ni, r_ni, s_k, r_k, s_i, r_i, s_ri, r_ri, s_ro, r_ro, s_gi, r_gi, s_go, r_go,
+    w_ref, held_k, near_k, held_i, near_i, got_q, got_k, land_i, land_o, own_o, sum_i, sum_o,
+    l_sem, s_q, r_q, s_nk, r_nk, s_ni, r_ni, s_k, r_k, s_ri, r_ri, s_ro, r_ro, s_gi, r_gi, s_go, r_go,
 ):
     rep, shard = place()
     core = lax.rem(shard, 2)
     chip = shard // 2
     sib = shard + 1 - 2 * core
-    greet(
-        [(rep, lax.rem(shard + i, 16)) for i in range(1, 16)]
-        + [(lax.rem(rep + i, 8), shard) for i in range(1, 8)]
-    )
+    fetch = pltpu.make_async_copy(w_hbm, w_ref, l_sem.at[20])
+    fetch.start()
+    own = pltpu.make_async_copy(out_ref.at[part_of(rep)], own_o, l_sem.at[16])
+    own.start()
+    loads = {}
+    for c in range(8):
+        for name, src, held, base in (("i", in_ref, held_i, 0), ("k", dkv_ref, held_k, 8)):
+            loads[name, c] = pltpu.make_async_copy(
+                src.at[2 * c + core], held.at[c], l_sem.at[base + c]
+            )
+            loads[name, c].start()
+    alone = rep == chip
+    barrier = pltpu.get_barrier_semaphore()
+    for device in [(rep, lax.rem(shard + i, 16)) for i in range(1, 16)] + [
+        (lax.rem(rep + i, 8), shard) for i in range(1, 8)
+    ]:
+        pl.semaphore_signal(barrier, inc=1, device_id=device, device_id_type=MESH)
+    for i in range(8):
+        device = (chip, 2 * lax.rem(chip + i, 8) + core)
+        if i:
+            pl.semaphore_signal(barrier, inc=1, device_id=device, device_id_type=MESH)
+        else:
+
+            @pl.when(jnp.logical_not(alone))
+            def _(device=device):
+                pl.semaphore_signal(barrier, inc=1, device_id=device, device_id_type=MESH)
+
+    pl.semaphore_wait(barrier, jnp.where(alone, 29, 30))
+
     sent = []
 
     def put(src, dst, s_sem, r_sem, device):
@@ -851,34 +1008,47 @@
         return copy
 
     def landed(ref, sem):
-        pltpu.make_async_remote_copy(
-            src_ref=ref, dst_ref=ref, send_sem=s_q.at[0], recv_sem=sem,
-            device_id=(rep, sib), device_id_type=MESH,
-        ).wait_recv()
-
-    order = [1, 7, 2, 6, 3, 5, 4, 0]
-    nears, loads = {}, {}
-    for name, src, held, near, s_n, r_n, base in (
-        ("i", in_ref, held_i, near_i, s_ni, r_ni, 0),
-        ("k", dkv_ref, held_k, near_k, s_nk, r_nk, 8),
+        landed_on(ref, sem, s_q.at[0], (rep, sib))
+
+    nears = {}
+    for name, src, near, s_n, r_n in (
+        ("i", in_ref, near_i, s_ni, r_ni),
+        ("k", dkv_ref, near_k, s_nk, r_nk),
     ):
-        for j in order:
-            c = lax.rem(chip + j, 8)
-            nears[name, j] = put(
-                src.at[2 * c + 1 - core], near.at[j], s_n.at[j], r_n.at[j], (rep, sib)
+        for c in range(8):
+            nears[name, c] = put(
+                src.at[2 * c + 1 - core], near.at[c], s_n.at[c], r_n.at[c], (rep, sib)
             )
-            loads[name, j] = pltpu.make_async_copy(
-                src.at[2 * c + core], held.at[j], l_sem.at[base + j]
-            )
-            loads[name, j].start()
-    own = pltpu.make_async_copy(out_ref.at[part_of(rep)], own_o, l_sem.at[16])
-    own.start()
+    for i in range(1, 8):
+        to = lax.rem(rep + i, 8)
+        put(out_ref.at[part_of(to)], land_o.at[i - 1], s_ro.at[i], r_ro.at[i], (to, shard))
+
+    def add_near(name, held, near, rows):
+        for c in range(8):
+            nears[name, c].wait_recv()
+            loads[name, c].wait()
+
+        def add(t, _):
+            at = pl.ds(pl.multiple_of(t * 32, 32), 32)
+            for c in range(8):
+                held[c, at] = (held[c, at].astype(f32) + near[c, at].astype(f32)).astype(bf16)
+            return 0
+
+        lax.fori_loop(0, rows // 32, add, 0)
+
+    add_near("i", held_i, near_i, 96)
+    for i in range(1, 8):
+        to = lax.rem(rep + i, 8)
+        put(held_i.at[to], land_i.at[i - 1], s_ri.at[i], r_ri.at[i], (to, shard))
+    add_near("k", held_k, near_k, OWN)
     for i in range(1, 8):
         c = lax.rem(chip + i, 8)
+        put(held_k.at[c], got_k.at[chip], s_k.at[i], r_k.at[i], (rep, 2 * c + core))
         put(
             dq_ref.at[c], got_q.at[chip], s_q.at[i], r_q.at[i],
             (rep, 2 * c + lax.rem(c + core, 2)),
         )
+    got_k[chip] = held_k[chip]
     mine = lax.rem(chip, 2) == 0
 
     @pl.when(mine)
@@ -891,42 +1061,40 @@
     def _():
         send(dq_ref.at[chip], got_q.at[chip], s_q.at[0], r_q.at[0], (rep, sib)).wait_send()
 
-    def add_near(name, held, near, j, rows, step):
-        nears[name, j].wait_recv()
-        loads[name, j].wait()
-
-        def add(t, _):
-            at = pl.ds(pl.multiple_of(t * step, step), step)
-            held[j, at] = (held[j, at].astype(f32) + near[j, at].astype(f32)).astype(bf16)
+    own.wait()
+    for land, total, r_x in ((land_o, sum_o, r_ro), (land_i, sum_i, r_ri)):
+        for i in range(1, 8):
+            landed(land.at[i - 1], r_x.at[i])
+
+        def add(t, _, land=land, total=total):
+            at = pl.ds(pl.multiple_of(t * 16, 16), 16)
+            value = own_o[at] if land is land_o else held_i[rep, at]
+            value = value.astype(f32)
+            for i in range(7):
+                value = value + land[i, at].astype(f32)
+            total[at] = value.astype(bf16)
             return 0
 
-        lax.fori_loop(0, rows // step, add, 0)
-
-    for name, held, near, got, s_x, r_x, rows in (
-        ("i", held_i, near_i, got_i, s_i, r_i, 96),
-        ("k", held_k, near_k, got_k, s_k, r_k, OWN),
-    ):
-        for j in order:
-            add_near(name, held, near, j, rows, 32)
-            if j:
-                c = lax.rem(chip + j, 8)
-                put(held.at[j], got.at[chip], s_x.at[j], r_x.at[j], (rep, 2 * c + core))
-            else:
-
-                def keep(t, _, held=held, got=got):
-                    at = pl.ds(pl.multiple_of(t * 32, 32), 32)
-                    got[chip, at] = held[0, at]
-                    return 0
-
-                lax.fori_loop(0, rows // 32, keep, 0)
+        lax.fori_loop(0, total.shape[0] // 16, add, 0)
+        if land is land_o:
+            keep = pltpu.make_async_copy(sum_o, out_sum.at[part_of(rep)], l_sem.at[18])
+            keep.start()
+            for i in range(1, 8):
+                to = lax.rem(rep + i, 8)
+                put(sum_o, out_sum.at[part_of(rep)], s_go.at[i], r_go.at[i], (to, shard))
+    owner = 2 * rep + core
     for i in range(1, 8):
-        to = lax.rem(rep + i, 8)
-        put(out_ref.at[part_of(to)], land_o.at[i - 1], s_ro.at[i], r_ro.at[i], (to, shard))
-    for i in range(1, 8):
-        landed(got_i.at[lax.rem(chip + 8 - i, 8)], r_i.at[i])
-    for i in range(1, 8):
-        to = lax.rem(rep + i, 8)
-        put(got_i.at[to], land_i.at[i - 1], s_ri.at[i], r_ri.at[i], (to, shard))
+        put(sum_i, in_sum.at[chip], s_gi.at[i], r_gi.at[chip], (lax.rem(rep + i, 8), owner))
+
+    @pl.when(alone)
+    def _():
+        copy = pltpu.make_async_copy(sum_i, in_sum.at[chip], l_sem.at[19])
+        copy.start()
+        copy.wait()
+
+    @pl.when(jnp.logical_not(alone))
+    def _():
+        send(sum_i, in_sum.at[chip], s_gi.at[0], r_gi.at[chip], (rep, owner)).wait_send()
 
     @pl.when(jnp.logical_not(mine))
     def _():
@@ -941,39 +1109,18 @@
         + [got_k[c][:, HEAD:] for c in range(CHIPS)],
         1,
     )
+    fetch.wait()
     dh_ref[...] = contract(joined, w_ref[...], ((1,), (1,)))
 
-    own.wait()
-    for land, total, part, r_x in ((land_o, sum_o, None, r_ro), (land_i, sum_i, got_i, r_ri)):
-        for i in range(1, 8):
-            landed(land.at[i - 1], r_x.at[i])
-
-        def add(t, _, land=land, total=total, part=part):
-            at = pl.ds(pl.multiple_of(t * 16, 16), 16)
-            value = own_o[at] if part is None else part[rep, at]
-            value = value.astype(f32)
-            for i in range(7):
-                value = value + land[i, at].astype(f32)
-            total[at] = value.astype(bf16)
-            return 0
-
-        lax.fori_loop(0, total.shape[0] // 16, add, 0)
-    keeps = [
-        pltpu.make_async_copy(sum_o, out_sum.at[part_of(rep)], l_sem.at[18]),
-        pltpu.make_async_copy(sum_i, in_sum.at[rep], l_sem.at[19]),
-    ]
-    for keep in keeps:
-        keep.start()
     for i in range(1, 8):
-        to = lax.rem(rep + i, 8)
-        put(sum_o, out_sum.at[part_of(rep)], s_go.at[i], r_go.at[i], (to, shard))
-        put(sum_i, in_sum.at[rep], s_gi.at[i], r_gi.at[i], (to, shard))
-    for i in range(1, 8):
-        back = lax.rem(rep + 8 - i, 8)
-        landed(out_sum.at[part_of(back)], r_go.at[i])
-        landed(in_sum.at[back], r_gi.at[i])
-    for keep in keeps:
-        keep.wait()
+        landed(out_sum.at[part_of(lax.rem(rep + 8 - i, 8))], r_go.at[i])
+    for j in range(8):
+
+        @pl.when(jnp.logical_not(jnp.logical_and(alone, chip == j)))
+        def _(j=j):
+            landed(in_sum.at[j], r_gi.at[j])
+
+    keep.wait()
     for copy in sent:
         copy.wait_send()
 
@@ -987,25 +1134,25 @@
             jax.ShapeDtypeStruct((CHIPS, 96, 320), bf16),
             jax.ShapeDtypeStruct((96, D), bf16),
         ),
-        in_specs=[ANY, ANY, ANY, ANY, VMEM],
+        in_specs=[ANY, ANY, ANY, ANY, HBM],
         out_specs=(VMEM, ANY, ANY),
         scratch_shapes=[
+            pltpu.VMEM(inward_all.shape, bf16),
             pltpu.VMEM((8, OWN, 128), bf16),
             pltpu.VMEM((8, OWN, 128), bf16),
             pltpu.VMEM((8, 96, 320), bf16),
             pltpu.VMEM((8, 96, 320), bf16),
             pltpu.VMEM((8, OWN, 192), bf16),
             pltpu.VMEM((8, OWN, 128), bf16),
-            pltpu.VMEM((8, 96, 320), bf16),
             pltpu.VMEM((7, 96, 320), bf16),
             pltpu.VMEM((7,) + PART, bf16),
             pltpu.VMEM(PART, bf16),
             pltpu.VMEM((96, 320), bf16),
             pltpu.VMEM(PART, bf16),
-            dma((20,)),
+            dma((21,)),
         ]
-        + [dma((8,))] * 18,
-        compiler_params=params(collective, 56 * 2**20),
+        + [dma((8,))] * 16,
+        compiler_params=params(collective, 62 * 2**20),
         name="tail",
     )(dq, dkv, inward_part, outward_own, inward_all)
 
@@ -1018,11 +1165,9 @@
     return jnp.where(lax.rem(lane, HEAD) < HEAD // 2, ahead, behind)
 
 
-def project_kernel(x_ref, w_ref, g_ref, cos_ref, sin_ref, q_ref, k_ref, v_ref, u_ref):
-    i = pl.program_id(0)
+def project_step(i, core, x_ref, w_ref, g_ref, cos_ref, sin_ref, q_ref, k_ref, v_ref, u_ref):
     stream = x_ref[...].astype(f32)
     u_ref[...] = (stream * inverse_root(stream) * g_ref[...]).astype(bf16)
-    core = lax.rem(lax.axis_index("shard"), 2)
     first = pl.multiple_of(lax.rem(i + core, 2) * OWN, OWN)
     own = pl.ds(first, OWN)
     queries = jnp.dot(u_ref[own, :], w_ref[:, :256], preferred_element_type=f32)
@@ -1031,40 +1176,13 @@
     turned = (queries * cos + swap_halves(queries) * sin).astype(bf16)
     turned = turned * jnp.bfloat16(HEAD**-0.5)
     for r in range(GROUP):
-        q_ref[0, r * OWN : (r + 1) * OWN, :] = turned[:, r * HEAD : (r + 1) * HEAD]
+        q_ref[i, r * OWN : (r + 1) * OWN, :] = turned[:, r * HEAD : (r + 1) * HEAD]
     pairs = jnp.dot(u_ref[...], w_ref[:, 256:], preferred_element_type=f32)
     keys = pairs * cos_ref[...] + swap_halves(pairs) * sin_ref[...]
-    k_ref[...] = keys[:, :HEAD].astype(bf16)
+    rows = pl.ds(pl.multiple_of(i * KEYS, KEYS), KEYS)
+    k_ref[rows, :] = keys[:, :HEAD].astype(bf16)
     lane = lax.broadcasted_iota(jnp.int32, pairs.shape, 1)
-    v_ref[...] = jnp.where(lane < HEAD, pltpu.roll(pairs, HEAD, 1), 1.0).astype(bf16)
-
-
-def project(x_all, weight, gain, cos, sin):
-    return pl.pallas_call(
-        project_kernel,
-        grid=(BLOCKS,),
-        in_specs=[
-            pl.BlockSpec((KEYS, D), lambda i: (i, 0)),
-            pl.BlockSpec((D, 384), lambda i: (0, 0)),
-            pl.BlockSpec((1, D), lambda i: (0, 0)),
-            pl.BlockSpec((KEYS, 128), lambda i: (i, 0)),
-            pl.BlockSpec((KEYS, 128), lambda i: (i, 0)),
-        ],
-        out_specs=(
-            pl.BlockSpec((1, ROWS, HEAD), lambda i: (i, 0, 0)),
-            pl.BlockSpec((KEYS, HEAD), lambda i: (i, 0)),
-            pl.BlockSpec((KEYS, 128), lambda i: (i, 0)),
-            pl.BlockSpec((KEYS, D), lambda i: (i, 0)),
-        ),
-        out_shape=(
-            jax.ShapeDtypeStruct((BLOCKS, ROWS, HEAD), bf16),
-            jax.ShapeDtypeStruct((SEQ, HEAD), bf16),
-            jax.ShapeDtypeStruct((SEQ, 128), bf16),
-            jax.ShapeDtypeStruct((SEQ, D), bf16),
-        ),
-        compiler_params=pltpu.CompilerParams(vmem_limit_bytes=48 * 2**20),
-        name="project_heads",
-    )(x_all, weight, gain, cos, sin)
+    v_ref[rows, :] = jnp.where(lane < HEAD, pltpu.roll(pairs, HEAD, 1), 1.0).astype(bf16)
 
 
 def contract(a, b, dims, precision=None):
@@ -1073,27 +1191,65 @@
     )
 
 
-def attend_kernel(q_ref, k_ref, v_ref, b_ref, o_ref, l_ref, bo_ref, local_sem, s_sem, r_sem):
+def attend_kernel(
+    x_ref, w_ref, g_ref, cos_ref, sin_ref, b_ref, d_ref,
+    q_ref, k_ref, v_ref, u_ref, o_ref, l_ref, bo_ref, do_ref,
+    local_sem, s_sem, r_sem, s_low, r_low,
+):
     i = pl.program_id(0)
     core = lax.rem(lax.axis_index("shard"), 2)
-    begin, relay, finish = spread(b_ref, bo_ref, local_sem.at[0], s_sem, r_sem)
+    steps = ring_spread(b_ref, bo_ref, 768, local_sem.at[0], s_sem, r_sem)
+    low_steps = ring_spread(d_ref, do_ref, 896, local_sem.at[1], s_low, r_low)
 
     @pl.when(i == 0)
     def _():
         rep, shard = place()
-        chip = shard // 2
+        y = lax.rem(shard // 2, 2)
         greet(
-            [(rep, shard + 1 - 2 * core)]
-            + [(rep, 2 * lax.rem(chip + n, 8) + core) for n in range(1, 8)]
+            [(rep, shard + 1 - 2 * core), (rep, shard + 2 - 4 * y)]
+            + [(rep, lax.rem(shard + 4, 16)), (rep, lax.rem(shard + 12, 16))]
         )
-        begin()
+        steps[0]()
+        low_steps[0]()
 
     @pl.when(i == 1)
     def _():
-        relay()
-
+        steps[1]()
+
+    @pl.when(i == 6)
+    def _():
+        low_steps[1]()
+
+    @pl.when(i == 11)
+    def _():
+        steps[2]()
+
+    @pl.when(i == 13)
+    def _():
+        low_steps[2]()
+
+    @pl.when(i == 15)
+    def _():
+        steps[3]()
+
+    @pl.when(i < BLOCKS)
+    def _():
+        project_step(i, core, x_ref, w_ref, g_ref, cos_ref, sin_ref, q_ref, k_ref, v_ref, u_ref)
+
+    @pl.when(i >= BLOCKS)
+    def _():
+        attend_step(i - BLOCKS, core, q_ref, k_ref, v_ref, o_ref, l_ref)
+
+    @pl.when(i == 2 * BLOCKS - 1)
+    def _():
+        low_steps[3]()
+        steps[4]()
+        low_steps[4]()
+
+
+def attend_step(i, core, q_ref, k_ref, v_ref, o_ref, l_ref):
     shift = lax.rem(i + core, 2) * OWN
-    q = q_ref[0]
+    q = q_ref[i]
 
     def step(c, carry, last=False):
         top, total = carry
@@ -1125,45 +1281,54 @@
         lax.Precision.HIGHEST,
     )
 
-    @pl.when(i == BLOCKS - 1)
-    def _():
-        finish()
-
-
-def attend(q, k, v, units, collective):
+
+def attend(x_all, weight, gain, cos, sin, units, low, collective):
+    dma = pltpu.SemaphoreType.DMA
+    whole = lambda i: (0, 0)
+    early = lambda i: (jnp.minimum(i, BLOCKS - 1), 0)
+    late = lambda i: (jnp.maximum(i - BLOCKS, 0), 0, 0)
     return pl.pallas_call(
         attend_kernel,
-        grid=(BLOCKS,),
+        grid=(2 * BLOCKS,),
         in_specs=[
-            pl.BlockSpec((1, ROWS, HEAD), lambda i: (i, 0, 0)),
-            pl.BlockSpec((SEQ, HEAD), lambda i: (0, 0)),
-            pl.BlockSpec((SEQ, 128), lambda i: (0, 0)),
+            pl.BlockSpec((KEYS, D), early),
+            pl.BlockSpec((D, 384), whole),
+            pl.BlockSpec((1, D), whole),
+            pl.BlockSpec((KEYS, 128), early),
+            pl.BlockSpec((KEYS, 128), early),
+            ANY,
             ANY,
         ],
         out_specs=(
-            pl.BlockSpec((1, OWN, GROUP * HEAD), lambda i: (i, 0, 0)),
-            pl.BlockSpec((1, 8, ROWS), lambda i: (i, 0, 0)),
+            pl.BlockSpec((BLOCKS, ROWS, HEAD), lambda i: (0, 0, 0)),
+            pl.BlockSpec((SEQ, HEAD), whole),
+            pl.BlockSpec((SEQ, 128), whole),
+            pl.BlockSpec((KEYS, D), early),
+            pl.BlockSpec((1, OWN, GROUP * HEAD), late),
+            pl.BlockSpec((1, 8, ROWS), late),
+            ANY,
             ANY,
         ),
         out_shape=(
+            jax.ShapeDtypeStruct((BLOCKS, ROWS, HEAD), bf16),
+            jax.ShapeDtypeStruct((SEQ, HEAD), bf16),
+            jax.ShapeDtypeStruct((SEQ, 128), bf16),
+            jax.ShapeDtypeStruct((SEQ, D), bf16),
             jax.ShapeDtypeStruct((BLOCKS, OWN, GROUP * HEAD), bf16),
             jax.ShapeDtypeStruct((BLOCKS, 8, ROWS), f32),
             jax.ShapeDtypeStruct((SHARDS,) + units.shape[1:], bf16),
+            jax.ShapeDtypeStruct((SHARDS,) + low.shape[1:], bf16),
         ),
-        scratch_shapes=[
-            pltpu.SemaphoreType.DMA((1,)),
-            pltpu.SemaphoreType.DMA((2, 8)),
-            pltpu.SemaphoreType.DMA((2, 8)),
-        ],
-        compiler_params=params(collective, 48 * 2**20),
+        scratch_shapes=[dma((2,))] + [dma((19,))] * 4,
+        compiler_params=params(collective, 62 * 2**20),
         name="attend",
-    )(q, k, v, units)
+    )(x_all, weight, gain, cos, sin, units, low)
 
 
 def attend_back_kernel(
-    q_ref, k_ref, v_ref, g_ref, a_ref, l_ref, cos_ref, sin_ref, qcos_ref, qsin_ref, part_ref,
-    lift_ref, down_ref, dq_ref, dkv_ref, part_out, lift_out, down_out,
-    dk, dv, dq, held, near, landed, local_sem, s_sem, r_sem, h_sem, s_near, r_near, s_far, r_far,
+    q_ref, k_ref, v_ref, g_ref, a_ref, l_ref, cos_ref, sin_ref, qcos_ref, qsin_ref, u_hbm, part_ref,
+    lift_ref, down_ref, dq_ref, dkv_ref, in_ref, part_out, lift_out, down_out,
+    u_ref, u_sem, dk, dv, dq, total_q, held, near, landed, local_sem, s_sem, r_sem, h_sem, s_near, r_near, s_far, r_far,
 ):
     i = pl.program_id(0)
     rep, shard = place()
@@ -1229,6 +1394,8 @@
             copy_same(n, src, dst).start()
             for dx in (1, 2, 3):
                 copy_x(n, src, dst, dx, x).start()
+        pltpu.make_async_copy(u_hbm, u_ref, u_sem).start()
+        total_q[...] = jnp.zeros_like(total_q)
         dk[...] = jnp.zeros_like(dk)
         dv[...] = jnp.zeros_like(dv)
 
@@ -1287,7 +1454,15 @@
     cos, sin = qcos_ref[...], qsin_ref[...]
     cos, sin = jnp.concatenate([cos, cos], 1), jnp.concatenate([sin, sin], 1)
     wide = wide * cos - swap_halves(wide) * sin
-    dq_ref[0] = wide[:, : GROUP * HEAD].astype(bf16)
+    wide = wide[:, : GROUP * HEAD].astype(bf16)
+    dq_ref[0] = wide
+
+    @pl.when(i == 0)
+    def _():
+        pltpu.make_async_copy(u_hbm, u_ref, u_sem).wait()
+
+    mine = pl.ds(pl.multiple_of(i * KEYS + shift, OWN), OWN)
+    total_q[...] += contract(wide, u_ref[mine, :], ((0,), (0,)))
 
     @pl.when(i == BLOCKS - 1)
     def _():
@@ -1300,6 +1475,15 @@
             return 0
 
         lax.fori_loop(0, SHARDS, turn, 0)
+        def add_pairs(c, both):
+            at = pl.ds(pl.multiple_of(c * 768, 768), 768)
+            return both + contract(dkv_ref[at, :], u_ref[at, :], ((0,), (0,)))
+
+        both = lax.fori_loop(0, SEQ // 768, add_pairs, jnp.zeros((128, D), f32))
+        both = jnp.concatenate([total_q[...], both], 0).T.astype(bf16)
+        for s in range(SHARDS):
+            in_ref[s] = both[s * 96 : (s + 1) * 96]
+
         for j in range(1, 8):
             copy_far(j).wait_recv()
 
@@ -1324,7 +1508,7 @@
                 copy_far(j).wait_send()
 
 
-def attend_back(q, k, v, grad, attended, lse, cos, sin, part, lift, down, collective):
+def attend_back(q, k, v, grad, attended, lse, cos, sin, u_all, part, lift, down, collective):
     def own(i):
         return (2 * i + lax.rem(i + lax.rem(lax.axis_index("shard"), 2), 2), 0)
 
@@ -1344,6 +1528,7 @@
             pl.BlockSpec((SEQ, 128), whole),
             pl.BlockSpec((OWN, 128), own),
             pl.BlockSpec((OWN, 128), own),
+            HBM,
             ANY,
             ANY,
             ANY,
@@ -1351,6 +1536,7 @@
         out_specs=(
             pl.BlockSpec((1, OWN, GROUP * HEAD), block),
             pl.BlockSpec((SEQ, 128), whole),
+            pl.BlockSpec((SHARDS, 96, 320), lambda i: (0, 0, 0)),
             pl.BlockSpec(part.shape[1:], whole),
             ANY,
             ANY,
@@ -1358,14 +1544,18 @@
         out_shape=(
             jax.ShapeDtypeStruct((BLOCKS, OWN, GROUP * HEAD), bf16),
             jax.ShapeDtypeStruct((SEQ, 128), bf16),
+            jax.ShapeDtypeStruct((SHARDS, 96, 320), bf16),
             jax.ShapeDtypeStruct(part.shape[1:], bf16),
             jax.ShapeDtypeStruct((PEERS,) + lift.shape[1:], bf16),
             jax.ShapeDtypeStruct((PEERS,) + down.shape[1:], bf16),
         ),
         scratch_shapes=[
+            pltpu.VMEM((SEQ, D), bf16),
+            pltpu.SemaphoreType.DMA,
             pltpu.VMEM((SEQ, HEAD), f32),
             pltpu.VMEM((SEQ, HEAD), f32),
             pltpu.VMEM((ROWS, HEAD), f32),
+            pltpu.VMEM((GROUP * HEAD, D), f32),
             pltpu.VMEM((8,) + part.shape[1:], bf16),
             pltpu.VMEM((8,) + part.shape[1:], bf16),
             pltpu.VMEM((7,) + part.shape[1:], bf16),
@@ -1374,9 +1564,9 @@
             pltpu.SemaphoreType.DMA((2, 4)),
         ]
         + [pltpu.SemaphoreType.DMA((8,))] * 5,
-        compiler_params=params(collective, 48 * 2**20),
+        compiler_params=params(collective, 62 * 2**20),
         name="attend_back",
-    )(q, k, v, grad, attended, lse, cos, sin, cos, sin, part, lift, down)
+    )(q, k, v, grad, attended, lse, cos, sin, cos, sin, u_all, part, lift, down)
 
 
 def experts_kernel(
@@ -1411,7 +1601,7 @@
         down_ref[...] = down[...].astype(bf16)
 
 
-def experts(u_all, y_all, wl, wd, spread):
+def experts(u_all, y_all, shares, wl, wd, spread):
     step = 384
     rows = lambda i: (i, 0)
     whole = lambda i: (0, 0)
@@ -1422,7 +1612,7 @@
         in_specs=[
             pl.BlockSpec((step, D), rows),
             pl.BlockSpec((step, D), rows),
-            pl.BlockSpec((step, 128), lambda i: (i, D // 128)),
+            pl.BlockSpec((step, 128), rows),
             pl.BlockSpec((D, EXP), whole, pipeline_mode=once),
             pl.BlockSpec((HID, D), whole, pipeline_mode=once),
             pl.BlockSpec((128, HID), whole, pipeline_mode=once),
@@ -1440,12 +1630,12 @@
             jax.ShapeDtypeStruct((HID, D), bf16),
         ),
         scratch_shapes=[pltpu.VMEM((D, EXP), f32), pltpu.VMEM((HID, D), f32)],
-        compiler_params=pltpu.CompilerParams(vmem_limit_bytes=60 * 2**20),
+        compiler_params=pltpu.CompilerParams(vmem_limit_bytes=62 * 2**20),
         name="experts",
-    )(u_all, y_all, y_all, wl, wd, spread)
-
-
-def units_kernel(w_ref, code_ref, out_ref):
+    )(u_all, y_all, shares, wl, wd, spread)
+
+
+def choose_units(w_ref, code_ref, out_ref):
     x = lax.axis_index("rep") // 2
     row = lax.broadcasted_iota(jnp.int32, (FF_EXP, HID), 0)
     there = (row // 32) * 1024 + lax.rem(row, 32)
@@ -1457,7 +1647,7 @@
             for i in range(3):
                 chosen = there + 32 * (base + i) == here + FLAT * (2 * x + k)
                 total = total + jnp.dot(
-                    w_ref[base + i][:, FF_EXP * part : FF_EXP * (part + 1)],
+                    w_ref[i][:, FF_EXP * part : FF_EXP * (part + 1)],
                     jnp.where(chosen, 1.0, 0.0).astype(bf16),
                     preferred_element_type=f32,
                 )
@@ -1470,7 +1660,7 @@
         in_specs=[VMEM] * len(arrays),
         out_specs=(VMEM,) * len(shapes),
         out_shape=tuple(jax.ShapeDtypeStruct(shape, dtype) for shape, dtype in shapes),
-        compiler_params=pltpu.CompilerParams(vmem_limit_bytes=56 * 2**20),
+        compiler_params=pltpu.CompilerParams(vmem_limit_bytes=62 * 2**20),
         name=name,
     )(*arrays)
 
@@ -1485,63 +1675,12 @@
     )
     mixed_ref[...] = mixed
     low_ref[...] = (mixed * inverse_root(mixed) * g_ref[...]).astype(bf16)
-
-
-def unmix_kernel(du_ref, e_ref, mixed_ref, y_ref, g_ref, w_ref, a_ref, out_ref, dz_ref, ga_ref, part_ref):
-    mixed = mixed_ref[...]
-    out_ref[...] = mixed + e_ref[...]
-    inverse = inverse_root(mixed)
-    dz = y_ref[...].astype(f32) + norm_back(du_ref[...] * g_ref[...], mixed * inverse, inverse)
-    dz_ref[...] = dz
-    low = dz.astype(bf16)
-    back = contract(low, w_ref[...], ((1,), (1,))).astype(bf16)
-    for c in range(CHIPS):
-        ga_ref[c] = back[:, c * 192 : (c + 1) * 192]
-    part = contract(side_by_side(a_ref), low, ((0,), (0,))).astype(bf16)
-    for s in range(SHARDS):
-        part_ref[s] = part[s * 96 : (s + 1) * 96]
 
 
 def finish_kernel(dh_ref, dz_ref, x_ref, g_ref, out_ref):
     stream = x_ref[...].astype(f32)
     inverse = inverse_root(stream)
     out_ref[...] = dz_ref[...] + norm_back(dh_ref[...] * g_ref[...], stream * inverse, inverse)
-
-
-def inward_part_kernel(u_ref, dq_ref, dkv_ref, out_ref, total):
-    i = pl.program_id(0)
-    core = lax.rem(lax.axis_index("shard"), 2)
-    first = pl.multiple_of(lax.rem(i + core, 2) * OWN, OWN)
-
-    @pl.when(i == 0)
-    def _():
-        total[...] = jnp.zeros_like(total)
-
-    total[:, :192] += contract(u_ref[pl.ds(first, OWN), :], dq_ref[0], ((0,), (0,)))
-    total[:, 256:] += contract(u_ref[...], dkv_ref[...], ((0,), (0,)))
-
-    @pl.when(i == BLOCKS - 1)
-    def _():
-        both = jnp.concatenate([total[:, :192], total[:, 256:]], 1).astype(bf16)
-        for s in range(SHARDS):
-            out_ref[s] = both[s * 96 : (s + 1) * 96]
-
-
-def inward_parts(u_all, dq, dkv):
-    return pl.pallas_call(
-        inward_part_kernel,
-        grid=(BLOCKS,),
-        in_specs=[
-            pl.BlockSpec((KEYS, D), lambda i: (i, 0)),
-            pl.BlockSpec((1, OWN, GROUP * HEAD), lambda i: (i, 0, 0)),
-            pl.BlockSpec((KEYS, 128), lambda i: (i, 0)),
-        ],
-        out_specs=pl.BlockSpec((SHARDS, 96, 320), lambda i: (0, 0, 0)),
-        out_shape=jax.ShapeDtypeStruct((SHARDS, 96, 320), bf16),
-        scratch_shapes=[pltpu.VMEM((D, 384), f32)],
-        compiler_params=pltpu.CompilerParams(vmem_limit_bytes=48 * 2**20),
-        name="inward_parts",
-    )(u_all, dq, dkv)
 
 
 def adam(weight, old_mean, square, gradient, step_rate, decay_rate):
@@ -1565,11 +1704,15 @@
     chosen_first = jnp.where(there == here + FLAT * first, 1.0, 0.0).astype(bf16)
     skip = jnp.where(first == last, 1 << 20, 0)
     chosen_last = jnp.where(there == here + (FLAT * last + skip), 1.0, 0.0).astype(bf16)
-    for part in range(2):
-        columns = slice(HID * part, HID * (part + 1))
-        grad[:, FF_EXP * part : FF_EXP * (part + 1)] = jnp.dot(
-            g_ref[first][:, columns], chosen_first, preferred_element_type=f32
-        ) + jnp.dot(g_ref[last][:, columns], chosen_last, preferred_element_type=f32)
+
+    def both(p):
+        return jnp.concatenate([g_ref[p][:, :HID], g_ref[p][:, HID:]], 0)
+
+    ordered = jnp.dot(both(first), chosen_first, preferred_element_type=f32) + jnp.dot(
+        both(last), chosen_last, preferred_element_type=f32
+    )
+    grad[:, :FF_EXP] = ordered[:96]
+    grad[:, FF_EXP:] = ordered[96:]
 
     @pl.when(e == 0)
     def _():
@@ -1598,7 +1741,7 @@
         out_specs=(block, block, block, pl.BlockSpec((96, 128), lambda e: (0, 0))),
         out_shape=(shape, shape, shape, jax.ShapeDtypeStruct((96, 128), f32)),
         scratch_shapes=[pltpu.VMEM((96, 2 * FF_EXP), f32)],
-        compiler_params=pltpu.CompilerParams(vmem_limit_bytes=48 * 2**20),
+        compiler_params=pltpu.CompilerParams(vmem_limit_bytes=62 * 2**20),
         name="adam_lifting",
     )(weight, mean, square, grad, code)
 
@@ -1622,7 +1765,7 @@
         in_specs=[VMEM] * 4,
         out_specs=(VMEM,) * 4,
         out_shape=(shape, shape, shape, jax.ShapeDtypeStruct((96, 128), f32)),
-        compiler_params=pltpu.CompilerParams(vmem_limit_bytes=48 * 2**20),
+        compiler_params=pltpu.CompilerParams(vmem_limit_bytes=62 * 2**20),
         name="adam_inward",
     )(weight, mean, square, grad)
 
@@ -1675,24 +1818,10 @@
     gains = norm_gains.astype(f32)
     cos, sin = (jnp.asarray(t) for t in tables())
 
-    by_head = jnp.concatenate(
-        [
-            inward[:, :1536].reshape(96, KV_HEADS, 192),
-            jnp.broadcast_to(
-                jnp.pad(norm_gains.T, ((0, 0), (0, HEAD - 2)))[:, None, :], (96, KV_HEADS, HEAD)
-            ),
-            inward[:, 1536:2048].reshape(96, KV_HEADS, HEAD),
-            inward[:, 2048:].reshape(96, KV_HEADS, HEAD),
-        ],
-        2,
-    ).transpose(1, 0, 2)
     lifting_rows = lifting.transpose(1, 0, 2)
     codes = jnp.asarray(unit_codes())
     x = lax.axis_index("rep") // 2
     position = 2 * x + lax.rem(lax.axis_index("shard"), 2)
-    (by_unit,) = one_step(
-        units_kernel, (lifting_rows, codes[None, :]), (((2, 96, EXP), bf16),), "choose_units"
-    )
     low_rows = lowering.transpose(1, 0, 2).reshape(EXPERTS * 32, D)
     low_rows = lax.dynamic_slice(low_rows, (2 * FLAT * x, 0), (2 * FLAT, D)).reshape(2, FLAT, D)
     low_rows = jnp.pad(low_rows, ((0, 0), (0, FLAT_PAD - FLAT), (0, 0)))
@@ -1700,16 +1829,8 @@
     row = jnp.arange(128)[:, None]
     share_table = ((row == expert) | (row == expert + 16)).astype(bf16)
 
-    gates = jax.nn.softmax(route_logits, axis=-1)
-    picked = routes[:, :, None] == jnp.arange(EXPERTS, dtype=jnp.int32)[None, None, :]
-    combine = jnp.sum(jnp.where(picked, gates[:, :, None], 0.0), axis=1)
-    high = lax.reduce_precision(combine, 8, 7)
-    rest = combine - high
-    shares = jnp.concatenate(
-        [jnp.pad(high, ((0, 0), (0, 6))), jnp.pad(rest, ((0, 0), (0, 102)))], 1
-    ).astype(bf16)
-    x_all, head_weight, y_all = start(
-        layer_input, by_head, jnp.concatenate([grad_output, shares], 1), 2
+    x_all, head_weight, y_all, shares, by_unit = start(
+        layer_input, grad_output, inward, norm_gains, routes, route_logits, lifting_rows, codes[None, :], 2
     )
     head_weight = head_weight.reshape(D, 384)
     gain_rows = head_weight[:, 192:194].T.astype(f32)
@@ -1717,8 +1838,9 @@
     late_outward, x_all = lax.optimization_barrier((outward, x_all))
     outward_all = lax.all_gather(late_outward, "shard", axis=0, tiled=True)
 
-    q, k, v, u_one = project(x_all, head_weight, gain_one, cos, sin)
-    attended, lse, unit_weight = attend(q, k, v, by_unit, 1)
+    q, k, v, u_one, attended, lse, unit_weight, down_weight = attend(
+        x_all, head_weight, gain_one, cos, sin, by_unit, low_rows, 1
+    )
     unit_weight = unit_weight.reshape(D, EXP)
     (own_attended,) = exchange((attended,), ("home",), 3, "attended_home")
     mixed, low_two = one_step(
@@ -1727,13 +1849,13 @@
         (((OWN, D), f32), ((OWN, D), bf16)),
         "mix",
     )
-    u_two, down_weight = second(low_two, low_rows, 4)
+    u_two = second(low_two, 4)
     down_weight = down_weight[:, :FLAT].reshape(HID, D)
     late_inward, u_two = lax.optimization_barrier((inward, u_two))
     inward_all = lax.all_gather(late_inward, "shard", axis=0, tiled=True)
 
     out_part, du_part, lift_part, down_part = experts(
-        u_two, y_all, unit_weight, down_weight, share_table
+        u_two, y_all, shares, unit_weight, down_weight, share_table
     )
     du, expert_out, lift_sum, down_sum = reduce_blocks(
         du_part.reshape(PEERS, OWN, D),
@@ -1742,20 +1864,15 @@
         down_part.reshape(CHIPS, 2 * FLAT, D),
         5,
     )
-    layer_output, grad_mixed, away, outward_part = one_step(
-        unmix_kernel,
-        (du, expert_out, mixed, grad_output, gain_two, outward_all, own_attended),
-        (((OWN, D), f32), ((OWN, D), f32), ((CHIPS, OWN, 192), bf16), ((SHARDS, 96, D), bf16)),
-        "unmix",
-    )
+    layer_output = mixed + expert_out
     down_sum = jnp.pad(down_sum.reshape(2, FLAT, D), ((0, 0), (0, FLAT_PAD - FLAT), (0, 0)))
-    head_grads, lift_pair, down_pair = grads_away(
-        away, lift_sum.reshape(2, 96, EXP), down_sum, 6
-    )
-    dq, dkv, outward_own, lift_got, down_got = attend_back(
-        q, k, v, head_grads, attended, lse, cos, sin, outward_part, lift_pair, down_pair, 8
-    )
-    inward_part = inward_parts(u_one, dq, dkv)
+    grad_mixed, outward_part, head_grads, lift_pair, down_pair = grads_away(
+        du, mixed, grad_output, gain_two, outward_all, own_attended,
+        lift_sum.reshape(2, 96, EXP), down_sum, 6,
+    )
+    dq, dkv, inward_part, outward_own, lift_got, down_got = attend_back(
+        q, k, v, head_grads, attended, lse, cos, sin, u_one, outward_part, lift_pair, down_pair, 8
+    )
     dh, inward_sum, outward_sum = tail(
         dq, dkv.reshape(SHARDS, OWN, 128), inward_part, outward_own, inward_all, 7
     )

time: 516 us -> 479 us (0.928)
  Pallas kernels: 465 us -> 439 us
  local copies, waits for them, and re-layouts: 19.2 us -> 13.2 us
    pallas_call x4 -> x2, Pallas kernels: 21.7 us -> 8.43 us  [one_step(): pl.pallas_call(kernel, in_specs=[VMEM] * len(arrays), out_specs=(VMEM,) *...]
    pallas_call x5 -> x3, Pallas kernels: 149 us -> 136 us  [the longest x1 72.5 us: attend(): pl.pallas_call(attend_kernel, grid=(2 * BLOCKS,), in_specs=[pl.BlockSpec(...]
    pallas_call x1, Pallas kernels: 43.7 us -> 56.1 us  [attend_back(): pl.pallas_call(attend_back_kernel, grid=(BLOCKS,), in_specs=[pl.BlockSpec...]
    pallas_call x1, Pallas kernels: 56 us -> 49.5 us  [start(): pl.pallas_call(start_kernel, out_shape=(jax.ShapeDtypeStruct((SHARDS, row...]
  transfers between devices with their start and end apart: 2 -> 2, of which waited for: 0 -> 0; matrix products, arithmetic and copies ran while one was open for 3% -> 4% of each run, Pallas kernels for 62% -> 64%
where the time goes in v4:
time: 479 us; the launch traced here: 478 us
  Pallas kernels  439 us (92%)
  between operations  14.3 us (3%)
  local copies, waits for them, and re-layouts  13.2 us (3%)
  other arithmetic  11.7 us (2%)
    pallas_call x1, Pallas kernels, attend(): pl.pallas_call(attend_kernel, grid=(2 * BLOCKS,), in_specs=[pl.BlockSpec(...  72.5 us
    pallas_call x1, Pallas kernels, reduce_blocks(): pl.pallas_call(reduce_kernel, out_shape=(jax.ShapeDtypeStruct((OWN, D), f...  62.8 us
    pallas_call x1, Pallas kernels, attend_back(): pl.pallas_call(attend_back_kernel, grid=(BLOCKS,), in_specs=[pl.BlockSpec...  56.1 us
    pallas_call x1, Pallas kernels, start(): pl.pallas_call(start_kernel, out_shape=(jax.ShapeDtypeStruct((SHARDS, row...  49.5 us
    pallas_call x1, Pallas kernels, tail(): pl.pallas_call(tail_kernel, out_shape=(jax.ShapeDtypeStruct((OWN, D), f32...  45.3 us
    pallas_call x1, Pallas kernels, experts(): pl.pallas_call(experts_kernel, grid=(PEERS * OWN // step,), in_specs=[pl....  43.3 us
    pallas_call x1, Pallas kernels, grads_away(): pl.pallas_call(away_kernel, out_shape=(jax.ShapeDtypeStruct((OWN, D), f32...  36.5 us
    pallas_call x1, Pallas kernels, second(): pl.pallas_call(second_kernel, out_shape=jax.ShapeDtypeStruct((PEERS,) + x...  27.3 us
  transfers between devices with their start and end apart: 2, of which 0 were waited for; matrix products, arithmetic and copies ran while one was open for 4% of the time, Pallas kernels for 64%

profile of v4, /device:TPU:1, one launch (start us, length us, event | category | flops | bytes accessed | tf_op | source)
XLA Modules:
  0.0 478.0 jit_solution(18032312712044528192)
XLA Ops:
  7.2 0.0 all-gather.3.cloned.1.call-start
  7.2 1.5 copy.43.routes_hbm
  8.7 1.5 copy.44.logits_hbm
  10.1 49.5 %start.1 = (bf16[16,192,1536]{2,1,0:T(8,128)(2,1)}, bf16[16,96,384]{2,1,0:T(8,128)(2,1)}, bf16[8,192,1536]{2,1,0:T(8,128)(2,1)}, bf16[8,192,128]{2,1,0:T(8,128)(2,1)}, bf16[2,96,1280]{2,1,0:T(8,128)(2,1)}) custom-call(bf16[192,1536]{1,0:T(8,128)(2,1)} %x_ref.5, bf16[192,1536]{1,0:T(8,128)(2,1)} %y_ref.1, bf16[96,2560]{1,0:T(8,128)(2,1)} %w_ref.1, ...), custom_call_target="tpu_custom_call" | custom-call | tf_op jit(solution)/shard_map/start/pallas_call | solution.py:431
  59.7 0.0 all-gather.3.cloned.1.call-update
  59.7 0.0 all-gather.5.cloned.1.call-start
  59.7 1.2 slice_convert_fusion
  60.9 0.3 copy.47
  61.2 1.0 constant_dynamic-slice_fusion
  62.2 0.7 pad.7.d_ref
  62.9 0.6 fusion.22
  63.5 72.5 %attend.1 = (bf16[8,576,64]{2,1,0:T(8,128)(2,1)}, bf16[3072,64]{1,0:T(8,128)(2,1)}, bf16[3072,128]{1,0:T(8,128)(2,1)}, bf16[3072,1536]{1,0:T(8,128)(2,1)}, bf16[...) custom-call(bf16[3072,1536]{1,0:T(8,128)(2,1)} %bitcast.40, ...), custom_call_target="tpu_custom_call" | custom-call | tf_op jit(solution)/shard_map/attend/pallas_call | solution.py:1290
  136.0 17.3 %attended_home.1.a_ref = bf16[8,192,192]{2,1,0:T(8,128)(2,1)} custom-call(bf16[8,192,192]{2,1,0:T(8,128)(2,1)} %get-tuple-element.70.refs_0_.a_ref), custom_call_target="tpu_custom_call" | custom-call | tf_op jit(solution)/shard_map/attended_home/pallas_call | solution.py:622
  153.3 0.0 all-gather.3.cloned.1.call-done.w_ref
  153.3 5.1 %mix.1 = (f32[192,1536]{1,0:T(8,128)}, bf16[192,1536]{1,0:T(8,128)(2,1)}) custom-call(bf16[8,192,192]{2,1,0:T(8,128)(2,1)} %attended_home.1.a_ref, bf16[1536,1536]{1,0:T(8,128)(2,1)} %all-gather.3.cloned.1.call-done.w_ref, bf16[192,1536]{1,0:T(8,128)(2,1)} %x_ref.5, f32[1,1536]{1,0:T(1,128)} %get-tuple-element.124.g_ref.gain_ref), custom_call_target="tpu_custom_call" | custom-call | tf_op jit(solution)/shard_map/mix/pallas_call | solution.py:1658
  158.4 27.3 %second_gather.1 = bf16[8,192,1536]{2,1,0:T(8,128)(2,1)} custom-call(bf16[192,1536]{1,0:T(8,128)(2,1)} %get-tuple-element.73.x_ref), custom_call_target="tpu_custom_call" | custom-call | tf_op jit(solution)/shard_map/second_gather/pallas_call | solution.py:483
  185.7 0.0 all-gather.5.cloned.1.call-update
  185.7 2.9 slice.24
  188.7 0.7 fusion.10.e_ref
  189.4 43.3 %experts.1 = (bf16[1536,1536]{1,0:T(8,128)(2,1)}, bf16[1536,1536]{1,0:T(8,128)(2,1)}, bf16[1536,1280]{1,0:T(8,128)(2,1)}, bf16[640,1536]{1,0:T(8,128)(2,1)}) custom-call(bf16[1536,1536]{1,0:T(8,128)(2,1)} %bitcast.39, bf16[1536,1536]{1,0:T(8,128)(2,1)} %bitcast.44, bf16[1536,128]{1,0:T(8,128)(2,1)} %bitcast.59, bf16[1536,1280]{1,0:T(8,128)(2,1)} %bitcast.48, ...), custom_call_target="tpu_custom_call" | custom-call | tf_op jit(solution)/shard_map/experts/pallas_call | solution.py:1609
  232.7 0.0 copy-start
  232.7 62.8 %reduce_rows.1 = (f32[192,1536]{1,0:T(8,128)}, f32[192,1536]{1,0:T(8,128)}, bf16[192,1280]{1,0:T(8,128)(2,1)}, bf16[80,1536]{1,0:T(8,128)(2,1)}) custom-call(bf16[8,192,1536]{2,1,0:T(8,128)(2,1)} %bitcast.46, bf16[8,192,1536]{2,1,0:T(8,128)(2,1)} %bitcast.45, bf16[8,192,1280]{2,1,0:T(8,128)(2,1)} %bitcast.49, bf16[8,80,1536]{2,1,0:T(8,128)(2,1)} %bitcast.54), custom_call_target="tpu_custom_call" | custom-call | tf_op jit(solution)/shard_map/reduce_rows/pallas_call | solution.py:819
  295.5 1.7 pad.8.down_ref
  297.2 0.0 copy-done
  297.2 2.4 add.96
  299.6 36.5 %grads_away.1 = (f32[192,1536]{1,0:T(8,128)}, bf16[16,96,1536]{2,1,0:T(8,128)(2,1)}, bf16[8,192,192]{2,1,0:T(8,128)(2,1)}, bf16[2,96,1280]{2,1,0:T(8,128)(2,1)}, bf16[2,48,1536]{2,1,0:T(8,128)(2,1)}) custom-call(f32[192,1536]{1,0:T(8,128)} %get-tuple-element.87.du_ref, f32[192,1536]{1,0:T(8,128)} %get-tuple-element.72.mixed_ref, bf16[192,1536]{1,0:T(8,128)(2,1)} %y_ref.1, ...), custom_call_target="tpu_custom_call" | custom-call | tf_op jit(solution)/shard_map/grads_away/pallas_call | solution.py:929
  336.1 56.1 %attend_back.1 = (bf16[8,192,192]{2,1,0:T(8,128)(2,1)}, bf16[3072,128]{1,0:T(8,128)(2,1)}, bf16[16,96,320]{2,1,0:T(8,128)(2,1)}, bf16[96,1536]{1,0:T(8,128)(2,1)...) custom-call(bf16[8,576,64]{2,1,0:T(8,128)(2,1)} %get-tuple-element.84.q_ref, ...), custom_call_target="tpu_custom_call" | custom-call | tf_op jit(solution)/shard_map/attend_back/pallas_call | solution.py:1517
  392.2 1.3 slice.27
  393.5 0.0 copy-start.1
  393.5 15.5 %adam_lifting.1 = (f32[10,96,1024]{2,1,0:T(8,128)}, f32[10,96,1024]{2,1,0:T(8,128)}, f32[10,96,1024]{2,1,0:T(8,128)}, f32[96,128]{1,0:T(8,128)}) custom-call(bf16[10,96,1024]{2,1,0:T(8,128)(2,1)} %bitcast.43, bf16[10,96,1024]{2,1,0:T(8,128)(2,1)} %bitcast.52, bf16[10,96,1024]{2,1,0:T(8,128)(2,1)} %bitcast.53, bf16[8,96,1280]{2,1,0:T(8,128)(2,1)} %get-tuple-element.105.g_ref, ...), custom_call_target="tpu_custom_call" | custom-call | tf_op jit(solution)/shard_map/adam_lifting/pallas_call | solution.py:1731
  409.0 0.9 slice_reduce_fusion
  409.9 0.0 copy-done.1
  409.9 5.2 %convert_subtract_fusion = (f32[32,10,1536]{2,0,1:T(8,128)}, f32[32,10,1536]{2,0,1:T(8,128)}, f32[32,10,1536]{2,0,1:T(8,128)}) fusion(bf16[32,10,1536]{2,0,1:T(8,128)(2,1)S(1)} %copy-done.1, bf16[10,32,1536]{2,1,0:T(8,128)(2,1)S(1)} %bitcast.47, bf16[32,10,1536]{2,0,1:T(8,128)(2,1)} %param.40, bf16[32,10,1536]{2,0,1:T(8,128)(2,1)} %param.35), kind=kLoop, calls=%fused_computation.1 | loop fusion | flops 9338880 | bytes 9830400 | tf_op jit(solution)/shard_map/sub | solution.py:1695
  415.1 45.3 %tail.1 = (f32[192,1536]{1,0:T(8,128)}, bf16[8,96,320]{2,1,0:T(8,128)(2,1)}, bf16[96,1536]{1,0:T(8,128)(2,1)}) custom-call(bf16[8,192,192]{2,1,0:T(8,128)(2,1)} %get-tuple-element.96.dq_ref, bf16[16,192,128]{2,1,0:T(8,128)(2,1)} %bitcast.57, bf16[16,96,320]{2,1,0:T(8,128)(2,1)} %get-tuple-element.98.in_ref, bf16[96,1536]{1,0:T(8,128)(2,1)} %get-tuple-element.99.out_ref, ...), custom_call_target="tpu_custom_call" | custom-call | tf_op jit(solution)/shard_map/tail/pallas_call | solution.py:1130
  460.5 4.2 adam_inward.1
  464.6 0.9 slice_reduce_fusion.1
  465.5 0.0 copy-start.2
  465.6 0.0 copy-start.3
  465.6 0.0 copy-start.4
  465.6 0.0 copy-start.5
  465.6 3.4 finish.1
  469.0 0.0 copy-done.2
  469.0 0.0 copy-done.3
  469.0 0.0 copy-done.4
  469.0 0.0 copy-done.5
  469.0 1.5 convert_subtract_fusion.1
  470.5 0.0 copy-done.6
  470.6 0.6 convert_subtract_fusion.2
  (7 shorter events, 0.0 us)
Async XLA Ops:
  7.2 146.1 %all-gather.3.cloned.1.call-start = ((), (), s32[]{:S(2)}) async-start(), calls=%async_computation | async-start | bytes 5013504 | tf_op jit(solution)/shard_map/all_gather | solution.py:1839
  59.7 355.5 %all-gather.5.cloned.1.call-start = ((), (), s32[]{:S(2)}) async-start(), calls=%async_computation.1 | async-start | bytes 8355840 | tf_op jit(solution)/shard_map/all_gather | solution.py:1855
  232.7 64.5 %copy-start = (f32[192,1536]{1,0:T(8,128)S(1)}, f32[192,1536]{1,0:T(8,128)}, u32[]{:S(2)}) copy-start(f32[192,1536]{1,0:T(8,128)} %get-tuple-element.72.mixed_ref) | copy-start | bytes 3538948
  393.5 16.4 %copy-start.1 = (bf16[32,10,1536]{2,0,1:T(8,128)(2,1)S(1)}, bf16[32,10,1536]{2,0,1:T(8,128)(2,1)}, u32[]{:S(2)}) copy-start(bf16[32,10,1536]{2,0,1:T(8,128)(2,1)} %param.30) | copy-start | bytes 2949124
  465.5 3.4 copy-start.2
  465.6 3.4 copy-start.3
  465.6 3.4 copy-start.4
  465.6 3.4 copy-start.5
  469.0 1.6 copy-start.6
  469.0 1.6 copy-start.7
  469.0 1.6 copy-start.8
Sparse Core Ops, SparseCore 0:
  59.8 51.3 all-gather.2
  185.8 50.2 all-gather.4

commit v5 on v4

--- a/solution.py
+++ b/solution.py
@@ -166,15 +166,22 @@
     own = pltpu.make_async_copy(x_ref.at[core], o_ref.at[shard], local_sem)
     first, last = pl.ds(0, split), pl.ds(split, x_ref.shape[2] - split)
 
+    mate = rep + 1 - 2 * lax.rem(rep, 2)
+
     def copy(src, dst, slot, chip_to=None):
+        across = slot in (18, 19, 20, 21, 22)
         return pltpu.make_async_remote_copy(
             src_ref=src,
             dst_ref=dst,
             send_sem=send_sem.at[slot],
             recv_sem=recv_sem.at[slot],
-            device_id=(rep, sib if chip_to is None else 2 * chip_to + core),
+            device_id=(mate if across else rep, sib if chip_to is None else 2 * chip_to + core),
             device_id_type=MESH,
         )
+
+    def push_pair(c, columns, slot, across):
+        push(block(c, columns, 0), slot, pair)
+        push(block(c, columns, 1), across, pair)
 
     def other(c):
         return c + 1 - 2 * y
@@ -197,22 +204,23 @@
     def one():
         copy(o_ref.at[sib], o_ref.at[sib], 0).wait_recv()
         own.wait()
-        push(block(chip, first), 1, pair)
+        push_pair(chip, first, 1, 19)
         push(block(chip, last), 10, up)
         push(block(chip, last), 12, down)
         push(block(chip, first), 2, up)
         push(block(chip, first), 6, down)
-        push(block(chip, last), 14, pair)
+        push_pair(chip, last, 14, 20)
 
     def two():
-        arrived(block(pair, first), 1)
+        arrived(block(pair, first, 0), 1)
+        arrived(block(pair, first, 1), 19)
         push(block(pair, first), 3, up)
         push(block(pair, first), 7, down)
         arrived(block(down, last), 10)
-        push(block(down, last), 15, pair)
+        push_pair(down, last, 15, 21)
         push(block(down, last, 0), 11, up)
         arrived(block(up, last), 12)
-        push(block(up, last), 16, pair)
+        push_pair(up, last, 16, 22)
         push(block(up, last, 1), 13, down)
 
     def three():
@@ -234,19 +242,19 @@
         arrived(block(far, first, 1), 8)
         arrived(block(other(far), first, 0), 5)
         arrived(block(other(far), first, 1), 9)
-        arrived(block(pair, last), 14)
-        arrived(block(other(down), last), 15)
-        arrived(block(other(up), last), 16)
+        for c, slot, across in ((pair, 14, 20), (other(down), 15, 21), (other(up), 16, 22)):
+            arrived(block(c, last, 0), slot)
+            arrived(block(c, last, 1), across)
         arrived(block(other(far), last, 0), 17)
         arrived(block(other(far), last, 1), 18)
         copy(x_ref.at[1 - core], o_ref.at[shard], 0).wait_send()
-        for slot in (1, 2, 3, 6, 7):
+        for slot in (2, 3, 6, 7):
             copy(block(chip, first), block(chip, first), slot, pair).wait_send()
-        for slot in (4, 5, 8, 9):
+        for slot in (1, 4, 5, 8, 9, 19):
             copy(block(chip, first, 0), block(chip, first, 0), slot, pair).wait_send()
-        for slot in (10, 12, 14, 15, 16):
+        for slot in (10, 12):
             copy(block(chip, last), block(chip, last), slot, pair).wait_send()
-        for slot in (11, 13, 17, 18):
+        for slot in (11, 13, 14, 15, 16, 17, 18, 20, 21, 22):
             copy(block(chip, last, 0), block(chip, last, 0), slot, pair).wait_send()
 
     return start, one, two, three, finish
@@ -468,376 +476,85 @@
     )
 
 
-def second_kernel(x_ref, o_ref, local_sem, s_x, r_x):
-    rep, shard = place()
-    core = lax.rem(shard, 2)
-    greet(
-        [(rep, shard + 1 - 2 * core), (along_x(rep, 1), shard), (along_x(rep, 3), shard)]
-    )
-    for step in x_gather(x_ref, o_ref, local_sem.at[0], s_x, r_x):
-        step()
-
-
-def second(x, collective):
-    dma = pltpu.SemaphoreType.DMA
-    gathered = pl.pallas_call(
-        second_kernel,
-        out_shape=jax.ShapeDtypeStruct((PEERS,) + x.shape, x.dtype),
-        in_specs=[ANY],
-        out_specs=ANY,
-        scratch_shapes=[dma((1,)), dma((9,)), dma((9,))],
-        compiler_params=params(collective, 62 * 2**20),
-        name="second_gather",
-    )(x)
-    return gathered.reshape(PEERS * OWN, D)
-
-
-def exchange_kernel(kinds, *refs):
-    count = len(kinds)
-    ins, outs = refs[:count], refs[count : 2 * count]
-    local_sem, send_sem, recv_sem = refs[2 * count :]
+def home_kernel(
+    x_ref, half_ref, in_ref, gain_ref,
+    mixed_ref, low_ref, o_ref, w_ref,
+    got, halves, local_sem, s_x, r_x, s_w, r_w,
+):
     rep, shard = place()
     core = lax.rem(shard, 2)
     chip = shard // 2
-    greet([(rep, lax.rem(shard + i, 16)) for i in range(1, 16)])
-    sent, due = [], []
-
-    def mine(device):
-        return lax.rem(lax.rem(device, 2) + lax.rem(device // 2, 2), 2)
-
-    for n, kind in enumerate(kinds):
-        x, o = ins[n], outs[n]
-        if kind == "all":
-            local = pltpu.make_async_copy(x.at[shard], o.at[shard], local_sem.at[n])
-            local.start()
-            due.append(local)
-            for i in range(1, 16):
-                to = lax.rem(shard + i, 16)
-                sent.append(
-                    send(x.at[to], o.at[shard], send_sem.at[n, i], recv_sem.at[n, i], (rep, to))
-                )
-        elif kind == "heads":
-            local = pltpu.make_async_copy(x.at[chip], o.at[shard], local_sem.at[n])
-            local.start()
-            due.append(local)
-            for i in range(1, 16):
-                to = lax.rem(shard + i, 16)
-                sent.append(
-                    send(
-                        x.at[to // 2], o.at[shard], send_sem.at[n, i], recv_sem.at[n, i], (rep, to)
-                    )
-                )
-        elif kind == "home":
-            for i in range(8):
-                c = lax.rem(chip + i, 8)
-                to = 2 * c + lax.rem(c + core, 2)
-                if i == 0:
-                    same = to == shard
-
-                    @pl.when(same)
-                    def _(x=x, o=o, c=c, n=n):
-                        local = pltpu.make_async_copy(x.at[c], o.at[chip], local_sem.at[n])
-                        local.start()
-                        local.wait()
-
-                    @pl.when(jnp.logical_not(same))
-                    def _(x=x, o=o, c=c, n=n, to=to):
-                        copy = send(
-                            x.at[c], o.at[chip], send_sem.at[n, 0], recv_sem.at[n, 0], (rep, to)
-                        )
-                        copy.wait_send()
-
-                else:
-                    sent.append(
-                        send(
-                            x.at[c], o.at[chip], send_sem.at[n, i], recv_sem.at[n, i], (rep, to)
-                        )
-                    )
-        elif kind == "away":
-            for i in range(8):
-                c = lax.rem(chip + i, 8)
-                to = 2 * c + mine(shard)
-                if i == 0:
-                    same = to == shard
-
-                    @pl.when(same)
-                    def _(x=x, o=o, c=c, n=n):
-                        local = pltpu.make_async_copy(x.at[c], o.at[chip], local_sem.at[n])
-                        local.start()
-                        local.wait()
-
-                    @pl.when(jnp.logical_not(same))
-                    def _(x=x, o=o, c=c, n=n, to=to):
-                        copy = send(
-                            x.at[c], o.at[chip], send_sem.at[n, 0], recv_sem.at[n, 0], (rep, to)
-                        )
-                        copy.wait_send()
-
-                else:
-                    sent.append(
-                        send(
-                            x.at[c], o.at[chip], send_sem.at[n, i], recv_sem.at[n, i], (rep, to)
-                        )
-                    )
-
-    def arrived(ref, n, i):
-        pltpu.make_async_remote_copy(
-            src_ref=ref,
-            dst_ref=ref,
-            send_sem=send_sem.at[n, 0],
-            recv_sem=recv_sem.at[n, i],
-            device_id=(rep, lax.rem(shard + 1, 16)),
-            device_id_type=MESH,
-        ).wait_recv()
-
-    for n, kind in enumerate(kinds):
-        o = outs[n]
-        if kind in ("all", "heads"):
-            for i in range(1, 16):
-                arrived(o.at[lax.rem(shard + 16 - i, 16)], n, i)
-        else:
-            away = kind == "away"
-            first = (
-                2 * chip + lax.rem(chip + core, 2) if away else 2 * chip + mine(shard)
+    sib = shard + 1 - 2 * core
+    own_half = pltpu.make_async_copy(half_ref, halves.at[core], local_sem.at[0])
+    own_half.start()
+    holder = lax.rem(core + chip, 2)
+    greet([(rep, 2 * lax.rem(chip + i, 8) + holder) for i in range(1, 8)] + [(rep, sib)])
+    sent = [send(half_ref, halves.at[core], s_w, r_w, (rep, sib))]
+    for i in range(1, 8):
+        c = lax.rem(chip + i, 8)
+        sent.append(
+            send(
+                x_ref.at[c], got.at[chip], s_x.at[i], r_x.at[i], (rep, 2 * c + lax.rem(c + core, 2))
             )
-
-            @pl.when(first != shard)
-            def _(o=o, n=n):
-                arrived(o.at[chip], n, 0)
-
-            for i in range(1, 8):
-                arrived(o.at[lax.rem(chip + 8 - i, 8)], n, i)
+        )
+    same = lax.rem(chip, 2) == 0
+
+    @pl.when(same)
+    def _():
+        copy = pltpu.make_async_copy(x_ref.at[chip], got.at[chip], local_sem.at[1])
+        copy.start()
+        copy.wait()
+
+    @pl.when(jnp.logical_not(same))
+    def _():
+        send(x_ref.at[chip], got.at[chip], s_x.at[0], r_x.at[0], (rep, sib)).wait_send()
+        landed_on(got.at[chip], r_x.at[0], s_x.at[0], (rep, sib))
+
+    own_half.wait()
+    landed_on(halves.at[1 - core], r_w, s_w, (rep, sib))
+    keeps = [pltpu.make_async_copy(halves, w_ref, local_sem.at[2])]
+    keeps[0].start()
+    for i in range(1, 8):
+        landed_on(got.at[lax.rem(chip + 8 - i, 8)], r_x.at[i], s_x.at[0], (rep, sib))
+    keeps.append(pltpu.make_async_copy(got, o_ref, local_sem.at[3]))
+    keeps[1].start()
+    rows = side_by_side(got)
+    mixed = in_ref[...].astype(f32) + jnp.concatenate(
+        [jnp.dot(rows, halves[k], preferred_element_type=f32) for k in range(2)], 1
+    )
+    mixed_ref[...] = mixed
+    low_ref[...] = (mixed * inverse_root(mixed) * gain_ref[...]).astype(bf16)
     for copy in sent:
         copy.wait_send()
-    for copy in due:
-        copy.wait()
-
-
-def exchange(arrays, kinds, collective, name):
-    shapes = []
-    for x, kind in zip(arrays, kinds):
-        lead = 16 if kind in ("all", "heads") else 8
-        shapes.append(jax.ShapeDtypeStruct((lead,) + x.shape[1:], x.dtype))
-    n = len(arrays)
+    for keep in keeps:
+        keep.wait()
+
+
+def home(attended, half, x, gain, collective):
+    dma = pltpu.SemaphoreType.DMA
+    halves = (2, D, D // 2)
     return pl.pallas_call(
-        functools.partial(exchange_kernel, kinds),
-        out_shape=tuple(shapes),
-        in_specs=[ANY] * n,
-        out_specs=(ANY,) * n,
+        home_kernel,
+        out_shape=(
+            jax.ShapeDtypeStruct((OWN, D), f32),
+            jax.ShapeDtypeStruct((OWN, D), bf16),
+            jax.ShapeDtypeStruct(attended.shape, bf16),
+            jax.ShapeDtypeStruct(halves, bf16),
+        ),
+        in_specs=[HBM, HBM, VMEM, VMEM],
+        out_specs=(VMEM, VMEM, ANY, ANY),
         scratch_shapes=[
-            pltpu.SemaphoreType.DMA((n,)),
-            pltpu.SemaphoreType.DMA((n, 16)),
-            pltpu.SemaphoreType.DMA((n, 16)),
+            pltpu.VMEM(attended.shape, bf16),
+            pltpu.VMEM(halves, bf16),
+            dma((4,)),
+            dma((8,)),
+            dma((8,)),
+            dma,
+            dma,
         ],
         compiler_params=params(collective, 62 * 2**20),
-        name=name,
-    )(*arrays)
-
-
-def reduce_kernel(*refs):
-    ins, grads = refs[:2], refs[2:4]
-    outs, grad_outs = refs[4:6], refs[6:8]
-    token_held, token_near, token_land = refs[8:11]
-    scratch = (refs[11:16], refs[16:21])
-    t_load, t_sn, t_rn, t_s, t_r, g_load, s_one, r_one, s_two, r_two = refs[21:]
-    rep, shard = place()
-    core = lax.rem(shard, 2)
-    chip = shard // 2
-    y = lax.rem(chip, 2)
-    z = chip // 2
-    x = rep // 2
-    sib = shard + 1 - 2 * core
-    pair = shard + 2 - 4 * y
-
-    def ahead(dz):
-        return lax.rem(z + dz, 4)
-
-    def device(dz):
-        return (rep, 4 * ahead(dz) + 2 * y + core)
-
-    greet(
-        [(rep, sib), (rep, pair)]
-        + [device(dz) for dz in (1, 2, 3)]
-        + [(along_x(rep, dx), shard) for dx in (1, 2, 3)]
-    )
-    near_copies, loads, token_sends = {}, {}, {}
-    for n in range(2):
-        for dx in (2, 1, 3, 0):
-            to = lax.rem(x + dx, 4)
-            near_copies[n, dx] = send(
-                ins[n].at[2 * to + 1 - core], token_near.at[n, dx], t_sn.at[n, dx], t_rn.at[n, dx],
-                (rep, sib),
-            )
-            loads[n, dx] = pltpu.make_async_copy(
-                ins[n].at[2 * to + core], token_held.at[n, dx], t_load.at[n, dx]
-            )
-            loads[n, dx].start()
-
-    ones, twos, grad_loads = {}, {}, {}
-    for m in range(2):
-        held, land_a, land_b, land_c, land_d = scratch[m]
-        columns = grads[m].shape[2]
-        first, last = pl.ds(0, columns // 2), pl.ds(columns // 2, columns // 2)
-        for j in (3, 5, 7, 1, 4, 2, 6, 0):
-            dz, dy = j // 2, j % 2
-            block = grads[m].at[2 * ahead(dz) + (1 - y if dy else y)]
-            if dy:
-                ones[m, 0, j] = send(
-                    block.at[:, first], land_a.at[dz], s_one.at[m, 0, j], r_one.at[m, 0, j], (rep, pair)
-                )
-            if dz:
-                ones[m, 1, j] = send(
-                    block.at[:, last], land_b.at[j - 2], s_one.at[m, 1, j], r_one.at[m, 1, j], device(dz)
-                )
-            if dy == 0 or dz == 0:
-                slot = dz if dy == 0 else 4
-                grad_loads[m, slot] = pltpu.make_async_copy(block, held.at[slot], g_load.at[m, slot])
-                grad_loads[m, slot].start()
-
-    def rows_of(t, step):
-        return pl.ds(pl.multiple_of(t * step, step), step)
-
-    def token_sums(n):
-        for dx in (2, 1, 3, 0):
-            near_copies[n, dx].wait_recv()
-            loads[n, dx].wait()
-
-            def add(t, _, dx=dx):
-                at = rows_of(t, 32)
-                token_held[n, dx, at] = (
-                    token_held[n, dx, at].astype(f32) + token_near[n, dx, at].astype(f32)
-                ).astype(bf16)
-                return 0
-
-            lax.fori_loop(0, OWN // 32, add, 0)
-            if dx:
-                token_sends[n, dx] = send(
-                    token_held.at[n, dx], token_land.at[n, dx - 1], t_s.at[n, dx], t_r.at[n, dx],
-                    (along_x(rep, dx), shard),
-                )
-
-    def token_result(n):
-        for dx in (1, 2, 3):
-            token_sends[n, dx].wait_recv()
-
-        def add(t, _):
-            at = rows_of(t, 32)
-            total = token_held[n, 0, at].astype(f32)
-            for dx in (1, 2, 3):
-                total = total + token_land[n, dx - 1, at].astype(f32)
-            outs[n][at] = total
-            return 0
-
-        lax.fori_loop(0, OWN // 32, add, 0)
-
-    def first_sums(m):
-        held, land_a, land_b, land_c, land_d = scratch[m]
-        rows, columns = held.shape[1:]
-        first, last = pl.ds(0, columns // 2), pl.ds(columns // 2, columns // 2)
-        for slot in range(5):
-            grad_loads[m, slot].wait()
-        for dz in (2, 1, 3, 0):
-            ones[m, 0, 2 * dz + 1].wait_recv()
-
-            def add(t, _, dz=dz):
-                at = rows_of(t, 16)
-                held[dz, at, first] = (
-                    held[dz, at, first].astype(f32) + land_a[dz, at].astype(f32)
-                ).astype(bf16)
-                return 0
-
-            lax.fori_loop(0, rows // 16, add, 0)
-            if dz:
-                twos[m, dz] = send(
-                    held.at[dz, :, first], land_c.at[dz - 1], s_two.at[m, dz], r_two.at[m, dz], device(dz)
-                )
-        for dy in (1, 0):
-            for dz in (1, 2, 3):
-                ones[m, 1, 2 * dz + dy].wait_recv()
-            slot = 4 if dy else 0
-
-            def add(t, _, dy=dy, slot=slot):
-                at = rows_of(t, 16)
-                total = held[slot, at, last].astype(f32)
-                for dz in (1, 2, 3):
-                    total = total + land_b[2 * dz + dy - 2, at].astype(f32)
-                held[slot, at, last] = total.astype(bf16)
-                return 0
-
-            lax.fori_loop(0, rows // 16, add, 0)
-            if dy:
-                twos[m, 0] = send(
-                    held.at[4, :, last], land_d, s_two.at[m, 0], r_two.at[m, 0], (rep, pair)
-                )
-
-    def last_sums(m):
-        held, land_a, land_b, land_c, land_d = scratch[m]
-        rows, columns = held.shape[1:]
-        first, last = pl.ds(0, columns // 2), pl.ds(columns // 2, columns // 2)
-        for dz in range(4):
-            twos[m, dz].wait_recv()
-
-        def add(t, _):
-            at = rows_of(t, 16)
-            total = held[0, at, first].astype(f32)
-            for dz in (1, 2, 3):
-                total = total + land_c[dz - 1, at].astype(f32)
-            grad_outs[m][at, first] = total.astype(bf16)
-            grad_outs[m][at, last] = (
-                held[0, at, last].astype(f32) + land_d[at].astype(f32)
-            ).astype(bf16)
-            return 0
-
-        lax.fori_loop(0, rows // 16, add, 0)
-
-    token_sums(0)
-    token_sums(1)
-    first_sums(0)
-    token_result(0)
-    first_sums(1)
-    token_result(1)
-    last_sums(0)
-    last_sums(1)
-    for copies in (near_copies, token_sends, ones, twos):
-        for copy in copies.values():
-            copy.wait_send()
-
-
-def reduce_blocks(du, out, lift, down, collective):
-    dma = pltpu.SemaphoreType.DMA
-
-    def slots(rows, columns):
-        half = columns // 2
-        return [
-            pltpu.VMEM((5, rows, columns), bf16),
-            pltpu.VMEM((4, rows, half), bf16),
-            pltpu.VMEM((6, rows, half), bf16),
-            pltpu.VMEM((3, rows, half), bf16),
-            pltpu.VMEM((rows, half), bf16),
-        ]
-
-    return pl.pallas_call(
-        reduce_kernel,
-        out_shape=(
-            jax.ShapeDtypeStruct((OWN, D), f32),
-            jax.ShapeDtypeStruct((OWN, D), f32),
-            jax.ShapeDtypeStruct(lift.shape[1:], bf16),
-            jax.ShapeDtypeStruct(down.shape[1:], bf16),
-        ),
-        in_specs=[ANY] * 4,
-        out_specs=(VMEM,) * 4,
-        scratch_shapes=[
-            pltpu.VMEM((2, 4, OWN, D), bf16),
-            pltpu.VMEM((2, 4, OWN, D), bf16),
-            pltpu.VMEM((2, 3, OWN, D), bf16),
-        ]
-        + slots(*lift.shape[1:])
-        + slots(*down.shape[1:])
-        + [dma((2, 4))] * 5
-        + [dma((2, 5)), dma((2, 2, 8)), dma((2, 2, 8)), dma((2, 4)), dma((2, 4))],
-        compiler_params=params(collective, 62 * 2**20),
-        name="reduce_rows",
-    )(du, out, lift, down)
+        name="attended_home",
+    )(attended, half, x, gain)
 
 
 def away_kernel(
@@ -851,7 +568,10 @@
     chip = shard // 2
     sib = shard + 1 - 2 * core
     mate = rep + 1 - 2 * lax.rem(rep, 2)
-    greet([(rep, lax.rem(shard + i, 16)) for i in range(1, 16)] + [(mate, shard)])
+    greet(
+        [(rep, 2 * c + lax.rem(c + core, 2)) for c in (lax.rem(chip + i, 8) for i in range(1, 8))]
+        + [(rep, sib), (mate, shard)]
+    )
     sent = []
     mates, loads = [], []
     for n, (src, own, land) in enumerate(
@@ -867,7 +587,8 @@
     dz = y_ref[...].astype(f32) + norm_back(du_ref[...] * gain_ref[...], mixed * inverse, inverse)
     dz_ref[...] = dz
     low = dz.astype(bf16)
-    back = contract(low, w_ref[...], ((1,), (1,))).astype(bf16)
+    back = contract(low[:, : D // 2], w_ref[0], ((1,), (1,)))
+    back = (back + contract(low[:, D // 2 :], w_ref[1], ((1,), (1,)))).astype(bf16)
     for c in range(CHIPS):
         x_ref[c] = back[:, c * 192 : (c + 1) * 192]
     for i in range(1, 8):
@@ -1192,14 +913,15 @@
 
 
 def attend_kernel(
-    x_ref, w_ref, g_ref, cos_ref, sin_ref, b_ref, d_ref,
-    q_ref, k_ref, v_ref, u_ref, o_ref, l_ref, bo_ref, do_ref,
-    local_sem, s_sem, r_sem, s_low, r_low,
+    x_ref, w_ref, g_ref, cos_ref, sin_ref, b_ref, d_ref, f_ref,
+    q_ref, k_ref, v_ref, u_ref, o_ref, l_ref, bo_ref, do_ref, fo_ref,
+    local_sem, s_sem, r_sem, s_low, r_low, s_out, r_out,
 ):
     i = pl.program_id(0)
     core = lax.rem(lax.axis_index("shard"), 2)
-    steps = ring_spread(b_ref, bo_ref, 768, local_sem.at[0], s_sem, r_sem)
-    low_steps = ring_spread(d_ref, do_ref, 896, local_sem.at[1], s_low, r_low)
+    steps = ring_spread(b_ref, bo_ref, 256, local_sem.at[0], s_sem, r_sem)
+    low_steps = ring_spread(d_ref, do_ref, 256, local_sem.at[1], s_low, r_low)
+    out_steps = ring_spread(f_ref, fo_ref, 128, local_sem.at[2], s_out, r_out)
 
     @pl.when(i == 0)
     def _():
@@ -1207,30 +929,42 @@
         y = lax.rem(shard // 2, 2)
         greet(
             [(rep, shard + 1 - 2 * core), (rep, shard + 2 - 4 * y)]
+            + [(rep + 1 - 2 * lax.rem(rep, 2), shard + 2 - 4 * y)]
             + [(rep, lax.rem(shard + 4, 16)), (rep, lax.rem(shard + 12, 16))]
         )
+        out_steps[0]()
         steps[0]()
         low_steps[0]()
 
     @pl.when(i == 1)
     def _():
+        out_steps[1]()
         steps[1]()
 
-    @pl.when(i == 6)
+    @pl.when(i == 4)
     def _():
         low_steps[1]()
 
+    @pl.when(i == 9)
+    def _():
+        out_steps[2]()
+
     @pl.when(i == 11)
     def _():
         steps[2]()
 
     @pl.when(i == 13)
     def _():
+        out_steps[3]()
         low_steps[2]()
 
+    @pl.when(i == 14)
+    def _():
+        steps[3]()
+
     @pl.when(i == 15)
     def _():
-        steps[3]()
+        low_steps[3]()
 
     @pl.when(i < BLOCKS)
     def _():
@@ -1242,7 +976,7 @@
 
     @pl.when(i == 2 * BLOCKS - 1)
     def _():
-        low_steps[3]()
+        out_steps[4]()
         steps[4]()
         low_steps[4]()
 
@@ -1282,7 +1016,7 @@
     )
 
 
-def attend(x_all, weight, gain, cos, sin, units, low, collective):
+def attend(x_all, weight, gain, cos, sin, units, low, half, collective):
     dma = pltpu.SemaphoreType.DMA
     whole = lambda i: (0, 0)
     early = lambda i: (jnp.minimum(i, BLOCKS - 1), 0)
@@ -1298,6 +1032,7 @@
             pl.BlockSpec((KEYS, 128), early),
             ANY,
             ANY,
+            ANY,
         ],
         out_specs=(
             pl.BlockSpec((BLOCKS, ROWS, HEAD), lambda i: (0, 0, 0)),
@@ -1306,6 +1041,7 @@
             pl.BlockSpec((KEYS, D), early),
             pl.BlockSpec((1, OWN, GROUP * HEAD), late),
             pl.BlockSpec((1, 8, ROWS), late),
+            ANY,
             ANY,
             ANY,
         ),
@@ -1318,11 +1054,12 @@
             jax.ShapeDtypeStruct((BLOCKS, 8, ROWS), f32),
             jax.ShapeDtypeStruct((SHARDS,) + units.shape[1:], bf16),
             jax.ShapeDtypeStruct((SHARDS,) + low.shape[1:], bf16),
+            jax.ShapeDtypeStruct((SHARDS,) + half.shape[1:], bf16),
         ),
-        scratch_shapes=[dma((2,))] + [dma((19,))] * 4,
+        scratch_shapes=[dma((3,))] + [dma((23,))] * 6,
         compiler_params=params(collective, 62 * 2**20),
         name="attend",
-    )(x_all, weight, gain, cos, sin, units, low)
+    )(x_all, weight, gain, cos, sin, units, low, half)
 
 
 def attend_back_kernel(
@@ -1345,15 +1082,20 @@
     def copy_same(n, src, dst):
         return pltpu.make_async_copy(src, dst.at[pl.ds(2 * x, 2)], local_sem.at[n])
 
-    def copy_x(n, src, dst, dx, at):
+    x_up, x_down, x_far = (lax.rem(x + d, 4) for d in (1, 3, 2))
+
+    def copy_x(n, src, dst, way):
         return pltpu.make_async_remote_copy(
             src_ref=src,
-            dst_ref=dst.at[pl.ds(2 * at, 2)],
-            send_sem=s_sem.at[n, dx],
-            recv_sem=r_sem.at[n, dx],
-            device_id=(along_x(rep, dx), shard),
+            dst_ref=dst,
+            send_sem=s_sem.at[n, way],
+            recv_sem=r_sem.at[n, way],
+            device_id=(along_x(rep, 3 if way % 2 else 1), shard),
             device_id_type=MESH,
         )
+
+    def two_of(dst, at):
+        return dst.at[pl.ds(2 * at, 2)]
 
     def copy_near(j):
         return pltpu.make_async_remote_copy(
@@ -1385,19 +1127,31 @@
         greet(
             [(rep, sib)]
             + [(rep, 2 * lax.rem(chip + n, 8) + core) for n in range(1, 8)]
-            + [(along_x(rep, dx), shard) for dx in (1, 2, 3)]
+            + [(along_x(rep, dx), shard) for dx in (1, 3)]
         )
         for j in range(8):
             copy_near(j).start()
             copy_own(j).start()
         for n, src, dst in kept:
             copy_same(n, src, dst).start()
-            for dx in (1, 2, 3):
-                copy_x(n, src, dst, dx, x).start()
+            copy_x(n, src, two_of(dst, x), 0).start()
+            copy_x(n, src, two_of(dst, x), 1).start()
         pltpu.make_async_copy(u_hbm, u_ref, u_sem).start()
         total_q[...] = jnp.zeros_like(total_q)
         dk[...] = jnp.zeros_like(dk)
         dv[...] = jnp.zeros_like(dv)
+
+    @pl.when(i == 6)
+    def _():
+        for n, src, dst in kept:
+            ref = two_of(dst, x_down)
+            copy_x(n, ref, ref, 0).wait_recv()
+            ref = dst.at[2 * x_down]
+            copy_x(n, ref, ref, 2).start()
+            ref = two_of(dst, x_up)
+            copy_x(n, ref, ref, 1).wait_recv()
+            ref = dst.at[2 * x_up + 1]
+            copy_x(n, ref, ref, 3).start()
 
     @pl.when(i == 3)
     def _():
@@ -1442,13 +1196,23 @@
         slope = (prob * (back - delta)).astype(bf16)
         dv[at, :] += jnp.dot(prob.astype(bf16), grad, preferred_element_type=f32)
         dk[at, :] += jnp.dot(slope, q, preferred_element_type=f32)
-        dq[...] += contract(slope, keys, ((0,), (0,)))
+        dq[...] += contract(keys, slope, ((0,), (0,)))
         return 0
 
-    lax.fori_loop(0, i, step, 0)
+    def two_steps(c, _):
+        step(2 * c, 0)
+        return step(2 * c + 1, 0)
+
+    lax.fori_loop(0, i // 2, two_steps, 0)
+
+    @pl.when(lax.rem(i, 2) == 1)
+    def _():
+        step(i - 1, 0)
+
     step(i, 0, True)
+    turned = dq[...].T
     wide = jnp.concatenate(
-        [dq[r * OWN : (r + 1) * OWN, :] for r in range(GROUP)] + [jnp.zeros((OWN, HEAD), f32)], 1
+        [turned[r * OWN : (r + 1) * OWN, :] for r in range(GROUP)] + [jnp.zeros((OWN, HEAD), f32)], 1
     )
     wide = wide * (HEAD**-0.5)
     cos, sin = qcos_ref[...], qsin_ref[...]
@@ -1498,10 +1262,12 @@
         lax.fori_loop(0, 3, add, 0)
         for n, src, dst in kept:
             copy_same(n, src, dst).wait()
-            for dx in (1, 2, 3):
-                copy_x(n, src, dst, dx, lax.rem(x + 4 - dx, 4)).wait_recv()
-            for dx in (1, 2, 3):
-                copy_x(n, src, dst, dx, x).wait_send()
+            for k in range(2):
+                ref = dst.at[2 * x_far + k]
+                copy_x(n, ref, ref, 2 + k).wait_recv()
+            for way in range(4):
+                ref = two_of(dst, x) if way < 2 else dst.at[2 * x]
+                copy_x(n, ref, ref, way).wait_send()
         for j in range(8):
             copy_near(j).wait_send()
             if j:
@@ -1554,7 +1320,7 @@
             pltpu.SemaphoreType.DMA,
             pltpu.VMEM((SEQ, HEAD), f32),
             pltpu.VMEM((SEQ, HEAD), f32),
-            pltpu.VMEM((ROWS, HEAD), f32),
+            pltpu.VMEM((HEAD, ROWS), f32),
             pltpu.VMEM((GROUP * HEAD, D), f32),
             pltpu.VMEM((8,) + part.shape[1:], bf16),
             pltpu.VMEM((8,) + part.shape[1:], bf16),
@@ -1569,70 +1335,382 @@
     )(q, k, v, grad, attended, lse, cos, sin, cos, sin, u_all, part, lift, down)
 
 
+def distance(i):
+    return jnp.where(i == 0, 0, jnp.where(i == 1, 1, jnp.where(i == 2, 3, 2)))
+
+
 def experts_kernel(
-    u_ref, y_ref, c_ref, wl_ref, wd_ref, e_ref, out_ref, du_ref, lift_ref, down_ref, lift, down
+    x_hbm, y_ref, c_ref, wl_hbm, wd_hbm, e_ref,
+    du_o, out_o, lift_o, down_o,
+    u, wl, wd, gl, acc, down, part, near, land, total,
+    la, lb, lc, ld, da, db, dc, dd,
+    l_sem, s_g, r_g, s_near, r_near, s_land, r_land, s_one, r_one, s_two, r_two,
 ):
     i = pl.program_id(0)
-    u, y = u_ref[...], y_ref[...]
-    lifted = jnp.dot(u, wl_ref[...], preferred_element_type=f32)
-    back = contract(y, wd_ref[...], ((1,), (1,)))
-    share = jnp.dot(c_ref[...], e_ref[...], preferred_element_type=f32)
-    gate, raised = lifted[:, :HID], lifted[:, HID:]
-    s = jax.nn.sigmoid(gate)
-    swish = gate * s
-    act = (share * swish * raised).astype(bf16)
-    back = back * share
-    grad_gate = back * raised * s * (1.0 + gate * (1.0 - s))
-    grad_lift = jnp.concatenate([grad_gate, back * swish], 1).astype(bf16)
-    out_ref[...] = jnp.dot(act, wd_ref[...], preferred_element_type=f32).astype(bf16)
-    du_ref[...] = contract(grad_lift, wl_ref[...], ((1,), (1,))).astype(bf16)
+    rep, shard = place()
+    core = lax.rem(shard, 2)
+    chip = shard // 2
+    y = lax.rem(chip, 2)
+    z = chip // 2
+    x = rep // 2
+    sib = shard + 1 - 2 * core
+    pair = shard + 2 - 4 * y
+
+    def remote(src, dst, s_sem, r_sem, device):
+        return pltpu.make_async_remote_copy(
+            src_ref=src, dst_ref=dst, send_sem=s_sem, recv_sem=r_sem,
+            device_id=device, device_id_type=MESH,
+        )
+
+    def tokens(dx, k, low=0, size=OWN):
+        return u.at[lax.rem(x + dx, 4), pl.ds(pl.multiple_of(OWN * k + low, 96), size)]
+
+    half = OWN // 2
+    ups, downs, sibs = (along_x(rep, 1), shard), (along_x(rep, 3), shard), (rep, sib)
+    slots = {
+        0: (tokens(3, core), None, ups),
+        1: (tokens(1, core), None, downs),
+        2: (tokens(2, core, 0, half), tokens(3, core, 0, half), ups),
+        3: (tokens(2, core, half, half), tokens(1, core, half, half), downs),
+        4: (tokens(0, 1 - core), None, sibs),
+        5: (tokens(3, 1 - core), tokens(3, core), sibs),
+        6: (tokens(1, 1 - core), tokens(1, core), sibs),
+        7: (tokens(2, 1 - core, 0, half), tokens(2, core, 0, half), sibs),
+        8: (tokens(2, 1 - core, half, half), tokens(2, core, half, half), sibs),
+    }
+
+    def gather_send(n):
+        _, out, device = slots[n]
+        src, dst = (x_hbm, tokens(0, core)) if out is None else (out, out)
+        return remote(src, dst, s_g.at[n], r_g.at[n], device)
+
+    def gather_arrival(n):
+        ref = slots[n][0]
+        remote(ref, ref, s_g.at[n], r_g.at[n], sibs).wait_recv()
+
+    own_tokens = pltpu.make_async_copy(x_hbm, tokens(0, core), l_sem.at[0])
+    fetch_wl = pltpu.make_async_copy(wl_hbm, wl, l_sem.at[1])
+    fetch_wd = pltpu.make_async_copy(wd_hbm, wd, l_sem.at[2])
+
+    def rows(k):
+        return pl.ds(pl.multiple_of(OWN * k, OWN), OWN)
+
+    def near_copy(n, t):
+        return remote(
+            part.at[t, n, rows(1 - core)], near.at[t, n], s_near.at[t, n], r_near.at[t, n], sibs
+        )
+
+    def land_copy(n, t):
+        return remote(
+            part.at[t, n, rows(core)], land.at[t - 1, n], s_land.at[t, n], r_land.at[t, n],
+            (along_x(rep, distance(t)), shard),
+        )
+
+    def pass_on(t):
+        for n in range(2):
+            near_copy(n, t).wait_recv()
+
+            def add(r, _, n=n):
+                at = pl.ds(pl.multiple_of(r * 32, 32), 32)
+                mine = pl.ds(pl.multiple_of(OWN * core + r * 32, 32), 32)
+                part[t, n, mine] = (
+                    part[t, n, mine].astype(f32) + near[t, n, at].astype(f32)
+                ).astype(bf16)
+                return 0
+
+            lax.fori_loop(0, OWN // 32, add, 0)
+
+            @pl.when(t > 0)
+            def _(n=n):
+                land_copy(n, t).start()
+
+    grads = ((wl, la, lb, lc, ld, lift_o, 192), (wd, da, db, dc, dd, down_o, 2 * FLAT))
+
+    def piece(m, dz, dy, columns):
+        buffer, size = grads[m][0], grads[m][6]
+        c = 2 * lax.rem(z + dz, 4) + (1 - y if dy else y)
+        return buffer.at[pl.ds(pl.multiple_of(size * c, size), size), columns]
+
+    def columns_of(m):
+        width = grads[m][0].shape[1] // 2
+        return pl.ds(0, width), pl.ds(width, width)
+
+    def to_z(dz):
+        return (rep, 4 * lax.rem(z + dz, 4) + 2 * y + core)
+
+    def one_a(m, dz):
+        return remote(
+            piece(m, dz, 1, columns_of(m)[0]), grads[m][1].at[dz], s_one.at[m, 0, dz], r_one.at[m, 0, dz],
+            (rep, pair),
+        )
+
+    def one_b(m, dz, dy):
+        j = 2 * dz + dy
+        return remote(
+            piece(m, dz, dy, columns_of(m)[1]), grads[m][2].at[j - 2], s_one.at[m, 1, j], r_one.at[m, 1, j],
+            to_z(dz),
+        )
+
+    def two_a(m, dz):
+        return remote(
+            piece(m, dz, 0, columns_of(m)[0]), grads[m][3].at[dz - 1], s_two.at[m, dz], r_two.at[m, dz],
+            to_z(dz),
+        )
+
+    def two_b(m):
+        return remote(
+            piece(m, 0, 1, columns_of(m)[1]), grads[m][4], s_two.at[m, 0], r_two.at[m, 0], (rep, pair)
+        )
+
+    def first_sums(m):
+        land_a, land_b, size = grads[m][1], grads[m][2], grads[m][6]
+        first, last = columns_of(m)
+        for dz in (2, 1, 3, 0):
+            one_a(m, dz).wait_recv()
+            mine = piece(m, dz, 0, first)
+
+            def add(t, _, mine=mine, dz=dz):
+                at = pl.ds(pl.multiple_of(t * 16, 16), 16)
+                mine[at] = (mine[at].astype(f32) + land_a[dz, at].astype(f32)).astype(bf16)
+                return 0
+
+            lax.fori_loop(0, size // 16, add, 0)
+            if dz:
+                two_a(m, dz).start()
+        for dy in (1, 0):
+            for dz in (1, 2, 3):
+                one_b(m, dz, dy).wait_recv()
+            mine = piece(m, 0, dy, last)
+
+            def add(t, _, mine=mine, dy=dy):
+                at = pl.ds(pl.multiple_of(t * 16, 16), 16)
+                value = mine[at].astype(f32)
+                for dz in (1, 2, 3):
+                    value = value + land_b[2 * dz + dy - 2, at].astype(f32)
+                mine[at] = value.astype(bf16)
+                return 0
+
+            lax.fori_loop(0, size // 16, add, 0)
+            if dy:
+                two_b(m).start()
+
+    def last_sums(m):
+        land_c, land_d, out, size = grads[m][3], grads[m][4], grads[m][5], grads[m][6]
+        first, last = columns_of(m)
+        for dz in (1, 2, 3):
+            two_a(m, dz).wait_recv()
+        two_b(m).wait_recv()
+        mine_a, mine_b = piece(m, 0, 0, first), piece(m, 0, 0, last)
+
+        def add(t, _):
+            at = pl.ds(pl.multiple_of(t * 16, 16), 16)
+            value = mine_a[at].astype(f32)
+            for dz in (1, 2, 3):
+                value = value + land_c[dz - 1, at].astype(f32)
+            out[at, first] = value.astype(bf16)
+            out[at, last] = (mine_b[at].astype(f32) + land_d[at].astype(f32)).astype(bf16)
+            return 0
+
+        lax.fori_loop(0, size // 16, add, 0)
 
     @pl.when(i == 0)
     def _():
-        lift[...] = jnp.zeros_like(lift)
+        fetch_wl.start()
+        fetch_wd.start()
+        own_tokens.start()
+        greet(
+            [(rep, sib), (rep, pair)]
+            + [to_z(dz) for dz in (1, 2, 3)]
+            + [(along_x(rep, dx), shard) for dx in (1, 2, 3)]
+        )
+        for n in (4, 0, 1):
+            gather_send(n).start()
         down[...] = jnp.zeros_like(down)
-
-    lift[...] += contract(u, grad_lift, ((0,), (0,)))
-    down[...] += contract(act, y, ((0,), (0,)))
-
-    @pl.when(i == pl.num_programs(0) - 1)
-    def _():
-        lift_ref[...] = lift[...].astype(bf16)
-        down_ref[...] = down[...].astype(bf16)
-
-
-def experts(u_all, y_all, shares, wl, wd, spread):
-    step = 384
-    rows = lambda i: (i, 0)
+        fetch_wl.wait()
+        fetch_wd.wait()
+        own_tokens.wait()
+        gather_arrival(4)
+
+    @pl.when(i == 1)
+    def _():
+        gather_arrival(1)
+        gather_send(6).start()
+        gather_send(3).start()
+        gather_arrival(0)
+        gather_send(5).start()
+        gather_send(2).start()
+        gather_arrival(6)
+
+    @pl.when(i == 2)
+    def _():
+        gather_arrival(2)
+        gather_send(7).start()
+        gather_arrival(3)
+        gather_send(8).start()
+        gather_arrival(5)
+
+    @pl.when(i == 3)
+    def _():
+        gather_arrival(7)
+        gather_arrival(8)
+
+    @pl.when(i > 0)
+    def _():
+        pass_on(i - 1)
+
+    @pl.when(i < 4)
+    def _():
+        h, dy = u[lax.rem(x + distance(i), 4)], y_ref[...]
+        lifted = jnp.dot(h, wl[...], preferred_element_type=f32)
+        back = contract(dy, wd[...], ((1,), (1,)))
+        share = jnp.dot(c_ref[...], e_ref[...], preferred_element_type=f32)
+        gate, raised = lifted[:, :HID], lifted[:, HID:]
+        s = jax.nn.sigmoid(gate)
+        swish = gate * s
+        act = (share * swish * raised).astype(bf16)
+        back = back * share
+        grad_gate = back * raised * s * (1.0 + gate * (1.0 - s))
+        gl[i] = jnp.concatenate([grad_gate, back * swish], 1).astype(bf16)
+        part[i, 0] = contract(gl[i], wl[...], ((1,), (1,))).astype(bf16)
+        near_copy(0, i).start()
+        part[i, 1] = jnp.dot(act, wd[...], preferred_element_type=f32).astype(bf16)
+        near_copy(1, i).start()
+        down[...] += contract(act, dy, ((0,), (0,)))
+
+    @pl.when(i == 4)
+    def _():
+        wd[...] = down[...].astype(bf16)
+        for dz in (2, 1, 3, 0):
+            one_a(1, dz).start()
+            if dz:
+                one_b(1, dz, 1).start()
+                one_b(1, dz, 0).start()
+        for part_of_lift in range(2):
+            columns = slice(HID * part_of_lift, HID * (part_of_lift + 1))
+            for t in range(4):
+                dx = (0, 1, 3, 2)[t]
+                term = contract(u[lax.rem(x + dx, 4)], gl[t][:, columns], ((0,), (0,)))
+                if t == 0:
+                    acc[...] = term
+                elif t < 3:
+                    acc[...] += term
+                else:
+                    wl[:, columns] = (acc[...] + term).astype(bf16)
+            if part_of_lift == 0:
+                for dz in (2, 1, 3, 0):
+                    one_a(0, dz).start()
+            else:
+                for dz in (2, 1, 3):
+                    one_b(0, dz, 1).start()
+                    one_b(0, dz, 0).start()
+        first_sums(1)
+        for n, out in ((0, du_o), (1, out_o)):
+            for t in (1, 2, 3):
+                land_copy(n, t).wait_recv()
+
+            def add(r, _, n=n):
+                at = pl.ds(pl.multiple_of(r * 32, 32), 32)
+                mine = pl.ds(pl.multiple_of(OWN * core + r * 32, 32), 32)
+                value = part[0, n, mine].astype(f32)
+                for t in range(3):
+                    value = value + land[t, n, at].astype(f32)
+                total[n, at] = value
+                return 0
+
+            lax.fori_loop(0, OWN // 32, add, 0)
+            pltpu.make_async_copy(total.at[n], out, l_sem.at[3 + n]).start()
+        first_sums(0)
+        last_sums(1)
+        last_sums(0)
+        for n, out in ((0, du_o), (1, out_o)):
+            pltpu.make_async_copy(total.at[n], out, l_sem.at[3 + n]).wait()
+        for n in range(9):
+            gather_send(n).wait_send()
+        for n in range(2):
+            for t in range(4):
+                near_copy(n, t).wait_send()
+                if t:
+                    land_copy(n, t).wait_send()
+        for m in range(2):
+            for dz in range(4):
+                one_a(m, dz).wait_send()
+                if dz:
+                    one_b(m, dz, 0).wait_send()
+                    one_b(m, dz, 1).wait_send()
+                    two_a(m, dz).wait_send()
+            two_b(m).wait_send()
+
+
+def experts(h, y_all, shares, wl, wd, table, collective):
+    dma = pltpu.SemaphoreType.DMA
+
+    def chip_at(i):
+        return (lax.rem(lax.axis_index("rep") // 2 + distance(jnp.minimum(i, 3)), 4), 0)
+
     whole = lambda i: (0, 0)
     once = pl.Buffered(1)
+
+    def slots(size, width):
+        return [
+            pltpu.VMEM((4, size, width // 2), bf16),
+            pltpu.VMEM((6, size, width // 2), bf16),
+            pltpu.VMEM((3, size, width // 2), bf16),
+            pltpu.VMEM((size, width // 2), bf16),
+        ]
+
     return pl.pallas_call(
         experts_kernel,
-        grid=(PEERS * OWN // step,),
+        grid=(5,),
         in_specs=[
-            pl.BlockSpec((step, D), rows),
-            pl.BlockSpec((step, D), rows),
-            pl.BlockSpec((step, 128), rows),
-            pl.BlockSpec((D, EXP), whole, pipeline_mode=once),
-            pl.BlockSpec((HID, D), whole, pipeline_mode=once),
+            HBM,
+            pl.BlockSpec((2 * OWN, D), chip_at),
+            pl.BlockSpec((2 * OWN, 128), chip_at),
+            HBM,
+            HBM,
             pl.BlockSpec((128, HID), whole, pipeline_mode=once),
         ],
         out_specs=(
-            pl.BlockSpec((step, D), rows),
-            pl.BlockSpec((step, D), rows),
-            pl.BlockSpec((D, EXP), whole),
-            pl.BlockSpec((HID, D), whole),
+            ANY,
+            ANY,
+            pl.BlockSpec((192, EXP), whole),
+            pl.BlockSpec((2 * FLAT, D), whole),
         ),
         out_shape=(
-            jax.ShapeDtypeStruct((PEERS * OWN, D), bf16),
-            jax.ShapeDtypeStruct((PEERS * OWN, D), bf16),
-            jax.ShapeDtypeStruct((D, EXP), bf16),
-            jax.ShapeDtypeStruct((HID, D), bf16),
+            jax.ShapeDtypeStruct((OWN, D), f32),
+            jax.ShapeDtypeStruct((OWN, D), f32),
+            jax.ShapeDtypeStruct((192, EXP), bf16),
+            jax.ShapeDtypeStruct((2 * FLAT, D), bf16),
         ),
-        scratch_shapes=[pltpu.VMEM((D, EXP), f32), pltpu.VMEM((HID, D), f32)],
-        compiler_params=pltpu.CompilerParams(vmem_limit_bytes=62 * 2**20),
+        scratch_shapes=[
+            pltpu.VMEM((4, 2 * OWN, D), bf16),
+            pltpu.VMEM((D, EXP), bf16),
+            pltpu.VMEM((HID, D), bf16),
+            pltpu.VMEM((4, 2 * OWN, EXP), bf16),
+            pltpu.VMEM((D, HID), f32),
+            pltpu.VMEM((HID, D), f32),
+            pltpu.VMEM((4, 2, 2 * OWN, D), bf16),
+            pltpu.VMEM((4, 2, OWN, D), bf16),
+            pltpu.VMEM((3, 2, OWN, D), bf16),
+            pltpu.VMEM((2, OWN, D), f32),
+        ]
+        + slots(192, EXP)
+        + slots(2 * FLAT, D)
+        + [
+            dma((5,)),
+            dma((9,)),
+            dma((9,)),
+            dma((4, 2)),
+            dma((4, 2)),
+            dma((4, 2)),
+            dma((4, 2)),
+            dma((2, 2, 8)),
+            dma((2, 2, 8)),
+            dma((2, 4)),
+            dma((2, 4)),
+        ],
+        compiler_params=params(collective, 63 * 2**20),
         name="experts",
-    )(u_all, y_all, shares, wl, wd, spread)
+    )(h, y_all, shares, wl, wd, table)
 
 
 def choose_units(w_ref, code_ref, out_ref):
@@ -1667,14 +1745,6 @@
 
 def side_by_side(ref):
     return jnp.concatenate([ref[c] for c in range(CHIPS)], 1)
-
-
-def mix_kernel(a_ref, w_ref, x_ref, g_ref, mixed_ref, low_ref):
-    mixed = x_ref[...].astype(f32) + jnp.dot(
-        side_by_side(a_ref), w_ref[...], preferred_element_type=f32
-    )
-    mixed_ref[...] = mixed
-    low_ref[...] = (mixed * inverse_root(mixed) * g_ref[...]).astype(bf16)
 
 
 def finish_kernel(dh_ref, dz_ref, x_ref, g_ref, out_ref):
@@ -1835,34 +1905,20 @@
     head_weight = head_weight.reshape(D, 384)
     gain_rows = head_weight[:, 192:194].T.astype(f32)
     gain_one, gain_two = gain_rows[0:1], gain_rows[1:2]
-    late_outward, x_all = lax.optimization_barrier((outward, x_all))
-    outward_all = lax.all_gather(late_outward, "shard", axis=0, tiled=True)
-
-    q, k, v, u_one, attended, lse, unit_weight, down_weight = attend(
-        x_all, head_weight, gain_one, cos, sin, by_unit, low_rows, 1
+    by_half = outward.reshape(96, 2, D // 2).transpose(1, 0, 2)
+
+    q, k, v, u_one, attended, lse, unit_weight, down_weight, half = attend(
+        x_all, head_weight, gain_one, cos, sin, by_unit, low_rows, by_half, 1
     )
     unit_weight = unit_weight.reshape(D, EXP)
-    (own_attended,) = exchange((attended,), ("home",), 3, "attended_home")
-    mixed, low_two = one_step(
-        mix_kernel,
-        (own_attended, outward_all, layer_input, gain_two),
-        (((OWN, D), f32), ((OWN, D), bf16)),
-        "mix",
-    )
-    u_two = second(low_two, 4)
+    mixed, low_two, own_attended, outward_all = home(
+        attended, half.reshape(D, D // 2), layer_input, gain_two, 3
+    )
+    late_inward, low_two = lax.optimization_barrier((inward, low_two))
+    inward_all = lax.all_gather(late_inward, "shard", axis=0, tiled=True)
     down_weight = down_weight[:, :FLAT].reshape(HID, D)
-    late_inward, u_two = lax.optimization_barrier((inward, u_two))
-    inward_all = lax.all_gather(late_inward, "shard", axis=0, tiled=True)
-
-    out_part, du_part, lift_part, down_part = experts(
-        u_two, y_all, shares, unit_weight, down_weight, share_table
-    )
-    du, expert_out, lift_sum, down_sum = reduce_blocks(
-        du_part.reshape(PEERS, OWN, D),
-        out_part.reshape(PEERS, OWN, D),
-        lift_part.reshape(CHIPS, 192, EXP),
-        down_part.reshape(CHIPS, 2 * FLAT, D),
-        5,
+    du, expert_out, lift_sum, down_sum = experts(
+        low_two, y_all, shares, unit_weight, down_weight, share_table, 5
     )
     layer_output = mixed + expert_out
     down_sum = jnp.pad(down_sum.reshape(2, FLAT, D), ((0, 0), (0, FLAT_PAD - FLAT), (0, 0)))

time: 479 us -> 438 us (0.914); the launches traced: 478 us -> 431 us
  Pallas kernels: 439 us -> 391 us
    pallas_call x4 -> x2, Pallas kernels: 151 us -> 115 us  [the longest x1 96.5 us: experts(): pl.pallas_call(experts_kernel, grid=(5,), in_specs=[HBM, pl.BlockSpec((2...]
    pallas_call x1, Pallas kernels: 72.5 us -> 63 us  [attend(): pl.pallas_call(attend_kernel, grid=(2 * BLOCKS,), in_specs=[pl.BlockSpec(...]
    pallas_call x2 -> x1, Pallas kernels: 8.43 us -> 3.37 us  [one_step(): pl.pallas_call(kernel, in_specs=[VMEM] * len(arrays), out_specs=(VMEM,) *...]
  transfers between devices with their start and end apart: 2 -> 1, of which waited for: 0 -> 0; matrix products, arithmetic and copies ran while one was open for 4% -> 4% of each run, Pallas kernels for 64% -> 48%
where the time goes in v5:
time: 438 us; the launch traced here: 431 us
  Pallas kernels  391 us (89%)
  between operations  14.7 us (3%)
  local copies, waits for them, and re-layouts  13.3 us (3%)
  other arithmetic  11.8 us (3%)
    pallas_call x1, Pallas kernels, experts(): pl.pallas_call(experts_kernel, grid=(5,), in_specs=[HBM, pl.BlockSpec((2...  96.5 us
    pallas_call x1, Pallas kernels, attend(): pl.pallas_call(attend_kernel, grid=(2 * BLOCKS,), in_specs=[pl.BlockSpec(...  63 us
    pallas_call x1, Pallas kernels, attend_back(): pl.pallas_call(attend_back_kernel, grid=(BLOCKS,), in_specs=[pl.BlockSpec...  57 us
    pallas_call x1, Pallas kernels, start(): pl.pallas_call(start_kernel, out_shape=(jax.ShapeDtypeStruct((SHARDS, row...  49.5 us
    pallas_call x1, Pallas kernels, tail(): pl.pallas_call(tail_kernel, out_shape=(jax.ShapeDtypeStruct((OWN, D), f32...  47.8 us
    pallas_call x1, Pallas kernels, grads_away(): pl.pallas_call(away_kernel, out_shape=(jax.ShapeDtypeStruct((OWN, D), f32...  35.9 us
    pallas_call x1, Pallas kernels, home(): pl.pallas_call(home_kernel, out_shape=(jax.ShapeDtypeStruct((OWN, D), f32...  18.1 us
    pallas_call x1, Pallas kernels, adam_lifting(): pl.pallas_call(adam_lifting_kernel, grid=(EXPERTS,), in_specs=[block, blo...  15.6 us
  transfers between devices with their start and end apart: 1, of which 0 were waited for; matrix products, arithmetic and copies ran while one was open for 4% of the time, Pallas kernels for 48%

profile of v5, /device:TPU:1, one launch (start us, length us, event | category | flops | bytes accessed | tf_op | source)
XLA Modules:
  0.0 430.7 jit_solution(9423375368264489600)
XLA Ops:
  7.2 0.0 all-gather.2.cloned.1.call-start
  7.3 1.5 copy.43.routes_hbm
  8.7 1.5 copy.44.logits_hbm
  10.2 0.0 copy-start.2
  10.2 49.5 %start.1 = (bf16[16,192,1536]{2,1,0:T(8,128)(2,1)}, bf16[16,96,384]{2,1,0:T(8,128)(2,1)}, bf16[8,192,1536]{2,1,0:T(8,128)(2,1)}, bf16[8,192,128]{2,1,0:T(8,128)(2,1)}, bf16[2,96,1280]{2,1,0:T(8,128)(2,1)}) custom-call(bf16[192,1536]{1,0:T(8,128)(2,1)} %x_ref.3, bf16[192,1536]{1,0:T(8,128)(2,1)} %y_ref.1, bf16[96,2560]{1,0:T(8,128)(2,1)} %w_ref.1, ...), custom_call_target="tpu_custom_call" | custom-call | tf_op jit(solution)/shard_map/start/pallas_call | solution.py:439
  59.7 0.0 copy-start.1
  59.7 1.2 slice_convert_fusion
  61.0 0.3 copy.49
  61.2 0.6 fusion.22
  61.8 0.0 copy-done.2
  61.8 0.7 copy.51
  62.6 0.0 copy-done.1
  62.6 0.7 pad.7.d_ref
  63.3 63.0 %attend.1 = (bf16[8,576,64]{2,1,0:T(8,128)(2,1)}, bf16[3072,64]{1,0:T(8,128)(2,1)}, bf16[3072,128]{1,0:T(8,128)(2,1)}, bf16[3072,1536]{1,0:T(8,128)(2,1)}, bf16[...) custom-call(bf16[3072,1536]{1,0:T(8,128)(2,1)} %bitcast.42, ...), custom_call_target="tpu_custom_call" | custom-call | tf_op jit(solution)/shard_map/attend/pallas_call | solution.py:1024
  126.3 18.1 %attended_home.1 = (f32[192,1536]{1,0:T(8,128)}, bf16[192,1536]{1,0:T(8,128)(2,1)}, bf16[8,192,192]{2,1,0:T(8,128)(2,1)}, bf16[2,1536,768]{2,1,0:T(8,128)(2,1)}) custom-call(bf16[8,192,192]{2,1,0:T(8,128)(2,1)} %get-tuple-element.66.x_ref.a_ref, bf16[1536,768]{1,0:T(8,128)(2,1)} %bitcast.49, bf16[192,1536]{1,0:T(8,128)(2,1)} %x_ref.3, ...), custom_call_target="tpu_custom_call" | custom-call | tf_op jit(solution)/shard_map/attended_home/pallas_call | solution.py:536
  144.4 0.0 all-gather.2.cloned.1.call-update
  144.5 2.9 slice.24
  147.4 0.7 fusion.10.e_ref
  148.1 96.5 %experts.1 = (f32[192,1536]{1,0:T(8,128)}, f32[192,1536]{1,0:T(8,128)}, bf16[192,1280]{1,0:T(8,128)(2,1)}, bf16[80,1536]{1,0:T(8,128)(2,1)}) custom-call(bf16[192,1536]{1,0:T(8,128)(2,1)} %get-tuple-element.70.x_hbm, bf16[1536,1536]{1,0:T(8,128)(2,1)} %bitcast.46, bf16[1536,128]{1,0:T(8,128)(2,1)} %bitcast.60, bf16[1536,1280]{1,0:T(8,128)(2,1)} %bitcast.47, ...), custom_call_target="tpu_custom_call" | custom-call | tf_op jit(solution)/shard_map/experts/pallas_call | solution.py:1661
  244.6 1.7 pad.8.down_ref
  246.3 35.9 %grads_away.1 = (f32[192,1536]{1,0:T(8,128)}, bf16[16,96,1536]{2,1,0:T(8,128)(2,1)}, bf16[8,192,192]{2,1,0:T(8,128)(2,1)}, bf16[2,96,1280]{2,1,0:T(8,128)(2,1)}, bf16[2,48,1536]{2,1,0:T(8,128)(2,1)}) custom-call(f32[192,1536]{1,0:T(8,128)} %get-tuple-element.79.du_ref, f32[192,1536]{1,0:T(8,128)} %get-tuple-element.68.mixed_ref, bf16[192,1536]{1,0:T(8,128)(2,1)} %y_ref.1, ...), custom_call_target="tpu_custom_call" | custom-call | tf_op jit(solution)/shard_map/grads_away/pallas_call | solution.py:650
  282.2 57.0 %attend_back.1 = (bf16[8,192,192]{2,1,0:T(8,128)(2,1)}, bf16[3072,128]{1,0:T(8,128)(2,1)}, bf16[16,96,320]{2,1,0:T(8,128)(2,1)}, bf16[96,1536]{1,0:T(8,128)(2,1)...) custom-call(bf16[8,576,64]{2,1,0:T(8,128)(2,1)} %get-tuple-element.76.q_ref, ...), custom_call_target="tpu_custom_call" | custom-call | tf_op jit(solution)/shard_map/attend_back/pallas_call | solution.py:1283
  339.1 0.0 copy-start
  339.2 1.4 slice.27
  340.5 0.2 copy-done
  340.7 2.5 add.96
  343.2 15.6 %adam_lifting.1 = (f32[10,96,1024]{2,1,0:T(8,128)}, f32[10,96,1024]{2,1,0:T(8,128)}, f32[10,96,1024]{2,1,0:T(8,128)}, f32[96,128]{1,0:T(8,128)}) custom-call(bf16[10,96,1024]{2,1,0:T(8,128)(2,1)} %bitcast.45, bf16[10,96,1024]{2,1,0:T(8,128)(2,1)} %bitcast.52, bf16[10,96,1024]{2,1,0:T(8,128)(2,1)} %bitcast.53, bf16[8,96,1280]{2,1,0:T(8,128)(2,1)} %get-tuple-element.99.g_ref, ...), custom_call_target="tpu_custom_call" | custom-call | tf_op jit(solution)/shard_map/adam_lifting/pallas_call | solution.py:1801
  358.8 0.9 slice_reduce_fusion
  359.7 5.2 %convert_subtract_fusion = (f32[32,10,1536]{2,0,1:T(8,128)}, f32[32,10,1536]{2,0,1:T(8,128)}, f32[32,10,1536]{2,0,1:T(8,128)}) fusion(bf16[32,10,1536]{2,0,1:T(8,128)(2,1)S(1)} %copy-done.1, bf16[10,32,1536]{2,1,0:T(8,128)(2,1)S(1)} %bitcast.48, bf16[32,10,1536]{2,0,1:T(8,128)(2,1)} %param.40, bf16[32,10,1536]{2,0,1:T(8,128)(2,1)} %param.35), kind=kLoop, calls=%fused_computation.1 | loop fusion | flops 9338880 | bytes 9830400 | tf_op jit(solution)/shard_map/sub | solution.py:1765
  365.0 0.0 all-gather.2.cloned.1.call-done.w_hbm
  365.0 47.8 %tail.1 = (f32[192,1536]{1,0:T(8,128)}, bf16[8,96,320]{2,1,0:T(8,128)(2,1)}, bf16[96,1536]{1,0:T(8,128)(2,1)}) custom-call(bf16[8,192,192]{2,1,0:T(8,128)(2,1)} %get-tuple-element.90.dq_ref, bf16[16,192,128]{2,1,0:T(8,128)(2,1)} %bitcast.58, bf16[16,96,320]{2,1,0:T(8,128)(2,1)} %get-tuple-element.92.in_ref, bf16[96,1536]{1,0:T(8,128)(2,1)} %get-tuple-element.93.out_ref, ...), custom_call_target="tpu_custom_call" | custom-call | tf_op jit(solution)/shard_map/tail/pallas_call | solution.py:851
  412.7 4.2 adam_inward.1
  416.9 0.9 slice_reduce_fusion.1
  417.8 0.0 copy-start.3
  417.8 0.0 copy-start.4
  417.8 0.0 copy-start.5
  417.8 0.0 copy-start.6
  417.8 3.4 finish.1
  421.2 0.0 copy-start.7
  421.2 0.0 copy-done.3
  421.2 0.0 copy-done.4
  421.2 0.0 copy-done.5
  421.3 0.0 copy-done.6
  421.3 1.5 convert_subtract_fusion.1
  422.8 0.0 copy-done.7
  422.8 0.0 copy-done.8
  422.8 0.0 copy-done.9
  422.8 0.6 convert_subtract_fusion.2
  (4 shorter events, 0.0 us)
Async XLA Ops:
  7.2 357.8 %all-gather.2.cloned.1.call-start = ((), (), s32[]{:S(2)}) async-start(), calls=%async_computation | async-start | bytes 8355840 | tf_op jit(solution)/shard_map/all_gather | solution.py:1918
  10.2 51.7 %copy-start.2 = (bf16[96,1536]{1,0:T(8,128)(2,1)S(1)}, bf16[96,1536]{1,0:T(8,128)(2,1)}, u32[]{:S(2)}) copy-start(bf16[96,1536]{1,0:T(8,128)(2,1)} %param.28) | copy-start | bytes 884740
  59.7 2.9 copy-start.1
  339.1 1.6 copy-start
  417.8 3.4 copy-start.3
  417.8 3.4 copy-start.4
  417.8 3.4 copy-start.5
  417.8 3.4 copy-start.6
  421.2 1.6 copy-start.7
  421.2 1.6 copy-start.8
  421.2 1.6 copy-start.9
Sparse Core Ops, SparseCore 0:
  144.6 48.5 all-gather.1

commit v6 on v5

--- a/solution.py
+++ b/solution.py
@@ -164,7 +164,7 @@
     pair = chip + 1 - 2 * y
     up, down, far = (lax.rem(chip + d, 8) for d in (2, 6, 4))
     own = pltpu.make_async_copy(x_ref.at[core], o_ref.at[shard], local_sem)
-    first, last = pl.ds(0, split), pl.ds(split, x_ref.shape[2] - split)
+    first, last = pl.ds(0, split), pl.ds(split, x_ref.shape[1] - split)
 
     mate = rep + 1 - 2 * lax.rem(rep, 2)
 
@@ -179,17 +179,17 @@
             device_id_type=MESH,
         )
 
-    def push_pair(c, columns, slot, across):
-        push(block(c, columns, 0), slot, pair)
-        push(block(c, columns, 1), across, pair)
+    def push_pair(c, rows, slot, across):
+        push(block(c, rows, 0), slot, pair)
+        push(block(c, rows, 1), across, pair)
 
     def other(c):
         return c + 1 - 2 * y
 
-    def block(c, columns, part=None):
+    def block(c, rows, part=None):
         if part is None:
-            return o_ref.at[pl.ds(2 * c, 2), :, columns]
-        return o_ref.at[2 * c + part, :, columns]
+            return o_ref.at[pl.ds(2 * c, 2), rows]
+        return o_ref.at[2 * c + part, rows]
 
     def push(ref, slot, to):
         copy(ref, ref, slot, to).start()
@@ -386,13 +386,14 @@
                 )
             )
     logits = logits_ref[...]
-    gates = jnp.exp(logits - jnp.max(logits, 1, keepdims=True))
-    gates = gates / jnp.sum(gates, 1, keepdims=True)
+    gates = jnp.exp(logits - jnp.max(logits, 0, keepdims=True))
+    gates = gates / jnp.sum(gates, 0, keepdims=True)
+    ones = [
+        jnp.sum(jnp.where(routes_ref[...] == e, gates, 0.0), 0, keepdims=True)
+        for e in range(EXPERTS)
+    ]
+    shares = jnp.concatenate(ones + [jnp.zeros((128 - EXPERTS, OWN), f32)], 0).T
     lane = lax.broadcasted_iota(jnp.int32, (OWN, 128), 1)
-    shares = jnp.zeros((OWN, 128), f32)
-    for e in range(EXPERTS):
-        one = jnp.sum(jnp.where(routes_ref[...] == e, gates, 0.0), 1, keepdims=True)
-        shares = jnp.where(lane == e, one, shares)
     high = shares.astype(bf16)
     rest = pltpu.roll(shares - high.astype(f32), 16, 1)
     share_ref[...] = jnp.where(lane < 16, high, rest.astype(bf16))
@@ -477,9 +478,9 @@
 
 
 def home_kernel(
-    x_ref, half_ref, in_ref, gain_ref,
-    mixed_ref, low_ref, o_ref, w_ref,
-    got, halves, local_sem, s_x, r_x, s_w, r_w,
+    x_ref, half_ref, rows_ref, in_ref, gain_ref,
+    mixed_ref, low_ref, down_ref, o_ref, w_ref,
+    got, halves, apart, local_sem, s_x, r_x, s_w, r_w,
 ):
     rep, shard = place()
     core = lax.rem(shard, 2)
@@ -487,6 +488,8 @@
     sib = shard + 1 - 2 * core
     own_half = pltpu.make_async_copy(half_ref, halves.at[core], local_sem.at[0])
     own_half.start()
+    fetch = pltpu.make_async_copy(rows_ref, apart, local_sem.at[4])
+    fetch.start()
     holder = lax.rem(core + chip, 2)
     greet([(rep, 2 * lax.rem(chip + i, 8) + holder) for i in range(1, 8)] + [(rep, sib)])
     sent = [send(half_ref, halves.at[core], s_w, r_w, (rep, sib))]
@@ -510,6 +513,8 @@
         send(x_ref.at[chip], got.at[chip], s_x.at[0], r_x.at[0], (rep, sib)).wait_send()
         landed_on(got.at[chip], r_x.at[0], s_x.at[0], (rep, sib))
 
+    fetch.wait()
+    down_ref[...] = jnp.concatenate([apart[d][:FLAT] for d in range(SHARDS)], 0)
     own_half.wait()
     landed_on(halves.at[1 - core], r_w, s_w, (rep, sib))
     keeps = [pltpu.make_async_copy(halves, w_ref, local_sem.at[2])]
@@ -530,7 +535,7 @@
         keep.wait()
 
 
-def home(attended, half, x, gain, collective):
+def home(attended, half, rows, x, gain, collective):
     dma = pltpu.SemaphoreType.DMA
     halves = (2, D, D // 2)
     return pl.pallas_call(
@@ -538,15 +543,17 @@
         out_shape=(
             jax.ShapeDtypeStruct((OWN, D), f32),
             jax.ShapeDtypeStruct((OWN, D), bf16),
+            jax.ShapeDtypeStruct((HID, D), bf16),
             jax.ShapeDtypeStruct(attended.shape, bf16),
             jax.ShapeDtypeStruct(halves, bf16),
         ),
-        in_specs=[HBM, HBM, VMEM, VMEM],
-        out_specs=(VMEM, VMEM, ANY, ANY),
+        in_specs=[HBM, HBM, HBM, VMEM, VMEM],
+        out_specs=(VMEM, VMEM, VMEM, ANY, ANY),
         scratch_shapes=[
             pltpu.VMEM(attended.shape, bf16),
             pltpu.VMEM(halves, bf16),
-            dma((4,)),
+            pltpu.VMEM(rows.shape, bf16),
+            dma((5,)),
             dma((8,)),
             dma((8,)),
             dma,
@@ -554,7 +561,7 @@
         ],
         compiler_params=params(collective, 62 * 2**20),
         name="attended_home",
-    )(attended, half, x, gain)
+    )(attended, half, rows, x, gain)
 
 
 def away_kernel(
@@ -919,9 +926,9 @@
 ):
     i = pl.program_id(0)
     core = lax.rem(lax.axis_index("shard"), 2)
-    steps = ring_spread(b_ref, bo_ref, 256, local_sem.at[0], s_sem, r_sem)
-    low_steps = ring_spread(d_ref, do_ref, 256, local_sem.at[1], s_low, r_low)
-    out_steps = ring_spread(f_ref, fo_ref, 128, local_sem.at[2], s_out, r_out)
+    steps = ring_spread(b_ref, bo_ref, 16, local_sem.at[0], s_sem, r_sem)
+    low_steps = ring_spread(d_ref, do_ref, 16, local_sem.at[1], s_low, r_low)
+    out_steps = ring_spread(f_ref, fo_ref, 16, local_sem.at[2], s_out, r_out)
 
     @pl.when(i == 0)
     def _():
@@ -1344,7 +1351,7 @@
     du_o, out_o, lift_o, down_o,
     u, wl, wd, gl, acc, down, part, near, land, total,
     la, lb, lc, ld, da, db, dc, dd,
-    l_sem, s_g, r_g, s_near, r_near, s_land, r_land, s_one, r_one, s_two, r_two,
+    down_sum, l_sem, s_g, r_g, s_near, r_near, s_land, r_land, s_one, r_one, s_two, r_two,
 ):
     i = pl.program_id(0)
     rep, shard = place()
@@ -1424,7 +1431,7 @@
             def _(n=n):
                 land_copy(n, t).start()
 
-    grads = ((wl, la, lb, lc, ld, lift_o, 192), (wd, da, db, dc, dd, down_o, 2 * FLAT))
+    grads = ((wl, la, lb, lc, ld, lift_o, 192), (wd, da, db, dc, dd, down_sum, 2 * FLAT))
 
     def piece(m, dz, dy, columns):
         buffer, size = grads[m][0], grads[m][6]
@@ -1621,6 +1628,14 @@
             pltpu.make_async_copy(total.at[n], out, l_sem.at[3 + n]).start()
         first_sums(0)
         last_sums(1)
+        for k in range(2):
+            down_o[k] = jnp.concatenate(
+                [
+                    down_sum[FLAT * k : FLAT * (k + 1)],
+                    jnp.zeros((FLAT_PAD - FLAT, D), bf16),
+                ],
+                0,
+            )
         last_sums(0)
         for n, out in ((0, du_o), (1, out_o)):
             pltpu.make_async_copy(total.at[n], out, l_sem.at[3 + n]).wait()
@@ -1673,13 +1688,13 @@
             ANY,
             ANY,
             pl.BlockSpec((192, EXP), whole),
-            pl.BlockSpec((2 * FLAT, D), whole),
+            pl.BlockSpec((2, FLAT_PAD, D), lambda i: (0, 0, 0)),
         ),
         out_shape=(
             jax.ShapeDtypeStruct((OWN, D), f32),
             jax.ShapeDtypeStruct((OWN, D), f32),
             jax.ShapeDtypeStruct((192, EXP), bf16),
-            jax.ShapeDtypeStruct((2 * FLAT, D), bf16),
+            jax.ShapeDtypeStruct((2, FLAT_PAD, D), bf16),
         ),
         scratch_shapes=[
             pltpu.VMEM((4, 2 * OWN, D), bf16),
@@ -1696,6 +1711,7 @@
         + slots(192, EXP)
         + slots(2 * FLAT, D)
         + [
+            pltpu.VMEM((2 * FLAT, D), bf16),
             dma((5,)),
             dma((9,)),
             dma((9,)),
@@ -1747,20 +1763,14 @@
     return jnp.concatenate([ref[c] for c in range(CHIPS)], 1)
 
 
-def finish_kernel(dh_ref, dz_ref, x_ref, g_ref, out_ref):
-    stream = x_ref[...].astype(f32)
-    inverse = inverse_root(stream)
-    out_ref[...] = dz_ref[...] + norm_back(dh_ref[...] * g_ref[...], stream * inverse, inverse)
-
-
 def adam(weight, old_mean, square, gradient, step_rate, decay_rate):
     values = weight.astype(f32)
     moment = beta_one * old_mean.astype(f32) + (1.0 - beta_one) * gradient
     variance = beta_two * square.astype(f32) + (1.0 - beta_two) * gradient * gradient
     normed_step = (
         moment
-        / (1.0 - beta_one**STEP)
-        / (jnp.sqrt(variance / (1.0 - beta_two**STEP)) + adam_epsilon)
+        * (1.0 / (1.0 - beta_one**STEP))
+        / (jnp.sqrt(variance * (1.0 / (1.0 - beta_two**STEP))) + adam_epsilon)
     )
     return (moment, variance, values - step_rate * (normed_step + decay_rate * values))
 
@@ -1816,28 +1826,26 @@
     )(weight, mean, square, grad, code)
 
 
-def adam_inward_kernel(w_ref, m_ref, s_ref, g_ref, mo_ref, so_ref, wo_ref, dot_ref):
-    parts = [g_ref[c].astype(f32) for c in range(CHIPS)]
+def last_kernel(
+    dh_ref, dz_ref, x_ref, g_ref, mixed_ref, e_ref, w_ref, m_ref, s_ref, gi_ref, wo_ref, mo_ref, so_ref, go_ref,
+    grad_ref, out_ref, mi_o, si_o, wi_o, dot_ref, mo_o, so_o, wo_o,
+):
+    out_ref[...] = mixed_ref[...] + e_ref[...]
+    stream = x_ref[...].astype(f32)
+    inverse = inverse_root(stream)
+    grad_ref[...] = dz_ref[...] + norm_back(dh_ref[...] * g_ref[...], stream * inverse, inverse)
+    parts = [gi_ref[c].astype(f32) for c in range(CHIPS)]
     grad = jnp.concatenate(
         [p[:, :192] for p in parts] + [p[:, 192:256] for p in parts] + [p[:, 256:] for p in parts], 1
     )
     dot = jnp.sum(w_ref[...].astype(f32) * grad, 1, keepdims=True)
     dot_ref[...] = jnp.broadcast_to(dot, dot_ref.shape)
-    mo_ref[...], so_ref[...], wo_ref[...] = adam(
+    mi_o[...], si_o[...], wi_o[...] = adam(
         w_ref[...], m_ref[...], s_ref[...], grad, rate_inward, weight_decay
     )
-
-
-def adam_inward(weight, mean, square, grad):
-    shape = jax.ShapeDtypeStruct(weight.shape, f32)
-    return pl.pallas_call(
-        adam_inward_kernel,
-        in_specs=[VMEM] * 4,
-        out_specs=(VMEM,) * 4,
-        out_shape=(shape, shape, shape, jax.ShapeDtypeStruct((96, 128), f32)),
-        compiler_params=pltpu.CompilerParams(vmem_limit_bytes=62 * 2**20),
-        name="adam_inward",
-    )(weight, mean, square, grad)
+    mo_o[...], so_o[...], wo_o[...] = adam(
+        wo_ref[...], mo_ref[...], so_ref[...], go_ref[...].astype(f32), rate_outward, weight_decay
+    )
 
 
 def tables():
@@ -1900,28 +1908,25 @@
     share_table = ((row == expert) | (row == expert + 16)).astype(bf16)
 
     x_all, head_weight, y_all, shares, by_unit = start(
-        layer_input, grad_output, inward, norm_gains, routes, route_logits, lifting_rows, codes[None, :], 2
+        layer_input, grad_output, inward, norm_gains, routes.T, route_logits.T, lifting_rows, codes[None, :], 2
     )
     head_weight = head_weight.reshape(D, 384)
     gain_rows = head_weight[:, 192:194].T.astype(f32)
     gain_one, gain_two = gain_rows[0:1], gain_rows[1:2]
     by_half = outward.reshape(96, 2, D // 2).transpose(1, 0, 2)
 
-    q, k, v, u_one, attended, lse, unit_weight, down_weight, half = attend(
+    q, k, v, u_one, attended, lse, unit_weight, down_rows, half = attend(
         x_all, head_weight, gain_one, cos, sin, by_unit, low_rows, by_half, 1
     )
     unit_weight = unit_weight.reshape(D, EXP)
-    mixed, low_two, own_attended, outward_all = home(
-        attended, half.reshape(D, D // 2), layer_input, gain_two, 3
+    mixed, low_two, down_weight, own_attended, outward_all = home(
+        attended, half.reshape(D, D // 2), down_rows, layer_input, gain_two, 3
     )
     late_inward, low_two = lax.optimization_barrier((inward, low_two))
     inward_all = lax.all_gather(late_inward, "shard", axis=0, tiled=True)
-    down_weight = down_weight[:, :FLAT].reshape(HID, D)
     du, expert_out, lift_sum, down_sum = experts(
         low_two, y_all, shares, unit_weight, down_weight, share_table, 5
     )
-    layer_output = mixed + expert_out
-    down_sum = jnp.pad(down_sum.reshape(2, FLAT, D), ((0, 0), (0, FLAT_PAD - FLAT), (0, 0)))
     grad_mixed, outward_part, head_grads, lift_pair, down_pair = grads_away(
         du, mixed, grad_output, gain_two, outward_all, own_attended,
         lift_sum.reshape(2, 96, EXP), down_sum, 6,
@@ -1932,10 +1937,6 @@
     dh, inward_sum, outward_sum = tail(
         dq, dkv.reshape(SHARDS, OWN, 128), inward_part, outward_own, inward_all, 7
     )
-    (input_grad,) = one_step(
-        finish_kernel, (dh, grad_mixed, layer_input, gain_one), (((OWN, D), f32),), "finish"
-    )
-    outward_grad = outward_sum.astype(f32)
     down_grad = (
         down_got[:, :FLAT].reshape(EXPERTS, 32, D).transpose(1, 0, 2).astype(f32)
     )
@@ -1949,12 +1950,20 @@
     )
     lifting_dot = new_lifting[3]
     new_lifting = tuple(t.transpose(1, 0, 2) for t in new_lifting[:3])
-    new_inward = adam_inward(inward, mean_inward, square_inward, inward_sum)
+    last = one_step(
+        last_kernel,
+        (dh, grad_mixed, layer_input, gain_one, mixed, expert_out)
+        + (inward, mean_inward, square_inward, inward_sum)
+        + (outward, mean_outward, square_outward, outward_sum),
+        (((OWN, D), f32),) * 2
+        + ((inward.shape, f32),) * 3
+        + (((96, 128), f32),)
+        + ((outward.shape, f32),) * 3,
+        "last",
+    )
+    input_grad, layer_output, new_inward, new_outward = last[0], last[1], last[2:6], last[6:9]
     gain_grad = jnp.stack([new_inward[3][:, 0], lifting_dot[:, 0]]) / gains
     new_gains = adam(norm_gains, mean_gains, square_gains, gain_grad, rate_gains, 0.0)
-    new_outward = adam(
-        outward, mean_outward, square_outward, outward_grad, rate_outward, weight_decay
-    )
     new_lowering = adam(
         lowering, mean_lowering, square_lowering, down_grad, rate_lowering, weight_decay
     )

time: 438 us -> 425 us (0.970)
  local copies, waits for them, and re-layouts: 13.3 us -> 5.47 us
  transfers between devices with their start and end apart: 1 -> 1, of which waited for: 0 -> 0; matrix products, arithmetic and copies ran while one was open for 4% -> 2% of each run, Pallas kernels for 48% -> 49%
where the time goes in v6:
time: 425 us; the launch traced here: 418 us
  Pallas kernels  390 us (92%)
  between operations  14.7 us (3%)
  other arithmetic  7.81 us (2%)
  local copies, waits for them, and re-layouts  5.47 us (1%)
    pallas_call x1, Pallas kernels, experts(): pl.pallas_call(experts_kernel, grid=(5,), in_specs=[HBM, pl.BlockSpec((2...  96.5 us
    pallas_call x1, Pallas kernels, attend(): pl.pallas_call(attend_kernel, grid=(2 * BLOCKS,), in_specs=[pl.BlockSpec(...  61.9 us
    pallas_call x1, Pallas kernels, attend_back(): pl.pallas_call(attend_back_kernel, grid=(BLOCKS,), in_specs=[pl.BlockSpec...  56.3 us
    pallas_call x1, Pallas kernels, start(): pl.pallas_call(start_kernel, out_shape=(jax.ShapeDtypeStruct((SHARDS, row...  49.7 us
    pallas_call x1, Pallas kernels, tail(): pl.pallas_call(tail_kernel, out_shape=(jax.ShapeDtypeStruct((OWN, D), f32...  46.8 us
    pallas_call x1, Pallas kernels, grads_away(): pl.pallas_call(away_kernel, out_shape=(jax.ShapeDtypeStruct((OWN, D), f32...  36.5 us
    pallas_call x1, Pallas kernels, home(): pl.pallas_call(home_kernel, out_shape=(jax.ShapeDtypeStruct((OWN, D), f32...  18.8 us
    pallas_call x1, Pallas kernels, adam_lifting(): pl.pallas_call(adam_lifting_kernel, grid=(EXPERTS,), in_specs=[block, blo...  15.7 us
  transfers between devices with their start and end apart: 1, of which 0 were waited for; matrix products, arithmetic and copies ran while one was open for 2% of the time, Pallas kernels for 49%

profile of v6, /device:TPU:1, one launch (start us, length us, event | category | flops | bytes accessed | tf_op | source)
XLA Modules:
  0.0 417.6 jit_solution(9898431268043278156)
XLA Ops:
  7.2 0.0 all-gather.2.cloned.1.call-start
  7.3 0.0 copy-start.1
  7.3 49.7 %start.1 = (bf16[16,192,1536]{2,1,0:T(8,128)(2,1)}, bf16[16,96,384]{2,1,0:T(8,128)(2,1)}, bf16[8,192,1536]{2,1,0:T(8,128)(2,1)}, bf16[8,192,128]{2,1,0:T(8,128)(2,1)}, bf16[2,96,1280]{2,1,0:T(8,128)(2,1)}) custom-call(bf16[192,1536]{1,0:T(8,128)(2,1)} %x_ref.3, bf16[192,1536]{1,0:T(8,128)(2,1)} %y_ref.1, bf16[96,2560]{1,0:T(8,128)(2,1)} %w_ref.1, ...), custom_call_target="tpu_custom_call" | custom-call | tf_op jit(solution)/shard_map/start/pallas_call | solution.py:440
  57.0 0.0 copy-start
  57.0 1.2 slice_convert_fusion
  58.2 0.3 copy.45
  58.5 0.6 fusion.16
  59.1 0.0 copy-done.1
  59.1 0.7 copy.47
  59.8 0.0 copy-done
  59.9 0.7 pad.4.d_ref
  60.6 61.9 %attend.1 = (bf16[8,576,64]{2,1,0:T(8,128)(2,1)}, bf16[3072,64]{1,0:T(8,128)(2,1)}, bf16[3072,128]{1,0:T(8,128)(2,1)}, bf16[3072,1536]{1,0:T(8,128)(2,1)}, bf16[...) custom-call(bf16[3072,1536]{1,0:T(8,128)(2,1)} %bitcast.42, ...), custom_call_target="tpu_custom_call" | custom-call | tf_op jit(solution)/shard_map/attend/pallas_call | solution.py:1031
  122.5 18.8 %attended_home.1 = (f32[192,1536]{1,0:T(8,128)}, bf16[192,1536]{1,0:T(8,128)(2,1)}, bf16[640,1536]{1,0:T(8,128)(2,1)}, bf16[8,192,192]{2,1,0:T(8,128)(2,1)}, bf16[2,1536,768]{2,1,0:T(8,128)(2,1)}) custom-call(bf16[8,192,192]{2,1,0:T(8,128)(2,1)} %get-tuple-element.75.x_ref.a_ref, bf16[1536,768]{1,0:T(8,128)(2,1)} %bitcast.48, ...), custom_call_target="tpu_custom_call" | custom-call | tf_op jit(solution)/shard_map/attended_home/pallas_call | solution.py:541
  141.2 0.0 all-gather.2.cloned.1.call-update
  141.3 0.7 fusion.6.e_ref
  142.0 96.5 %experts.1 = (f32[192,1536]{1,0:T(8,128)}, f32[192,1536]{1,0:T(8,128)}, bf16[192,1280]{1,0:T(8,128)(2,1)}, bf16[2,48,1536]{2,1,0:T(8,128)(2,1)}) custom-call(bf16[192,1536]{1,0:T(8,128)(2,1)} %get-tuple-element.79.x_hbm, bf16[1536,1536]{1,0:T(8,128)(2,1)} %bitcast.45, bf16[1536,128]{1,0:T(8,128)(2,1)} %bitcast.59, bf16[1536,1280]{1,0:T(8,128)(2,1)} %bitcast.46, ...), custom_call_target="tpu_custom_call" | custom-call | tf_op jit(solution)/shard_map/experts/pallas_call | solution.py:1676
  238.6 36.5 %grads_away.1 = (f32[192,1536]{1,0:T(8,128)}, bf16[16,96,1536]{2,1,0:T(8,128)(2,1)}, bf16[8,192,192]{2,1,0:T(8,128)(2,1)}, bf16[2,96,1280]{2,1,0:T(8,128)(2,1)}, bf16[2,48,1536]{2,1,0:T(8,128)(2,1)}) custom-call(f32[192,1536]{1,0:T(8,128)} %get-tuple-element.84.du_ref, f32[192,1536]{1,0:T(8,128)} %get-tuple-element.85.mixed_ref, bf16[192,1536]{1,0:T(8,128)(2,1)} %y_ref.1, ...), custom_call_target="tpu_custom_call" | custom-call | tf_op jit(solution)/shard_map/grads_away/pallas_call | solution.py:657
  275.0 56.3 %attend_back.1 = (bf16[8,192,192]{2,1,0:T(8,128)(2,1)}, bf16[3072,128]{1,0:T(8,128)(2,1)}, bf16[16,96,320]{2,1,0:T(8,128)(2,1)}, bf16[96,1536]{1,0:T(8,128)(2,1)...) custom-call(bf16[8,576,64]{2,1,0:T(8,128)(2,1)} %get-tuple-element.72.q_ref, ...), custom_call_target="tpu_custom_call" | custom-call | tf_op jit(solution)/shard_map/attend_back/pallas_call | solution.py:1290
  331.4 1.3 slice.23
  332.6 15.7 %adam_lifting.1 = (f32[10,96,1024]{2,1,0:T(8,128)}, f32[10,96,1024]{2,1,0:T(8,128)}, f32[10,96,1024]{2,1,0:T(8,128)}, f32[96,128]{1,0:T(8,128)}) custom-call(bf16[10,96,1024]{2,1,0:T(8,128)(2,1)} %bitcast.44, bf16[10,96,1024]{2,1,0:T(8,128)(2,1)} %bitcast.51, bf16[10,96,1024]{2,1,0:T(8,128)(2,1)} %bitcast.52, bf16[8,96,1280]{2,1,0:T(8,128)(2,1)} %get-tuple-element.109.g_ref, ...), custom_call_target="tpu_custom_call" | custom-call | tf_op jit(solution)/shard_map/adam_lifting/pallas_call | solution.py:1811
  348.3 0.9 slice_reduce_fusion
  349.2 5.2 %convert_subtract_fusion = (f32[32,10,1536]{2,0,1:T(8,128)}, f32[32,10,1536]{2,0,1:T(8,128)}, f32[32,10,1536]{2,0,1:T(8,128)}) fusion(bf16[32,10,1536]{2,0,1:T(8,128)(2,1)S(1)} %copy-done, bf16[10,32,1536]{2,1,0:T(8,128)(2,1)S(1)} %bitcast.47, bf16[32,10,1536]{2,0,1:T(8,128)(2,1)} %param.40, bf16[32,10,1536]{2,0,1:T(8,128)(2,1)} %param.35), kind=kLoop, calls=%fused_computation.1 | loop fusion | flops 9338880 | bytes 9830400 | tf_op jit(solution)/shard_map/sub | solution.py:1775
  354.4 0.0 all-gather.2.cloned.1.call-done.w_hbm
  354.4 46.8 %tail.1 = (f32[192,1536]{1,0:T(8,128)}, bf16[8,96,320]{2,1,0:T(8,128)(2,1)}, bf16[96,1536]{1,0:T(8,128)(2,1)}) custom-call(bf16[8,192,192]{2,1,0:T(8,128)(2,1)} %get-tuple-element.96.dq_ref, bf16[16,192,128]{2,1,0:T(8,128)(2,1)} %bitcast.57, bf16[16,96,320]{2,1,0:T(8,128)(2,1)} %get-tuple-element.98.in_ref, bf16[96,1536]{1,0:T(8,128)(2,1)} %get-tuple-element.99.out_ref, ...), custom_call_target="tpu_custom_call" | custom-call | tf_op jit(solution)/shard_map/tail/pallas_call | solution.py:858
  401.2 0.0 copy-start.2
  401.3 0.0 copy-start.3
  401.3 0.0 copy-start.4
  401.3 7.5 %last.1 = (f32[192,1536]{1,0:T(8,128)}, f32[192,1536]{1,0:T(8,128)}, f32[96,2560]{1,0:T(8,128)}, f32[96,2560]{1,0:T(8,128)}, f32[96,2560]{1,0:T(8,128)}, /*index...) custom-call(f32[192,1536]{1,0:T(8,128)} %get-tuple-element.101.dh_ref, ...), custom_call_target="tpu_custom_call" | custom-call | tf_op jit(solution)/shard_map/last/pallas_call | solution.py:1752
  408.8 0.9 slice_reduce_fusion.1
  409.7 0.0 copy-done.2
  409.7 0.0 copy-done.3
  409.7 0.0 copy-done.4
  409.7 0.6 convert_subtract_fusion.1
  (2 shorter events, 0.0 us)
Async XLA Ops:
  7.2 347.3 %all-gather.2.cloned.1.call-start = ((), (), s32[]{:S(2)}) async-start(), calls=%async_computation | async-start | bytes 8355840 | tf_op jit(solution)/shard_map/all_gather | solution.py:1926
  7.3 51.8 %copy-start.1 = (bf16[96,1536]{1,0:T(8,128)(2,1)S(1)}, bf16[96,1536]{1,0:T(8,128)(2,1)}, u32[]{:S(2)}) copy-start(bf16[96,1536]{1,0:T(8,128)(2,1)} %wo_ref.1) | copy-start | bytes 884740
  57.0 2.9 copy-start
  401.2 8.5 %copy-start.2 = (bf16[2,96]{1,0:T(2,128)(2,1)S(1)}, bf16[2,96]{1,0:T(2,128)(2,1)}, u32[]{:S(2)}) copy-start(bf16[2,96]{1,0:T(2,128)(2,1)} %gain_hbm.1) | copy-start | bytes 1156
  401.3 8.5 %copy-start.3 = (bf16[2,96]{1,0:T(2,128)(2,1)S(1)}, bf16[2,96]{1,0:T(2,128)(2,1)}, u32[]{:S(2)}) copy-start(bf16[2,96]{1,0:T(2,128)(2,1)} %param.36) | copy-start | bytes 1156
  401.3 8.5 %copy-start.4 = (bf16[2,96]{1,0:T(2,128)(2,1)S(1)}, bf16[2,96]{1,0:T(2,128)(2,1)}, u32[]{:S(2)}) copy-start(bf16[2,96]{1,0:T(2,128)(2,1)} %param.31) | copy-start | bytes 1156
Sparse Core Ops, SparseCore 0:
  141.4 51.0 all-gather.1

commit v7 on v6

--- a/solution.py
+++ b/solution.py
@@ -1775,15 +1775,23 @@
     return (moment, variance, values - step_rate * (normed_step + decay_rate * values))
 
 
-def adam_lifting_kernel(w_ref, m_ref, s_ref, g_ref, code_ref, mo_ref, so_ref, wo_ref, dot_ref, grad):
+def adam_experts_kernel(
+    w_ref, m_ref, s_ref, g_ref, code_ref, dw_ref, dm_ref, ds_ref, dg_ref,
+    mo_ref, so_ref, wo_ref, dot_ref, dmo_ref, dso_ref, dwo_ref, grad, apart,
+):
     e = pl.program_id(0)
     first, last = (4 * e) // 5, (4 * e + 3) // 5
-    column = lax.broadcasted_iota(jnp.int32, (HID, FF_EXP), 1)
-    there = (column // 32) * 1024 + lax.rem(column, 32) + 32 * e
-    here = jnp.broadcast_to(code_ref[...], (HID, FF_EXP))
-    chosen_first = jnp.where(there == here + FLAT * first, 1.0, 0.0).astype(bf16)
-    skip = jnp.where(first == last, 1 << 20, 0)
-    chosen_last = jnp.where(there == here + (FLAT * last + skip), 1.0, 0.0).astype(bf16)
+
+    @pl.when(e == 0)
+    def _():
+        column = lax.broadcasted_iota(jnp.int32, (HID, FF_EXP), 1)
+        there = (column // 32) * 1024 + lax.rem(column, 32)
+        apart[...] = there - jnp.broadcast_to(code_ref[...], (HID, FF_EXP))
+
+    distances = apart[...]
+    chosen_first = jnp.where(distances == FLAT * first - 32 * e, 1.0, 0.0).astype(bf16)
+    other = jnp.where(first == last, 1 << 24, FLAT * last - 32 * e)
+    chosen_last = jnp.where(distances == other, 1.0, 0.0).astype(bf16)
 
     def both(p):
         return jnp.concatenate([g_ref[p][:, :HID], g_ref[p][:, HID:]], 0)
@@ -1803,13 +1811,18 @@
     mo_ref[0], so_ref[0], wo_ref[0] = adam(
         w_ref[0], m_ref[0], s_ref[0], grad[...], rate_lifting, weight_decay
     )
-
-
-def adam_lifting(weight, mean, square, grad, code):
+    dmo_ref[0], dso_ref[0], dwo_ref[0] = adam(
+        dw_ref[0], dm_ref[0], ds_ref[0], dg_ref[0].astype(f32), rate_lowering, weight_decay
+    )
+
+
+def adam_experts(weight, mean, square, grad, code, down, down_mean, down_square, down_grad):
     block = pl.BlockSpec((1, 96, 2 * FF_EXP), lambda e: (e, 0, 0))
     shape = jax.ShapeDtypeStruct(weight.shape, f32)
+    down_block = pl.BlockSpec((1, 32, D), lambda e: (e, 0, 0))
+    down_shape = jax.ShapeDtypeStruct(down.shape, f32)
     return pl.pallas_call(
-        adam_lifting_kernel,
+        adam_experts_kernel,
         grid=(EXPERTS,),
         in_specs=[
             block,
@@ -1817,13 +1830,21 @@
             block,
             pl.BlockSpec(grad.shape, lambda e: (0, 0, 0)),
             pl.BlockSpec(code.shape, lambda e: (0, 0)),
+            down_block,
+            down_block,
+            down_block,
+            down_block,
         ],
-        out_specs=(block, block, block, pl.BlockSpec((96, 128), lambda e: (0, 0))),
-        out_shape=(shape, shape, shape, jax.ShapeDtypeStruct((96, 128), f32)),
-        scratch_shapes=[pltpu.VMEM((96, 2 * FF_EXP), f32)],
+        out_specs=(block, block, block, pl.BlockSpec((96, 128), lambda e: (0, 0)))
+        + (down_block,) * 3,
+        out_shape=(shape, shape, shape, jax.ShapeDtypeStruct((96, 128), f32)) + (down_shape,) * 3,
+        scratch_shapes=[
+            pltpu.VMEM((96, 2 * FF_EXP), f32),
+            pltpu.VMEM((HID, FF_EXP), jnp.int32),
+        ],
         compiler_params=pltpu.CompilerParams(vmem_limit_bytes=62 * 2**20),
-        name="adam_lifting",
-    )(weight, mean, square, grad, code)
+        name="adam_experts",
+    )(weight, mean, square, grad, code, down, down_mean, down_square, down_grad)
 
 
 def last_kernel(
@@ -1937,17 +1958,18 @@
     dh, inward_sum, outward_sum = tail(
         dq, dkv.reshape(SHARDS, OWN, 128), inward_part, outward_own, inward_all, 7
     )
-    down_grad = (
-        down_got[:, :FLAT].reshape(EXPERTS, 32, D).transpose(1, 0, 2).astype(f32)
-    )
-
-    new_lifting = adam_lifting(
+    new_lifting = adam_experts(
         lifting_rows,
         mean_lifting.transpose(1, 0, 2),
         square_lifting.transpose(1, 0, 2),
         lift_got,
         codes[:, None],
-    )
+        lowering.transpose(1, 0, 2),
+        mean_lowering.transpose(1, 0, 2),
+        square_lowering.transpose(1, 0, 2),
+        down_got[:, :FLAT].reshape(EXPERTS, 32, D),
+    )
+    new_lowering = tuple(t.transpose(1, 0, 2) for t in new_lifting[4:])
     lifting_dot = new_lifting[3]
     new_lifting = tuple(t.transpose(1, 0, 2) for t in new_lifting[:3])
     last = one_step(
@@ -1964,9 +1986,6 @@
     input_grad, layer_output, new_inward, new_outward = last[0], last[1], last[2:6], last[6:9]
     gain_grad = jnp.stack([new_inward[3][:, 0], lifting_dot[:, 0]]) / gains
     new_gains = adam(norm_gains, mean_gains, square_gains, gain_grad, rate_gains, 0.0)
-    new_lowering = adam(
-        lowering, mean_lowering, square_lowering, down_grad, rate_lowering, weight_decay
-    )
     return (
         layer_output,
         input_grad,

time: 425 us -> 424 us (level)
  other arithmetic: 7.81 us -> 2.5 us
    sub x2 -> x1, other arithmetic: 5.83 us -> 0.6 us  [adam(): values - step_rate * (normed_step + decay_rate * values)]
  transfers between devices with their start and end apart: 1 -> 1, of which waited for: 0 -> 0; matrix products, arithmetic and copies ran while one was open for 2% -> 1% of each run, Pallas kernels for 49% -> 50%
where the time goes in v7:
time: 424 us; the launch traced here: 417 us
  Pallas kernels  392 us (92%)
  between operations  14.7 us (3%)
  local copies, waits for them, and re-layouts  7.35 us (2%)
    pallas_call x1, Pallas kernels, experts(): pl.pallas_call(experts_kernel, grid=(5,), in_specs=[HBM, pl.BlockSpec((2...  96.5 us
    pallas_call x1, Pallas kernels, attend(): pl.pallas_call(attend_kernel, grid=(2 * BLOCKS,), in_specs=[pl.BlockSpec(...  61.9 us
    pallas_call x1, Pallas kernels, attend_back(): pl.pallas_call(attend_back_kernel, grid=(BLOCKS,), in_specs=[pl.BlockSpec...  56.3 us
    pallas_call x1, Pallas kernels, start(): pl.pallas_call(start_kernel, out_shape=(jax.ShapeDtypeStruct((SHARDS, row...  49.7 us
    pallas_call x1, Pallas kernels, tail(): pl.pallas_call(tail_kernel, out_shape=(jax.ShapeDtypeStruct((OWN, D), f32...  47.5 us
    pallas_call x1, Pallas kernels, grads_away(): pl.pallas_call(away_kernel, out_shape=(jax.ShapeDtypeStruct((OWN, D), f32...  36.5 us
    pallas_call x1, Pallas kernels, home(): pl.pallas_call(home_kernel, out_shape=(jax.ShapeDtypeStruct((OWN, D), f32...  18.7 us
    pallas_call x1, Pallas kernels, adam_experts(): pl.pallas_call(adam_experts_kernel, grid=(EXPERTS,), in_specs=[block, blo...  17.9 us
  transfers between devices with their start and end apart: 1, of which 0 were waited for; matrix products, arithmetic and copies ran while one was open for 1% of the time, Pallas kernels for 50%

profile of v7, /device:TPU:1, one launch (start us, length us, event | category | flops | bytes accessed | tf_op | source)
XLA Modules:
  0.0 417.0 jit_solution(14368286474793385704)
XLA Ops:
  7.2 0.0 all-gather.2.cloned.1.call-start
  7.3 0.0 copy-start
  7.3 49.7 %start.1 = (bf16[16,192,1536]{2,1,0:T(8,128)(2,1)}, bf16[16,96,384]{2,1,0:T(8,128)(2,1)}, bf16[8,192,1536]{2,1,0:T(8,128)(2,1)}, bf16[8,192,128]{2,1,0:T(8,128)(2,1)}, bf16[2,96,1280]{2,1,0:T(8,128)(2,1)}) custom-call(bf16[192,1536]{1,0:T(8,128)(2,1)} %x_ref.3, bf16[192,1536]{1,0:T(8,128)(2,1)} %y_ref.1, bf16[96,2560]{1,0:T(8,128)(2,1)} %w_ref.1, ...), custom_call_target="tpu_custom_call" | custom-call | tf_op jit(solution)/shard_map/start/pallas_call | solution.py:440
  57.0 1.2 slice_convert_fusion
  58.1 0.3 copy.45
  58.4 0.6 fusion.9
  59.0 0.0 copy-done
  59.0 0.7 copy.47
  59.8 1.0 constant_dynamic-slice_fusion
  60.7 0.7 pad.4.d_ref
  61.5 61.9 %attend.1 = (bf16[8,576,64]{2,1,0:T(8,128)(2,1)}, bf16[3072,64]{1,0:T(8,128)(2,1)}, bf16[3072,128]{1,0:T(8,128)(2,1)}, bf16[3072,1536]{1,0:T(8,128)(2,1)}, bf16[...) custom-call(bf16[3072,1536]{1,0:T(8,128)(2,1)} %bitcast.36, ...), custom_call_target="tpu_custom_call" | custom-call | tf_op jit(solution)/shard_map/attend/pallas_call | solution.py:1031
  123.3 18.7 %attended_home.1 = (f32[192,1536]{1,0:T(8,128)}, bf16[192,1536]{1,0:T(8,128)(2,1)}, bf16[640,1536]{1,0:T(8,128)(2,1)}, bf16[8,192,192]{2,1,0:T(8,128)(2,1)}, bf16[2,1536,768]{2,1,0:T(8,128)(2,1)}) custom-call(bf16[8,192,192]{2,1,0:T(8,128)(2,1)} %get-tuple-element.78.x_ref.a_ref, bf16[1536,768]{1,0:T(8,128)(2,1)} %bitcast.42, ...), custom_call_target="tpu_custom_call" | custom-call | tf_op jit(solution)/shard_map/attended_home/pallas_call | solution.py:541
  142.1 0.0 all-gather.2.cloned.1.call-update
  142.1 0.7 fusion.1.e_ref
  142.9 96.5 %experts.1 = (f32[192,1536]{1,0:T(8,128)}, f32[192,1536]{1,0:T(8,128)}, bf16[192,1280]{1,0:T(8,128)(2,1)}, bf16[2,48,1536]{2,1,0:T(8,128)(2,1)}) custom-call(bf16[192,1536]{1,0:T(8,128)(2,1)} %get-tuple-element.82.x_hbm, bf16[1536,1536]{1,0:T(8,128)(2,1)} %bitcast.39, bf16[1536,128]{1,0:T(8,128)(2,1)} %bitcast.56, bf16[1536,1280]{1,0:T(8,128)(2,1)} %bitcast.40, ...), custom_call_target="tpu_custom_call" | custom-call | tf_op jit(solution)/shard_map/experts/pallas_call | solution.py:1676
  239.4 36.5 %grads_away.1 = (f32[192,1536]{1,0:T(8,128)}, bf16[16,96,1536]{2,1,0:T(8,128)(2,1)}, bf16[8,192,192]{2,1,0:T(8,128)(2,1)}, bf16[2,96,1280]{2,1,0:T(8,128)(2,1)}, bf16[2,48,1536]{2,1,0:T(8,128)(2,1)}) custom-call(f32[192,1536]{1,0:T(8,128)} %get-tuple-element.87.du_ref, f32[192,1536]{1,0:T(8,128)} %get-tuple-element.88.mixed_ref, bf16[192,1536]{1,0:T(8,128)(2,1)} %y_ref.1, ...), custom_call_target="tpu_custom_call" | custom-call | tf_op jit(solution)/shard_map/grads_away/pallas_call | solution.py:657
  275.9 56.3 %attend_back.1 = (bf16[8,192,192]{2,1,0:T(8,128)(2,1)}, bf16[3072,128]{1,0:T(8,128)(2,1)}, bf16[16,96,320]{2,1,0:T(8,128)(2,1)}, bf16[96,1536]{1,0:T(8,128)(2,1)...) custom-call(bf16[8,576,64]{2,1,0:T(8,128)(2,1)} %get-tuple-element.75.q_ref, ...), custom_call_target="tpu_custom_call" | custom-call | tf_op jit(solution)/shard_map/attend_back/pallas_call | solution.py:1290
  332.2 2.2 slice.22
  334.4 17.9 %adam_experts.1 = (f32[10,96,1024]{2,1,0:T(8,128)}, f32[10,96,1024]{2,1,0:T(8,128)}, f32[10,96,1024]{2,1,0:T(8,128)}, f32[96,128]{1,0:T(8,128)}, f32[10,32,1536]...) custom-call(bf16[10,96,1024]{2,1,0:T(8,128)(2,1)} %bitcast.38, bf16[10,96,1024]{2,1,0:T(8,128)(2,1)} %bitcast.45, ...), custom_call_target="tpu_custom_call" | custom-call | tf_op jit(solution)/shard_map/adam_experts/pallas_call | solution.py:1824
  352.2 0.9 slice_reduce_fusion
  353.1 0.0 all-gather.2.cloned.1.call-done.w_hbm
  353.2 47.5 %tail.1 = (f32[192,1536]{1,0:T(8,128)}, bf16[8,96,320]{2,1,0:T(8,128)(2,1)}, bf16[96,1536]{1,0:T(8,128)(2,1)}) custom-call(bf16[8,192,192]{2,1,0:T(8,128)(2,1)} %get-tuple-element.99.dq_ref, bf16[16,192,128]{2,1,0:T(8,128)(2,1)} %bitcast.54, bf16[16,96,320]{2,1,0:T(8,128)(2,1)} %get-tuple-element.101.in_ref, bf16[96,1536]{1,0:T(8,128)(2,1)} %get-tuple-element.102.out_ref, ...), custom_call_target="tpu_custom_call" | custom-call | tf_op jit(solution)/shard_map/tail/pallas_call | solution.py:858
  400.6 0.0 copy-start.1
  400.6 0.0 copy-start.2
  400.7 0.0 copy-start.3
  400.7 7.5 %last.1 = (f32[192,1536]{1,0:T(8,128)}, f32[192,1536]{1,0:T(8,128)}, f32[96,2560]{1,0:T(8,128)}, f32[96,2560]{1,0:T(8,128)}, f32[96,2560]{1,0:T(8,128)}, /*index...) custom-call(f32[192,1536]{1,0:T(8,128)} %get-tuple-element.104.dh_ref, ...), custom_call_target="tpu_custom_call" | custom-call | tf_op jit(solution)/shard_map/last/pallas_call | solution.py:1752
  408.2 0.9 slice_reduce_fusion.1
  409.1 0.0 copy-done.1
  409.1 0.0 copy-done.2
  409.1 0.0 copy-done.3
  409.1 0.6 convert_subtract_fusion
  (1 shorter events, 0.0 us)
Async XLA Ops:
  7.2 346.0 %all-gather.2.cloned.1.call-start = ((), (), s32[]{:S(2)}) async-start(), calls=%async_computation | async-start | bytes 8355840 | tf_op jit(solution)/shard_map/all_gather | solution.py:1947
  7.3 51.8 %copy-start = (bf16[96,1536]{1,0:T(8,128)(2,1)S(1)}, bf16[96,1536]{1,0:T(8,128)(2,1)}, u32[]{:S(2)}) copy-start(bf16[96,1536]{1,0:T(8,128)(2,1)} %wo_ref.1) | copy-start | bytes 884740
  400.6 8.5 %copy-start.1 = (bf16[2,96]{1,0:T(2,128)(2,1)S(1)}, bf16[2,96]{1,0:T(2,128)(2,1)}, u32[]{:S(2)}) copy-start(bf16[2,96]{1,0:T(2,128)(2,1)} %gain_hbm.1) | copy-start | bytes 1156
  400.6 8.5 %copy-start.2 = (bf16[2,96]{1,0:T(2,128)(2,1)S(1)}, bf16[2,96]{1,0:T(2,128)(2,1)}, u32[]{:S(2)}) copy-start(bf16[2,96]{1,0:T(2,128)(2,1)} %param.36) | copy-start | bytes 1156
  400.7 8.5 %copy-start.3 = (bf16[2,96]{1,0:T(2,128)(2,1)S(1)}, bf16[2,96]{1,0:T(2,128)(2,1)}, u32[]{:S(2)}) copy-start(bf16[2,96]{1,0:T(2,128)(2,1)} %param.31) | copy-start | bytes 1156
Sparse Core Ops, SparseCore 0:
  142.2 51.0 all-gather.1
